TPU v7x, 256 devices: a whole 4x4x8 slice. The times are simulated.
256 devices in a mesh: dp: 8 (over x, core), feat: 32 (over z, y).
Axes of the slice: x: 4, y: 4, z: 8, core: 2. Of those that a mesh axis runs over, the one named last changes fastest.
Arguments:
- feature_table: bfloat16 [768, 32768], P('feat'), may hold values from -6 to 6
- node_ids: int32 [131072], P('dp'), may hold values from 0 to 32767
- hop_cols: int32 [256, 8], P('dp'), may hold values from 0 to 127
- hop_tiles: bfloat16 [256, 8, 128, 128], P('dp'), may hold values from -0.1875 to 0.1875
- target_cols: int32 [64, 8], P('dp'), may hold values from 0 to 31
- target_tiles: bfloat16 [64, 8, 128, 128], P('dp'), may hold values from -0.1875 to 0.1875
- self_weight: bfloat16 [768, 1024], P('feat'), may hold values from -0.21875 to 0.21875
- neigh_weight: bfloat16 [768, 1024], P('feat'), may hold values from -0.21875 to 0.21875
- hidden_bias: float32 [1024], P('feat'), may hold values from -3 to 3
- head_self: bfloat16 [1024, 153], P('feat'), may hold values from -0.25 to 0.25
- head_neigh: bfloat16 [1024, 153], P('feat'), may hold values from -0.25 to 0.25
- batch_sizes: int32 [8], replicated, may hold values from 256 to 1024, as said below
- logit_cotangent: bfloat16 [153, 8192], P(None, 'dp'), may hold values from -6 to 6
Outputs:
- logits: float32 [153, 8192], P(None, 'dp')
- grad_self: float32 [768, 1024], P('feat')
- grad_neigh: float32 [768, 1024], P('feat')
- grad_head_self: float32 [1024, 153], P('feat')
- grad_head_neigh: float32 [1024, 153], P('feat')
- grad_bias: float32 [1024], P('feat')
Inputs may be any that keep to these rules, and one draw needn't show every extreme that they name: `batch_sizes`: at least one mini-batch has exactly 1024 live targets.
All inputs are finite; a program needn't handle non-finite values.
Results may differ from a plain program's by a relative error of at most 0.024.
The roundings to bfloat16 on the way count: a program that leaves them out, or rounds other values in their place, can miss the bound.
Values may be sent and summed in bfloat16 or wider, within the bound.
No kernel may reach another device: no remote copies, remote signals or barrier semaphores. Data moves between devices by JAX's collectives and lax.ppermute only.
A program may use at most 128 MiB of HBM per device.

v0:
```python
import jax
import jax.numpy as jnp
from jax import lax
from jax.sharding import PartitionSpec as P


def aggregate(source, tile_cols, tile_vals):
    width = tile_vals.shape[-1]
    blocks = source.reshape(source.shape[0], -1, width)
    chosen = blocks[:, tile_cols]
    merged = jnp.einsum("pmkj,mkij->pmi", chosen, tile_vals, preferred_element_type=jnp.float32)
    return merged.reshape(source.shape[0], -1)


def spread_back(grads, tile_cols, tile_vals, count):
    width = tile_vals.shape[-1]
    shaped = grads.reshape(grads.shape[0], -1, width)
    pieces = jnp.einsum("pmi,mkij->pmkj", shaped, tile_vals, preferred_element_type=jnp.float32)
    total = jnp.zeros((grads.shape[0], count, width), jnp.float32).at[:, tile_cols].add(pieces)
    return total.reshape(grads.shape[0], -1)


def contract_nodes(left, right):
    return lax.dot_general(
        left, right, (((1,), (1,)), ((), ())), preferred_element_type=jnp.float32
    )


def shards(
    feature_table,
    node_ids,
    hop_cols,
    hop_tiles,
    target_cols,
    target_tiles,
    self_weight,
    neigh_weight,
    hidden_bias,
    head_self,
    head_neigh,
    batch_sizes,
    logit_cotangent,
):
    width = hop_tiles.shape[-1]
    first_rows = hop_cols.shape[0] * width
    target_rows = logit_cotangent.shape[1]
    features = jnp.take(feature_table, node_ids, axis=1)
    own_rows = features[:, :first_rows]
    first_agg = aggregate(features, hop_cols, hop_tiles).astype(jnp.bfloat16)
    term = jnp.dot(self_weight.T, own_rows, preferred_element_type=jnp.float32)
    preact = lax.psum_scatter(
        term + jnp.dot(neigh_weight.T, first_agg, preferred_element_type=jnp.float32),
        "feat",
        scatter_dimension=0,
        tiled=True,
    )
    preact = preact + hidden_bias[:, None]
    hidden = jnp.maximum(preact, 0.0).astype(jnp.bfloat16)
    second_agg = aggregate(hidden, target_cols, target_tiles).astype(jnp.bfloat16)
    targets = hidden[:, :target_rows]
    partial_scores = jnp.dot(head_self.T, targets, preferred_element_type=jnp.float32)
    partial_scores = partial_scores + jnp.dot(
        head_neigh.T, second_agg, preferred_element_type=jnp.float32
    )
    logits = lax.psum(partial_scores.astype(jnp.bfloat16), "feat").astype(jnp.float32)
    live_count = batch_sizes[lax.axis_index("dp")]
    live = jnp.arange(target_rows)[None, :] < live_count
    cot = jnp.where(live, logit_cotangent, jnp.zeros_like(logit_cotangent))
    back_agg = jnp.dot(head_neigh, cot, preferred_element_type=jnp.float32).astype(jnp.bfloat16)
    direct = jnp.dot(head_self, cot, preferred_element_type=jnp.float32)
    dhidden = spread_back(back_agg, target_cols, target_tiles, first_rows // width)
    dhidden = dhidden.at[:, :target_rows].add(direct)
    dpre = jnp.where(preact > 0.0, dhidden, jnp.zeros_like(dhidden))
    dpre_low = dpre.astype(jnp.bfloat16)
    bias_grad = jnp.sum(dpre, axis=1)
    head_grad_self = jnp.dot(targets, cot.T, preferred_element_type=jnp.float32)
    head_grad_neigh = jnp.dot(second_agg, cot.T, preferred_element_type=jnp.float32)
    piece = lax.all_gather(dpre_low, "feat", axis=0, tiled=True)
    stacked = jnp.stack([contract_nodes(own_rows, piece), contract_nodes(first_agg, piece)])
    first_self = stacked[0]
    first_neigh = stacked[1]
    summed = lax.psum((first_self, first_neigh, head_grad_self, head_grad_neigh, bias_grad), "dp")
    return (logits, summed[0], summed[1], summed[2], summed[3], summed[4])


def solution(mesh):
    return jax.shard_map(
        shards,
        mesh=mesh,
        in_specs=(
            P("feat", None),
            P("dp"),
            P("dp", None),
            P("dp", None, None, None),
            P("dp", None),
            P("dp", None, None, None),
            P("feat", None),
            P("feat", None),
            P("feat"),
            P("feat", None),
            P("feat", None),
            P(),
            P(None, "dp"),
        ),
        out_specs=(
            P(None, "dp"),
            P("feat", None),
            P("feat", None),
            P("feat", None),
            P("feat", None),
            P("feat"),
        ),
        check_vma=False,
    )
```

profile of v0, /device:TPU:1, one launch (start us, length us, event | category | flops | bytes accessed | tf_op | source)
XLA Modules:
  0.0 704.6 jit_solution(1727248376669056351)
XLA Ops:
  7.2 0.0 reduce-scatter.4.cloned.1.call-start
  7.2 1.0 fusion.32
  8.2 0.9 fusion.54
  9.1 0.9 compare_and_fusion
  10.0 7.4 %copy.43 = bf16[24,32768]{0,1:T(8,128)(2,1)} copy(bf16[24,32768]{1,0:T(8,128)(2,1)} %param.15) | data formatting | bytes 3145728 | tf_op args[0]
  17.4 0.1 copy.44
  17.5 0.1 reshape.81
  17.6 59.4 %gather_fusion = bf16[16384,24]{1,0:T(8,128)(2,1)} fusion(bf16[24,32768]{0,1:T(8,128)(2,1)} %copy.43, s32[16384]{0:T(1024)S(1)} %fusion.32), kind=kCustom, calls=%fused_computation | custom fusion | bytes 1638400 | tf_op jit(solution)/shard_map/jit(_take)/gather | solution.py:47
  77.0 7.7 %broadcast_select_fusion = bf16[24,128,128]{0,2,1:T(8,128)(2,1)} fusion(bf16[24,128,128]{0,2,1:T(8,128)(2,1)} %bitcast.87, pred[128,128]{1,0:T(8,128)(4,1)S(1)} %fusion.54), kind=kLoop, calls=%fused_computation.5 | loop fusion | flops 393216 | bytes 1589248 | tf_op jit(solution)/shard_map/jit(_take)/select_n | solution.py:47
  84.7 10.8 %gather_fusion.1 = bf16[256,24,128]{1,2,0:T(8,128)(2,1)} fusion(bf16[24,128,128]{0,2,1:T(8,128)(2,1)} %broadcast_select_fusion, s32[1024]{0:T(1024)S(1)} %pad_clamp_fusion.1), kind=kCustom, calls=%fused_computation.1 | custom fusion | bytes 3146752 | tf_op jit(solution)/shard_map/gather | solution.py:10
  95.5 7.8 %copy.45 = bf16[256,24,128]{2,1,0:T(8,128)(2,1)} copy(bf16[256,24,128]{1,2,0:T(8,128)(2,1)} %gather_fusion.1) | data formatting | bytes 3145728 | tf_op jit(solution)/shard_map/gather | solution.py:10
  103.2 6.2 fusion.3
  109.4 2.4 fusion.15
  111.9 8.1 %add_bitcast_fusion = f32[1024,4096]{0,1:T(8,128)} fusion(f32[4096,1024]{1,0:T(8,128)S(1)} %fusion.15, bf16[24,1024]{1,0:T(8,128)(2,1)S(1)} %copy-done.5, bf16[24,16384]{0,1:T(8,128)(2,1)} %bitcast.88, pred[4096]{0:T(1024)(128)(4,1)S(1)} %slice.34), kind=kOutput, calls=%fused_computation.4 | convolution fusion | flops 205619200 | bytes 34656256 | tf_op jit(solution)/shard_map/dot_general | solution.py:50
  120.0 17.5 %copy.57 = f32[1024,4096]{1,0:T(8,128)} copy(f32[1024,4096]{0,1:T(8,128)} %add_bitcast_fusion) | data formatting | bytes 33554432
  137.5 0.0 reduce-scatter.4.cloned.1.call-update
  137.5 0.0 all-gather.2.cloned.1.call-start
  137.6 0.6 copy-done.13
  138.1 0.6 dynamic_slice.3
  138.7 0.6 iota_compare_fusion
  139.4 0.2 fusion.8
  139.6 0.1 reshape.89
  139.7 1.4 fusion.25
  141.1 6.1 scatter_fusion
  147.3 0.6 compare_reduce_fusion
  148.0 1.8 fusion.6
  149.8 232.5 %reduce-scatter.4.cloned.1.call-done = f32[32,4096]{1,0:T(8,128)} async-done(((f32[1024,4096]{1,0:T(8,128)}), f32[32,4096]{1,0:T(8,128)}) %reduce-scatter.4.cloned.1.call-update) | async-done | bytes 524304 | tf_op jit(solution)/shard_map/reduce_scatter | solution.py:51
  382.3 1.9 fusion.34
  384.2 0.0 all-gather.2.cloned.1.call-update
  384.2 0.2 all-reduce.5.cloned.1.call-start
  384.5 1.3 fusion.33
  385.8 0.7 copy-done.2
  386.6 0.7 gather_fusion.2
  387.2 0.8 fusion.9
  388.0 1.2 fusion.11
  389.2 0.3 fusion.30
  389.5 1.0 fusion.1
  390.5 0.0 all-reduce.7.cloned.1.call-start
  390.6 94.9 %all-gather.2.cloned.1.call-done = bf16[1024,4096]{1,0:T(8,128)(2,1)} async-done(((bf16[32,4096]{1,0:T(8,128)(2,1)}), bf16[1024,4096]{1,0:T(8,128)(2,1)}) %all-gather.2.cloned.1.call-update) | async-done | bytes 8388624 | tf_op jit(solution)/shard_map/all_gather | solution.py:78
  485.5 6.5 fusion.10
  492.0 2.9 fusion.13
  494.9 0.2 fusion.12
  495.1 24.9 %all-reduce = (f32[32,153]{1,0:T(8,128)}, f32[32,153]{1,0:T(8,128)}, f32[32]{0:T(128)}) all-reduce(f32[32,153]{1,0:T(8,128)S(1)} %fusion.12, f32[32,153]{1,0:T(8,128)S(1)} %fusion.11, f32[32]{0:T(128)S(1)} %get-tuple-element.23), channel_id=1, replica_groups=mesh['dp'=8,'feat'=32] {'dp'}, use_global_device_ids=true, to_apply=%region_6.7 | all-reduce | flops 9824 | bytes 78592 | tf_op jit(solution)/shard_map/psum | solution.py:82
  520.0 107.3 %all-reduce.5.cloned.1.call-done = bf16[153,1024]{1,0:T(8,128)(2,1)} async-done(((bf16[153,1024]{1,0:T(8,128)(2,1)}), bf16[153,1024]{1,0:T(8,128)(2,1)}) %all-reduce.5.cloned.1.call-update) | async-done | bytes 313360 | tf_op jit(solution)/shard_map/psum | solution.py:65
  627.3 1.9 convert_element_type.48
  629.2 65.8 %all-reduce.7.cloned.1.call-done = (f32[24,1024]{1,0:T(8,128)}, f32[24,1024]{1,0:T(8,128)}) async-done(((f32[24,1024]{1,0:T(8,128)}, f32[24,1024]{1,0:T(8,128)}), (f32[24,1024]{1,0:T(8,128)}, f32[24,1024]{1,0:T(8,128)})) %all-reduce.7.cloned.1.call-update) | async-done | bytes 196624 | tf_op jit(solution)/shard_map/psum | solution.py:82
  695.0 1.5 copy.89
  696.5 1.5 copy.90
  (37 shorter events, 0.3 us)
Async XLA Ops:
  7.2 132.5 %copy-start = (bf16[8,8,128,128]{3,2,1,0:T(8,128)(2,1)S(1)}, bf16[8,8,128,128]{3,2,1,0:T(8,128)(2,1)}, u32[]{:S(2)}) copy-start(bf16[8,8,128,128]{3,2,1,0:T(8,128)(2,1)} %param.20) | copy-start | bytes 6291460
  7.2 375.1 %reduce-scatter.4.cloned.1.call-start = ((), (), s32[]{:S(2)}) async-start(), calls=%async_computation.3 | async-start | bytes 17301504 | tf_op jit(solution)/shard_map/reduce_scatter | solution.py:51
  10.0 7.4 %copy-start.8 = (s32[32,8]{0,1:T(8,128)S(1)}, s32[32,8]{0,1:T(8,128)}, u32[]{:S(2)}) copy-start(s32[32,8]{0,1:T(8,128)} %param.17) | copy-start | bytes 3076
  103.2 6.2 copy-start.4
  109.4 2.4 copy-start.5
  137.5 0.7 copy-start.13
  137.5 1.9 copy-start.6
  137.5 1.9 copy-start.11
  137.5 2.1 copy-start.9
  137.5 348.0 %all-gather.2.cloned.1.call-start = ((), (), s32[]{:S(2)}) async-start(), calls=%async_computation.2 | async-start | bytes 8650752 | tf_op jit(solution)/shard_map/all_gather | solution.py:78
  139.4 8.6 %copy-start.7 = (bf16[32,153]{1,0:T(8,128)(2,1)S(1)}, bf16[32,153]{1,0:T(8,128)(2,1)}, u32[]{:S(2)}) copy-start(bf16[32,153]{1,0:T(8,128)(2,1)} %param.24) | copy-start | bytes 29380
  139.7 242.6 %copy-start.10 = (f32[32]{0:T(128)S(1)}, f32[32]{0:T(128)}, u32[]{:S(2)}) copy-start(f32[32]{0:T(128)} %param.23) | copy-start | bytes 388
  384.2 243.1 %all-reduce.5.cloned.1.call-start = ((), (), s32[]{:S(2)}) async-start(), calls=%async_computation.1 | async-start | bytes 655360 | tf_op jit(solution)/shard_map/psum | solution.py:65
  385.8 0.7 copy-start.2
  386.5 2.7 copy-start.3
  390.5 304.4 %all-reduce.7.cloned.1.call-start = ((), (), s32[]{:S(2)}) async-start(), calls=%async_computation.4 | async-start | bytes 393216 | tf_op jit(solution)/shard_map/psum | solution.py:82
  485.5 6.5 copy-start.1
  492.0 3.0 copy-start.12
Sparse Core Ops, SparseCore 0:
  137.6 244.6 reduce-scatter.3
  384.9 100.5 all-gather.1
  489.5 137.7 all-reduce.4
  630.3 64.6 all-reduce.6
where the time goes:
time: 707 us; the launch traced here: 705 us
  waiting for transfers between devices  501 us (71%)
  local copies, waits for them, and re-layouts  109 us (15%)
  matrix products  32.9 us (5%)
  blocking collectives  24.9 us (4%)
  other arithmetic  22.9 us (3%)
  between operations  14 us (2%)
    reduce_scatter x1, waiting for transfers between devices, shards(): lax.psum_scatter(term + jnp.dot(neigh_weight.T, first_agg, preferred_elem...  233 us
    psum x1, waiting for transfers between devices, shards(): lax.psum(partial_scores.astype(jnp.bfloat16), 'feat').astype(jnp.float32)  107 us
    all_gather x1, waiting for transfers between devices, shards(): piece = lax.all_gather(dpre_low, 'feat', axis=0, tiled=True)  94.9 us
    psum x1, waiting for transfers between devices, shards(): lax.psum((first_self, first_neigh, head_grad_self, head_grad_neigh, bias_...  65.8 us
    gather x1, local copies, waits for them, and re-layouts, shards(): features = jnp.take(feature_table, node_ids, axis=1)  59.4 us
    unnamed x33, local copies, waits for them, and re-layouts  29.3 us
    psum x1, blocking collectives, shards(): lax.psum((first_self, first_neigh, head_grad_self, head_grad_neigh, bias_...  24.9 us
    gather x3, local copies, waits for them, and re-layouts, aggregate(): chosen = blocks[:, tile_cols]  19.2 us
  transfers between devices with their start and end apart: 4, of which 4 were waited for; matrix products, arithmetic and copies ran while one was open for 4% of the time, Pallas kernels for 0%

commit v1 on v0

v1 whole, which is shorter than its diff:
```python
import jax
import jax.numpy as jnp
from jax import lax
from jax.experimental import pallas as pl
from jax.experimental.pallas import tpu as pltpu
from jax.sharding import Mesh, PartitionSpec as P

TILE = 128
FEAT = ("z", "y")
DP = ("x", "core")
CLS = 192
BF = jnp.bfloat16
F32 = jnp.float32
NT = (((1,), (1,)), ((), ()))
VMEM = pl.BlockSpec(memory_space=pltpu.VMEM)
SMEM = pl.BlockSpec(memory_space=pltpu.SMEM)
HBM = pl.BlockSpec(memory_space=pl.ANY)
LIMIT = pltpu.CompilerParams(vmem_limit_bytes=56 * 2**20)


def aligned(index, size):
    return pl.ds(pl.multiple_of(index * size, size), size)


def hop_kernel(ids, cols, table, tiles_hbm, out, rows, picked, tiles, sem):
    width = table.shape[0]
    blocks = tiles.shape[0]
    group = blocks // 8
    copies = [
        pltpu.make_async_copy(
            tiles_hbm.at[pl.ds(j * group, group)], tiles.at[pl.ds(j * group, group)], sem.at[j]
        )
        for j in range(8)
    ]
    for copy in copies:
        copy.start()

    def turn(b, carry):
        rows[aligned(b, TILE), 0:width] = table[:, aligned(b, TILE)].astype(F32).T
        return carry

    lax.fori_loop(0, table.shape[1] // TILE, turn, 0, unroll=8)
    step = 64

    def pick(g, carry):
        base = pl.multiple_of(g * step, step)
        for u in range(step):
            picked[pl.ds(base + u, 1), :] = rows[pl.ds(ids[base + u], 1), :]
        return carry

    lax.fori_loop(0, ids.shape[0] // step, pick, 0)
    for copy in copies:
        copy.wait()

    def merge(r, carry):
        out[r, 0:width, :] = picked[aligned(r, TILE), :].T[0:width].astype(BF)
        left = jnp.concatenate([tiles[r, k] for k in range(8)], axis=1)
        right = jnp.concatenate(
            [picked[aligned(cols[r * 8 + k], TILE), :].astype(BF) for k in range(8)], axis=0
        )
        total = jnp.dot(left, right, preferred_element_type=F32)
        out[r, width : 2 * width, :] = total.T[0:width].astype(BF)
        return carry

    lax.fori_loop(0, blocks, merge, 0, unroll=2)


def hop(table, ids, cols, tiles):
    blocks = tiles.shape[0]
    return pl.pallas_call(
        hop_kernel,
        in_specs=[SMEM, SMEM, VMEM, HBM],
        out_specs=VMEM,
        scratch_shapes=[
            pltpu.VMEM((table.shape[1], TILE), F32),
            pltpu.VMEM((ids.shape[0], TILE), F32),
            pltpu.VMEM(tiles.shape, BF),
            pltpu.SemaphoreType.DMA((8,)),
        ],
        out_shape=jax.ShapeDtypeStruct((blocks, 2 * table.shape[0], TILE), BF),
        compiler_params=LIMIT,
        cost_estimate=pl.CostEstimate(flops=10**9, bytes_accessed=60 * 10**6, transcendentals=0),
    )(ids, cols.reshape(-1), table, tiles)


def spread_kernel(cols, back, direct, tiles, out):
    out[...] = jnp.zeros_like(out)
    for r in range(tiles.shape[0]):
        out[r] = direct[:, r * TILE : (r + 1) * TILE]
    for r in range(tiles.shape[0]):
        part = back[:, r * TILE : (r + 1) * TILE]
        for k in range(8):
            out[cols[r * 8 + k]] += jnp.dot(part, tiles[r, k], preferred_element_type=F32)


def spread(cols, back, direct, tiles, blocks):
    return pl.pallas_call(
        spread_kernel,
        in_specs=[SMEM, VMEM, VMEM, VMEM],
        out_specs=VMEM,
        out_shape=jax.ShapeDtypeStruct((blocks, back.shape[0], TILE), F32),
        compiler_params=LIMIT,
    )(cols.reshape(-1), back, direct, tiles)


def last_kernel(
    place, cols, hidden, dhidden, feats, tiles, cot, self_t, neigh_t, out, heads, second, total, bias
):
    y = place[0]
    groups, blocks, deep, _ = feats.shape
    own = pl.ds(pl.multiple_of(y * 32, 32), 32)
    for r in range(tiles.shape[0]):
        left = jnp.concatenate([hidden[cols[r * 8 + k]] for k in range(8)], axis=1)
        right = jnp.concatenate([tiles[r, k] for k in range(8)], axis=1)
        second[r] = lax.dot_general(left, right, NT, preferred_element_type=F32).astype(BF)
    for half in range(2):
        at = 2 * y + half
        scores = jnp.dot(self_t[...], hidden[at], preferred_element_type=F32)
        scores = scores + jnp.dot(neigh_t[...], second[at], preferred_element_type=F32)
        for z in range(groups):
            out[z, deep + 24 * half : deep + 24 * (half + 1), :] = scores[24 * z : 24 * (z + 1)]
    total[...] = jnp.zeros_like(total)
    bias[...] = jnp.zeros_like(bias)

    def grow(b, carry):
        kept = jnp.where(hidden[b].astype(F32) > 0.0, dhidden[b], 0.0)
        low = kept.astype(BF)
        stack = jnp.concatenate([feats[z, b] for z in range(groups)], axis=0)
        total[...] += lax.dot_general(stack, low, NT, preferred_element_type=F32)
        bias[...] += kept
        return carry

    lax.fori_loop(0, blocks, grow, 0, unroll=4)
    for z in range(groups):
        out[z, 0:deep, :] = total[z * deep : (z + 1) * deep]
    targets = jnp.concatenate([hidden[r, own, :] for r in range(tiles.shape[0])], axis=1)
    merged = jnp.concatenate([second[r, own, :] for r in range(tiles.shape[0])], axis=1)
    mine = jnp.sum(bias[own, :], axis=1, keepdims=True)
    lane = lax.broadcasted_iota(jnp.int32, (32, 256), 1)
    grad = lax.dot_general(targets, cot[...], NT, preferred_element_type=F32)
    heads[:, 0:256] = jnp.where(lane == 255, mine, grad)
    heads[:, 256:512] = lax.dot_general(merged, cot[...], NT, preferred_element_type=F32)


def last(place, cols, hidden, dhidden, feats, tiles, cot, self_t, neigh_t):
    groups, blocks, deep, _ = feats.shape
    return pl.pallas_call(
        last_kernel,
        in_specs=[SMEM, SMEM] + [VMEM] * 7,
        out_specs=[VMEM, VMEM],
        scratch_shapes=[
            pltpu.VMEM((tiles.shape[0], TILE, TILE), BF),
            pltpu.VMEM((groups * deep, TILE), F32),
            pltpu.VMEM((TILE, TILE), F32),
        ],
        out_shape=[
            jax.ShapeDtypeStruct((groups, deep + 48, TILE), F32),
            jax.ShapeDtypeStruct((32, 512), F32),
        ],
        compiler_params=LIMIT,
    )(place, cols.reshape(-1), hidden, dhidden, feats, tiles, cot, self_t, neigh_t)


def swap_core(value):
    return lax.ppermute(value, "core", [(0, 1), (1, 0)])


def sum_dp(value):
    value = value + swap_core(value)
    value = value + lax.ppermute(value, "x", [(0, 1), (1, 0), (2, 3), (3, 2)])
    return value + lax.ppermute(value, "x", [(0, 3), (3, 0), (1, 2), (2, 1)])


def shards(
    feature_table,
    node_ids,
    hop_cols,
    hop_tiles,
    target_cols,
    target_tiles,
    self_weight,
    neigh_weight,
    hidden_bias,
    head_self,
    head_neigh,
    batch_sizes,
    logit_cotangent,
):
    blocks = hop_cols.shape[0]
    classes, target_rows = logit_cotangent.shape
    first_core = lax.axis_index("core") == 0
    y = lax.axis_index("y")

    mine = lax.all_gather(
        jnp.where(first_core, self_weight, neigh_weight), FEAT, axis=0, tiled=True
    )
    other = swap_core(mine)

    every_bias = lax.all_to_all(
        jnp.broadcast_to(hidden_bias[None, None], (32, 1, 32)), FEAT, 0, 0, tiled=True
    ).reshape(-1)
    pair = jnp.concatenate([head_self, head_neigh], axis=1)
    pair = lax.all_to_all(
        jnp.broadcast_to(pair[None], (4,) + pair.shape), "y", 0, 0, tiled=True
    ).reshape(TILE, 2 * classes)
    heads_self, heads_neigh = pair[:, :classes], pair[:, classes:]

    live_count = batch_sizes[lax.axis_index("x") * 2 + lax.axis_index("core")]
    live = jnp.arange(target_rows)[None, :] < live_count
    cot = jnp.where(live, logit_cotangent, jnp.zeros_like(logit_cotangent))
    back_agg = jnp.dot(heads_neigh, cot, preferred_element_type=F32).astype(BF)
    direct = jnp.dot(heads_self, cot, preferred_element_type=F32)
    dhidden = spread(target_cols, back_agg, direct, target_tiles, blocks)

    send = hop(feature_table, node_ids, hop_cols, hop_tiles)
    feats = lax.all_gather(send, "z", axis=0, tiled=False)
    got = lax.all_to_all(send, FEAT, 0, 0, tiled=True)
    deep = feature_table.shape[0]
    own_rows = got[:, :deep].reshape(-1, TILE)
    first_agg = got[:, deep:].reshape(-1, TILE)
    with_mine = jnp.where(first_core, own_rows, first_agg)
    with_other = jnp.where(first_core, first_agg, own_rows)
    preact = jnp.dot(mine.T, with_mine, preferred_element_type=F32)
    preact = preact + jnp.dot(other.T, with_other, preferred_element_type=F32)
    preact = preact + every_bias[:, None]
    hidden = jnp.maximum(preact, 0.0).astype(BF)
    hidden = jnp.broadcast_to(hidden.reshape(8, 1, TILE, TILE), (8, 4, TILE, TILE))
    hidden = lax.all_to_all(hidden.reshape(32, TILE, TILE), FEAT, 0, 0, tiled=True)

    pad = ((0, CLS - classes), (0, 0))
    out, heads = last(
        y.reshape(1),
        target_cols,
        hidden,
        dhidden,
        feats,
        target_tiles,
        jnp.pad(cot, ((0, 256 - classes), (0, 0))),
        jnp.pad(heads_self.T, pad),
        jnp.pad(heads_neigh.T, pad),
    )
    out = lax.all_to_all(out, "z", 0, 0, tiled=True)
    scores = jnp.sum(out[:, 2 * deep :], axis=0).astype(BF)
    scores = lax.all_to_all(
        jnp.broadcast_to(scores[None], (32,) + scores.shape), FEAT, 0, 0, tiled=True
    )
    scores = scores.reshape(8, 4, 2, 24, TILE).transpose(0, 3, 1, 2, 4).reshape(CLS, target_rows)
    logits = scores[:classes].astype(F32)

    packed = jnp.concatenate(
        [out[:, : 2 * deep].reshape(-1, TILE), heads.reshape(-1, TILE)], axis=0
    )
    packed = sum_dp(packed)
    grads = packed[: 16 * deep].reshape(8, 2, deep, TILE).transpose(1, 2, 0, 3)
    grads = grads.reshape(2, deep, 8 * TILE)
    heads = packed[16 * deep :].reshape(32, 512)
    return (
        logits,
        grads[0],
        grads[1],
        heads[:, :classes],
        heads[:, 256 : 256 + classes],
        heads[:, 255],
    )


def solution(mesh):
    split = Mesh(mesh.devices.reshape(4, 2, 8, 4), DP + FEAT)
    return jax.shard_map(
        shards,
        mesh=split,
        in_specs=(
            P(FEAT, None),
            P(DP),
            P(DP, None),
            P(DP, None, None, None),
            P(DP, None),
            P(DP, None, None, None),
            P(FEAT, None),
            P(FEAT, None),
            P(FEAT),
            P(FEAT, None),
            P(FEAT, None),
            P(),
            P(None, DP),
        ),
        out_specs=(
            P(None, DP),
            P(FEAT, None),
            P(FEAT, None),
            P(FEAT, None),
            P(FEAT, None),
            P(FEAT),
        ),
        check_vma=False,
    )
```

time: 707 us -> 230 us (0.33)
  waiting for transfers between devices: 501 us -> 100 us
  local copies, waits for them, and re-layouts: 109 us -> 15.1 us
  Pallas kernels: 0 us -> 38.3 us
  starting transfers between devices: 0.34 us -> 35.6 us
  matrix products: 32.9 us -> 4.9 us
  other arithmetic: 22.9 us -> 5.99 us
  blocking collectives: 24.9 us -> 14.1 us
    reduce_scatter x1 -> x0, waiting for transfers between devices: 233 us -> none  [shards(): lax.psum_scatter(term + jnp.dot(neigh_weight.T, first_agg, preferred_elem...]
    psum x2 -> x0, waiting for transfers between devices: 173 us -> none  [the longest x1 107 us: shards(): lax.psum(partial_scores.astype(jnp.bfloat16), 'feat').astype(jnp.float32)]
    gather x4 -> x0, local copies, waits for them, and re-layouts: 78.6 us -> none  [the longest x1 59.4 us: shards(): features = jnp.take(feature_table, node_ids, axis=1)]
    all_gather x1 -> x2, waiting for transfers between devices: 94.9 us -> 51.1 us  [the longest x1 51.1 us: shards(): lax.all_gather(jnp.where(first_core, self_weight, neigh_weight), FEAT, ax...]
    all_to_all x0 -> x5, waiting for transfers between devices: none -> 42.5 us  [the longest x1 14.1 us: shards(): got = lax.all_to_all(send, FEAT, 0, 0, tiled=True)]
    pallas_call x0 -> x3, Pallas kernels: none -> 38.3 us  [the longest x1 26.6 us: hop(): pl.pallas_call(hop_kernel, in_specs=[SMEM, SMEM, VMEM, HBM], out_specs=VM...]
    dot_general x13 -> x4, matrix products: 32.9 us -> 4.9 us  [the longest x1 1.85 us: shards(): direct = jnp.dot(heads_self, cot, preferred_element_type=F32)]
    unnamed x33 -> x20, local copies, waits for them, and re-layouts: 29.3 us -> 3 us
  transfers between devices with their start and end apart: 4 -> 11, of which waited for: 4 -> 7; matrix products, arithmetic and copies ran while one was open for 4% -> 9% of each run, Pallas kernels for 0% -> 13%
where the time goes in v1:
time: 230 us; the launch traced here: 229 us
  waiting for transfers between devices  100 us (43%)
  Pallas kernels  38.3 us (17%)
  starting transfers between devices  35.6 us (15%)
  local copies, waits for them, and re-layouts  15.1 us (7%)
  between operations  14.3 us (6%)
  blocking collectives  14.1 us (6%)
  other arithmetic  5.99 us (3%)
  matrix products  4.9 us (2%)
    all_gather x1, waiting for transfers between devices, shards(): lax.all_gather(jnp.where(first_core, self_weight, neigh_weight), FEAT, ax...  51.1 us
    pallas_call x1, Pallas kernels, hop(): pl.pallas_call(hop_kernel, in_specs=[SMEM, SMEM, VMEM, HBM], out_specs=VM...  26.6 us
    all_to_all x1, waiting for transfers between devices, shards(): got = lax.all_to_all(send, FEAT, 0, 0, tiled=True)  14.1 us
    all_to_all x1, blocking collectives, shards(): lax.all_to_all(jnp.broadcast_to(hidden_bias[None, None], (32, 1, 32)), FE...  14.1 us
    ppermute x2, starting transfers between devices, swap_core(): return lax.ppermute(value, 'core', [(0, 1), (1, 0)])  11.1 us
    all_to_all x1, waiting for transfers between devices, shards(): lax.all_to_all(hidden.reshape(32, TILE, TILE), FEAT, 0, 0, tiled=True)  10.8 us
    all_to_all x1, waiting for transfers between devices, shards(): out = lax.all_to_all(out, 'z', 0, 0, tiled=True)  10 us
    pallas_call x1, Pallas kernels, last(): pl.pallas_call(last_kernel, in_specs=[SMEM, SMEM] + [VMEM] * 7, out_specs...  7.67 us
  transfers between devices with their start and end apart: 11, of which 7 were waited for; matrix products, arithmetic and copies ran while one was open for 9% of the time, Pallas kernels for 13%

profile of v1, /device:TPU:1, one launch (start us, length us, event | category | flops | bytes accessed | tf_op | source)
XLA Modules:
  0.0 228.6 jit_solution(14199123527588637582)
XLA Ops:
  7.2 1.4 broadcast_select_fusion.3
  8.7 0.8 copy.30
  9.5 0.7 reshape.74.cols
  10.2 26.6 %shard_map.172 = bf16[32,48,128]{2,1,0:T(8,128)(2,1)} custom-call(s32[16384]{0:T(1024)} %ids.1, s32[256]{0:T(256)} %reshape.74.cols, bf16[24,32768]{1,0:T(8,128)(2,1)} %table.1, bf16[32,8,128,128]{3,2,1,0:T(8,128)(2,1)} %tiles_hbm.1), custom_call_target="tpu_custom_call" | custom-call | flops 1000000000 | bytes 60000000 | tf_op jit(solution)/shard_map/pallas_call | solution.py:70
  36.8 51.1 %all-gather.4.cloned.1.call-done = bf16[768,1024]{1,0:T(8,128)(2,1)} async-done(((bf16[24,1024]{1,0:T(8,128)(2,1)}), bf16[768,1024]{1,0:T(8,128)(2,1)}) %all-gather.4.cloned.1.call-update) | async-done | bytes 1572880 | tf_op jit(solution)/shard_map/all_gather | solution.py:194
  87.9 5.1 %collective-permute-start = (bf16[768,1024]{1,0:T(8,128)(2,1)}, bf16[768,1024]{1,0:T(8,128)(2,1)S(1)}, u32[]{:S(2)}, u32[]{:S(2)}) collective-permute-start(bf16[768,1024]{1,0:T(8,128)(2,1)} %all-gather.4.cloned.1.call-done), channel_id=1, source_target_pairs={{0,32},{32,0},{1,33},{33,1},{2,34},{34,2},{3,35},{35,3},{4,36},{36... | collective-permute-start | bytes 4718600 | tf_op jit(solution)/shard_map/ppermute | solution.py:165
  93.0 14.1 %all_to_all.30 = f32[32,1,32]{2,1,0:T(1,128)} all-to-all(f32[32,1,32]{2,1,0:T(1,128)S(1)} %broadcast_in_dim.20), channel_id=1, replica_groups=mesh['x'=4,'core'=2,'z'=8,'y'=4] {'z','y'}, dimensions={0} | all-to-all | bytes 8192 | tf_op jit(solution)/shard_map/all_to_all | solution.py:199
  107.1 3.9 %all-to-all-start = ((bf16[32,48,128]{2,1,0:T(8,128)(2,1)}), bf16[32,48,128]{2,1,0:T(8,128)(2,1)S(1)}, u32[]{:S(2)}, u32[]{:S(2)}) async-start(bf16[32,48,128]{2,1,0:T(8,128)(2,1)} %shard_map.172), calls=%async_computation | async-start | bytes 786432 | tf_op jit(solution)/shard_map/all_to_all | solution.py:217
  111.0 1.4 pad_maximum_fusion.1
  112.4 0.5 broadcast.22
  112.9 1.4 reduce.5
  114.4 0.7 add.35
  115.0 14.1 %all-to-all-done = bf16[32,48,128]{2,1,0:T(8,128)(2,1)S(1)} async-done(((bf16[32,48,128]{2,1,0:T(8,128)(2,1)}), bf16[32,48,128]{2,1,0:T(8,128)(2,1)S(1)}, u32[]{:S(2)}, u32[]{:S(2)}) %all-to-all-start) | async-done | bytes 393248 | tf_op jit(solution)/shard_map/all_to_all | solution.py:217
  129.2 1.4 broadcast_in_dim.40
  130.6 4.3 %all-to-all-start.3 = ((bf16[4,32,306]{2,1,0:T(8,128)(2,1)}), bf16[4,32,306]{2,1,0:T(8,128)(2,1)}, u32[]{:S(2)}, u32[]{:S(2)}) async-start(bf16[4,32,306]{2,1,0:T(8,128)(2,1)} %broadcast_in_dim.40), calls=%async_computation.3 | async-start | bytes 196608 | tf_op jit(solution)/shard_map/all_to_all | solution.py:203
  134.9 0.6 fusion.11
  135.5 0.6 fusion.2
  136.2 3.4 %all-to-all-done.3 = bf16[4,32,306]{2,1,0:T(8,128)(2,1)} async-done(((bf16[4,32,306]{2,1,0:T(8,128)(2,1)}), bf16[4,32,306]{2,1,0:T(8,128)(2,1)}, u32[]{:S(2)}, u32[]{:S(2)}) %all-to-all-start.3) | async-done | bytes 78368 | tf_op jit(solution)/shard_map/all_to_all | solution.py:203
  139.6 1.2 broadcast_in_dim.22
  140.8 3.9 %all-to-all-start.2 = ((bf16[32,128,128]{2,1,0:T(8,128)(2,1)}), bf16[32,128,128]{2,1,0:T(8,128)(2,1)S(1)}, u32[]{:S(2)}, u32[]{:S(2)}) async-start(bf16[32,128,128]{2,1,0:T(8,128)(2,1)} %bitcast.4), calls=%async_computation.2 | async-start | bytes 2097152 | tf_op jit(solution)/shard_map/all_to_all | solution.py:228
  144.8 0.6 reshape.73.cols
  145.4 0.6 dynamic_slice.3
  146.0 0.6 iota_compare_fusion
  146.7 0.9 pad.11.cot
  147.5 1.0 fusion.9
  148.6 0.6 pad.12.self_t
  149.4 0.6 pad.13.neigh_t
  150.0 1.8 convolution_convert_fusion.back
  151.8 1.9 fusion.3.direct
  153.7 4.0 %shard_map.173.dhidden = f32[32,128,128]{2,1,0:T(8,128)} custom-call(s32[64]{0:T(128)} %reshape.73.cols, bf16[128,1024]{1,0:T(8,128)(2,1)} %convolution_convert_fusion.back, f32[128,1024]{1,0:T(8,128)} %fusion.3.direct, bf16[8,8,128,128]{3,2,1,0:T(8,128)(2,1)} %tiles.3), custom_call_target="tpu_custom_call" | custom-call | tf_op jit(solution)/shard_map/pallas_call | solution.py:97
  157.7 10.8 %all-to-all-done.2.hidden = bf16[32,128,128]{2,1,0:T(8,128)(2,1)S(1)} async-done(((bf16[32,128,128]{2,1,0:T(8,128)(2,1)}), bf16[32,128,128]{2,1,0:T(8,128)(2,1)S(1)}, u32[]{:S(2)}, u32[]{:S(2)}) %all-to-all-start.2) | async-done | bytes 1048608 | tf_op jit(solution)/shard_map/all_to_all | solution.py:228
  168.6 1.0 copy-done
  169.5 7.7 %shard_map.174 = (f32[8,96,128]{2,1,0:T(8,128)}, f32[32,512]{1,0:T(8,128)}) custom-call(s32[1]{0:T(128)} %bitcast.place, s32[64]{0:T(128)} %reshape.73.cols, bf16[32,128,128]{2,1,0:T(8,128)(2,1)} %copy-done, f32[32,128,128]{2,1,0:T(8,128)} %shard_map.173.dhidden, bf16[8,32,48,128]{3,2,1,0:T(8,128)(2,1)} %bitcast.32, bf16[8,8,128,128]{3,2,1,0:T(8,128)(2,1)} %tiles.3, ...), custom_call_target="tpu_custom_call" | custom-call | tf_op jit(solution)/shard_map/pallas_call | solution.py:147
  177.2 4.6 %all-to-all-start.4 = ((f32[8,96,128]{2,1,0:T(8,128)}), f32[8,96,128]{2,1,0:T(8,128)S(1)}, u32[]{:S(2)}, u32[]{:S(2)}) async-start(f32[8,96,128]{2,1,0:T(8,128)} %get-tuple-element.8), calls=%async_computation.4 | async-start | bytes 786432 | tf_op jit(solution)/shard_map/all_to_all | solution.py:242
  181.8 0.8 reshape.80
  182.7 10.0 %all-to-all-done.4 = f32[8,96,128]{2,1,0:T(8,128)S(1)} async-done(((f32[8,96,128]{2,1,0:T(8,128)}), f32[8,96,128]{2,1,0:T(8,128)S(1)}, u32[]{:S(2)}, u32[]{:S(2)}) %all-to-all-start.4) | async-done | bytes 393248 | tf_op jit(solution)/shard_map/all_to_all | solution.py:242
  192.7 6.0 %collective-permute-start.1 = (f32[512,128]{1,0:T(8,128)S(1)}, f32[512,128]{1,0:T(8,128)S(1)}, u32[]{:S(2)}, u32[]{:S(2)}) collective-permute-start(f32[512,128]{1,0:T(8,128)S(1)} %pad_maximum_fusion), channel_id=1, source_target_pairs={{0,32},{32,0},{1,33},{33,1},{2,34},{34,2},{3,35},{35,3},{4,36},{36... | collective-permute-start | bytes 786440 | tf_op jit(solution)/shard_map/ppermute | solution.py:165
  198.8 0.8 broadcast_in_dim.43
  199.6 3.9 %all-to-all-start.5 = ((bf16[32,48,128]{2,1,0:T(8,128)(2,1)}), bf16[32,48,128]{2,1,0:T(8,128)(2,1)S(1)}, u32[]{:S(2)}, u32[]{:S(2)}) async-start(bf16[32,48,128]{2,1,0:T(8,128)(2,1)} %broadcast_in_dim.43), calls=%async_computation.5 | async-start | bytes 786432 | tf_op jit(solution)/shard_map/all_to_all | solution.py:244
  203.5 1.3 collective-permute-start.2
  204.8 6.6 %collective-permute-done.2 = f32[512,128]{1,0:T(8,128)S(1)} collective-permute-done((f32[512,128]{1,0:T(8,128)S(1)}, f32[512,128]{1,0:T(8,128)S(1)}, u32[]{:S(2)}, u32[]{:S(2)}) %collective-permute-start.2) | collective-permute-done | bytes 262176 | tf_op jit(solution)/shard_map/ppermute | solution.py:170
  211.4 2.5 %collective-permute-start.3 = (f32[512,128]{1,0:T(8,128)S(1)}, f32[512,128]{1,0:T(8,128)S(1)}, u32[]{:S(2)}, u32[]{:S(2)}) collective-permute-start(f32[512,128]{1,0:T(8,128)S(1)} %add.41), channel_id=1, source_target_pairs={{0,192},{192,0},{64,128},{128,64},{1,193},{193,1},{65,129},{129,65... | collective-permute-start | bytes 786440 | tf_op jit(solution)/shard_map/ppermute | solution.py:171
  213.9 4.1 %all-to-all-done.5 = bf16[32,48,128]{2,1,0:T(8,128)(2,1)S(1)} async-done(((bf16[32,48,128]{2,1,0:T(8,128)(2,1)}), bf16[32,48,128]{2,1,0:T(8,128)(2,1)S(1)}, u32[]{:S(2)}, u32[]{:S(2)}) %all-to-all-start.5) | async-done | bytes 393248 | tf_op jit(solution)/shard_map/all_to_all | solution.py:244
  218.0 0.3 copy.33
  218.6 0.9 slice_convert_fusion
  219.6 0.6 fusion.10
  220.2 0.7 slice_reduce_fusion.1
  221.0 0.7 copy_bitcast_fusion.1
  (39 shorter events, 1.0 us)
Async XLA Ops:
  7.2 80.7 %all-gather.4.cloned.1.call-start = ((), (), s32[]{:S(2)}) async-start(), calls=%async_computation.6 | async-start | bytes 1622016 | tf_op jit(solution)/shard_map/all_gather | solution.py:194
  8.7 149.0 %all-gather.6.cloned.1.call-start = ((), (), s32[]{:S(2)}) async-start(), calls=%async_computation.7 | async-start | bytes 3538944 | tf_op jit(solution)/shard_map/all_gather | solution.py:216
  10.2 82.8 %copy-start.6 = (f32[32]{0:T(128)S(1)}, f32[32]{0:T(128)}, u32[]{:S(2)}) copy-start(f32[32]{0:T(128)} %param.21) | copy-start | bytes 388
  10.2 100.9 %copy-start.4 = (bf16[32,153]{1,0:T(8,128)(2,1)S(1)}, bf16[32,153]{1,0:T(8,128)(2,1)}, u32[]{:S(2)}) copy-start(bf16[32,153]{1,0:T(8,128)(2,1)} %param.23) | copy-start | bytes 29380
  87.9 47.0 %copy-start.1 = (bf16[768,1024]{1,0:T(8,128)(2,1)S(1)}, bf16[768,1024]{1,0:T(8,128)(2,1)}, u32[]{:S(2)}) copy-start(bf16[768,1024]{1,0:T(8,128)(2,1)} %all-gather.4.cloned.1.call-done) | copy-start | bytes 4718596
  87.9 47.6 %collective-permute-start = (bf16[768,1024]{1,0:T(8,128)(2,1)}, bf16[768,1024]{1,0:T(8,128)(2,1)S(1)}, u32[]{:S(2)}, u32[]{:S(2)}) collective-permute-start(bf16[768,1024]{1,0:T(8,128)(2,1)} %all-gather.4.cloned.1.call-done), channel_id=1, source_target_pairs={{0,32},{32,0},{1,33},{33,1},{2,34},{34,2},{3,35},{35,3},{4,36},{36... | collective-permute-start | bytes 4718600 | tf_op jit(solution)/shard_map/ppermute | solution.py:165
  107.1 22.0 %all-to-all-start = ((bf16[32,48,128]{2,1,0:T(8,128)(2,1)}), bf16[32,48,128]{2,1,0:T(8,128)(2,1)S(1)}, u32[]{:S(2)}, u32[]{:S(2)}) async-start(bf16[32,48,128]{2,1,0:T(8,128)(2,1)} %shard_map.172), calls=%async_computation | async-start | bytes 786432 | tf_op jit(solution)/shard_map/all_to_all | solution.py:217
  130.6 9.0 %all-to-all-start.3 = ((bf16[4,32,306]{2,1,0:T(8,128)(2,1)}), bf16[4,32,306]{2,1,0:T(8,128)(2,1)}, u32[]{:S(2)}, u32[]{:S(2)}) async-start(bf16[4,32,306]{2,1,0:T(8,128)(2,1)} %broadcast_in_dim.40), calls=%async_computation.3 | async-start | bytes 196608 | tf_op jit(solution)/shard_map/all_to_all | solution.py:203
  134.8 0.7 copy-start.3
  139.6 5.2 %copy-start.5 = (s32[8,8]{1,0:T(8,128)S(1)}, s32[8,8]{1,0:T(8,128)}, u32[]{:S(2)}) copy-start(s32[8,8]{1,0:T(8,128)} %param.17) | copy-start | bytes 772
  139.6 5.8 %copy-start.7 = (s32[8]{0:T(128)S(1)}, s32[8]{0:T(128)}, u32[]{:S(2)}) copy-start(s32[8]{0:T(128)} %param.24) | copy-start | bytes 100
  139.6 7.0 %copy-start.2 = (bf16[153,1024]{1,0:T(8,128)(2,1)S(1)}, bf16[153,1024]{1,0:T(8,128)(2,1)}, u32[]{:S(2)}) copy-start(bf16[153,1024]{1,0:T(8,128)(2,1)} %param.25) | copy-start | bytes 940036
  140.8 27.7 %all-to-all-start.2 = ((bf16[32,128,128]{2,1,0:T(8,128)(2,1)}), bf16[32,128,128]{2,1,0:T(8,128)(2,1)S(1)}, u32[]{:S(2)}, u32[]{:S(2)}) async-start(bf16[32,128,128]{2,1,0:T(8,128)(2,1)} %bitcast.4), calls=%async_computation.2 | async-start | bytes 2097152 | tf_op jit(solution)/shard_map/all_to_all | solution.py:228
  168.6 1.0 copy-start
  177.2 15.5 %all-to-all-start.4 = ((f32[8,96,128]{2,1,0:T(8,128)}), f32[8,96,128]{2,1,0:T(8,128)S(1)}, u32[]{:S(2)}, u32[]{:S(2)}) async-start(f32[8,96,128]{2,1,0:T(8,128)} %get-tuple-element.8), calls=%async_computation.4 | async-start | bytes 786432 | tf_op jit(solution)/shard_map/all_to_all | solution.py:242
  192.7 10.7 %collective-permute-start.1 = (f32[512,128]{1,0:T(8,128)S(1)}, f32[512,128]{1,0:T(8,128)S(1)}, u32[]{:S(2)}, u32[]{:S(2)}) collective-permute-start(f32[512,128]{1,0:T(8,128)S(1)} %pad_maximum_fusion), channel_id=1, source_target_pairs={{0,32},{32,0},{1,33},{33,1},{2,34},{34,2},{3,35},{35,3},{4,36},{36... | collective-permute-start | bytes 786440 | tf_op jit(solution)/shard_map/ppermute | solution.py:165
  199.6 18.4 %all-to-all-start.5 = ((bf16[32,48,128]{2,1,0:T(8,128)(2,1)}), bf16[32,48,128]{2,1,0:T(8,128)(2,1)S(1)}, u32[]{:S(2)}, u32[]{:S(2)}) async-start(bf16[32,48,128]{2,1,0:T(8,128)(2,1)} %broadcast_in_dim.43), calls=%async_computation.5 | async-start | bytes 786432 | tf_op jit(solution)/shard_map/all_to_all | solution.py:244
  203.5 7.8 %collective-permute-start.2 = (f32[512,128]{1,0:T(8,128)S(1)}, f32[512,128]{1,0:T(8,128)S(1)}, u32[]{:S(2)}, u32[]{:S(2)}) collective-permute-start(f32[512,128]{1,0:T(8,128)S(1)} %fusion.6), channel_id=1, source_target_pairs={{0,64},{64,0},{128,192},{192,128},{1,65},{65,1},{129,193},{193,129... | collective-permute-start | bytes 786440 | tf_op jit(solution)/shard_map/ppermute | solution.py:170
  211.4 8.1 %collective-permute-start.3 = (f32[512,128]{1,0:T(8,128)S(1)}, f32[512,128]{1,0:T(8,128)S(1)}, u32[]{:S(2)}, u32[]{:S(2)}) collective-permute-start(f32[512,128]{1,0:T(8,128)S(1)} %add.41), channel_id=1, source_target_pairs={{0,192},{192,0},{64,128},{128,64},{1,193},{193,1},{65,129},{129,65... | collective-permute-start | bytes 786440 | tf_op jit(solution)/shard_map/ppermute | solution.py:171
Sparse Core Ops, SparseCore 0:
  11.2 76.7 all-gather.3
  89.7 54.9 all-gather.5

commit v2 on v1

v2 whole, which is shorter than its diff:
```python
import jax
import jax.numpy as jnp
from jax import lax
from jax.experimental import pallas as pl
from jax.experimental.pallas import tpu as pltpu
from jax.sharding import Mesh, PartitionSpec as P

TILE = 128
FEAT = ("z", "y")
DP = ("x", "core")
BF = jnp.bfloat16
F32 = jnp.float32
NT = (((1,), (1,)), ((), ()))
VMEM = pl.BlockSpec(memory_space=pltpu.VMEM)
SMEM = pl.BlockSpec(memory_space=pltpu.SMEM)
HBM = pl.BlockSpec(memory_space=pl.ANY)
LIMIT = pltpu.CompilerParams(vmem_limit_bytes=56 * 2**20)


def aligned(index, size):
    return pl.ds(pl.multiple_of(index * size, size), size)


def hop_kernel(ids, cols, table, tiles_hbm, out, rows, picked, tiles, sem):
    width = table.shape[0]
    blocks = tiles.shape[0]
    group = blocks // 8
    copies = [
        pltpu.make_async_copy(
            tiles_hbm.at[pl.ds(j * group, group)], tiles.at[pl.ds(j * group, group)], sem.at[j]
        )
        for j in range(8)
    ]
    for copy in copies:
        copy.start()

    def turn(b, carry):
        rows[aligned(b, TILE), 0:width] = table[:, aligned(b, TILE)].astype(F32).T
        return carry

    lax.fori_loop(0, table.shape[1] // TILE, turn, 0, unroll=8)
    step = 64

    def pick(g, carry):
        base = pl.multiple_of(g * step, step)
        for u in range(step):
            picked[pl.ds(base + u, 1), :] = rows[pl.ds(ids[base + u], 1), :]
        return carry

    lax.fori_loop(0, ids.shape[0] // step, pick, 0)
    for copy in copies:
        copy.wait()

    def merge(r, carry):
        out[r, 0:width, :] = picked[aligned(r, TILE), :].T[0:width].astype(BF)
        left = jnp.concatenate([tiles[r, k] for k in range(8)], axis=1)
        right = jnp.concatenate(
            [picked[aligned(cols[r * 8 + k], TILE), :].astype(BF) for k in range(8)], axis=0
        )
        total = jnp.dot(left, right, preferred_element_type=F32)
        out[r, width : 2 * width, :] = total.T[0:width].astype(BF)
        return carry

    lax.fori_loop(0, blocks, merge, 0, unroll=2)


def hop(table, ids, cols, tiles):
    blocks = tiles.shape[0]
    return pl.pallas_call(
        hop_kernel,
        in_specs=[SMEM, SMEM, VMEM, HBM],
        out_specs=VMEM,
        scratch_shapes=[
            pltpu.VMEM((table.shape[1], TILE), F32),
            pltpu.VMEM((ids.shape[0], TILE), F32),
            pltpu.VMEM(tiles.shape, BF),
            pltpu.SemaphoreType.DMA((8,)),
        ],
        out_shape=jax.ShapeDtypeStruct((blocks, 2 * table.shape[0], TILE), BF),
        compiler_params=LIMIT,
        cost_estimate=pl.CostEstimate(flops=10**9, bytes_accessed=60 * 10**6, transcendentals=0),
    )(ids, cols.reshape(-1), table, tiles)


def pack_kernel(place, own, neigh, bias, head_self, head_neigh, weights, heads):
    core, x, feat = place[0], place[1], place[2]
    cols = aligned(x, 256)
    chosen = jnp.where(core == 0, own[:, cols], neigh[:, cols]).astype(F32)
    lane = lax.broadcasted_iota(jnp.int32, (8, 256), 1) + x * 256
    row = lax.broadcasted_iota(jnp.int32, (8, 256), 0)
    left = jnp.concatenate([bias[...]] * 8, axis=1)
    high = left.astype(BF).astype(F32)
    left = left - high
    middle = left.astype(BF).astype(F32)
    low = left - middle
    term = jnp.where(row == 0, high, jnp.where(row == 1, middle, jnp.where(row == 2, low, 0.0)))
    inside = jnp.logical_and(lane >= feat * 32, lane < feat * 32 + 32)
    term = jnp.where(jnp.logical_and(inside, core == 0), term, 0.0)
    block = jnp.concatenate([chosen, term], axis=0).astype(BF)
    for d in range(weights.shape[0]):
        weights[d] = block
    classes = head_self.shape[1]
    heads[...] = jnp.zeros_like(heads)
    for d in range(heads.shape[0]):
        heads[d, 0:32, 0:classes] = head_self[...]
        heads[d, 32:64, 0:classes] = head_neigh[...]


def pack(place, own, neigh, bias, head_self, head_neigh):
    return pl.pallas_call(
        pack_kernel,
        in_specs=[SMEM] + [VMEM] * 5,
        out_specs=[VMEM, VMEM],
        out_shape=[
            jax.ShapeDtypeStruct((32, 32, 256), BF),
            jax.ShapeDtypeStruct((4, 64, 256), BF),
        ],
        compiler_params=LIMIT,
    )(place, own, neigh, bias.reshape(1, -1), head_self, head_neigh)


def spread_kernel(cols, live, logit_cot, heads, tiles, out, cot):
    classes, slots = logit_cot.shape
    lane = lax.broadcasted_iota(jnp.int32, (classes, slots), 1)
    kept = jnp.where(lane < live[0], logit_cot[...].astype(F32), 0.0)
    cot[...] = jnp.concatenate([kept, jnp.zeros((256 - classes, slots), F32)], axis=0).astype(BF)
    out[...] = jnp.zeros_like(out)
    own = jnp.concatenate([heads[j, 0:32] for j in range(4)], axis=0)
    neigh = jnp.concatenate([heads[j, 32:64] for j in range(4)], axis=0)
    for r in range(tiles.shape[0]):
        part = cot[:, r * TILE : (r + 1) * TILE]
        out[r] = jnp.dot(own, part, preferred_element_type=F32)
    for r in range(tiles.shape[0]):
        part = cot[:, r * TILE : (r + 1) * TILE]
        back = jnp.dot(neigh, part, preferred_element_type=F32).astype(BF)
        for k in range(8):
            out[cols[r * 8 + k]] += jnp.dot(back, tiles[r, k], preferred_element_type=F32)


def spread(cols, live, logit_cot, heads, tiles, blocks):
    return pl.pallas_call(
        spread_kernel,
        in_specs=[SMEM, SMEM, VMEM, VMEM, VMEM],
        out_specs=[VMEM, VMEM],
        out_shape=[
            jax.ShapeDtypeStruct((blocks, TILE, TILE), F32),
            jax.ShapeDtypeStruct((256, logit_cot.shape[1]), BF),
        ],
        compiler_params=LIMIT,
        cost_estimate=pl.CostEstimate(flops=10**9, bytes_accessed=8 * 10**6, transcendentals=0),
    )(cols.reshape(-1), live.reshape(1), logit_cot, heads, tiles)


def layer_kernel(place, got, w0, w1, w2, w3, o0, o1, o2, o3, out, mine, other):
    core, x = place[0], place[1]
    deep = got.shape[1] // 2
    row = lax.broadcasted_iota(jnp.int32, (8, TILE), 0)
    ones = jnp.where(row < 3, 1.0, 0.0)

    for j in range(8):
        own, agg = [], []
        for i in range(4):
            piece = got[4 * j + i].astype(F32)
            own += [piece[0:deep], ones]
            agg += [piece[deep : 2 * deep], ones]
        own = jnp.concatenate(own, axis=0).T.astype(BF)
        agg = jnp.concatenate(agg, axis=0).T.astype(BF)
        at = slice(j * TILE, (j + 1) * TILE)
        mine[:, at] = jnp.where(core == 0, own, agg)
        other[:, at] = jnp.where(core == 0, agg, own)
    for s, (w, o) in enumerate(((w0, o0), (w1, o1), (w2, o2), (w3, o3))):
        chunk = lax.rem(x + 4 - s, 4)
        preact = jnp.dot(mine[...], w[...], preferred_element_type=F32)
        preact = preact + jnp.dot(other[...], o[...], preferred_element_type=F32)
        hidden = jnp.maximum(preact, 0.0)
        for half in range(2):
            piece = hidden[:, half * TILE : (half + 1) * TILE].T.astype(BF)
            for y in range(4):
                out[(2 * chunk + half) * 4 + y] = piece


def layer(place, got, mine, other):
    return pl.pallas_call(
        layer_kernel,
        in_specs=[SMEM] + [VMEM] * 9,
        out_specs=VMEM,
        scratch_shapes=[pltpu.VMEM((TILE, 1024), BF), pltpu.VMEM((TILE, 1024), BF)],
        out_shape=jax.ShapeDtypeStruct((32, TILE, TILE), BF),
        compiler_params=LIMIT,
    )(place, got, *mine, *other)


def score_kernel(place, cols, hidden, dhidden, tiles, cot, pair, out, heads, second):
    y = place[3]
    own = pl.ds(pl.multiple_of(y * 32, 32), 32)
    for r in range(tiles.shape[0]):
        left = jnp.concatenate([hidden[cols[r * 8 + k]] for k in range(8)], axis=1)
        right = jnp.concatenate([tiles[r, k] for k in range(8)], axis=1)
        second[r] = lax.dot_general(left, right, NT, preferred_element_type=F32).astype(BF)
    self_t = jnp.concatenate([pair[j, 0:32] for j in range(4)], axis=0).astype(F32).T.astype(BF)
    neigh_t = jnp.concatenate([pair[j, 32:64] for j in range(4)], axis=0).astype(F32).T.astype(BF)
    for half in range(2):
        at = 2 * y + half
        scores = jnp.dot(self_t, hidden[at], preferred_element_type=F32)
        scores = scores + jnp.dot(neigh_t, second[at], preferred_element_type=F32)
        for z in range(out.shape[0]):
            out[z, 32 * half : 32 * half + 24, :] = scores[24 * z : 24 * (z + 1)].astype(BF)
    total = jnp.zeros((32, TILE), F32)
    for b in range(hidden.shape[0]):
        total = total + jnp.where(hidden[b, own, :].astype(F32) > 0.0, dhidden[b, own, :], 0.0)
    mine = jnp.sum(total, axis=1, keepdims=True)
    targets = jnp.concatenate([hidden[r, own, :] for r in range(tiles.shape[0])], axis=1)
    merged = jnp.concatenate([second[r, own, :] for r in range(tiles.shape[0])], axis=1)
    lane = lax.broadcasted_iota(jnp.int32, (32, 256), 1)
    grad = lax.dot_general(targets, cot[...], NT, preferred_element_type=F32)
    heads[:, 0:256] = jnp.where(lane == 255, mine, grad)
    heads[:, 256:512] = lax.dot_general(merged, cot[...], NT, preferred_element_type=F32)


def score(place, cols, hidden, dhidden, tiles, cot, pair):
    return pl.pallas_call(
        score_kernel,
        in_specs=[SMEM, SMEM] + [VMEM] * 5,
        out_specs=[VMEM, VMEM],
        scratch_shapes=[pltpu.VMEM((tiles.shape[0], TILE, TILE), BF)],
        out_shape=[
            jax.ShapeDtypeStruct((8, 64, TILE), BF),
            jax.ShapeDtypeStruct((32, 512), F32),
        ],
        compiler_params=LIMIT,
    )(place, cols.reshape(-1), hidden, dhidden, tiles, cot, pair)


def grad_kernel(place, hidden, dhidden, feats, keep, send, total):
    core = place[0]
    groups, blocks, deep, _ = feats.shape
    half = deep // 2
    total[...] = jnp.zeros_like(total)

    def grow(b, carry):
        low = jnp.where(hidden[b].astype(F32) > 0.0, dhidden[b], 0.0).astype(BF)
        stack = jnp.concatenate([feats[z, b] for z in range(groups)], axis=0)
        total[...] += lax.dot_general(stack, low, NT, preferred_element_type=F32)
        return carry

    lax.fori_loop(0, blocks, grow, 0, unroll=4)
    for z in range(groups):
        keep[z] = total[pl.ds(pl.multiple_of(z * deep + core * half, 8), half), :]
        send[z] = total[pl.ds(pl.multiple_of(z * deep + (1 - core) * half, 8), half), :]


def grad(place, hidden, dhidden, feats):
    groups, blocks, deep, _ = feats.shape
    shape = jax.ShapeDtypeStruct((groups, deep // 2, TILE), F32)
    return pl.pallas_call(
        grad_kernel,
        in_specs=[SMEM] + [VMEM] * 3,
        out_specs=[VMEM, VMEM],
        scratch_shapes=[pltpu.VMEM((groups * deep, TILE), F32)],
        out_shape=[shape, shape],
        compiler_params=LIMIT,
        cost_estimate=pl.CostEstimate(flops=10**9, bytes_accessed=7 * 10**6, transcendentals=0),
    )(place, hidden, dhidden, feats)


def swap_core(value):
    return lax.ppermute(value, "core", [(0, 1), (1, 0)])


def sum_x(value):
    value = value + lax.ppermute(value, "x", [(0, 1), (1, 0), (2, 3), (3, 2)])
    return value + lax.ppermute(value, "x", [(0, 3), (3, 0), (1, 2), (2, 1)])


def shards(
    feature_table,
    node_ids,
    hop_cols,
    hop_tiles,
    target_cols,
    target_tiles,
    self_weight,
    neigh_weight,
    hidden_bias,
    head_self,
    head_neigh,
    batch_sizes,
    logit_cotangent,
):
    blocks = hop_cols.shape[0]
    classes, target_rows = logit_cotangent.shape
    x, core = lax.axis_index("x"), lax.axis_index("core")
    y = lax.axis_index("y")
    place = jnp.stack([core, x, lax.axis_index("z") * 4 + y, y])

    weights, pair = pack(place, self_weight, neigh_weight, hidden_bias, head_self, head_neigh)
    weights = lax.all_to_all(weights, FEAT, 0, 0, tiled=True).reshape(1024, 256)
    mine = [weights] + [
        lax.ppermute(weights, "x", [(i, (i + s) % 4) for i in range(4)]) for s in (1, 2, 3)
    ]
    other = [swap_core(w) for w in mine]
    pair = lax.all_to_all(pair, "y", 0, 0, tiled=True)

    live = batch_sizes[x * 2 + core]
    dhidden, cot = spread(target_cols, live, logit_cotangent, pair, target_tiles, blocks)

    send = hop(feature_table, node_ids, hop_cols, hop_tiles)
    feats = lax.all_gather(send, "z", axis=0, tiled=False)
    got = lax.all_to_all(send, FEAT, 0, 0, tiled=True)
    hidden = layer(place, got, mine, other)
    hidden = lax.all_to_all(hidden, FEAT, 0, 0, tiled=True)

    scores, heads = score(place, target_cols, hidden, dhidden, target_tiles, cot, pair)
    scores = lax.all_to_all(scores, "z", 0, 0, tiled=True)
    scores = jnp.sum(scores.astype(F32), axis=0).astype(BF)
    scores = lax.all_to_all(
        jnp.broadcast_to(scores[None], (32,) + scores.shape), FEAT, 0, 0, tiled=True
    )
    scores = scores.reshape(8, 4, 2, 32, TILE)[:, :, :, :24].transpose(0, 3, 1, 2, 4)
    logits = scores.reshape(192, target_rows)[:classes].astype(F32)

    heads = sum_x(heads + swap_core(heads))
    keep, send = grad(place, hidden, dhidden, feats)
    keep = keep + swap_core(send)
    keep = sum_x(lax.all_to_all(keep, "z", 0, 0, tiled=True))
    keep = keep.transpose(1, 0, 2).reshape(-1, 1024)
    rest = swap_core(keep)
    return (
        logits,
        jnp.where(core == 0, keep, rest),
        jnp.where(core == 0, rest, keep),
        heads[:, :classes],
        heads[:, 256 : 256 + classes],
        heads[:, 255],
    )


def solution(mesh):
    split = Mesh(mesh.devices.reshape(4, 2, 8, 4), DP + FEAT)
    return jax.shard_map(
        shards,
        mesh=split,
        in_specs=(
            P(FEAT, None),
            P(DP),
            P(DP, None),
            P(DP, None, None, None),
            P(DP, None),
            P(DP, None, None, None),
            P(FEAT, None),
            P(FEAT, None),
            P(FEAT),
            P(FEAT, None),
            P(FEAT, None),
            P(),
            P(None, DP),
        ),
        out_specs=(
            P(None, DP),
            P(FEAT, None),
            P(FEAT, None),
            P(FEAT, None),
            P(FEAT, None),
            P(FEAT),
        ),
        check_vma=False,
    )
```

time: 230 us -> 215 us (0.935)
  waiting for transfers between devices: 100 us -> 44.5 us
  starting transfers between devices: 35.6 us -> 62.4 us
  blocking collectives: 14.1 us -> 33.5 us
  Pallas kernels: 38.3 us -> 48.6 us
  local copies, waits for them, and re-layouts: 15.1 us -> 7.42 us
  matrix products: 4.9 us -> 0 us
    all_gather x1 -> x0, waiting for transfers between devices: 51.1 us -> none  [shards(): lax.all_gather(jnp.where(first_core, self_weight, neigh_weight), FEAT, ax...]
    all_to_all x1, blocking collectives: 14.1 us -> 33.5 us  [shards(): weights = lax.all_to_all(weights, FEAT, 0, 0, tiled=True).reshape(1024, 256)]
    all_to_all x1, waiting for transfers between devices: 14.1 us -> 0.01 us  [shards(): got = lax.all_to_all(send, FEAT, 0, 0, tiled=True)]
    ppermute x2 -> x7, waiting for transfers between devices: 6.6 us -> 17.7 us  [the longest x3 7.34 us: shards(): lax.ppermute(weights, 'x', [(i, (i + s) % 4) for i in range(4)])]
    ppermute x2 -> x7, starting transfers between devices: 11.1 us -> 21.7 us  [swap_core(): return lax.ppermute(value, 'core', [(0, 1), (1, 0)])]
    pallas_call x2 -> x5, Pallas kernels: 11.7 us -> 22 us  [the longest x1 5.87 us: spread(): pl.pallas_call(spread_kernel, in_specs=[SMEM, SMEM, VMEM, VMEM, VMEM], ou...]
    all_to_all x3 -> x4, starting transfers between devices: 12.8 us -> 21.3 us  [the longest x1 6.9 us: shards(): keep = sum_x(lax.all_to_all(keep, 'z', 0, 0, tiled=True))]
    ppermute x2 -> x7, starting transfers between devices: 3.78 us -> 9.91 us  [the longest x3 4.86 us: shards(): lax.ppermute(weights, 'x', [(i, (i + s) % 4) for i in range(4)])]
  transfers between devices with their start and end apart: 11 -> 21, of which waited for: 7 -> 9; matrix products, arithmetic and copies ran while one was open for 9% -> 3% of each run, Pallas kernels for 13% -> 10%
where the time goes in v2:
time: 215 us
  starting transfers between devices  62.4 us (29%)
  Pallas kernels  48.6 us (23%)
  waiting for transfers between devices  44.5 us (21%)
  blocking collectives  33.5 us (16%)
  between operations  14.2 us (7%)
  local copies, waits for them, and re-layouts  7.42 us (3%)
  other arithmetic  3.82 us (2%)
    all_to_all x1, blocking collectives, shards(): weights = lax.all_to_all(weights, FEAT, 0, 0, tiled=True).reshape(1024, 256)  33.5 us
    pallas_call x1, Pallas kernels, hop(): pl.pallas_call(hop_kernel, in_specs=[SMEM, SMEM, VMEM, HBM], out_specs=VM...  26.5 us
    ppermute x7, starting transfers between devices, swap_core(): return lax.ppermute(value, 'core', [(0, 1), (1, 0)])  21.7 us
    all_to_all x1, waiting for transfers between devices, shards(): hidden = lax.all_to_all(hidden, FEAT, 0, 0, tiled=True)  17.2 us
    all_to_all x1, waiting for transfers between devices, shards(): keep = sum_x(lax.all_to_all(keep, 'z', 0, 0, tiled=True))  7.43 us
    ppermute x3, waiting for transfers between devices, shards(): lax.ppermute(weights, 'x', [(i, (i + s) % 4) for i in range(4)])  7.34 us
    all_to_all x1, starting transfers between devices, shards(): keep = sum_x(lax.all_to_all(keep, 'z', 0, 0, tiled=True))  6.9 us
    all_to_all x1, starting transfers between devices, shards(): hidden = lax.all_to_all(hidden, FEAT, 0, 0, tiled=True)  6.1 us
  transfers between devices with their start and end apart: 21, of which 9 were waited for; matrix products, arithmetic and copies ran while one was open for 3% of the time, Pallas kernels for 10%

profile of v2, /device:TPU:1, one launch (start us, length us, event | category | flops | bytes accessed | tf_op | source)
XLA Modules:
  0.0 214.5 jit_solution(4906964167234317213)
XLA Ops:
  7.2 0.8 copy.24
  8.0 0.7 reshape.36.cols
  8.6 26.5 %shard_map.172 = bf16[32,48,128]{2,1,0:T(8,128)(2,1)} custom-call(s32[16384]{0:T(1024)} %ids.1, s32[256]{0:T(256)} %reshape.36.cols, bf16[24,32768]{1,0:T(8,128)(2,1)} %table.1, bf16[32,8,128,128]{3,2,1,0:T(8,128)(2,1)} %tiles_hbm.1), custom_call_target="tpu_custom_call" | custom-call | flops 1000000000 | bytes 60000000 | tf_op jit(solution)/shard_map/pallas_call | solution.py:69
  35.2 0.6 pad_add_fusion.place
  35.8 1.7 shard_map.173
  37.5 33.5 %all_to_all.35 = bf16[32,32,256]{2,1,0:T(8,128)(2,1)S(1)} all-to-all(bf16[32,32,256]{2,1,0:T(8,128)(2,1)} %get-tuple-element.14), channel_id=1, replica_groups=mesh['x'=4,'core'=2,'z'=8,'y'=4] {'z','y'}, dimensions={0} | all-to-all | bytes 1048576 | tf_op jit(solution)/shard_map/all_to_all | solution.py:297
  71.1 1.2 collective-permute-start
  72.3 2.5 %collective-permute-start.1 = (bf16[1024,256]{1,0:T(8,128)(2,1)S(1)}, bf16[1024,256]{1,0:T(8,128)(2,1)S(1)}, u32[]{:S(2)}, u32[]{:S(2)}) collective-permute-start(bf16[1024,256]{1,0:T(8,128)(2,1)S(1)} %bitcast.23), channel_id=1, source_target_pairs={{0,128},{64,192},{128,0},{192,64},{1,129},{65,193},{129,1},{193,65... | collective-permute-start | bytes 1572872 | tf_op jit(solution)/shard_map/ppermute | solution.py:299
  74.8 1.1 collective-permute-start.2
  76.0 5.0 %all-to-all-start = ((bf16[32,48,128]{2,1,0:T(8,128)(2,1)}), bf16[32,48,128]{2,1,0:T(8,128)(2,1)S(1)}, u32[]{:S(2)}, u32[]{:S(2)}) async-start(bf16[32,48,128]{2,1,0:T(8,128)(2,1)} %shard_map.172), calls=%async_computation | async-start | bytes 786432 | tf_op jit(solution)/shard_map/all_to_all | solution.py:309
  81.0 2.8 %collective-permute-start.3 = (bf16[1024,256]{1,0:T(8,128)(2,1)S(1)}, bf16[1024,256]{1,0:T(8,128)(2,1)S(1)}, u32[]{:S(2)}, u32[]{:S(2)}) collective-permute-start(bf16[1024,256]{1,0:T(8,128)(2,1)S(1)} %bitcast.25), channel_id=1, source_target_pairs={{0,32},{32,0},{1,33},{33,1},{2,34},{34,2},{3,35},{35,3},{4,36},{36... | collective-permute-start | bytes 1572872 | tf_op jit(solution)/shard_map/ppermute | solution.py:267
  83.8 4.6 %collective-permute-start.4 = (bf16[1024,256]{1,0:T(8,128)(2,1)S(1)}, bf16[1024,256]{1,0:T(8,128)(2,1)S(1)}, u32[]{:S(2)}, u32[]{:S(2)}) collective-permute-start(bf16[1024,256]{1,0:T(8,128)(2,1)S(1)} %collective-permute-done.w1), channel_id=1, source_target_pairs={{0,32},{32,0},{1,33},{33,1},{2,34},{34,2},{3,35},{35,3},{4,36},{36... | collective-permute-start | bytes 1572872 | tf_op jit(solution)/shard_map/ppermute | solution.py:267
  88.4 7.3 %collective-permute-done.1.w2 = bf16[1024,256]{1,0:T(8,128)(2,1)S(1)} collective-permute-done((bf16[1024,256]{1,0:T(8,128)(2,1)S(1)}, bf16[1024,256]{1,0:T(8,128)(2,1)S(1)}, u32[]{:S(2)}, u32[]{:S(2)}) %collective-permute-start.1) | collective-permute-done | bytes 524320 | tf_op jit(solution)/shard_map/ppermute | solution.py:299
  95.7 3.2 %collective-permute-start.5 = (bf16[1024,256]{1,0:T(8,128)(2,1)S(1)}, bf16[1024,256]{1,0:T(8,128)(2,1)}, u32[]{:S(2)}, u32[]{:S(2)}) collective-permute-start(bf16[1024,256]{1,0:T(8,128)(2,1)S(1)} %collective-permute-done.1.w2), channel_id=1, source_target_pairs={{0,32},{32,0},{1,33},{33,1},{2,34},{34,2},{3,35},{35,3},{4,36},{36... | collective-permute-start | bytes 1572872 | tf_op jit(solution)/shard_map/ppermute | solution.py:267
  99.1 4.3 %all-to-all-start.3 = ((bf16[4,64,256]{2,1,0:T(8,128)(2,1)}), bf16[4,64,256]{2,1,0:T(8,128)(2,1)}, u32[]{:S(2)}, u32[]{:S(2)}) async-start(bf16[4,64,256]{2,1,0:T(8,128)(2,1)} %get-tuple-element.15), calls=%async_computation.3 | async-start | bytes 262144 | tf_op jit(solution)/shard_map/all_to_all | solution.py:302
  103.5 0.7 copy-done.6
  104.4 4.2 %shard_map.174 = bf16[32,128,128]{2,1,0:T(8,128)(2,1)} custom-call(s32[4]{0:T(128)} %pad_add_fusion.place, bf16[32,48,128]{2,1,0:T(8,128)(2,1)} %copy-done.2, bf16[1024,256]{1,0:T(8,128)(2,1)} %bitcast.26, bf16[1024,256]{1,0:T(8,128)(2,1)} %copy-done.3, bf16[1024,256]{1,0:T(8,128)(2,1)} %copy-done.4, bf16[1024,256]{1,0:T(8,128)(2,1)} %copy-done.5, ...), custom_call_target="tpu_custom_call" | custom-call | tf_op jit(solution)/shard_map/pallas_call | solution.py:183
  108.6 6.1 %all-to-all-start.2 = ((bf16[32,128,128]{2,1,0:T(8,128)(2,1)}), bf16[32,128,128]{2,1,0:T(8,128)(2,1)S(1)}, u32[]{:S(2)}, u32[]{:S(2)}) async-start(bf16[32,128,128]{2,1,0:T(8,128)(2,1)} %shard_map.174), calls=%async_computation.2 | async-start | bytes 2097152 | tf_op jit(solution)/shard_map/all_to_all | solution.py:311
  114.7 0.6 reshape.35.cols
  115.3 0.6 dynamic_slice.3.live
  115.9 5.9 %shard_map.175 = (f32[32,128,128]{2,1,0:T(8,128)}, bf16[256,1024]{1,0:T(8,128)(2,1)}) custom-call(s32[64]{0:T(128)} %reshape.35.cols, s32[1]{0:T(128)} %dynamic_slice.3.live, bf16[153,1024]{1,0:T(8,128)(2,1)} %logit_cot.1, bf16[4,64,256]{2,1,0:T(8,128)(2,1)} %all-to-all-done.3.heads.pair, bf16[8,8,128,128]{3,2,1,0:T(8,128)(2,1)} %tiles.3), custom_call_target="tpu_custom_call" | custom-call | flops 1000000000 | bytes 8000000 | tf_op jit(solution)/shard_map/pallas_call | solution.py:141
  121.8 17.2 %all-to-all-done.2.hidden = bf16[32,128,128]{2,1,0:T(8,128)(2,1)S(1)} async-done(((bf16[32,128,128]{2,1,0:T(8,128)(2,1)}), bf16[32,128,128]{2,1,0:T(8,128)(2,1)S(1)}, u32[]{:S(2)}, u32[]{:S(2)}) %all-to-all-start.2) | async-done | bytes 1048608 | tf_op jit(solution)/shard_map/all_to_all | solution.py:311
  139.0 1.0 copy-done
  140.0 4.5 %shard_map.176 = (bf16[8,64,128]{2,1,0:T(8,128)(2,1)}, f32[32,512]{1,0:T(8,128)}) custom-call(s32[4]{0:T(128)} %pad_add_fusion.place, s32[64]{0:T(128)} %reshape.35.cols, bf16[32,128,128]{2,1,0:T(8,128)(2,1)} %copy-done, f32[32,128,128]{2,1,0:T(8,128)} %get-tuple-element.16.dhidden, bf16[8,8,128,128]{3,2,1,0:T(8,128)(2,1)} %tiles.3, ...), custom_call_target="tpu_custom_call" | custom-call | tf_op jit(solution)/shard_map/pallas_call | solution.py:221
  144.6 3.9 %all-to-all-start.4 = ((bf16[8,64,128]{2,1,0:T(8,128)(2,1)}), bf16[8,64,128]{2,1,0:T(8,128)(2,1)S(1)}, u32[]{:S(2)}, u32[]{:S(2)}) async-start(bf16[8,64,128]{2,1,0:T(8,128)(2,1)} %get-tuple-element.18), calls=%async_computation.4 | async-start | bytes 262144 | tf_op jit(solution)/shard_map/all_to_all | solution.py:314
  148.5 5.7 %shard_map.177 = (f32[8,24,128]{2,1,0:T(8,128)}, f32[8,24,128]{2,1,0:T(8,128)}) custom-call(s32[4]{0:T(128)} %pad_add_fusion.place, bf16[32,128,128]{2,1,0:T(8,128)(2,1)} %copy-done, f32[32,128,128]{2,1,0:T(8,128)} %get-tuple-element.16.dhidden, bf16[8,32,48,128]{3,2,1,0:T(8,128)(2,1)} %bitcast.21), custom_call_target="tpu_custom_call" | custom-call | flops 1000000000 | bytes 7000000 | tf_op jit(solution)/shard_map/pallas_call | solution.py:255
  154.2 4.9 %collective-permute-start.7 = (f32[8,24,128]{2,1,0:T(8,128)}, f32[8,24,128]{2,1,0:T(8,128)S(1)}, u32[]{:S(2)}, u32[]{:S(2)}) collective-permute-start(f32[8,24,128]{2,1,0:T(8,128)} %get-tuple-element.20), channel_id=1, source_target_pairs={{0,32},{32,0},{1,33},{33,1},{2,34},{34,2},{3,35},{35,3},{4,36},{36... | collective-permute-start | bytes 294920 | tf_op jit(solution)/shard_map/ppermute | solution.py:267
  159.1 1.2 collective-permute-done.7
  160.3 1.5 add.30
  161.8 6.9 %all-to-all-start.6 = ((f32[8,24,128]{2,1,0:T(8,128)}), f32[8,24,128]{2,1,0:T(8,128)S(1)}, u32[]{:S(2)}, u32[]{:S(2)}) async-start(f32[8,24,128]{2,1,0:T(8,128)} %add.30), calls=%async_computation.6 | async-start | bytes 196608 | tf_op jit(solution)/shard_map/all_to_all | solution.py:325
  168.7 7.4 %all-to-all-done.6 = f32[8,24,128]{2,1,0:T(8,128)S(1)} async-done(((f32[8,24,128]{2,1,0:T(8,128)}), f32[8,24,128]{2,1,0:T(8,128)S(1)}, u32[]{:S(2)}, u32[]{:S(2)}) %all-to-all-start.6) | async-done | bytes 98336 | tf_op jit(solution)/shard_map/all_to_all | solution.py:325
  176.2 0.9 broadcast_in_dim.2
  177.1 4.5 %all-to-all-start.5 = ((bf16[32,64,128]{2,1,0:T(8,128)(2,1)}), bf16[32,64,128]{2,1,0:T(8,128)(2,1)S(1)}, u32[]{:S(2)}, u32[]{:S(2)}) async-start(bf16[32,64,128]{2,1,0:T(8,128)(2,1)} %broadcast_in_dim.2), calls=%async_computation.5 | async-start | bytes 1048576 | tf_op jit(solution)/shard_map/all_to_all | solution.py:316
  181.6 2.0 collective-permute-start.11
  183.5 0.9 collective-permute-done.11
  184.4 1.1 collective-permute-start.12
  185.5 2.4 %collective-permute-done.12 = f32[32,512]{1,0:T(8,128)S(1)} collective-permute-done((f32[32,512]{1,0:T(8,128)S(1)}, f32[32,512]{1,0:T(8,128)S(1)}, u32[]{:S(2)}, u32[]{:S(2)}) %collective-permute-start.12) | collective-permute-done | bytes 65568 | tf_op jit(solution)/shard_map/ppermute | solution.py:271
  188.0 2.0 collective-permute-start.13
  189.9 2.7 %collective-permute-done.13 = f32[32,512]{1,0:T(8,128)S(1)} collective-permute-done((f32[32,512]{1,0:T(8,128)S(1)}, f32[32,512]{1,0:T(8,128)S(1)}, u32[]{:S(2)}, u32[]{:S(2)}) %collective-permute-start.13) | collective-permute-done | bytes 65568 | tf_op jit(solution)/shard_map/ppermute | solution.py:272
  192.7 0.6 fusion
  193.3 0.7 slice_reduce_fusion
  194.0 3.1 %collective-permute-done.8 = f32[8,24,128]{2,1,0:T(8,128)S(1)} collective-permute-done((f32[8,24,128]{2,1,0:T(8,128)S(1)}, f32[8,24,128]{2,1,0:T(8,128)S(1)}, u32[]{:S(2)}, u32[]{:S(2)}) %collective-permute-start.8) | collective-permute-done | bytes 98336 | tf_op jit(solution)/shard_map/ppermute | solution.py:271
  197.1 2.0 collective-permute-start.9
  199.1 0.3 copy.25
  199.7 2.1 collective-permute-done.9
  201.9 4.2 %collective-permute-start.10 = (f32[24,1024]{1,0:T(8,128)S(1)}, f32[24,1024]{1,0:T(8,128)S(1)}, u32[]{:S(2)}, u32[]{:S(2)}) collective-permute-start(f32[24,1024]{1,0:T(8,128)S(1)} %copy_bitcast_fusion), channel_id=1, source_target_pairs={{0,32},{32,0},{1,33},{33,1},{2,34},{34,2},{3,35},{35,3},{4,36},{36... | collective-permute-start | bytes 294920 | tf_op jit(solution)/shard_map/ppermute | solution.py:267
  206.0 0.9 slice_convert_fusion
  207.0 0.7 broadcast_select_fusion
  (44 shorter events, 0.9 us)
Async XLA Ops:
  7.2 141.4 %all-gather.3.cloned.1.call-start = ((), (), s32[]{:S(2)}) async-start(), calls=%async_computation.7 | async-start | bytes 3538944 | tf_op jit(solution)/shard_map/all_gather | solution.py:308
  71.1 32.4 %copy-start.1 = (bf16[32,32,256]{2,1,0:T(8,128)(2,1)}, bf16[32,32,256]{2,1,0:T(8,128)(2,1)S(1)}, u32[]{:S(2)}) copy-start(bf16[32,32,256]{2,1,0:T(8,128)(2,1)S(1)} %all_to_all.35) | copy-start | bytes 1572868
  71.1 12.7 %collective-permute-start = (bf16[1024,256]{1,0:T(8,128)(2,1)S(1)}, bf16[1024,256]{1,0:T(8,128)(2,1)S(1)}, u32[]{:S(2)}, u32[]{:S(2)}) collective-permute-start(bf16[1024,256]{1,0:T(8,128)(2,1)S(1)} %bitcast.22), channel_id=1, source_target_pairs={{0,64},{64,128},{128,192},{192,0},{1,65},{65,129},{129,193},{193,1... | collective-permute-start | bytes 1572872 | tf_op jit(solution)/shard_map/ppermute | solution.py:299
  72.3 23.4 %collective-permute-start.1 = (bf16[1024,256]{1,0:T(8,128)(2,1)S(1)}, bf16[1024,256]{1,0:T(8,128)(2,1)S(1)}, u32[]{:S(2)}, u32[]{:S(2)}) collective-permute-start(bf16[1024,256]{1,0:T(8,128)(2,1)S(1)} %bitcast.23), channel_id=1, source_target_pairs={{0,128},{64,192},{128,0},{192,64},{1,129},{65,193},{129,1},{193,65... | collective-permute-start | bytes 1572872 | tf_op jit(solution)/shard_map/ppermute | solution.py:299
  74.8 24.1 %collective-permute-start.2 = (bf16[1024,256]{1,0:T(8,128)(2,1)S(1)}, bf16[1024,256]{1,0:T(8,128)(2,1)S(1)}, u32[]{:S(2)}, u32[]{:S(2)}) collective-permute-start(bf16[1024,256]{1,0:T(8,128)(2,1)S(1)} %bitcast.24), channel_id=1, source_target_pairs={{0,192},{64,0},{128,64},{192,128},{1,193},{65,1},{129,65},{193,129... | collective-permute-start | bytes 1572872 | tf_op jit(solution)/shard_map/ppermute | solution.py:299
  76.0 23.1 %all-to-all-start = ((bf16[32,48,128]{2,1,0:T(8,128)(2,1)}), bf16[32,48,128]{2,1,0:T(8,128)(2,1)S(1)}, u32[]{:S(2)}, u32[]{:S(2)}) async-start(bf16[32,48,128]{2,1,0:T(8,128)(2,1)} %shard_map.172), calls=%async_computation | async-start | bytes 786432 | tf_op jit(solution)/shard_map/all_to_all | solution.py:309
  81.0 22.4 %collective-permute-start.3 = (bf16[1024,256]{1,0:T(8,128)(2,1)S(1)}, bf16[1024,256]{1,0:T(8,128)(2,1)S(1)}, u32[]{:S(2)}, u32[]{:S(2)}) collective-permute-start(bf16[1024,256]{1,0:T(8,128)(2,1)S(1)} %bitcast.25), channel_id=1, source_target_pairs={{0,32},{32,0},{1,33},{33,1},{2,34},{34,2},{3,35},{35,3},{4,36},{36... | collective-permute-start | bytes 1572872 | tf_op jit(solution)/shard_map/ppermute | solution.py:267
  83.8 19.6 %copy-start.3 = (bf16[1024,256]{1,0:T(8,128)(2,1)}, bf16[1024,256]{1,0:T(8,128)(2,1)S(1)}, u32[]{:S(2)}) copy-start(bf16[1024,256]{1,0:T(8,128)(2,1)S(1)} %collective-permute-done.w1) | copy-start | bytes 1572868
  83.8 19.6 %collective-permute-start.4 = (bf16[1024,256]{1,0:T(8,128)(2,1)S(1)}, bf16[1024,256]{1,0:T(8,128)(2,1)S(1)}, u32[]{:S(2)}, u32[]{:S(2)}) collective-permute-start(bf16[1024,256]{1,0:T(8,128)(2,1)S(1)} %collective-permute-done.w1), channel_id=1, source_target_pairs={{0,32},{32,0},{1,33},{33,1},{2,34},{34,2},{3,35},{35,3},{4,36},{36... | collective-permute-start | bytes 1572872 | tf_op jit(solution)/shard_map/ppermute | solution.py:267
  95.7 7.7 %copy-start.4 = (bf16[1024,256]{1,0:T(8,128)(2,1)}, bf16[1024,256]{1,0:T(8,128)(2,1)S(1)}, u32[]{:S(2)}) copy-start(bf16[1024,256]{1,0:T(8,128)(2,1)S(1)} %collective-permute-done.1.w2) | copy-start | bytes 1572868
  95.7 7.7 %collective-permute-start.5 = (bf16[1024,256]{1,0:T(8,128)(2,1)S(1)}, bf16[1024,256]{1,0:T(8,128)(2,1)}, u32[]{:S(2)}, u32[]{:S(2)}) collective-permute-start(bf16[1024,256]{1,0:T(8,128)(2,1)S(1)} %collective-permute-done.1.w2), channel_id=1, source_target_pairs={{0,32},{32,0},{1,33},{33,1},{2,34},{34,2},{3,35},{35,3},{4,36},{36... | collective-permute-start | bytes 1572872 | tf_op jit(solution)/shard_map/ppermute | solution.py:267
  98.9 4.5 %copy-start.5 = (bf16[1024,256]{1,0:T(8,128)(2,1)}, bf16[1024,256]{1,0:T(8,128)(2,1)S(1)}, u32[]{:S(2)}) copy-start(bf16[1024,256]{1,0:T(8,128)(2,1)S(1)} %collective-permute-done.2.w3) | copy-start | bytes 1572868
  98.9 4.5 %collective-permute-start.6 = (bf16[1024,256]{1,0:T(8,128)(2,1)S(1)}, bf16[1024,256]{1,0:T(8,128)(2,1)}, u32[]{:S(2)}, u32[]{:S(2)}) collective-permute-start(bf16[1024,256]{1,0:T(8,128)(2,1)S(1)} %collective-permute-done.2.w3), channel_id=1, source_target_pairs={{0,32},{32,0},{1,33},{33,1},{2,34},{34,2},{3,35},{35,3},{4,36},{36... | collective-permute-start | bytes 1572872 | tf_op jit(solution)/shard_map/ppermute | solution.py:267
  99.0 4.4 %copy-start.2 = (bf16[32,48,128]{2,1,0:T(8,128)(2,1)}, bf16[32,48,128]{2,1,0:T(8,128)(2,1)S(1)}, u32[]{:S(2)}) copy-start(bf16[32,48,128]{2,1,0:T(8,128)(2,1)S(1)} %all-to-all-done.got) | copy-start | bytes 1179652
  99.1 9.6 %all-to-all-start.3 = ((bf16[4,64,256]{2,1,0:T(8,128)(2,1)}), bf16[4,64,256]{2,1,0:T(8,128)(2,1)}, u32[]{:S(2)}, u32[]{:S(2)}) async-start(bf16[4,64,256]{2,1,0:T(8,128)(2,1)} %get-tuple-element.15), calls=%async_computation.3 | async-start | bytes 262144 | tf_op jit(solution)/shard_map/all_to_all | solution.py:302
  103.4 0.8 copy-start.6
  103.4 1.0 copy-start.7
  108.6 6.1 %copy-start.9 = (s32[8,8]{1,0:T(8,128)S(1)}, s32[8,8]{1,0:T(8,128)}, u32[]{:S(2)}) copy-start(s32[8,8]{1,0:T(8,128)} %param.17) | copy-start | bytes 772
  108.6 6.7 %copy-start.10 = (s32[8]{0:T(128)S(1)}, s32[8]{0:T(128)}, u32[]{:S(2)}) copy-start(s32[8]{0:T(128)} %param.24) | copy-start | bytes 100
  108.6 30.4 %all-to-all-start.2 = ((bf16[32,128,128]{2,1,0:T(8,128)(2,1)}), bf16[32,128,128]{2,1,0:T(8,128)(2,1)S(1)}, u32[]{:S(2)}, u32[]{:S(2)}) async-start(bf16[32,128,128]{2,1,0:T(8,128)(2,1)} %shard_map.174), calls=%async_computation.2 | async-start | bytes 2097152 | tf_op jit(solution)/shard_map/all_to_all | solution.py:311
  139.0 1.0 copy-start
  144.6 17.2 %all-to-all-start.4 = ((bf16[8,64,128]{2,1,0:T(8,128)(2,1)}), bf16[8,64,128]{2,1,0:T(8,128)(2,1)S(1)}, u32[]{:S(2)}, u32[]{:S(2)}) async-start(bf16[8,64,128]{2,1,0:T(8,128)(2,1)} %get-tuple-element.18), calls=%async_computation.4 | async-start | bytes 262144 | tf_op jit(solution)/shard_map/all_to_all | solution.py:314
  154.2 27.3 %copy-start.8 = (f32[32,512]{1,0:T(8,128)S(1)}, f32[32,512]{1,0:T(8,128)}, u32[]{:S(2)}) copy-start(f32[32,512]{1,0:T(8,128)} %get-tuple-element.21) | copy-start | bytes 196612
  154.2 6.0 %collective-permute-start.7 = (f32[8,24,128]{2,1,0:T(8,128)}, f32[8,24,128]{2,1,0:T(8,128)S(1)}, u32[]{:S(2)}, u32[]{:S(2)}) collective-permute-start(f32[8,24,128]{2,1,0:T(8,128)} %get-tuple-element.20), channel_id=1, source_target_pairs={{0,32},{32,0},{1,33},{33,1},{2,34},{34,2},{3,35},{35,3},{4,36},{36... | collective-permute-start | bytes 294920 | tf_op jit(solution)/shard_map/ppermute | solution.py:267
  161.8 14.4 %all-to-all-start.6 = ((f32[8,24,128]{2,1,0:T(8,128)}), f32[8,24,128]{2,1,0:T(8,128)S(1)}, u32[]{:S(2)}, u32[]{:S(2)}) async-start(f32[8,24,128]{2,1,0:T(8,128)} %add.30), calls=%async_computation.6 | async-start | bytes 196608 | tf_op jit(solution)/shard_map/all_to_all | solution.py:325
  177.1 22.0 %all-to-all-start.5 = ((bf16[32,64,128]{2,1,0:T(8,128)(2,1)}), bf16[32,64,128]{2,1,0:T(8,128)(2,1)S(1)}, u32[]{:S(2)}, u32[]{:S(2)}) async-start(bf16[32,64,128]{2,1,0:T(8,128)(2,1)} %broadcast_in_dim.2), calls=%async_computation.5 | async-start | bytes 1048576 | tf_op jit(solution)/shard_map/all_to_all | solution.py:316
  181.6 2.9 %collective-permute-start.11 = (f32[32,512]{1,0:T(8,128)S(1)}, f32[32,512]{1,0:T(8,128)S(1)}, u32[]{:S(2)}, u32[]{:S(2)}) collective-permute-start(f32[32,512]{1,0:T(8,128)S(1)} %copy-done.8), channel_id=1, source_target_pairs={{0,32},{32,0},{1,33},{33,1},{2,34},{34,2},{3,35},{35,3},{4,36},{36... | collective-permute-start | bytes 196616 | tf_op jit(solution)/shard_map/ppermute | solution.py:267
  184.4 3.5 %collective-permute-start.12 = (f32[32,512]{1,0:T(8,128)S(1)}, f32[32,512]{1,0:T(8,128)S(1)}, u32[]{:S(2)}, u32[]{:S(2)}) collective-permute-start(f32[32,512]{1,0:T(8,128)S(1)} %add.33), channel_id=1, source_target_pairs={{0,64},{64,0},{128,192},{192,128},{1,65},{65,1},{129,193},{193,129... | collective-permute-start | bytes 196616 | tf_op jit(solution)/shard_map/ppermute | solution.py:271
  188.0 4.7 %collective-permute-start.13 = (f32[32,512]{1,0:T(8,128)S(1)}, f32[32,512]{1,0:T(8,128)S(1)}, u32[]{:S(2)}, u32[]{:S(2)}) collective-permute-start(f32[32,512]{1,0:T(8,128)S(1)} %add.34), channel_id=1, source_target_pairs={{0,192},{192,0},{64,128},{128,64},{1,193},{193,1},{65,129},{129,65... | collective-permute-start | bytes 196616 | tf_op jit(solution)/shard_map/ppermute | solution.py:272
  193.3 3.8 %collective-permute-start.8 = (f32[8,24,128]{2,1,0:T(8,128)S(1)}, f32[8,24,128]{2,1,0:T(8,128)S(1)}, u32[]{:S(2)}, u32[]{:S(2)}) collective-permute-start(f32[8,24,128]{2,1,0:T(8,128)S(1)} %all-to-all-done.6), channel_id=1, source_target_pairs={{0,64},{64,0},{128,192},{192,128},{1,65},{65,1},{129,193},{193,129... | collective-permute-start | bytes 294920 | tf_op jit(solution)/shard_map/ppermute | solution.py:271
  197.1 4.8 %collective-permute-start.9 = (f32[8,24,128]{2,1,0:T(8,128)S(1)}, f32[8,24,128]{2,1,0:T(8,128)S(1)}, u32[]{:S(2)}, u32[]{:S(2)}) collective-permute-start(f32[8,24,128]{2,1,0:T(8,128)S(1)} %add.31), channel_id=1, source_target_pairs={{0,192},{192,0},{64,128},{128,64},{1,193},{193,1},{65,129},{129,65... | collective-permute-start | bytes 294920 | tf_op jit(solution)/shard_map/ppermute | solution.py:272
  201.9 5.1 %collective-permute-start.10 = (f32[24,1024]{1,0:T(8,128)S(1)}, f32[24,1024]{1,0:T(8,128)S(1)}, u32[]{:S(2)}, u32[]{:S(2)}) collective-permute-start(f32[24,1024]{1,0:T(8,128)S(1)} %copy_bitcast_fusion), channel_id=1, source_target_pairs={{0,32},{32,0},{1,33},{33,1},{2,34},{34,2},{3,35},{35,3},{4,36},{36... | collective-permute-start | bytes 294920 | tf_op jit(solution)/shard_map/ppermute | solution.py:267
Sparse Core Ops, SparseCore 0:
  35.3 67.3 all-gather.2

commit v3 on v2

--- a/solution.py
+++ b/solution.py
@@ -21,7 +21,7 @@
     return pl.ds(pl.multiple_of(index * size, size), size)
 
 
-def hop_kernel(ids, cols, table, tiles_hbm, out, rows, picked, tiles, sem):
+def hop_kernel(place, ids, cols, table, bias, tiles_hbm, _, out, feats, rows, picked, tiles, sem):
     width = table.shape[0]
     blocks = tiles.shape[0]
     group = blocks // 8
@@ -40,6 +40,15 @@
 
     lax.fori_loop(0, table.shape[1] // TILE, turn, 0, unroll=8)
     step = 64
+    lane = lax.broadcasted_iota(jnp.int32, (8, TILE), 1)
+    row = lax.broadcasted_iota(jnp.int32, (8, TILE), 0)
+    left = jnp.concatenate([bias[...]] * 4, axis=1)
+    high = left.astype(BF).astype(F32)
+    left = left - high
+    middle = left.astype(BF).astype(F32)
+    low = left - middle
+    term = jnp.where(row == 0, high, jnp.where(row == 1, middle, jnp.where(row == 2, low, 0.0)))
+    term = jnp.where(lane // 32 == place[3], term, 0.0).astype(BF)
 
     def pick(g, carry):
         base = pl.multiple_of(g * step, step)
@@ -52,51 +61,46 @@
         copy.wait()
 
     def merge(r, carry):
-        out[r, 0:width, :] = picked[aligned(r, TILE), :].T[0:width].astype(BF)
+        own = picked[aligned(r, TILE), :].T[0:width]
         left = jnp.concatenate([tiles[r, k] for k in range(8)], axis=1)
         right = jnp.concatenate(
             [picked[aligned(cols[r * 8 + k], TILE), :].astype(BF) for k in range(8)], axis=0
         )
         total = jnp.dot(left, right, preferred_element_type=F32)
-        out[r, width : 2 * width, :] = total.T[0:width].astype(BF)
+        both = jnp.concatenate([own, total.T[0:width]], axis=0).astype(BF)
+        out[r, 0 : 2 * width, :] = both
+        feats[r] = both
+        out[r, 2 * width :, :] = term
         return carry
 
     lax.fori_loop(0, blocks, merge, 0, unroll=2)
 
 
-def hop(table, ids, cols, tiles):
-    blocks = tiles.shape[0]
+def hop(place, table, ids, cols, bias, tiles, after):
+    blocks, deep = tiles.shape[0], 2 * table.shape[0]
     return pl.pallas_call(
         hop_kernel,
-        in_specs=[SMEM, SMEM, VMEM, HBM],
-        out_specs=VMEM,
+        in_specs=[SMEM, SMEM, SMEM, VMEM, VMEM, HBM, HBM],
+        out_specs=[VMEM, VMEM],
         scratch_shapes=[
             pltpu.VMEM((table.shape[1], TILE), F32),
             pltpu.VMEM((ids.shape[0], TILE), F32),
             pltpu.VMEM(tiles.shape, BF),
             pltpu.SemaphoreType.DMA((8,)),
         ],
-        out_shape=jax.ShapeDtypeStruct((blocks, 2 * table.shape[0], TILE), BF),
+        out_shape=[
+            jax.ShapeDtypeStruct((blocks, deep + 8, TILE), BF),
+            jax.ShapeDtypeStruct((blocks, deep, TILE), BF),
+        ],
         compiler_params=LIMIT,
         cost_estimate=pl.CostEstimate(flops=10**9, bytes_accessed=60 * 10**6, transcendentals=0),
-    )(ids, cols.reshape(-1), table, tiles)
-
-
-def pack_kernel(place, own, neigh, bias, head_self, head_neigh, weights, heads):
-    core, x, feat = place[0], place[1], place[2]
+    )(place, ids, cols.reshape(-1), table, bias.reshape(1, -1), tiles, after)
+
+
+def pack_kernel(place, own, neigh, head_self, head_neigh, weights, heads):
+    core, x = place[0], place[1]
     cols = aligned(x, 256)
-    chosen = jnp.where(core == 0, own[:, cols], neigh[:, cols]).astype(F32)
-    lane = lax.broadcasted_iota(jnp.int32, (8, 256), 1) + x * 256
-    row = lax.broadcasted_iota(jnp.int32, (8, 256), 0)
-    left = jnp.concatenate([bias[...]] * 8, axis=1)
-    high = left.astype(BF).astype(F32)
-    left = left - high
-    middle = left.astype(BF).astype(F32)
-    low = left - middle
-    term = jnp.where(row == 0, high, jnp.where(row == 1, middle, jnp.where(row == 2, low, 0.0)))
-    inside = jnp.logical_and(lane >= feat * 32, lane < feat * 32 + 32)
-    term = jnp.where(jnp.logical_and(inside, core == 0), term, 0.0)
-    block = jnp.concatenate([chosen, term], axis=0).astype(BF)
+    block = jnp.where(core == 0, own[:, cols].astype(F32), neigh[:, cols].astype(F32)).astype(BF)
     for d in range(weights.shape[0]):
         weights[d] = block
     classes = head_self.shape[1]
@@ -106,17 +110,17 @@
         heads[d, 32:64, 0:classes] = head_neigh[...]
 
 
-def pack(place, own, neigh, bias, head_self, head_neigh):
+def pack(place, own, neigh, head_self, head_neigh):
     return pl.pallas_call(
         pack_kernel,
-        in_specs=[SMEM] + [VMEM] * 5,
+        in_specs=[SMEM] + [VMEM] * 4,
         out_specs=[VMEM, VMEM],
         out_shape=[
-            jax.ShapeDtypeStruct((32, 32, 256), BF),
+            jax.ShapeDtypeStruct((32, own.shape[0], 256), BF),
             jax.ShapeDtypeStruct((4, 64, 256), BF),
         ],
         compiler_params=LIMIT,
-    )(place, own, neigh, bias.reshape(1, -1), head_self, head_neigh)
+    )(place, own, neigh, head_self, head_neigh)
 
 
 def spread_kernel(cols, live, logit_cot, heads, tiles, out, cot):
@@ -153,30 +157,24 @@
 
 def layer_kernel(place, got, w0, w1, w2, w3, o0, o1, o2, o3, out, mine, other):
     core, x = place[0], place[1]
-    deep = got.shape[1] // 2
-    row = lax.broadcasted_iota(jnp.int32, (8, TILE), 0)
-    ones = jnp.where(row < 3, 1.0, 0.0)
-
+    deep = w0.shape[0] // 32
     for j in range(8):
-        own, agg = [], []
-        for i in range(4):
-            piece = got[4 * j + i].astype(F32)
-            own += [piece[0:deep], ones]
-            agg += [piece[deep : 2 * deep], ones]
-        own = jnp.concatenate(own, axis=0).T.astype(BF)
-        agg = jnp.concatenate(agg, axis=0).T.astype(BF)
-        at = slice(j * TILE, (j + 1) * TILE)
+        pieces = [got[4 * j + i, 0 : 2 * deep, :].astype(F32) for i in range(4)]
+        own = jnp.concatenate([piece[0:deep] for piece in pieces], axis=0).T.astype(BF)
+        agg = jnp.concatenate([piece[deep:] for piece in pieces], axis=0).T.astype(BF)
+        at = slice(j * 4 * deep, (j + 1) * 4 * deep)
         mine[:, at] = jnp.where(core == 0, own, agg)
         other[:, at] = jnp.where(core == 0, agg, own)
     for s, (w, o) in enumerate(((w0, o0), (w1, o1), (w2, o2), (w3, o3))):
         chunk = lax.rem(x + 4 - s, 4)
         preact = jnp.dot(mine[...], w[...], preferred_element_type=F32)
         preact = preact + jnp.dot(other[...], o[...], preferred_element_type=F32)
-        hidden = jnp.maximum(preact, 0.0)
         for half in range(2):
-            piece = hidden[:, half * TILE : (half + 1) * TILE].T.astype(BF)
-            for y in range(4):
-                out[(2 * chunk + half) * 4 + y] = piece
+            z = 2 * chunk + half
+            terms = sum(got[4 * z + i, 2 * deep : 2 * deep + 8, :].astype(F32) for i in range(4))
+            bias = jnp.sum(terms, axis=0, keepdims=True)
+            hidden = jnp.maximum(preact[:, half * TILE : (half + 1) * TILE] + bias, 0.0)
+            out[z] = hidden.T.astype(BF)
 
 
 def layer(place, got, mine, other):
@@ -184,14 +182,19 @@
         layer_kernel,
         in_specs=[SMEM] + [VMEM] * 9,
         out_specs=VMEM,
-        scratch_shapes=[pltpu.VMEM((TILE, 1024), BF), pltpu.VMEM((TILE, 1024), BF)],
-        out_shape=jax.ShapeDtypeStruct((32, TILE, TILE), BF),
+        scratch_shapes=[pltpu.VMEM((TILE, mine[0].shape[0]), BF)] * 2,
+        out_shape=jax.ShapeDtypeStruct((8, TILE, TILE), BF),
         compiler_params=LIMIT,
     )(place, got, *mine, *other)
 
 
-def score_kernel(place, cols, hidden, dhidden, tiles, cot, pair, out, heads, second):
+def score_kernel(
+    place, cols, h0, h1, h2, h3, dhidden, tiles, cot, pair, out, heads, second, hidden
+):
     y = place[3]
+    for s, part in enumerate((h0, h1, h2, h3)):
+        for z in range(part.shape[0]):
+            hidden[4 * z + lax.rem(y + 4 - s, 4)] = part[z]
     own = pl.ds(pl.multiple_of(y * 32, 32), 32)
     for r in range(tiles.shape[0]):
         left = jnp.concatenate([hidden[cols[r * 8 + k]] for k in range(8)], axis=1)
@@ -220,30 +223,36 @@
 def score(place, cols, hidden, dhidden, tiles, cot, pair):
     return pl.pallas_call(
         score_kernel,
-        in_specs=[SMEM, SMEM] + [VMEM] * 5,
-        out_specs=[VMEM, VMEM],
-        scratch_shapes=[pltpu.VMEM((tiles.shape[0], TILE, TILE), BF)],
+        in_specs=[SMEM, SMEM] + [VMEM] * 8,
+        out_specs=[VMEM, VMEM],
+        scratch_shapes=[
+            pltpu.VMEM((tiles.shape[0], TILE, TILE), BF),
+            pltpu.VMEM((32, TILE, TILE), BF),
+        ],
         out_shape=[
             jax.ShapeDtypeStruct((8, 64, TILE), BF),
             jax.ShapeDtypeStruct((32, 512), F32),
         ],
         compiler_params=LIMIT,
-    )(place, cols.reshape(-1), hidden, dhidden, tiles, cot, pair)
-
-
-def grad_kernel(place, hidden, dhidden, feats, keep, send, total):
-    core = place[0]
+    )(place, cols.reshape(-1), *hidden, dhidden, tiles, cot, pair)
+
+
+def grad_kernel(place, h0, h1, h2, h3, dhidden, feats, keep, send, total):
+    core, y = place[0], place[3]
     groups, blocks, deep, _ = feats.shape
     half = deep // 2
     total[...] = jnp.zeros_like(total)
-
-    def grow(b, carry):
-        low = jnp.where(hidden[b].astype(F32) > 0.0, dhidden[b], 0.0).astype(BF)
-        stack = jnp.concatenate([feats[z, b] for z in range(groups)], axis=0)
-        total[...] += lax.dot_general(stack, low, NT, preferred_element_type=F32)
-        return carry
-
-    lax.fori_loop(0, blocks, grow, 0, unroll=4)
+    for s, part in enumerate((h0, h1, h2, h3)):
+        first = lax.rem(y + 4 - s, 4)
+
+        def grow(z, carry):
+            b = 4 * z + first
+            low = jnp.where(part[z].astype(F32) > 0.0, dhidden[b], 0.0).astype(BF)
+            stack = jnp.concatenate([feats[g, b] for g in range(groups)], axis=0)
+            total[...] += lax.dot_general(stack, low, NT, preferred_element_type=F32)
+            return carry
+
+        lax.fori_loop(0, part.shape[0], grow, 0, unroll=4)
     for z in range(groups):
         keep[z] = total[pl.ds(pl.multiple_of(z * deep + core * half, 8), half), :]
         send[z] = total[pl.ds(pl.multiple_of(z * deep + (1 - core) * half, 8), half), :]
@@ -254,13 +263,17 @@
     shape = jax.ShapeDtypeStruct((groups, deep // 2, TILE), F32)
     return pl.pallas_call(
         grad_kernel,
-        in_specs=[SMEM] + [VMEM] * 3,
+        in_specs=[SMEM] + [VMEM] * 6,
         out_specs=[VMEM, VMEM],
         scratch_shapes=[pltpu.VMEM((groups * deep, TILE), F32)],
         out_shape=[shape, shape],
         compiler_params=LIMIT,
         cost_estimate=pl.CostEstimate(flops=10**9, bytes_accessed=7 * 10**6, transcendentals=0),
-    )(place, hidden, dhidden, feats)
+    )(place, *hidden, dhidden, feats)
+
+
+def shift(value, axis, by):
+    return lax.ppermute(value, axis, [(i, (i + by) % 4) for i in range(4)])
 
 
 def swap_core(value):
@@ -293,25 +306,30 @@
     y = lax.axis_index("y")
     place = jnp.stack([core, x, lax.axis_index("z") * 4 + y, y])
 
-    weights, pair = pack(place, self_weight, neigh_weight, hidden_bias, head_self, head_neigh)
-    weights = lax.all_to_all(weights, FEAT, 0, 0, tiled=True).reshape(1024, 256)
-    mine = [weights] + [
-        lax.ppermute(weights, "x", [(i, (i + s) % 4) for i in range(4)]) for s in (1, 2, 3)
-    ]
+    packed, pair = pack(place, self_weight, neigh_weight, head_self, head_neigh)
+    weights = lax.all_to_all(packed, FEAT, 0, 0, tiled=True)
+    pair = lax.all_to_all(pair, "y", 0, 0, tiled=True)
+
+    send, feats = hop(
+        place, feature_table, node_ids, hop_cols, hidden_bias, hop_tiles, packed
+    )
+    weights, pair, send, feats = lax.optimization_barrier((weights, pair, send, feats))
+    got = lax.all_to_all(send, FEAT, 0, 0, tiled=True)
+    feats = lax.all_gather(feats, "z", axis=0, tiled=False)
+    weights = weights.reshape(-1, 256)
+    mine = [weights] + [shift(weights, "x", s) for s in (1, 2, 3)]
     other = [swap_core(w) for w in mine]
-    pair = lax.all_to_all(pair, "y", 0, 0, tiled=True)
 
     live = batch_sizes[x * 2 + core]
     dhidden, cot = spread(target_cols, live, logit_cotangent, pair, target_tiles, blocks)
 
-    send = hop(feature_table, node_ids, hop_cols, hop_tiles)
-    feats = lax.all_gather(send, "z", axis=0, tiled=False)
-    got = lax.all_to_all(send, FEAT, 0, 0, tiled=True)
     hidden = layer(place, got, mine, other)
-    hidden = lax.all_to_all(hidden, FEAT, 0, 0, tiled=True)
+    hidden = lax.all_to_all(hidden, "z", 0, 0, tiled=True)
+    hidden = [hidden] + [shift(hidden, "y", s) for s in (1, 2, 3)]
 
     scores, heads = score(place, target_cols, hidden, dhidden, target_tiles, cot, pair)
     scores = lax.all_to_all(scores, "z", 0, 0, tiled=True)
+    keep, send = grad(place, hidden, dhidden, feats)
     scores = jnp.sum(scores.astype(F32), axis=0).astype(BF)
     scores = lax.all_to_all(
         jnp.broadcast_to(scores[None], (32,) + scores.shape), FEAT, 0, 0, tiled=True
@@ -319,11 +337,12 @@
     scores = scores.reshape(8, 4, 2, 32, TILE)[:, :, :, :24].transpose(0, 3, 1, 2, 4)
     logits = scores.reshape(192, target_rows)[:classes].astype(F32)
 
-    heads = sum_x(heads + swap_core(heads))
-    keep, send = grad(place, hidden, dhidden, feats)
     keep = keep + swap_core(send)
-    keep = sum_x(lax.all_to_all(keep, "z", 0, 0, tiled=True))
-    keep = keep.transpose(1, 0, 2).reshape(-1, 1024)
+    keep = lax.all_to_all(keep, "z", 0, 0, tiled=True)
+    heads = heads + swap_core(heads)
+    joined = sum_x(jnp.concatenate([keep.reshape(-1, TILE), heads.reshape(-1, TILE)], axis=0))
+    heads = joined[keep.size // TILE :].reshape(heads.shape)
+    keep = joined[: keep.size // TILE].reshape(keep.shape).transpose(1, 0, 2).reshape(-1, 1024)
     rest = swap_core(keep)
     return (
         logits,

time: 215 us -> 208 us (0.967)
  waiting for transfers between devices: 44.5 us -> 38.1 us
  blocking collectives: 33.5 us -> 30.9 us
  starting transfers between devices: 62.4 us -> 64.8 us
    all_to_all x3 -> x2, waiting for transfers between devices: 24.7 us -> 7.44 us  [the longest x1 7.43 us: shards(): keep = lax.all_to_all(keep, 'z', 0, 0, tiled=True)]
    all_to_all x1, waiting for transfers between devices: 0.01 us -> 11.8 us  [shards(): lax.all_to_all(jnp.broadcast_to(scores[None], (32,) + scores.shape), FEAT...]
    ppermute x2 -> x1, waiting for transfers between devices: 5.5 us -> 0.01 us  [sum_x(): value = value + lax.ppermute(value, 'x', [(0, 1), (1, 0), (2, 3), (3, 2)])]
    ppermute x3 -> x6, waiting for transfers between devices: 7.34 us -> 11.8 us  [shift(): return lax.ppermute(value, axis, [(i, (i + by) % 4) for i in range(4)])]
    all_to_all x1, starting transfers between devices: 5.03 us -> 9.23 us  [shards(): got = lax.all_to_all(send, FEAT, 0, 0, tiled=True)]
    ppermute x2 -> x1, starting transfers between devices: 3.99 us -> 1.23 us  [sum_x(): return value + lax.ppermute(value, 'x', [(0, 3), (3, 0), (1, 2), (2, 1)])]
    all_to_all x1 -> x2, blocking collectives: 33.5 us -> 30.9 us  [the longest x1 21 us: shards(): hidden = lax.all_to_all(hidden, 'z', 0, 0, tiled=True)]
    ppermute x7, starting transfers between devices: 21.7 us -> 23.9 us  [swap_core(): return lax.ppermute(value, 'core', [(0, 1), (1, 0)])]
  transfers between devices with their start and end apart: 21 -> 21, of which waited for: 9 -> 11; matrix products, arithmetic and copies ran while one was open for 3% -> 3% of each run, Pallas kernels for 10% -> 22%
where the time goes in v3:
time: 208 us; the launch traced here: 207 us
  starting transfers between devices  64.8 us (31%)
  Pallas kernels  48.2 us (23%)
  waiting for transfers between devices  38.1 us (18%)
  blocking collectives  30.9 us (15%)
  between operations  14.3 us (7%)
  local copies, waits for them, and re-layouts  7.05 us (3%)
  other arithmetic  3.89 us (2%)
    pallas_call x1, Pallas kernels, hop(): pl.pallas_call(hop_kernel, in_specs=[SMEM, SMEM, SMEM, VMEM, VMEM, HBM, H...  26.7 us
    ppermute x7, starting transfers between devices, swap_core(): return lax.ppermute(value, 'core', [(0, 1), (1, 0)])  23.9 us
    all_to_all x1, blocking collectives, shards(): hidden = lax.all_to_all(hidden, 'z', 0, 0, tiled=True)  21 us
    all_to_all x1, waiting for transfers between devices, shards(): lax.all_to_all(jnp.broadcast_to(scores[None], (32,) + scores.shape), FEAT...  11.8 us
    ppermute x6, waiting for transfers between devices, shift(): return lax.ppermute(value, axis, [(i, (i + by) % 4) for i in range(4)])  11.8 us
    all_to_all x1, blocking collectives, shards(): pair = lax.all_to_all(pair, 'y', 0, 0, tiled=True)  9.94 us
    all_to_all x1, starting transfers between devices, shards(): got = lax.all_to_all(send, FEAT, 0, 0, tiled=True)  9.23 us
    all_to_all x1, starting transfers between devices, shards(): weights = lax.all_to_all(packed, FEAT, 0, 0, tiled=True)  9.18 us
  transfers between devices with their start and end apart: 21, of which 11 were waited for; matrix products, arithmetic and copies ran while one was open for 3% of the time, Pallas kernels for 22%

profile of v3, /device:TPU:1, one launch (start us, length us, event | category | flops | bytes accessed | tf_op | source)
XLA Modules:
  0.0 207.4 jit_solution(15445314938244713968)
XLA Ops:
  7.2 0.7 pad_add_fusion.place
  7.8 1.7 shard_map.172
  9.5 9.9 %all_to_all.35.heads.pair = bf16[4,64,256]{2,1,0:T(8,128)(2,1)} all-to-all(bf16[4,64,256]{2,1,0:T(8,128)(2,1)} %get-tuple-element.21), channel_id=1, replica_groups=mesh['x'=4,'core'=2,'z'=8,'y'=4] {'y'}, dimensions={0} | all-to-all | bytes 262144 | tf_op jit(solution)/shard_map/all_to_all | solution.py:311
  19.4 9.2 %all-to-all-start = ((bf16[32,24,256]{2,1,0:T(8,128)(2,1)}), bf16[32,24,256]{2,1,0:T(8,128)(2,1)S(1)}, u32[]{:S(2)}, u32[]{:S(2)}) async-start(bf16[32,24,256]{2,1,0:T(8,128)(2,1)} %get-tuple-element.20._), calls=%async_computation | async-start | bytes 786432 | tf_op jit(solution)/shard_map/all_to_all | solution.py:310
  28.7 0.8 copy.25
  29.4 0.7 reshape.48.cols
  30.1 26.7 %shard_map.173 = (bf16[32,56,128]{2,1,0:T(8,128)(2,1)}, bf16[32,48,128]{2,1,0:T(8,128)(2,1)}) custom-call(s32[4]{0:T(128)} %pad_add_fusion.place, s32[16384]{0:T(1024)} %ids.1, s32[256]{0:T(256)} %reshape.48.cols, bf16[24,32768]{1,0:T(8,128)(2,1)} %table.1, f32[1,32]{1,0:T(1,128)} %bitcast.34, bf16[32,8,128,128]{3,2,1,0:T(8,128)(2,1)} %tiles_hbm.1, ...), custom_call_target="tpu_custom_call" | custom-call | flops 1000000000 | bytes 60000000 | tf_op jit(solution)/shard_map/pallas_call | solution.py:81
  56.9 9.2 %all-to-all-start.2 = ((bf16[32,56,128]{2,1,0:T(8,128)(2,1)}), bf16[32,56,128]{2,1,0:T(8,128)(2,1)S(1)}, u32[]{:S(2)}, u32[]{:S(2)}) async-start(bf16[32,56,128]{2,1,0:T(8,128)(2,1)} %get-tuple-element.24), calls=%async_computation.2 | async-start | bytes 917504 | tf_op jit(solution)/shard_map/all_to_all | solution.py:317
  66.1 2.6 %collective-permute-start.2 = (bf16[768,256]{1,0:T(8,128)(2,1)S(1)}, bf16[768,256]{1,0:T(8,128)(2,1)S(1)}, u32[]{:S(2)}, u32[]{:S(2)}) collective-permute-start(bf16[768,256]{1,0:T(8,128)(2,1)S(1)} %bitcast.23), channel_id=1, source_target_pairs={{0,192},{64,0},{128,64},{192,128},{1,193},{65,1},{129,65},{193,129... | collective-permute-start | bytes 1179656 | tf_op jit(solution)/shard_map/ppermute | solution.py:276
  68.7 0.5 collective-permute-start.1
  69.2 0.6 collective-permute-start
  69.8 3.8 %collective-permute-start.3 = (bf16[768,256]{1,0:T(8,128)(2,1)S(1)}, bf16[768,256]{1,0:T(8,128)(2,1)S(1)}, u32[]{:S(2)}, u32[]{:S(2)}) collective-permute-start(bf16[768,256]{1,0:T(8,128)(2,1)S(1)} %bitcast.26), channel_id=1, source_target_pairs={{0,32},{32,0},{1,33},{33,1},{2,34},{34,2},{3,35},{35,3},{4,36},{36... | collective-permute-start | bytes 1179656 | tf_op jit(solution)/shard_map/ppermute | solution.py:280
  73.6 1.3 collective-permute-done.2.w3
  74.9 11.6 %collective-permute-start.6 = (bf16[768,256]{1,0:T(8,128)(2,1)S(1)}, bf16[768,256]{1,0:T(8,128)(2,1)S(1)}, u32[]{:S(2)}, u32[]{:S(2)}) collective-permute-start(bf16[768,256]{1,0:T(8,128)(2,1)S(1)} %collective-permute-done.2.w3), channel_id=1, source_target_pairs={{0,32},{32,0},{1,33},{33,1},{2,34},{34,2},{3,35},{35,3},{4,36},{36... | collective-permute-start | bytes 1179656 | tf_op jit(solution)/shard_map/ppermute | solution.py:280
  86.6 3.2 %collective-permute-done.w1 = bf16[768,256]{1,0:T(8,128)(2,1)S(1)} collective-permute-done((bf16[768,256]{1,0:T(8,128)(2,1)S(1)}, bf16[768,256]{1,0:T(8,128)(2,1)S(1)}, u32[]{:S(2)}, u32[]{:S(2)}) %collective-permute-start) | collective-permute-done | bytes 393248 | tf_op jit(solution)/shard_map/ppermute | solution.py:276
  89.8 0.4 collective-permute-start.4
  90.2 1.4 collective-permute-done.4.o1
  91.7 0.8 copy-done.1
  92.5 3.7 %shard_map.174 = bf16[8,128,128]{2,1,0:T(8,128)(2,1)} custom-call(s32[4]{0:T(128)} %pad_add_fusion.place, bf16[32,56,128]{2,1,0:T(8,128)(2,1)} %copy-done.1, bf16[768,256]{1,0:T(8,128)(2,1)} %bitcast.27, bf16[768,256]{1,0:T(8,128)(2,1)} %copy-done.8, bf16[768,256]{1,0:T(8,128)(2,1)} %copy-done.7, bf16[768,256]{1,0:T(8,128)(2,1)} %copy-done.6, ...), custom_call_target="tpu_custom_call" | custom-call | tf_op jit(solution)/shard_map/pallas_call | solution.py:181
  96.1 21.0 %all_to_all.36.h0 = bf16[8,128,128]{2,1,0:T(8,128)(2,1)S(1)} all-to-all(bf16[8,128,128]{2,1,0:T(8,128)(2,1)} %shard_map.174), channel_id=1, replica_groups=mesh['x'=4,'core'=2,'z'=8,'y'=4] {'z'}, dimensions={0} | all-to-all | bytes 524288 | tf_op jit(solution)/shard_map/all_to_all | solution.py:327
  117.1 2.4 %collective-permute-start.9 = (bf16[8,128,128]{2,1,0:T(8,128)(2,1)S(1)}, bf16[8,128,128]{2,1,0:T(8,128)(2,1)S(1)}, u32[]{:S(2)}, u32[]{:S(2)}) collective-permute-start(bf16[8,128,128]{2,1,0:T(8,128)(2,1)S(1)} %all_to_all.36.h0), channel_id=1, source_target_pairs={{0,3},{1,0},{2,1},{3,2},{4,7},{5,4},{6,5},{7,6},{8,11},{9,8},{10,9... | collective-permute-start | bytes 786440 | tf_op jit(solution)/shard_map/ppermute | solution.py:276
  119.5 0.6 collective-permute-start.8
  120.1 0.4 collective-permute-start.7
  120.5 0.6 reshape.47.cols
  121.1 0.6 dynamic_slice.3.live
  121.7 5.9 %shard_map.175 = (f32[32,128,128]{2,1,0:T(8,128)}, bf16[256,1024]{1,0:T(8,128)(2,1)}) custom-call(s32[64]{0:T(128)} %reshape.47.cols, s32[1]{0:T(128)} %dynamic_slice.3.live, bf16[153,1024]{1,0:T(8,128)(2,1)} %logit_cot.1, bf16[4,64,256]{2,1,0:T(8,128)(2,1)} %all_to_all.35.heads.pair, bf16[8,8,128,128]{3,2,1,0:T(8,128)(2,1)} %tiles.3), custom_call_target="tpu_custom_call" | custom-call | flops 1000000000 | bytes 8000000 | tf_op jit(solution)/shard_map/pallas_call | solution.py:145
  127.8 7.1 %collective-permute-done.7.h1 = bf16[8,128,128]{2,1,0:T(8,128)(2,1)S(1)} collective-permute-done((bf16[8,128,128]{2,1,0:T(8,128)(2,1)S(1)}, bf16[8,128,128]{2,1,0:T(8,128)(2,1)S(1)}, u32[]{:S(2)}, u32[]{:S(2)}) %collective-permute-start.7) | collective-permute-done | bytes 262176 | tf_op jit(solution)/shard_map/ppermute | solution.py:276
  134.9 0.7 copy-done.5
  135.6 4.5 %shard_map.176 = (bf16[8,64,128]{2,1,0:T(8,128)(2,1)}, f32[32,512]{1,0:T(8,128)}) custom-call(s32[4]{0:T(128)} %pad_add_fusion.place, s32[64]{0:T(128)} %reshape.47.cols, bf16[8,128,128]{2,1,0:T(8,128)(2,1)} %copy-done, bf16[8,128,128]{2,1,0:T(8,128)(2,1)} %copy-done.5, bf16[8,128,128]{2,1,0:T(8,128)(2,1)} %copy-done.4, bf16[8,128,128]{2,1,0:T(8,128)(2,1)} %copy-done.3, ...), custom_call_target="tpu_custom_call" | custom-call | tf_op jit(solution)/shard_map/pallas_call | solution.py:224
  140.1 3.5 %all-to-all-start.4 = ((bf16[8,64,128]{2,1,0:T(8,128)(2,1)}), bf16[8,64,128]{2,1,0:T(8,128)(2,1)S(1)}, u32[]{:S(2)}, u32[]{:S(2)}) async-start(bf16[8,64,128]{2,1,0:T(8,128)(2,1)} %get-tuple-element.29), calls=%async_computation.4 | async-start | bytes 262144 | tf_op jit(solution)/shard_map/all_to_all | solution.py:331
  143.7 5.8 %shard_map.177 = (f32[8,24,128]{2,1,0:T(8,128)}, f32[8,24,128]{2,1,0:T(8,128)}) custom-call(s32[4]{0:T(128)} %pad_add_fusion.place, bf16[8,128,128]{2,1,0:T(8,128)(2,1)} %copy-done, bf16[8,128,128]{2,1,0:T(8,128)(2,1)} %copy-done.5, bf16[8,128,128]{2,1,0:T(8,128)(2,1)} %copy-done.4, bf16[8,128,128]{2,1,0:T(8,128)(2,1)} %copy-done.3, ...), custom_call_target="tpu_custom_call" | custom-call | flops 1000000000 | bytes 7000000 | tf_op jit(solution)/shard_map/pallas_call | solution.py:264
  149.4 0.5 collective-permute-start.10
  149.9 1.2 collective-permute-done.10
  151.1 1.5 add.24
  152.6 6.6 %all-to-all-start.6 = ((f32[8,24,128]{2,1,0:T(8,128)}), f32[8,24,128]{2,1,0:T(8,128)S(1)}, u32[]{:S(2)}, u32[]{:S(2)}) async-start(f32[8,24,128]{2,1,0:T(8,128)} %add.24), calls=%async_computation.6 | async-start | bytes 196608 | tf_op jit(solution)/shard_map/all_to_all | solution.py:341
  159.3 7.4 %all-to-all-done.6 = f32[8,24,128]{2,1,0:T(8,128)S(1)} async-done(((f32[8,24,128]{2,1,0:T(8,128)}), f32[8,24,128]{2,1,0:T(8,128)S(1)}, u32[]{:S(2)}, u32[]{:S(2)}) %all-to-all-start.6) | async-done | bytes 98336 | tf_op jit(solution)/shard_map/all_to_all | solution.py:341
  166.7 0.9 broadcast_in_dim.2
  167.6 3.9 %all-to-all-start.5 = ((bf16[32,64,128]{2,1,0:T(8,128)(2,1)}), bf16[32,64,128]{2,1,0:T(8,128)(2,1)S(1)}, u32[]{:S(2)}, u32[]{:S(2)}) async-start(bf16[32,64,128]{2,1,0:T(8,128)(2,1)} %broadcast_in_dim.2), calls=%async_computation.5 | async-start | bytes 1048576 | tf_op jit(solution)/shard_map/all_to_all | solution.py:334
  171.6 2.1 %collective-permute-start.11 = (f32[32,512]{1,0:T(8,128)S(1)}, f32[32,512]{1,0:T(8,128)S(1)}, u32[]{:S(2)}, u32[]{:S(2)}) collective-permute-start(f32[32,512]{1,0:T(8,128)S(1)} %copy-done.12), channel_id=1, source_target_pairs={{0,32},{32,0},{1,33},{33,1},{2,34},{34,2},{3,35},{35,3},{4,36},{36... | collective-permute-start | bytes 196616 | tf_op jit(solution)/shard_map/ppermute | solution.py:280
  173.6 0.9 collective-permute-done.11
  174.7 11.8 %all-to-all-done.5 = bf16[32,64,128]{2,1,0:T(8,128)(2,1)S(1)} async-done(((bf16[32,64,128]{2,1,0:T(8,128)(2,1)}), bf16[32,64,128]{2,1,0:T(8,128)(2,1)S(1)}, u32[]{:S(2)}, u32[]{:S(2)}) %all-to-all-start.5) | async-done | bytes 524320 | tf_op jit(solution)/shard_map/all_to_all | solution.py:334
  187.2 1.2 collective-permute-start.13
  188.4 0.9 slice_convert_fusion
  189.3 3.3 %collective-permute-done.13 = f32[320,128]{1,0:T(8,128)S(1)} collective-permute-done((f32[320,128]{1,0:T(8,128)S(1)}, f32[320,128]{1,0:T(8,128)S(1)}, u32[]{:S(2)}, u32[]{:S(2)}) %collective-permute-start.13) | collective-permute-done | bytes 163872 | tf_op jit(solution)/shard_map/ppermute | solution.py:285
  192.7 0.6 fusion.1
  193.4 5.5 %collective-permute-start.14 = (f32[24,1024]{1,0:T(8,128)S(1)}, f32[24,1024]{1,0:T(8,128)S(1)}, u32[]{:S(2)}, u32[]{:S(2)}) collective-permute-start(f32[24,1024]{1,0:T(8,128)S(1)} %bitcast.33), channel_id=1, source_target_pairs={{0,32},{32,0},{1,33},{33,1},{2,34},{34,2},{3,35},{35,3},{4,36},{36... | collective-permute-start | bytes 294920 | tf_op jit(solution)/shard_map/ppermute | solution.py:280
  198.9 0.7 slice_reduce_fusion
  199.8 0.7 broadcast_select_fusion
  (58 shorter events, 1.7 us)
Async XLA Ops:
  19.4 37.4 %all-to-all-start = ((bf16[32,24,256]{2,1,0:T(8,128)(2,1)}), bf16[32,24,256]{2,1,0:T(8,128)(2,1)S(1)}, u32[]{:S(2)}, u32[]{:S(2)}) async-start(bf16[32,24,256]{2,1,0:T(8,128)(2,1)} %get-tuple-element.20._), calls=%async_computation | async-start | bytes 786432 | tf_op jit(solution)/shard_map/all_to_all | solution.py:310
  28.6 115.1 %all-gather.3.cloned.1.call-start = ((), (), s32[]{:S(2)}) async-start(), calls=%async_computation.7 | async-start | bytes 3538944 | tf_op jit(solution)/shard_map/all_gather | solution.py:318
  56.8 34.8 %copy-start.2 = (bf16[32,24,256]{2,1,0:T(8,128)(2,1)}, bf16[32,24,256]{2,1,0:T(8,128)(2,1)S(1)}, u32[]{:S(2)}) copy-start(bf16[32,24,256]{2,1,0:T(8,128)(2,1)S(1)} %all-to-all-done) | copy-start | bytes 1179652
  56.9 34.8 %all-to-all-start.2 = ((bf16[32,56,128]{2,1,0:T(8,128)(2,1)}), bf16[32,56,128]{2,1,0:T(8,128)(2,1)S(1)}, u32[]{:S(2)}, u32[]{:S(2)}) async-start(bf16[32,56,128]{2,1,0:T(8,128)(2,1)} %get-tuple-element.24), calls=%async_computation.2 | async-start | bytes 917504 | tf_op jit(solution)/shard_map/all_to_all | solution.py:317
  66.1 54.4 %copy-start.13 = (s32[8,8]{1,0:T(8,128)S(1)}, s32[8,8]{1,0:T(8,128)}, u32[]{:S(2)}) copy-start(s32[8,8]{1,0:T(8,128)} %param.17) | copy-start | bytes 772
  66.1 55.0 %copy-start.14 = (s32[8]{0:T(128)S(1)}, s32[8]{0:T(128)}, u32[]{:S(2)}) copy-start(s32[8]{0:T(128)} %param.24) | copy-start | bytes 100
  66.1 8.8 %collective-permute-start.2 = (bf16[768,256]{1,0:T(8,128)(2,1)S(1)}, bf16[768,256]{1,0:T(8,128)(2,1)S(1)}, u32[]{:S(2)}, u32[]{:S(2)}) collective-permute-start(bf16[768,256]{1,0:T(8,128)(2,1)S(1)} %bitcast.23), channel_id=1, source_target_pairs={{0,192},{64,0},{128,64},{192,128},{1,193},{65,1},{129,65},{193,129... | collective-permute-start | bytes 1179656 | tf_op jit(solution)/shard_map/ppermute | solution.py:276
  68.7 17.8 %collective-permute-start.1 = (bf16[768,256]{1,0:T(8,128)(2,1)S(1)}, bf16[768,256]{1,0:T(8,128)(2,1)S(1)}, u32[]{:S(2)}, u32[]{:S(2)}) collective-permute-start(bf16[768,256]{1,0:T(8,128)(2,1)S(1)} %bitcast.24), channel_id=1, source_target_pairs={{0,128},{64,192},{128,0},{192,64},{1,129},{65,193},{129,1},{193,65... | collective-permute-start | bytes 1179656 | tf_op jit(solution)/shard_map/ppermute | solution.py:276
  69.2 20.6 %collective-permute-start = (bf16[768,256]{1,0:T(8,128)(2,1)S(1)}, bf16[768,256]{1,0:T(8,128)(2,1)S(1)}, u32[]{:S(2)}, u32[]{:S(2)}) collective-permute-start(bf16[768,256]{1,0:T(8,128)(2,1)S(1)} %bitcast.25), channel_id=1, source_target_pairs={{0,64},{64,128},{128,192},{192,0},{1,65},{65,129},{129,193},{193,1... | collective-permute-start | bytes 1179656 | tf_op jit(solution)/shard_map/ppermute | solution.py:276
  69.8 20.3 %collective-permute-start.3 = (bf16[768,256]{1,0:T(8,128)(2,1)S(1)}, bf16[768,256]{1,0:T(8,128)(2,1)S(1)}, u32[]{:S(2)}, u32[]{:S(2)}) collective-permute-start(bf16[768,256]{1,0:T(8,128)(2,1)S(1)} %bitcast.26), channel_id=1, source_target_pairs={{0,32},{32,0},{1,33},{33,1},{2,34},{34,2},{3,35},{35,3},{4,36},{36... | collective-permute-start | bytes 1179656 | tf_op jit(solution)/shard_map/ppermute | solution.py:280
  74.9 16.8 %copy-start.6 = (bf16[768,256]{1,0:T(8,128)(2,1)}, bf16[768,256]{1,0:T(8,128)(2,1)S(1)}, u32[]{:S(2)}) copy-start(bf16[768,256]{1,0:T(8,128)(2,1)S(1)} %collective-permute-done.2.w3) | copy-start | bytes 1179652
  74.9 15.3 %collective-permute-start.6 = (bf16[768,256]{1,0:T(8,128)(2,1)S(1)}, bf16[768,256]{1,0:T(8,128)(2,1)S(1)}, u32[]{:S(2)}, u32[]{:S(2)}) collective-permute-start(bf16[768,256]{1,0:T(8,128)(2,1)S(1)} %collective-permute-done.2.w3), channel_id=1, source_target_pairs={{0,32},{32,0},{1,33},{33,1},{2,34},{34,2},{3,35},{35,3},{4,36},{36... | collective-permute-start | bytes 1179656 | tf_op jit(solution)/shard_map/ppermute | solution.py:280
  86.5 5.2 %copy-start.7 = (bf16[768,256]{1,0:T(8,128)(2,1)}, bf16[768,256]{1,0:T(8,128)(2,1)S(1)}, u32[]{:S(2)}) copy-start(bf16[768,256]{1,0:T(8,128)(2,1)S(1)} %collective-permute-done.1.w2) | copy-start | bytes 1179652
  86.5 3.7 %collective-permute-start.5 = (bf16[768,256]{1,0:T(8,128)(2,1)S(1)}, bf16[768,256]{1,0:T(8,128)(2,1)S(1)}, u32[]{:S(2)}, u32[]{:S(2)}) collective-permute-start(bf16[768,256]{1,0:T(8,128)(2,1)S(1)} %collective-permute-done.1.w2), channel_id=1, source_target_pairs={{0,32},{32,0},{1,33},{33,1},{2,34},{34,2},{3,35},{35,3},{4,36},{36... | collective-permute-start | bytes 1179656 | tf_op jit(solution)/shard_map/ppermute | solution.py:280
  89.8 1.9 copy-start.8
  89.8 1.9 collective-permute-start.4
  90.1 1.5 copy-start.9
  90.2 1.5 copy-start.10
  90.2 1.5 copy-start.11
  91.7 0.8 copy-start.1
  117.1 17.8 %copy-start = (bf16[8,128,128]{2,1,0:T(8,128)(2,1)}, bf16[8,128,128]{2,1,0:T(8,128)(2,1)S(1)}, u32[]{:S(2)}) copy-start(bf16[8,128,128]{2,1,0:T(8,128)(2,1)S(1)} %all_to_all.36.h0) | copy-start | bytes 786436
  117.1 10.4 %collective-permute-start.9 = (bf16[8,128,128]{2,1,0:T(8,128)(2,1)S(1)}, bf16[8,128,128]{2,1,0:T(8,128)(2,1)S(1)}, u32[]{:S(2)}, u32[]{:S(2)}) collective-permute-start(bf16[8,128,128]{2,1,0:T(8,128)(2,1)S(1)} %all_to_all.36.h0), channel_id=1, source_target_pairs={{0,3},{1,0},{2,1},{3,2},{4,7},{5,4},{6,5},{7,6},{8,11},{9,8},{10,9... | collective-permute-start | bytes 786440 | tf_op jit(solution)/shard_map/ppermute | solution.py:276
  119.5 8.3 %collective-permute-start.8 = (bf16[8,128,128]{2,1,0:T(8,128)(2,1)S(1)}, bf16[8,128,128]{2,1,0:T(8,128)(2,1)S(1)}, u32[]{:S(2)}, u32[]{:S(2)}) collective-permute-start(bf16[8,128,128]{2,1,0:T(8,128)(2,1)S(1)} %all_to_all.36.h0), channel_id=1, source_target_pairs={{0,2},{1,3},{2,0},{3,1},{4,6},{5,7},{6,4},{7,5},{8,10},{9,11},{10,... | collective-permute-start | bytes 786440 | tf_op jit(solution)/shard_map/ppermute | solution.py:276
  120.1 14.8 %collective-permute-start.7 = (bf16[8,128,128]{2,1,0:T(8,128)(2,1)S(1)}, bf16[8,128,128]{2,1,0:T(8,128)(2,1)S(1)}, u32[]{:S(2)}, u32[]{:S(2)}) collective-permute-start(bf16[8,128,128]{2,1,0:T(8,128)(2,1)S(1)} %all_to_all.36.h0), channel_id=1, source_target_pairs={{0,1},{1,2},{2,3},{3,0},{4,5},{5,6},{6,7},{7,4},{8,9},{9,10},{10,1... | collective-permute-start | bytes 786440 | tf_op jit(solution)/shard_map/ppermute | solution.py:276
  127.5 7.3 %copy-start.3 = (bf16[8,128,128]{2,1,0:T(8,128)(2,1)}, bf16[8,128,128]{2,1,0:T(8,128)(2,1)S(1)}, u32[]{:S(2)}) copy-start(bf16[8,128,128]{2,1,0:T(8,128)(2,1)S(1)} %collective-permute-done.9.h3) | copy-start | bytes 786436
  127.8 7.1 %copy-start.4 = (bf16[8,128,128]{2,1,0:T(8,128)(2,1)}, bf16[8,128,128]{2,1,0:T(8,128)(2,1)S(1)}, u32[]{:S(2)}) copy-start(bf16[8,128,128]{2,1,0:T(8,128)(2,1)S(1)} %collective-permute-done.8.h2) | copy-start | bytes 786436
  134.9 0.7 copy-start.5
  140.1 12.5 %all-to-all-start.4 = ((bf16[8,64,128]{2,1,0:T(8,128)(2,1)}), bf16[8,64,128]{2,1,0:T(8,128)(2,1)S(1)}, u32[]{:S(2)}, u32[]{:S(2)}) async-start(bf16[8,64,128]{2,1,0:T(8,128)(2,1)} %get-tuple-element.29), calls=%async_computation.4 | async-start | bytes 262144 | tf_op jit(solution)/shard_map/all_to_all | solution.py:331
  149.4 22.1 %copy-start.12 = (f32[32,512]{1,0:T(8,128)S(1)}, f32[32,512]{1,0:T(8,128)}, u32[]{:S(2)}) copy-start(f32[32,512]{1,0:T(8,128)} %get-tuple-element.33) | copy-start | bytes 196612
  149.4 1.6 collective-permute-start.10
  152.6 14.1 %all-to-all-start.6 = ((f32[8,24,128]{2,1,0:T(8,128)}), f32[8,24,128]{2,1,0:T(8,128)S(1)}, u32[]{:S(2)}, u32[]{:S(2)}) async-start(f32[8,24,128]{2,1,0:T(8,128)} %add.24), calls=%async_computation.6 | async-start | bytes 196608 | tf_op jit(solution)/shard_map/all_to_all | solution.py:341
  167.6 18.8 %all-to-all-start.5 = ((bf16[32,64,128]{2,1,0:T(8,128)(2,1)}), bf16[32,64,128]{2,1,0:T(8,128)(2,1)S(1)}, u32[]{:S(2)}, u32[]{:S(2)}) async-start(bf16[32,64,128]{2,1,0:T(8,128)(2,1)} %broadcast_in_dim.2), calls=%async_computation.5 | async-start | bytes 1048576 | tf_op jit(solution)/shard_map/all_to_all | solution.py:334
  171.6 3.0 %collective-permute-start.11 = (f32[32,512]{1,0:T(8,128)S(1)}, f32[32,512]{1,0:T(8,128)S(1)}, u32[]{:S(2)}, u32[]{:S(2)}) collective-permute-start(f32[32,512]{1,0:T(8,128)S(1)} %copy-done.12), channel_id=1, source_target_pairs={{0,32},{32,0},{1,33},{33,1},{2,34},{34,2},{3,35},{35,3},{4,36},{36... | collective-permute-start | bytes 196616 | tf_op jit(solution)/shard_map/ppermute | solution.py:280
  174.6 12.6 %collective-permute-start.12 = (f32[320,128]{1,0:T(8,128)S(1)}, f32[320,128]{1,0:T(8,128)S(1)}, u32[]{:S(2)}, u32[]{:S(2)}) collective-permute-start(f32[320,128]{1,0:T(8,128)S(1)} %pad_maximum_fusion), channel_id=1, source_target_pairs={{0,64},{64,0},{128,192},{192,128},{1,65},{65,1},{129,193},{193,129... | collective-permute-start | bytes 491528 | tf_op jit(solution)/shard_map/ppermute | solution.py:284
  187.2 5.5 %collective-permute-start.13 = (f32[320,128]{1,0:T(8,128)S(1)}, f32[320,128]{1,0:T(8,128)S(1)}, u32[]{:S(2)}, u32[]{:S(2)}) collective-permute-start(f32[320,128]{1,0:T(8,128)S(1)} %fusion), channel_id=1, source_target_pairs={{0,192},{192,0},{64,128},{128,64},{1,193},{193,1},{65,129},{129,65... | collective-permute-start | bytes 491528 | tf_op jit(solution)/shard_map/ppermute | solution.py:285
  193.4 6.4 %collective-permute-start.14 = (f32[24,1024]{1,0:T(8,128)S(1)}, f32[24,1024]{1,0:T(8,128)S(1)}, u32[]{:S(2)}, u32[]{:S(2)}) collective-permute-start(f32[24,1024]{1,0:T(8,128)S(1)} %bitcast.33), channel_id=1, source_target_pairs={{0,32},{32,0},{1,33},{33,1},{2,34},{34,2},{3,35},{35,3},{4,36},{36... | collective-permute-start | bytes 294920 | tf_op jit(solution)/shard_map/ppermute | solution.py:280
Sparse Core Ops, SparseCore 0:
  57.0 56.2 all-gather.2

commit v4 on v3

v4 whole, which is shorter than its diff:
```python
import jax
import jax.numpy as jnp
from jax import lax
from jax.experimental import pallas as pl
from jax.experimental.pallas import tpu as pltpu
from jax.sharding import Mesh, PartitionSpec as P

TILE = 128
FEAT = ("zq", "zr", "y")
DP = ("x", "core")
BF = jnp.bfloat16
F32 = jnp.float32
NT = (((1,), (1,)), ((), ()))
VMEM = pl.BlockSpec(memory_space=pltpu.VMEM)
SMEM = pl.BlockSpec(memory_space=pltpu.SMEM)
HBM = pl.BlockSpec(memory_space=pl.ANY)
LIMIT = pltpu.CompilerParams(vmem_limit_bytes=56 * 2**20)


def aligned(index, size):
    return pl.ds(pl.multiple_of(index * size, size), size)


def split_bias(bias):
    row = lax.broadcasted_iota(jnp.int32, (8, bias.shape[1]), 0)
    left = jnp.broadcast_to(bias, row.shape)
    high = left.astype(BF).astype(F32)
    left = left - high
    middle = left.astype(BF).astype(F32)
    low = left - middle
    return jnp.where(row == 0, high, jnp.where(row == 1, middle, jnp.where(row == 2, low, 0.0)))


def hop_kernel(place, ids, cols, table, bias, tiles_hbm, _, out, feats, rows, picked, tiles, sem):
    width = table.shape[0]
    blocks = tiles.shape[0]
    group = blocks // 8
    copies = [
        pltpu.make_async_copy(
            tiles_hbm.at[pl.ds(j * group, group)], tiles.at[pl.ds(j * group, group)], sem.at[j]
        )
        for j in range(8)
    ]
    for copy in copies:
        copy.start()

    def turn(b, carry):
        rows[aligned(b, TILE), 0:width] = table[:, aligned(b, TILE)].astype(F32).T
        return carry

    lax.fori_loop(0, table.shape[1] // TILE, turn, 0, unroll=8)
    step = 64

    def pick(g, carry):
        base = pl.multiple_of(g * step, step)
        for u in range(step):
            picked[pl.ds(base + u, 1), :] = rows[pl.ds(ids[base + u], 1), :]
        return carry

    lax.fori_loop(0, ids.shape[0] // step, pick, 0)
    lane = lax.broadcasted_iota(jnp.int32, (8, TILE), 1)
    term = split_bias(jnp.concatenate([bias[...]] * 4, axis=1))
    term = jnp.where(lane // 32 == place[4], term, 0.0)
    for copy in copies:
        copy.wait()

    def merge(r, carry):
        own = picked[aligned(r, TILE), :].T[0:width]
        left = jnp.concatenate([tiles[r, k] for k in range(8)], axis=1)
        right = jnp.concatenate(
            [picked[aligned(cols[r, k], TILE), :].astype(BF) for k in range(8)], axis=0
        )
        total = jnp.dot(left, right, preferred_element_type=F32)
        both = jnp.concatenate([own, total.T[0:width]], axis=0)
        feats[r] = both.astype(BF)
        out[r] = jnp.concatenate([both, term], axis=0).astype(BF)
        return carry

    lax.fori_loop(0, blocks, merge, 0, unroll=2)


def hop(place, table, ids, cols, bias, tiles, after):
    blocks, deep = tiles.shape[0], 2 * table.shape[0]
    return pl.pallas_call(
        hop_kernel,
        in_specs=[SMEM, SMEM, SMEM, VMEM, VMEM, HBM, HBM],
        out_specs=[VMEM, VMEM],
        scratch_shapes=[
            pltpu.VMEM((table.shape[1], TILE), F32),
            pltpu.VMEM((ids.shape[0], TILE), F32),
            pltpu.VMEM(tiles.shape, BF),
            pltpu.SemaphoreType.DMA((8,)),
        ],
        out_shape=[
            jax.ShapeDtypeStruct((blocks, deep + 8, TILE), BF),
            jax.ShapeDtypeStruct((blocks, deep, TILE), BF),
        ],
        compiler_params=LIMIT,
        cost_estimate=pl.CostEstimate(flops=10**9, bytes_accessed=60 * 10**6, transcendentals=0),
    )(place, ids, cols, table, bias.reshape(1, -1), tiles, after)


def pack_kernel(place, own, neigh, head_self, head_neigh, weights, heads):
    core, x = place[0], place[1]
    cols = aligned(lax.rem(x, 2), 512)
    block = jnp.where(core == 0, own[:, cols].astype(F32), neigh[:, cols].astype(F32)).astype(BF)
    for d in range(weights.shape[0]):
        weights[d] = block
    classes = head_self.shape[1]
    heads[...] = jnp.zeros_like(heads)
    heads[0:32, 0:classes] = head_self[...]
    heads[32:64, 0:classes] = head_neigh[...]


def pack(place, own, neigh, head_self, head_neigh):
    return pl.pallas_call(
        pack_kernel,
        in_specs=[SMEM] + [VMEM] * 4,
        out_specs=[VMEM, VMEM],
        out_shape=[
            jax.ShapeDtypeStruct((32, own.shape[0], 512), BF),
            jax.ShapeDtypeStruct((64, 256), BF),
        ],
        compiler_params=LIMIT,
    )(place, own, neigh, head_self, head_neigh)


def spread_kernel(
    place, cols, live, logit_cot, p0, p1, p2, p3, tiles, out, cot, self_t, neigh_t, own, neigh
):
    classes, slots = logit_cot.shape
    lane = lax.broadcasted_iota(jnp.int32, (classes, slots), 1)
    kept = jnp.where(lane < live[0], logit_cot[...].astype(F32), 0.0)
    cot[...] = jnp.concatenate([kept, jnp.zeros((256 - classes, slots), F32)], axis=0).astype(BF)
    out[...] = jnp.zeros_like(out)
    for s, part in enumerate((p0, p1, p2, p3)):
        at = aligned(lax.rem(place[2] + 4 - s, 4), 32)
        own[at, :] = part[0:32]
        neigh[at, :] = part[32:64]
    self_t[...] = own[...].astype(F32).T.astype(BF)
    neigh_t[...] = neigh[...].astype(F32).T.astype(BF)
    for r in range(tiles.shape[0]):
        part = cot[:, r * TILE : (r + 1) * TILE]
        out[r] = jnp.dot(own[...], part, preferred_element_type=F32)
    for r in range(tiles.shape[0]):
        part = cot[:, r * TILE : (r + 1) * TILE]
        back = jnp.dot(neigh[...], part, preferred_element_type=F32).astype(BF)
        for k in range(8):
            out[cols[r, k]] += jnp.dot(back, tiles[r, k], preferred_element_type=F32)


def spread(place, cols, live, logit_cot, pairs, tiles, blocks):
    return pl.pallas_call(
        spread_kernel,
        in_specs=[SMEM, SMEM, SMEM] + [VMEM] * 6,
        out_specs=[VMEM] * 4,
        scratch_shapes=[pltpu.VMEM((TILE, 256), BF)] * 2,
        out_shape=[
            jax.ShapeDtypeStruct((blocks, TILE, TILE), F32),
            jax.ShapeDtypeStruct((256, logit_cot.shape[1]), BF),
            jax.ShapeDtypeStruct((256, TILE), BF),
            jax.ShapeDtypeStruct((256, TILE), BF),
        ],
        compiler_params=LIMIT,
        cost_estimate=pl.CostEstimate(flops=10**9, bytes_accessed=8 * 10**6, transcendentals=0),
    )(place, cols, live.reshape(1), logit_cot, *pairs, tiles)


def layer_kernel(place, got, w0, w1, w2, o0, o1, o2, out, mine, other):
    core, x = place[0], place[1]
    deep = w0.shape[0] // 32
    for j in range(8):
        pieces = [got[4 * j + i].astype(F32) for i in range(4)]
        own = jnp.concatenate([piece[0:deep] for piece in pieces], axis=0).T.astype(BF)
        agg = jnp.concatenate([piece[deep : 2 * deep] for piece in pieces], axis=0).T.astype(BF)
        at = slice(j * 4 * deep, (j + 1) * 4 * deep)
        mine[:, at] = jnp.where(core == 0, own, agg)
        other[:, at] = jnp.where(core == 0, agg, own)

    def emit(chunk, w, o):
        preact = jnp.dot(mine[...], w, preferred_element_type=F32)
        preact = preact + jnp.dot(other[...], o, preferred_element_type=F32)
        rows = aligned(chunk, 32)
        for half in range(2):
            z = 2 * chunk + half
            terms = sum(got[4 * z + i].astype(F32)[2 * deep :] for i in range(4))
            bias = jnp.sum(terms, axis=0, keepdims=True)
            hidden = jnp.maximum(preact[:, half * TILE : (half + 1) * TILE] + bias, 0.0)
            hidden = hidden.T.astype(BF)
            for y in range(4):
                for zq in range(4):
                    out[8 * zq + 4 * half + y, rows, :] = hidden[32 * y : 32 * y + 32]

    near = 2 * lax.rem(x, 2)
    far = 2 - near
    emit(near, w0[:, 0:256], o0[:, 0:256])
    emit(near + 1, w0[:, 256:512], o0[:, 256:512])
    emit(far, w1[...], o1[...])
    emit(far + 1, w2[...], o2[...])


def layer(place, got, mine, other):
    return pl.pallas_call(
        layer_kernel,
        in_specs=[SMEM] + [VMEM] * 7,
        out_specs=VMEM,
        scratch_shapes=[pltpu.VMEM((TILE, mine[0].shape[0]), BF)] * 2,
        out_shape=jax.ShapeDtypeStruct((32, TILE, TILE), BF),
        compiler_params=LIMIT,
    )(place, got, *mine, *other)


def score_kernel(
    place, cols, hidden, dhidden, tiles, cot, self_t, neigh_t, out, keep, send, second
):
    core, zq = place[0], place[2]
    own = aligned(zq, 32)
    for r in range(tiles.shape[0]):
        left = jnp.concatenate([hidden[cols[r, k]] for k in range(8)], axis=1)
        right = jnp.concatenate([tiles[r, k] for k in range(8)], axis=1)
        second[r] = lax.dot_general(left, right, NT, preferred_element_type=F32).astype(BF)
    halves = []
    for half in range(2):
        at = 2 * zq + half
        scores = jnp.dot(self_t[...], hidden[at], preferred_element_type=F32)
        halves.append(scores + jnp.dot(neigh_t[...], second[at], preferred_element_type=F32))
    for z in range(out.shape[0]):
        both = [scores[24 * z : 24 * (z + 1)] for scores in halves]
        out[z] = jnp.concatenate(both, axis=0).astype(BF)
    total = jnp.zeros((32, TILE), F32)
    for b in range(hidden.shape[0]):
        total = total + jnp.where(hidden[b, own, :].astype(F32) > 0.0, dhidden[b, own, :], 0.0)
    mine = jnp.sum(total, axis=1, keepdims=True)
    targets = jnp.concatenate([hidden[r, own, :] for r in range(tiles.shape[0])], axis=1)
    merged = jnp.concatenate([second[r, own, :] for r in range(tiles.shape[0])], axis=1)
    lane = lax.broadcasted_iota(jnp.int32, (32, 256), 1)
    first = lax.dot_general(targets, cot[...], NT, preferred_element_type=F32)
    first = jnp.where(lane == 255, mine, first)
    later = lax.dot_general(merged, cot[...], NT, preferred_element_type=F32)
    kept = jnp.where(core == 0, first, later)
    sent = jnp.where(core == 0, later, first)
    for half in range(2):
        keep[32 * half : 32 * half + 32, :] = kept[:, half * TILE : (half + 1) * TILE]
        send[32 * half : 32 * half + 32, :] = sent[:, half * TILE : (half + 1) * TILE]


def score(place, cols, hidden, dhidden, tiles, cot, self_t, neigh_t):
    shape = jax.ShapeDtypeStruct((64, TILE), F32)
    return pl.pallas_call(
        score_kernel,
        in_specs=[SMEM, SMEM] + [VMEM] * 6,
        out_specs=[VMEM] * 3,
        scratch_shapes=[pltpu.VMEM((tiles.shape[0], TILE, TILE), BF)],
        out_shape=[jax.ShapeDtypeStruct((8, 48, TILE), BF), shape, shape],
        compiler_params=LIMIT,
    )(place, cols, hidden, dhidden, tiles, cot, self_t, neigh_t)


def fan_kernel(parts, out):
    total = parts[0].astype(F32)
    for j in range(1, parts.shape[0]):
        total = total + parts[j].astype(F32)
    for d in range(out.shape[0]):
        out[d] = total.astype(BF)


def fan(parts):
    return pl.pallas_call(
        fan_kernel,
        in_specs=[VMEM],
        out_specs=VMEM,
        out_shape=jax.ShapeDtypeStruct((32,) + parts.shape[1:], BF),
        compiler_params=LIMIT,
    )(parts)


def logit_kernel(parts, out):
    classes = out.shape[0]
    for j in range(8):
        rows = min(24, classes - 24 * j)
        if rows <= 0:
            continue
        for zq in range(4):
            block = parts[8 * zq + j].astype(F32)
            for half in range(2):
                at = (2 * zq + half) * TILE
                out[24 * j : 24 * j + rows, at : at + TILE] = block[24 * half : 24 * half + rows]


def join(parts, classes, slots):
    return pl.pallas_call(
        logit_kernel,
        in_specs=[VMEM],
        out_specs=VMEM,
        out_shape=jax.ShapeDtypeStruct((classes, slots), F32),
        compiler_params=LIMIT,
    )(parts)


def grad_kernel(place, hidden, dhidden, f0, f1, f2, f3, g0, g1, g2, g3, keep, send, total):
    core, zr, y = place[0], place[3], place[4]
    blocks, deep, _ = f0.shape
    half = deep // 2
    parts = (f0, f1, f2, f3, g0, g1, g2, g3)
    total[...] = jnp.zeros_like(total)

    def grow(b, carry):
        low = jnp.where(hidden[b].astype(F32) > 0.0, dhidden[b], 0.0).astype(BF)
        stack = jnp.concatenate([part[b] for part in parts], axis=0)
        total[...] += lax.dot_general(stack, low, NT, preferred_element_type=F32)
        return carry

    lax.fori_loop(0, blocks, grow, 0, unroll=4)
    for j in range(len(parts)):
        owner = 4 * (zr if j < 4 else 1 - zr) + lax.rem(y + 8 - j, 4)
        keep[owner] = total[pl.ds(pl.multiple_of(j * deep + core * half, 8), half), :]
        send[owner] = total[pl.ds(pl.multiple_of(j * deep + (1 - core) * half, 8), half), :]


def grad(place, hidden, dhidden, feats):
    _, deep, _ = feats[0].shape
    shape = jax.ShapeDtypeStruct((8, deep // 2, TILE), F32)
    return pl.pallas_call(
        grad_kernel,
        in_specs=[SMEM] + [VMEM] * 10,
        out_specs=[VMEM, VMEM],
        scratch_shapes=[pltpu.VMEM((8 * deep, TILE), F32)],
        out_shape=[shape, shape],
        compiler_params=LIMIT,
        cost_estimate=pl.CostEstimate(flops=10**9, bytes_accessed=7 * 10**6, transcendentals=0),
    )(place, hidden, dhidden, *feats)


def finish_kernel(place, keep, rest, grad_self, grad_neigh, head_self, head_neigh, bias):
    core = place[0]
    deep = grad_self.shape[0]
    classes = head_self.shape[1]
    first = jnp.where(core == 0, keep[...], rest[...])
    later = jnp.where(core == 0, rest[...], keep[...])
    for value, weight, head in ((first, grad_self, head_self), (later, grad_neigh, head_neigh)):
        for zq in range(4):
            for zr in range(2):
                pieces = [
                    value[(4 * zr + y) * deep : (4 * zr + y + 1) * deep, 32 * zq : 32 * zq + 32]
                    for y in range(4)
                ]
                at = (2 * zq + zr) * TILE
                weight[:, at : at + TILE] = jnp.concatenate(pieces, axis=1)
        base = 8 * deep
        head[:, 0:TILE] = value[base : base + 32]
        head[:, TILE:classes] = value[base + 32 : base + 64, 0 : classes - TILE]
    bias[...] = first[8 * deep + 32 : 8 * deep + 64, TILE - 1 : TILE]


def finish(place, keep, rest, deep, classes):
    weight = jax.ShapeDtypeStruct((deep, 1024), F32)
    head = jax.ShapeDtypeStruct((32, classes), F32)
    return pl.pallas_call(
        finish_kernel,
        in_specs=[SMEM, VMEM, VMEM],
        out_specs=[VMEM] * 5,
        out_shape=[weight, weight, head, head, jax.ShapeDtypeStruct((32, 1), F32)],
        compiler_params=LIMIT,
    )(place, keep, rest)


def shift(value, axis, by):
    return lax.ppermute(value, axis, [(i, (i + by) % 4) for i in range(4)])


def swap(value, axis):
    return lax.ppermute(value, axis, [(0, 1), (1, 0)])


def sum_x(value):
    value = value + lax.ppermute(value, "x", [(0, 1), (1, 0), (2, 3), (3, 2)])
    return value + lax.ppermute(value, "x", [(0, 3), (3, 0), (1, 2), (2, 1)])


def shards(
    feature_table,
    node_ids,
    hop_cols,
    hop_tiles,
    target_cols,
    target_tiles,
    self_weight,
    neigh_weight,
    hidden_bias,
    head_self,
    head_neigh,
    batch_sizes,
    logit_cotangent,
):
    blocks = hop_cols.shape[0]
    deep = feature_table.shape[0]
    classes, target_rows = logit_cotangent.shape
    place = jnp.stack([lax.axis_index(axis) for axis in ("core", "x") + FEAT])

    packed, pair = pack(place, self_weight, neigh_weight, head_self, head_neigh)
    weights = lax.all_to_all(packed, FEAT, 0, 0, tiled=True)
    send, feats = hop(
        place, feature_table, node_ids, hop_cols, hidden_bias, hop_tiles, packed
    )
    weights, pair, send, feats = lax.optimization_barrier((weights, pair, send, feats))
    got = lax.all_to_all(send, FEAT, 0, 0, tiled=True)
    weights = weights.reshape(-1, 512)
    mine = [weights, shift(weights[:, :256], "x", 1), shift(weights[:, 256:], "x", 3)]
    other = [swap(w, "core") for w in mine]

    twin = swap(feats, "zr")
    feats = [feats] + [shift(feats, "y", s) for s in (1, 2, 3)]

    hidden = layer(place, got, mine, other)
    hidden, pair, twin, feats = lax.optimization_barrier((hidden, pair, twin, feats))
    hidden = lax.all_to_all(hidden, FEAT, 0, 0, tiled=True)
    pairs = [pair] + [shift(pair, "zq", s) for s in (1, 2, 3)]
    feats = feats + [twin] + [shift(twin, "y", s) for s in (1, 2, 3)]
    live = batch_sizes[lax.axis_index("x") * 2 + lax.axis_index("core")]
    dhidden, cot, self_t, neigh_t = spread(
        place, target_cols, live, logit_cotangent, pairs, target_tiles, blocks
    )

    scores, keep_head, send_head = score(
        place, target_cols, hidden, dhidden, target_tiles, cot, self_t, neigh_t
    )
    scores = lax.all_to_all(scores, ("zr", "y"), 0, 0, tiled=True)
    keep_head = keep_head + swap(send_head, "core")
    keep, send = grad(place, hidden, dhidden, feats)
    keep = keep + swap(send, "core")
    keep = lax.all_to_all(keep, ("zr", "y"), 0, 0, tiled=True)
    scores = lax.all_to_all(fan(scores), FEAT, 0, 0, tiled=True)
    keep = sum_x(jnp.concatenate([keep.reshape(-1, TILE), keep_head], axis=0))
    results = finish(place, keep, swap(keep, "core"), deep, classes)
    return (join(scores, classes, target_rows), *results[:4], results[4].reshape(-1))


def solution(mesh):
    split = Mesh(mesh.devices.reshape(4, 2, 4, 2, 4), DP + FEAT)
    return jax.shard_map(
        shards,
        mesh=split,
        in_specs=(
            P(FEAT, None),
            P(DP),
            P(DP, None),
            P(DP, None, None, None),
            P(DP, None),
            P(DP, None, None, None),
            P(FEAT, None),
            P(FEAT, None),
            P(FEAT),
            P(FEAT, None),
            P(FEAT, None),
            P(),
            P(None, DP),
        ),
        out_specs=(
            P(None, DP),
            P(FEAT, None),
            P(FEAT, None),
            P(FEAT, None),
            P(FEAT, None),
            P(FEAT),
        ),
        check_vma=False,
    )
```

time: 208 us -> 190 us (0.913)
  blocking collectives: 30.9 us -> 0 us
  starting transfers between devices: 64.8 us -> 80.3 us
  between operations: 14.3 us -> 0.91 us
  Pallas kernels: 48.2 us -> 54.4 us
  waiting for transfers between devices: 38.1 us -> 42.6 us
    all_to_all x2 -> x0, blocking collectives: 30.9 us -> none  [the longest x1 21 us: shards(): hidden = lax.all_to_all(hidden, 'z', 0, 0, tiled=True)]
    all_to_all x3 -> x4, waiting for transfers between devices: 19.2 us -> 2.93 us  [the longest x1 2.92 us: shards(): keep = lax.all_to_all(keep, ('zr', 'y'), 0, 0, tiled=True)]
    ppermute x6 -> x11, waiting for transfers between devices: 11.8 us -> 24.9 us  [shift(): return lax.ppermute(value, axis, [(i, (i + by) % 4) for i in range(4)])]
    ppermute x6 -> x11, starting transfers between devices: 7.04 us -> 19.3 us  [shift(): return lax.ppermute(value, axis, [(i, (i + by) % 4) for i in range(4)])]
    ppermute x7, starting transfers between devices: 23.9 us -> 13 us  [swap(): return lax.ppermute(value, axis, [(0, 1), (1, 0)])]
    all_to_all x3 -> x4, starting transfers between devices: 14.1 us -> 24.2 us  [the longest x1 6.8 us: shards(): scores = lax.all_to_all(scores, ('zr', 'y'), 0, 0, tiled=True)]
    all_to_all x1, waiting for transfers between devices: 0.01 us -> 5.87 us  [shards(): got = lax.all_to_all(send, FEAT, 0, 0, tiled=True)]
    pallas_call x4 -> x7, Pallas kernels: 19.8 us -> 25.5 us  [the longest x1 5.94 us: spread(): pl.pallas_call(spread_kernel, in_specs=[SMEM, SMEM, SMEM] + [VMEM] * 6, o...]
  transfers between devices with their start and end apart: 21 -> 26, of which waited for: 11 -> 11; matrix products, arithmetic and copies ran while one was open for 3% -> 3% of each run, Pallas kernels for 22% -> 27%
where the time goes in v4:
time: 190 us; the launch traced here: 189 us
  starting transfers between devices  80.3 us (42%)
  Pallas kernels  54.4 us (29%)
  waiting for transfers between devices  42.6 us (22%)
  local copies, waits for them, and re-layouts  8.15 us (4%)
  other arithmetic  2.94 us (2%)
    pallas_call x1, Pallas kernels, hop(): pl.pallas_call(hop_kernel, in_specs=[SMEM, SMEM, SMEM, VMEM, VMEM, HBM, H...  27.1 us
    ppermute x11, waiting for transfers between devices, shift(): return lax.ppermute(value, axis, [(i, (i + by) % 4) for i in range(4)])  24.9 us
    ppermute x11, starting transfers between devices, shift(): return lax.ppermute(value, axis, [(i, (i + by) % 4) for i in range(4)])  19.3 us
    ppermute x7, starting transfers between devices, swap(): return lax.ppermute(value, axis, [(0, 1), (1, 0)])  13 us
    all_to_all x1, starting transfers between devices, shards(): weights = lax.all_to_all(packed, FEAT, 0, 0, tiled=True)  12 us
    all_to_all x1, starting transfers between devices, shards(): got = lax.all_to_all(send, FEAT, 0, 0, tiled=True)  9.22 us
    unnamed x47, local copies, waits for them, and re-layouts  6.89 us
    all_to_all x1, starting transfers between devices, shards(): scores = lax.all_to_all(scores, ('zr', 'y'), 0, 0, tiled=True)  6.8 us
  transfers between devices with their start and end apart: 26, of which 11 were waited for; matrix products, arithmetic and copies ran while one was open for 3% of the time, Pallas kernels for 27%

profile of v4, /device:TPU:1, one launch (start us, length us, event | category | flops | bytes accessed | tf_op | source)
XLA Modules:
  0.0 189.3 jit_solution(13078594879219392605)
XLA Ops:
  0.6 0.6 stack.23.place
  1.3 1.8 shard_map.172
  3.1 12.0 %all-to-all-start = ((bf16[32,24,512]{2,1,0:T(8,128)(2,1)}), bf16[32,24,512]{2,1,0:T(8,128)(2,1)S(1)}, u32[]{:S(2)}, u32[]{:S(2)}) async-start(bf16[32,24,512]{2,1,0:T(8,128)(2,1)} %get-tuple-element.35._), calls=%async_computation | async-start | bytes 1572864 | tf_op jit(solution)/shard_map/all_to_all | solution.py:401
  15.1 1.4 copy.20.cols
  16.5 27.1 %shard_map.173 = (bf16[32,56,128]{2,1,0:T(8,128)(2,1)}, bf16[32,48,128]{2,1,0:T(8,128)(2,1)}) custom-call(s32[5]{0:T(128)} %stack.23.place, s32[16384]{0:T(1024)} %ids.1, s32[32,8]{1,0:T(8,128)} %copy.20.cols, bf16[24,32768]{1,0:T(8,128)(2,1)} %table.1, f32[1,32]{1,0:T(1,128)} %bitcast.13, bf16[32,8,128,128]{3,2,1,0:T(8,128)(2,1)} %tiles_hbm.1, ...), custom_call_target="tpu_custom_call" | custom-call | flops 1000000000 | bytes 60000000 | tf_op jit(solution)/shard_map/pallas_call | solution.py:84
  43.7 2.6 %collective-permute-start.1 = (bf16[768,256]{1,0:T(8,128)(2,1)S(1)}, bf16[768,256]{1,0:T(8,128)(2,1)}, u32[]{:S(2)}, u32[]{:S(2)}) collective-permute-start(bf16[768,256]{1,0:T(8,128)(2,1)S(1)} %get-tuple-element.64), channel_id=1, source_target_pairs={{0,192},{64,0},{128,64},{192,128},{1,193},{65,1},{129,65},{193,129... | collective-permute-start | bytes 1179656 | tf_op jit(solution)/shard_map/ppermute | solution.py:368
  46.3 9.2 %all-to-all-start.1 = ((bf16[32,56,128]{2,1,0:T(8,128)(2,1)}), bf16[32,56,128]{2,1,0:T(8,128)(2,1)S(1)}, u32[]{:S(2)}, u32[]{:S(2)}) async-start(bf16[32,56,128]{2,1,0:T(8,128)(2,1)} %get-tuple-element.39), calls=%async_computation.1 | async-start | bytes 917504 | tf_op jit(solution)/shard_map/all_to_all | solution.py:406
  55.5 1.9 collective-permute-start.2
  57.5 1.6 collective-permute-start.3
  59.1 2.4 %collective-permute-start.8 = (bf16[32,48,128]{2,1,0:T(8,128)(2,1)S(1)}, bf16[32,48,128]{2,1,0:T(8,128)(2,1)S(1)}, u32[]{:S(2)}, u32[]{:S(2)}) collective-permute-start(bf16[32,48,128]{2,1,0:T(8,128)(2,1)S(1)} %copy-done.6), channel_id=1, source_target_pairs={{0,3},{1,0},{2,1},{3,2},{4,7},{5,4},{6,5},{7,6},{8,11},{9,8},{10,9... | collective-permute-start | bytes 1179656 | tf_op jit(solution)/shard_map/ppermute | solution.py:368
  62.7 1.2 collective-permute-start.5
  63.9 5.9 %all-to-all-done.1.got = bf16[32,56,128]{2,1,0:T(8,128)(2,1)S(1)} async-done(((bf16[32,56,128]{2,1,0:T(8,128)(2,1)}), bf16[32,56,128]{2,1,0:T(8,128)(2,1)S(1)}, u32[]{:S(2)}, u32[]{:S(2)}) %all-to-all-start.1) | async-done | bytes 458784 | tf_op jit(solution)/shard_map/all_to_all | solution.py:406
  69.8 0.8 copy-done.2
  70.6 3.9 %shard_map.174 = bf16[32,128,128]{2,1,0:T(8,128)(2,1)} custom-call(s32[5]{0:T(128)} %stack.23.place, bf16[32,56,128]{2,1,0:T(8,128)(2,1)} %copy-done.2, bf16[768,512]{1,0:T(8,128)(2,1)} %bitcast.10, bf16[768,256]{1,0:T(8,128)(2,1)} %collective-permute-done.w1, bf16[768,256]{1,0:T(8,128)(2,1)} %collective-permute-done.1.w2, bf16[768,512]{1,0:T(8,128)(2,1)} %copy-done.4, ...), custom_call_target="tpu_custom_call" | custom-call | tf_op jit(solution)/shard_map/pallas_call | solution.py:203
  74.5 1.9 %collective-permute-done.7.f2 = bf16[32,48,128]{2,1,0:T(8,128)(2,1)S(1)} collective-permute-done((bf16[32,48,128]{2,1,0:T(8,128)(2,1)S(1)}, bf16[32,48,128]{2,1,0:T(8,128)(2,1)S(1)}, u32[]{:S(2)}, u32[]{:S(2)}) %collective-permute-start.7) | collective-permute-done | bytes 393248 | tf_op jit(solution)/shard_map/ppermute | solution.py:368
  76.4 8.8 %collective-permute-done.6.f1 = bf16[32,48,128]{2,1,0:T(8,128)(2,1)} collective-permute-done((bf16[32,48,128]{2,1,0:T(8,128)(2,1)S(1)}, bf16[32,48,128]{2,1,0:T(8,128)(2,1)}, u32[]{:S(2)}, u32[]{:S(2)}) %collective-permute-start.6) | collective-permute-done | bytes 393248 | tf_op jit(solution)/shard_map/ppermute | solution.py:368
  85.2 5.9 %all-to-all-start.2 = ((bf16[32,128,128]{2,1,0:T(8,128)(2,1)}), bf16[32,128,128]{2,1,0:T(8,128)(2,1)S(1)}, u32[]{:S(2)}, u32[]{:S(2)}) async-start(bf16[32,128,128]{2,1,0:T(8,128)(2,1)} %shard_map.174), calls=%async_computation.2 | async-start | bytes 2097152 | tf_op jit(solution)/shard_map/all_to_all | solution.py:416
  91.1 2.5 %collective-permute-start.14 = (bf16[32,48,128]{2,1,0:T(8,128)(2,1)}, bf16[32,48,128]{2,1,0:T(8,128)(2,1)S(1)}, u32[]{:S(2)}, u32[]{:S(2)}) collective-permute-start(bf16[32,48,128]{2,1,0:T(8,128)(2,1)} %collective-permute-done.5.g0), channel_id=1, source_target_pairs={{0,3},{1,0},{2,1},{3,2},{4,7},{5,4},{6,5},{7,6},{8,11},{9,8},{10,9... | collective-permute-start | bytes 1179656 | tf_op jit(solution)/shard_map/ppermute | solution.py:368
  94.8 3.4 %collective-permute-start.11 = (bf16[64,256]{1,0:T(8,128)(2,1)S(1)}, bf16[64,256]{1,0:T(8,128)(2,1)S(1)}, u32[]{:S(2)}, u32[]{:S(2)}) collective-permute-start(bf16[64,256]{1,0:T(8,128)(2,1)S(1)} %copy-done.17), channel_id=1, source_target_pairs={{0,24},{8,0},{16,8},{24,16},{1,25},{9,1},{17,9},{25,17},{2,26},{10... | collective-permute-start | bytes 98312 | tf_op jit(solution)/shard_map/ppermute | solution.py:368
  98.2 2.0 %collective-permute-start.10 = (bf16[64,256]{1,0:T(8,128)(2,1)S(1)}, bf16[64,256]{1,0:T(8,128)(2,1)S(1)}, u32[]{:S(2)}, u32[]{:S(2)}) collective-permute-start(bf16[64,256]{1,0:T(8,128)(2,1)S(1)} %copy-done.17), channel_id=1, source_target_pairs={{0,16},{8,24},{16,0},{24,8},{1,17},{9,25},{17,1},{25,9},{2,18},{10... | collective-permute-start | bytes 98312 | tf_op jit(solution)/shard_map/ppermute | solution.py:368
  100.2 13.1 %collective-permute-done.11.p3 = bf16[64,256]{1,0:T(8,128)(2,1)S(1)} collective-permute-done((bf16[64,256]{1,0:T(8,128)(2,1)S(1)}, bf16[64,256]{1,0:T(8,128)(2,1)S(1)}, u32[]{:S(2)}, u32[]{:S(2)}) %collective-permute-start.11) | collective-permute-done | bytes 32800 | tf_op jit(solution)/shard_map/ppermute | solution.py:368
  113.3 4.1 %collective-permute-start.9 = (bf16[64,256]{1,0:T(8,128)(2,1)S(1)}, bf16[64,256]{1,0:T(8,128)(2,1)S(1)}, u32[]{:S(2)}, u32[]{:S(2)}) collective-permute-start(bf16[64,256]{1,0:T(8,128)(2,1)S(1)} %copy-done.17), channel_id=1, source_target_pairs={{0,8},{8,16},{16,24},{24,0},{1,9},{9,17},{17,25},{25,1},{2,10},{10... | collective-permute-start | bytes 98312 | tf_op jit(solution)/shard_map/ppermute | solution.py:368
  119.2 0.6 copy-done.21
  119.8 5.9 %shard_map.175 = (f32[32,128,128]{2,1,0:T(8,128)}, bf16[256,1024]{1,0:T(8,128)(2,1)}, bf16[256,128]{1,0:T(8,128)(2,1)}, bf16[256,128]{1,0:T(8,128)(2,1)}) custom-call(s32[5]{0:T(128)} %stack.23.place, s32[8,8]{1,0:T(8,128)} %cols.4, s32[1]{0:T(128)} %dynamic_slice.3.live, bf16[153,1024]{1,0:T(8,128)(2,1)} %logit_cot.1, ...), custom_call_target="tpu_custom_call" | custom-call | flops 1000000000 | bytes 8000000 | tf_op jit(solution)/shard_map/pallas_call | solution.py:153
  125.8 1.0 copy-done
  126.7 4.5 %shard_map.176 = (bf16[8,48,128]{2,1,0:T(8,128)(2,1)}, f32[64,128]{1,0:T(8,128)}, f32[64,128]{1,0:T(8,128)}) custom-call(s32[5]{0:T(128)} %stack.23.place, s32[8,8]{1,0:T(8,128)} %cols.4, bf16[32,128,128]{2,1,0:T(8,128)(2,1)} %copy-done, f32[32,128,128]{2,1,0:T(8,128)} %get-tuple-element.45.dhidden, bf16[8,8,128,128]{3,2,1,0:T(8,128)(2,1)} %tiles.3, ...), custom_call_target="tpu_custom_call" | custom-call | tf_op jit(solution)/shard_map/pallas_call | solution.py:249
  131.3 6.8 %all-to-all-start.3 = ((bf16[8,48,128]{2,1,0:T(8,128)(2,1)}), bf16[8,48,128]{2,1,0:T(8,128)(2,1)S(1)}, u32[]{:S(2)}, u32[]{:S(2)}) async-start(bf16[8,48,128]{2,1,0:T(8,128)(2,1)} %get-tuple-element.49), calls=%async_computation.3 | async-start | bytes 196608 | tf_op jit(solution)/shard_map/all_to_all | solution.py:427
  138.1 0.7 copy-done.9
  139.0 0.7 copy-done.11
  139.7 5.6 %shard_map.179 = (f32[8,24,128]{2,1,0:T(8,128)}, f32[8,24,128]{2,1,0:T(8,128)}) custom-call(s32[5]{0:T(128)} %stack.23.place, bf16[32,128,128]{2,1,0:T(8,128)(2,1)} %copy-done, f32[32,128,128]{2,1,0:T(8,128)} %get-tuple-element.45.dhidden, bf16[32,48,128]{2,1,0:T(8,128)(2,1)} %get-tuple-element.50.f0, bf16[32,48,128]{2,1,0:T(8,128)(2,1)} %collective-permute-done.6.f1, ...), custom_call_target="tpu_custom_call" | custom-call | flops 1000000000 | bytes 7000000 | tf_op jit(solution)/shard_map/pallas_call | solution.py:323
  145.4 3.4 %collective-permute-start.15 = (f32[8,24,128]{2,1,0:T(8,128)}, f32[8,24,128]{2,1,0:T(8,128)S(1)}, u32[]{:S(2)}, u32[]{:S(2)}) collective-permute-start(f32[8,24,128]{2,1,0:T(8,128)} %get-tuple-element.56), channel_id=1, source_target_pairs={{0,32},{32,0},{1,33},{33,1},{2,34},{34,2},{3,35},{35,3},{4,36},{36... | collective-permute-start | bytes 294920 | tf_op jit(solution)/shard_map/ppermute | solution.py:372
  148.8 1.2 collective-permute-done.15
  149.9 1.5 add.20
  151.5 5.4 %all-to-all-start.5 = ((f32[8,24,128]{2,1,0:T(8,128)}), f32[8,24,128]{2,1,0:T(8,128)S(1)}, u32[]{:S(2)}, u32[]{:S(2)}) async-start(f32[8,24,128]{2,1,0:T(8,128)} %add.20), calls=%async_computation.5 | async-start | bytes 196608 | tf_op jit(solution)/shard_map/all_to_all | solution.py:431
  156.9 0.7 collective-permute-start.16
  157.6 1.7 shard_map.177
  159.3 2.9 %all-to-all-done.5 = f32[8,24,128]{2,1,0:T(8,128)S(1)} async-done(((f32[8,24,128]{2,1,0:T(8,128)}), f32[8,24,128]{2,1,0:T(8,128)S(1)}, u32[]{:S(2)}, u32[]{:S(2)}) %all-to-all-start.5) | async-done | bytes 98336 | tf_op jit(solution)/shard_map/all_to_all | solution.py:431
  162.2 6.1 %all-to-all-start.4 = ((bf16[32,48,128]{2,1,0:T(8,128)(2,1)}), bf16[32,48,128]{2,1,0:T(8,128)(2,1)S(1)}, u32[]{:S(2)}, u32[]{:S(2)}) async-start(bf16[32,48,128]{2,1,0:T(8,128)(2,1)} %shard_map.177), calls=%async_computation.4 | async-start | bytes 786432 | tf_op jit(solution)/shard_map/all_to_all | solution.py:432
  168.5 3.8 %collective-permute-done.17 = f32[256,128]{1,0:T(8,128)S(1)} collective-permute-done((f32[256,128]{1,0:T(8,128)S(1)}, f32[256,128]{1,0:T(8,128)S(1)}, u32[]{:S(2)}, u32[]{:S(2)}) %collective-permute-start.17) | collective-permute-done | bytes 131104 | tf_op jit(solution)/shard_map/ppermute | solution.py:376
  172.3 2.4 %collective-permute-start.18 = (f32[256,128]{1,0:T(8,128)S(1)}, f32[256,128]{1,0:T(8,128)S(1)}, u32[]{:S(2)}, u32[]{:S(2)}) collective-permute-start(f32[256,128]{1,0:T(8,128)S(1)} %fusion), channel_id=1, source_target_pairs={{0,192},{192,0},{64,128},{128,64},{1,193},{193,1},{65,129},{129,65... | collective-permute-start | bytes 393224 | tf_op jit(solution)/shard_map/ppermute | solution.py:377
  174.7 3.0 %collective-permute-done.18 = f32[256,128]{1,0:T(8,128)S(1)} collective-permute-done((f32[256,128]{1,0:T(8,128)S(1)}, f32[256,128]{1,0:T(8,128)S(1)}, u32[]{:S(2)}, u32[]{:S(2)}) %collective-permute-start.18) | collective-permute-done | bytes 131104 | tf_op jit(solution)/shard_map/ppermute | solution.py:377
  177.7 4.1 %collective-permute-start.19 = (f32[256,128]{1,0:T(8,128)S(1)}, f32[256,128]{1,0:T(8,128)S(1)}, u32[]{:S(2)}, u32[]{:S(2)}) collective-permute-start(f32[256,128]{1,0:T(8,128)S(1)} %add.23.keep), channel_id=1, source_target_pairs={{0,32},{32,0},{1,33},{33,1},{2,34},{34,2},{3,35},{35,3},{4,36},{36... | collective-permute-start | bytes 393224 | tf_op jit(solution)/shard_map/ppermute | solution.py:372
  181.8 1.0 collective-permute-done.19.rest
  182.8 0.6 copy-done.15
  183.5 1.9 shard_map.180
  185.3 1.3 reduce
  186.7 0.8 copy-done.3
  187.4 1.9 shard_map.178
  (69 shorter events, 4.6 us)
Async XLA Ops:
  3.1 40.5 %all-to-all-start = ((bf16[32,24,512]{2,1,0:T(8,128)(2,1)}), bf16[32,24,512]{2,1,0:T(8,128)(2,1)S(1)}, u32[]{:S(2)}, u32[]{:S(2)}) async-start(bf16[32,24,512]{2,1,0:T(8,128)(2,1)} %get-tuple-element.35._), calls=%async_computation | async-start | bytes 1572864 | tf_op jit(solution)/shard_map/all_to_all | solution.py:401
  43.6 15.5 %copy-start.6 = (bf16[32,48,128]{2,1,0:T(8,128)(2,1)S(1)}, bf16[32,48,128]{2,1,0:T(8,128)(2,1)}, u32[]{:S(2)}) copy-start(bf16[32,48,128]{2,1,0:T(8,128)(2,1)} %get-tuple-element.50.f0) | copy-start | bytes 1179652
  43.6 26.2 %copy-start.1 = (bf16[32,24,512]{2,1,0:T(8,128)(2,1)}, bf16[32,24,512]{2,1,0:T(8,128)(2,1)S(1)}, u32[]{:S(2)}) copy-start(bf16[32,24,512]{2,1,0:T(8,128)(2,1)S(1)} %all-to-all-done) | copy-start | bytes 2359300
  43.7 13.7 %collective-permute-start.1 = (bf16[768,256]{1,0:T(8,128)(2,1)S(1)}, bf16[768,256]{1,0:T(8,128)(2,1)}, u32[]{:S(2)}, u32[]{:S(2)}) collective-permute-start(bf16[768,256]{1,0:T(8,128)(2,1)S(1)} %get-tuple-element.64), channel_id=1, source_target_pairs={{0,192},{64,0},{128,64},{192,128},{1,193},{65,1},{129,65},{193,129... | collective-permute-start | bytes 1179656 | tf_op jit(solution)/shard_map/ppermute | solution.py:368
  46.3 11.2 %collective-permute-start = (bf16[768,256]{1,0:T(8,128)(2,1)S(1)}, bf16[768,256]{1,0:T(8,128)(2,1)}, u32[]{:S(2)}, u32[]{:S(2)}) collective-permute-start(bf16[768,256]{1,0:T(8,128)(2,1)S(1)} %get-tuple-element.65), channel_id=1, source_target_pairs={{0,64},{64,128},{128,192},{192,0},{1,65},{65,129},{129,193},{193,1... | collective-permute-start | bytes 1179656 | tf_op jit(solution)/shard_map/ppermute | solution.py:368
  46.3 23.5 %all-to-all-start.1 = ((bf16[32,56,128]{2,1,0:T(8,128)(2,1)}), bf16[32,56,128]{2,1,0:T(8,128)(2,1)S(1)}, u32[]{:S(2)}, u32[]{:S(2)}) async-start(bf16[32,56,128]{2,1,0:T(8,128)(2,1)} %get-tuple-element.39), calls=%async_computation.1 | async-start | bytes 917504 | tf_op jit(solution)/shard_map/all_to_all | solution.py:406
  55.5 8.4 %collective-permute-start.2 = (bf16[768,512]{1,0:T(8,128)(2,1)S(1)}, bf16[768,512]{1,0:T(8,128)(2,1)S(1)}, u32[]{:S(2)}, u32[]{:S(2)}) collective-permute-start(bf16[768,512]{1,0:T(8,128)(2,1)S(1)} %bitcast.9), channel_id=1, source_target_pairs={{0,32},{32,0},{1,33},{33,1},{2,34},{34,2},{3,35},{35,3},{4,36},{36... | collective-permute-start | bytes 2359304 | tf_op jit(solution)/shard_map/ppermute | solution.py:372
  57.4 4.8 %collective-permute-start.4 = (bf16[768,256]{1,0:T(8,128)(2,1)}, bf16[768,256]{1,0:T(8,128)(2,1)S(1)}, u32[]{:S(2)}, u32[]{:S(2)}) collective-permute-start(bf16[768,256]{1,0:T(8,128)(2,1)} %collective-permute-done.1.w2), channel_id=1, source_target_pairs={{0,32},{32,0},{1,33},{33,1},{2,34},{34,2},{3,35},{35,3},{4,36},{36... | collective-permute-start | bytes 1179656 | tf_op jit(solution)/shard_map/ppermute | solution.py:372
  57.5 5.2 %collective-permute-start.3 = (bf16[768,256]{1,0:T(8,128)(2,1)}, bf16[768,256]{1,0:T(8,128)(2,1)S(1)}, u32[]{:S(2)}, u32[]{:S(2)}) collective-permute-start(bf16[768,256]{1,0:T(8,128)(2,1)} %collective-permute-done.w1), channel_id=1, source_target_pairs={{0,32},{32,0},{1,33},{33,1},{2,34},{34,2},{3,35},{35,3},{4,36},{36... | collective-permute-start | bytes 1179656 | tf_op jit(solution)/shard_map/ppermute | solution.py:372
  59.1 15.4 %collective-permute-start.8 = (bf16[32,48,128]{2,1,0:T(8,128)(2,1)S(1)}, bf16[32,48,128]{2,1,0:T(8,128)(2,1)S(1)}, u32[]{:S(2)}, u32[]{:S(2)}) collective-permute-start(bf16[32,48,128]{2,1,0:T(8,128)(2,1)S(1)} %copy-done.6), channel_id=1, source_target_pairs={{0,3},{1,0},{2,1},{3,2},{4,7},{5,4},{6,5},{7,6},{8,11},{9,8},{10,9... | collective-permute-start | bytes 1179656 | tf_op jit(solution)/shard_map/ppermute | solution.py:368
  61.5 14.9 %collective-permute-start.7 = (bf16[32,48,128]{2,1,0:T(8,128)(2,1)S(1)}, bf16[32,48,128]{2,1,0:T(8,128)(2,1)S(1)}, u32[]{:S(2)}, u32[]{:S(2)}) collective-permute-start(bf16[32,48,128]{2,1,0:T(8,128)(2,1)S(1)} %copy-done.6), channel_id=1, source_target_pairs={{0,2},{1,3},{2,0},{3,1},{4,6},{5,7},{6,4},{7,5},{8,10},{9,11},{10,... | collective-permute-start | bytes 1179656 | tf_op jit(solution)/shard_map/ppermute | solution.py:368
  62.1 1.8 copy-start.12
  62.1 23.1 %collective-permute-start.6 = (bf16[32,48,128]{2,1,0:T(8,128)(2,1)S(1)}, bf16[32,48,128]{2,1,0:T(8,128)(2,1)}, u32[]{:S(2)}, u32[]{:S(2)}) collective-permute-start(bf16[32,48,128]{2,1,0:T(8,128)(2,1)S(1)} %copy-done.6), channel_id=1, source_target_pairs={{0,1},{1,2},{2,3},{3,0},{4,5},{5,6},{6,7},{7,4},{8,9},{9,10},{10,1... | collective-permute-start | bytes 1179656 | tf_op jit(solution)/shard_map/ppermute | solution.py:368
  62.7 1.2 copy-start.13
  62.7 22.5 %collective-permute-start.5 = (bf16[32,48,128]{2,1,0:T(8,128)(2,1)S(1)}, bf16[32,48,128]{2,1,0:T(8,128)(2,1)}, u32[]{:S(2)}, u32[]{:S(2)}) collective-permute-start(bf16[32,48,128]{2,1,0:T(8,128)(2,1)S(1)} %copy-done.6), channel_id=1, source_target_pairs={{0,4},{4,0},{1,5},{5,1},{2,6},{6,2},{3,7},{7,3},{8,12},{12,8},{9,1... | collective-permute-start | bytes 1179656 | tf_op jit(solution)/shard_map/ppermute | solution.py:372
  63.9 5.9 %copy-start.4 = (bf16[768,512]{1,0:T(8,128)(2,1)}, bf16[768,512]{1,0:T(8,128)(2,1)S(1)}, u32[]{:S(2)}) copy-start(bf16[768,512]{1,0:T(8,128)(2,1)S(1)} %collective-permute-done.2.o0) | copy-start | bytes 2359300
  69.8 0.8 copy-start.2
  74.5 20.3 %copy-start.17 = (bf16[64,256]{1,0:T(8,128)(2,1)S(1)}, bf16[64,256]{1,0:T(8,128)(2,1)}, u32[]{:S(2)}) copy-start(bf16[64,256]{1,0:T(8,128)(2,1)} %get-tuple-element.44.p0) | copy-start | bytes 98308
  74.5 42.9 %copy-start.22 = (s32[8]{0:T(128)S(1)}, s32[8]{0:T(128)}, u32[]{:S(2)}) copy-start(s32[8]{0:T(128)} %param.24) | copy-start | bytes 100
  74.5 51.2 %copy-start.7 = (bf16[32,48,128]{2,1,0:T(8,128)(2,1)}, bf16[32,48,128]{2,1,0:T(8,128)(2,1)S(1)}, u32[]{:S(2)}) copy-start(bf16[32,48,128]{2,1,0:T(8,128)(2,1)S(1)} %collective-permute-done.8.f3) | copy-start | bytes 1179652
  76.4 49.3 %copy-start.8 = (bf16[32,48,128]{2,1,0:T(8,128)(2,1)}, bf16[32,48,128]{2,1,0:T(8,128)(2,1)S(1)}, u32[]{:S(2)}) copy-start(bf16[32,48,128]{2,1,0:T(8,128)(2,1)S(1)} %collective-permute-done.7.f2) | copy-start | bytes 1179652
  85.2 40.5 %all-to-all-start.2 = ((bf16[32,128,128]{2,1,0:T(8,128)(2,1)}), bf16[32,128,128]{2,1,0:T(8,128)(2,1)S(1)}, u32[]{:S(2)}, u32[]{:S(2)}) async-start(bf16[32,128,128]{2,1,0:T(8,128)(2,1)} %shard_map.174), calls=%async_computation.2 | async-start | bytes 2097152 | tf_op jit(solution)/shard_map/all_to_all | solution.py:416
  91.1 46.9 %collective-permute-start.14 = (bf16[32,48,128]{2,1,0:T(8,128)(2,1)}, bf16[32,48,128]{2,1,0:T(8,128)(2,1)S(1)}, u32[]{:S(2)}, u32[]{:S(2)}) collective-permute-start(bf16[32,48,128]{2,1,0:T(8,128)(2,1)} %collective-permute-done.5.g0), channel_id=1, source_target_pairs={{0,3},{1,0},{2,1},{3,2},{4,7},{5,4},{6,5},{7,6},{8,11},{9,8},{10,9... | collective-permute-start | bytes 1179656 | tf_op jit(solution)/shard_map/ppermute | solution.py:368
  93.7 44.4 %collective-permute-start.13 = (bf16[32,48,128]{2,1,0:T(8,128)(2,1)}, bf16[32,48,128]{2,1,0:T(8,128)(2,1)S(1)}, u32[]{:S(2)}, u32[]{:S(2)}) collective-permute-start(bf16[32,48,128]{2,1,0:T(8,128)(2,1)} %collective-permute-done.5.g0), channel_id=1, source_target_pairs={{0,2},{1,3},{2,0},{3,1},{4,6},{5,7},{6,4},{7,5},{8,10},{9,11},{10,... | collective-permute-start | bytes 1179656 | tf_op jit(solution)/shard_map/ppermute | solution.py:368
  94.2 43.9 %collective-permute-start.12 = (bf16[32,48,128]{2,1,0:T(8,128)(2,1)}, bf16[32,48,128]{2,1,0:T(8,128)(2,1)S(1)}, u32[]{:S(2)}, u32[]{:S(2)}) collective-permute-start(bf16[32,48,128]{2,1,0:T(8,128)(2,1)} %collective-permute-done.5.g0), channel_id=1, source_target_pairs={{0,1},{1,2},{2,3},{3,0},{4,5},{5,6},{6,7},{7,4},{8,9},{9,10},{10,1... | collective-permute-start | bytes 1179656 | tf_op jit(solution)/shard_map/ppermute | solution.py:368
  94.8 18.5 %collective-permute-start.11 = (bf16[64,256]{1,0:T(8,128)(2,1)S(1)}, bf16[64,256]{1,0:T(8,128)(2,1)S(1)}, u32[]{:S(2)}, u32[]{:S(2)}) collective-permute-start(bf16[64,256]{1,0:T(8,128)(2,1)S(1)} %copy-done.17), channel_id=1, source_target_pairs={{0,24},{8,0},{16,8},{24,16},{1,25},{9,1},{17,9},{25,17},{2,26},{10... | collective-permute-start | bytes 98312 | tf_op jit(solution)/shard_map/ppermute | solution.py:368
  98.2 20.4 %collective-permute-start.10 = (bf16[64,256]{1,0:T(8,128)(2,1)S(1)}, bf16[64,256]{1,0:T(8,128)(2,1)S(1)}, u32[]{:S(2)}, u32[]{:S(2)}) collective-permute-start(bf16[64,256]{1,0:T(8,128)(2,1)S(1)} %copy-done.17), channel_id=1, source_target_pairs={{0,16},{8,24},{16,0},{24,8},{1,17},{9,25},{17,1},{25,9},{2,18},{10... | collective-permute-start | bytes 98312 | tf_op jit(solution)/shard_map/ppermute | solution.py:368
  113.3 5.7 %copy-start.19 = (bf16[64,256]{1,0:T(8,128)(2,1)}, bf16[64,256]{1,0:T(8,128)(2,1)S(1)}, u32[]{:S(2)}) copy-start(bf16[64,256]{1,0:T(8,128)(2,1)S(1)} %collective-permute-done.11.p3) | copy-start | bytes 98308
  113.3 5.7 %collective-permute-start.9 = (bf16[64,256]{1,0:T(8,128)(2,1)S(1)}, bf16[64,256]{1,0:T(8,128)(2,1)S(1)}, u32[]{:S(2)}, u32[]{:S(2)}) collective-permute-start(bf16[64,256]{1,0:T(8,128)(2,1)S(1)} %copy-done.17), channel_id=1, source_target_pairs={{0,8},{8,16},{16,24},{24,0},{1,9},{9,17},{17,25},{25,1},{2,10},{10... | collective-permute-start | bytes 98312 | tf_op jit(solution)/shard_map/ppermute | solution.py:368
  118.5 0.6 copy-start.20
  125.7 1.0 copy-start
  131.3 20.2 %all-to-all-start.3 = ((bf16[8,48,128]{2,1,0:T(8,128)(2,1)}), bf16[8,48,128]{2,1,0:T(8,128)(2,1)S(1)}, u32[]{:S(2)}, u32[]{:S(2)}) async-start(bf16[8,48,128]{2,1,0:T(8,128)(2,1)} %get-tuple-element.49), calls=%async_computation.3 | async-start | bytes 196608 | tf_op jit(solution)/shard_map/all_to_all | solution.py:427
  138.1 18.8 %copy-start.18 = (f32[64,128]{1,0:T(8,128)S(1)}, f32[64,128]{1,0:T(8,128)}, u32[]{:S(2)}) copy-start(f32[64,128]{1,0:T(8,128)} %get-tuple-element.58) | copy-start | bytes 98308
  138.1 30.3 %copy-start.16 = (f32[64,128]{1,0:T(8,128)S(1)}, f32[64,128]{1,0:T(8,128)}, u32[]{:S(2)}) copy-start(f32[64,128]{1,0:T(8,128)} %get-tuple-element.57) | copy-start | bytes 98308
  138.1 0.8 copy-start.9
  138.1 0.9 copy-start.10
  139.0 0.7 copy-start.11
  145.4 4.6 %collective-permute-start.15 = (f32[8,24,128]{2,1,0:T(8,128)}, f32[8,24,128]{2,1,0:T(8,128)S(1)}, u32[]{:S(2)}, u32[]{:S(2)}) collective-permute-start(f32[8,24,128]{2,1,0:T(8,128)} %get-tuple-element.56), channel_id=1, source_target_pairs={{0,32},{32,0},{1,33},{33,1},{2,34},{34,2},{3,35},{35,3},{4,36},{36... | collective-permute-start | bytes 294920 | tf_op jit(solution)/shard_map/ppermute | solution.py:372
  151.5 6.1 %copy-start.14 = (bf16[8,48,128]{2,1,0:T(8,128)(2,1)}, bf16[8,48,128]{2,1,0:T(8,128)(2,1)S(1)}, u32[]{:S(2)}) copy-start(bf16[8,48,128]{2,1,0:T(8,128)(2,1)S(1)} %all-to-all-done.3.parts) | copy-start | bytes 294916
  151.5 10.7 %all-to-all-start.5 = ((f32[8,24,128]{2,1,0:T(8,128)}), f32[8,24,128]{2,1,0:T(8,128)S(1)}, u32[]{:S(2)}, u32[]{:S(2)}) async-start(f32[8,24,128]{2,1,0:T(8,128)} %add.20), calls=%async_computation.5 | async-start | bytes 196608 | tf_op jit(solution)/shard_map/all_to_all | solution.py:431
  156.9 11.4 %collective-permute-start.16 = (f32[64,128]{1,0:T(8,128)S(1)}, f32[64,128]{1,0:T(8,128)S(1)}, u32[]{:S(2)}, u32[]{:S(2)}) collective-permute-start(f32[64,128]{1,0:T(8,128)S(1)} %copy-done.18), channel_id=1, source_target_pairs={{0,32},{32,0},{1,33},{33,1},{2,34},{34,2},{3,35},{35,3},{4,36},{36... | collective-permute-start | bytes 98312 | tf_op jit(solution)/shard_map/ppermute | solution.py:372
  162.2 24.4 %all-to-all-start.4 = ((bf16[32,48,128]{2,1,0:T(8,128)(2,1)}), bf16[32,48,128]{2,1,0:T(8,128)(2,1)S(1)}, u32[]{:S(2)}, u32[]{:S(2)}) async-start(bf16[32,48,128]{2,1,0:T(8,128)(2,1)} %shard_map.177), calls=%async_computation.4 | async-start | bytes 786432 | tf_op jit(solution)/shard_map/all_to_all | solution.py:432
  168.4 3.9 %collective-permute-start.17 = (f32[256,128]{1,0:T(8,128)S(1)}, f32[256,128]{1,0:T(8,128)S(1)}, u32[]{:S(2)}, u32[]{:S(2)}) collective-permute-start(f32[256,128]{1,0:T(8,128)S(1)} %pad_maximum_fusion), channel_id=1, source_target_pairs={{0,64},{64,0},{128,192},{192,128},{1,65},{65,1},{129,193},{193,129... | collective-permute-start | bytes 393224 | tf_op jit(solution)/shard_map/ppermute | solution.py:376
  172.3 5.4 %collective-permute-start.18 = (f32[256,128]{1,0:T(8,128)S(1)}, f32[256,128]{1,0:T(8,128)S(1)}, u32[]{:S(2)}, u32[]{:S(2)}) collective-permute-start(f32[256,128]{1,0:T(8,128)S(1)} %fusion), channel_id=1, source_target_pairs={{0,192},{192,0},{64,128},{128,64},{1,193},{193,1},{65,129},{129,65... | collective-permute-start | bytes 393224 | tf_op jit(solution)/shard_map/ppermute | solution.py:377
  177.7 5.1 %copy-start.5 = (f32[256,128]{1,0:T(8,128)}, f32[256,128]{1,0:T(8,128)S(1)}, u32[]{:S(2)}) copy-start(f32[256,128]{1,0:T(8,128)S(1)} %add.23.keep) | copy-start | bytes 393220
  177.7 5.1 %collective-permute-start.19 = (f32[256,128]{1,0:T(8,128)S(1)}, f32[256,128]{1,0:T(8,128)S(1)}, u32[]{:S(2)}, u32[]{:S(2)}) collective-permute-start(f32[256,128]{1,0:T(8,128)S(1)} %add.23.keep), channel_id=1, source_target_pairs={{0,32},{32,0},{1,33},{33,1},{2,34},{34,2},{3,35},{35,3},{4,36},{36... | collective-permute-start | bytes 393224 | tf_op jit(solution)/shard_map/ppermute | solution.py:372
  182.8 0.6 copy-start.15
  186.7 0.8 copy-start.3
  (1 other events, 0.6 us)

commit v5 on v4

--- a/solution.py
+++ b/solution.py
@@ -224,9 +224,9 @@
         at = 2 * zq + half
         scores = jnp.dot(self_t[...], hidden[at], preferred_element_type=F32)
         halves.append(scores + jnp.dot(neigh_t[...], second[at], preferred_element_type=F32))
+    block = jnp.concatenate(halves, axis=1)[0 : out.shape[1]].astype(BF)
     for z in range(out.shape[0]):
-        both = [scores[24 * z : 24 * (z + 1)] for scores in halves]
-        out[z] = jnp.concatenate(both, axis=0).astype(BF)
+        out[z] = block
     total = jnp.zeros((32, TILE), F32)
     for b in range(hidden.shape[0]):
         total = total + jnp.where(hidden[b, own, :].astype(F32) > 0.0, dhidden[b, own, :], 0.0)
@@ -251,50 +251,43 @@
         in_specs=[SMEM, SMEM] + [VMEM] * 6,
         out_specs=[VMEM] * 3,
         scratch_shapes=[pltpu.VMEM((tiles.shape[0], TILE, TILE), BF)],
-        out_shape=[jax.ShapeDtypeStruct((8, 48, TILE), BF), shape, shape],
+        out_shape=[jax.ShapeDtypeStruct((8, 160, 256), BF), shape, shape],
         compiler_params=LIMIT,
     )(place, cols, hidden, dhidden, tiles, cot, self_t, neigh_t)
 
 
-def fan_kernel(parts, out):
+def total_kernel(parts, out):
     total = parts[0].astype(F32)
     for j in range(1, parts.shape[0]):
         total = total + parts[j].astype(F32)
-    for d in range(out.shape[0]):
-        out[d] = total.astype(BF)
-
-
-def fan(parts):
-    return pl.pallas_call(
-        fan_kernel,
+    out[...] = total.astype(BF)
+
+
+def total(parts):
+    return pl.pallas_call(
+        total_kernel,
         in_specs=[VMEM],
         out_specs=VMEM,
-        out_shape=jax.ShapeDtypeStruct((32,) + parts.shape[1:], BF),
+        out_shape=jax.ShapeDtypeStruct(parts.shape[1:], BF),
         compiler_params=LIMIT,
     )(parts)
 
 
-def logit_kernel(parts, out):
+def logit_kernel(place, s0, s1, s2, s3, out):
     classes = out.shape[0]
-    for j in range(8):
-        rows = min(24, classes - 24 * j)
-        if rows <= 0:
-            continue
-        for zq in range(4):
-            block = parts[8 * zq + j].astype(F32)
-            for half in range(2):
-                at = (2 * zq + half) * TILE
-                out[24 * j : 24 * j + rows, at : at + TILE] = block[24 * half : 24 * half + rows]
-
-
-def join(parts, classes, slots):
+    for s, part in enumerate((s0, s1, s2, s3)):
+        at = aligned(lax.rem(place[2] + 4 - s, 4), 256)
+        out[:, at] = part[...].astype(F32)[0:classes]
+
+
+def join(place, parts, classes):
     return pl.pallas_call(
         logit_kernel,
-        in_specs=[VMEM],
+        in_specs=[SMEM] + [VMEM] * 4,
         out_specs=VMEM,
-        out_shape=jax.ShapeDtypeStruct((classes, slots), F32),
-        compiler_params=LIMIT,
-    )(parts)
+        out_shape=jax.ShapeDtypeStruct((classes, 4 * parts[0].shape[1]), F32),
+        compiler_params=LIMIT,
+    )(place, *parts)
 
 
 def grad_kernel(place, hidden, dhidden, f0, f1, f2, f3, g0, g1, g2, g3, keep, send, total):
@@ -349,7 +342,7 @@
         base = 8 * deep
         head[:, 0:TILE] = value[base : base + 32]
         head[:, TILE:classes] = value[base + 32 : base + 64, 0 : classes - TILE]
-    bias[...] = first[8 * deep + 32 : 8 * deep + 64, TILE - 1 : TILE]
+    bias[...] = first[8 * deep + 32 : 8 * deep + 64].T[TILE - 1 : TILE]
 
 
 def finish(place, keep, rest, deep, classes):
@@ -359,7 +352,7 @@
         finish_kernel,
         in_specs=[SMEM, VMEM, VMEM],
         out_specs=[VMEM] * 5,
-        out_shape=[weight, weight, head, head, jax.ShapeDtypeStruct((32, 1), F32)],
+        out_shape=[weight, weight, head, head, jax.ShapeDtypeStruct((1, 32), F32)],
         compiler_params=LIMIT,
     )(place, keep, rest)
 
@@ -402,37 +395,41 @@
     send, feats = hop(
         place, feature_table, node_ids, hop_cols, hidden_bias, hop_tiles, packed
     )
-    weights, pair, send, feats = lax.optimization_barrier((weights, pair, send, feats))
+    pairs = [pair] + [shift(pair, "zq", s) for s in (1, 2, 3)]
+    weights, pairs, send, feats = lax.optimization_barrier((weights, pairs, send, feats))
     got = lax.all_to_all(send, FEAT, 0, 0, tiled=True)
     weights = weights.reshape(-1, 512)
     mine = [weights, shift(weights[:, :256], "x", 1), shift(weights[:, 256:], "x", 3)]
     other = [swap(w, "core") for w in mine]
 
     twin = swap(feats, "zr")
+
+    live = batch_sizes[lax.axis_index("x") * 2 + lax.axis_index("core")]
+    ready = spread(place, target_cols, live, logit_cotangent, pairs, target_tiles, blocks)
+    hidden = layer(place, got, mine, other)
+    hidden, ready, feats, twin = lax.optimization_barrier((hidden, ready, feats, twin))
+    dhidden, cot, self_t, neigh_t = ready
+    hidden = lax.all_to_all(hidden, FEAT, 0, 0, tiled=True)
     feats = [feats] + [shift(feats, "y", s) for s in (1, 2, 3)]
-
-    hidden = layer(place, got, mine, other)
-    hidden, pair, twin, feats = lax.optimization_barrier((hidden, pair, twin, feats))
-    hidden = lax.all_to_all(hidden, FEAT, 0, 0, tiled=True)
-    pairs = [pair] + [shift(pair, "zq", s) for s in (1, 2, 3)]
     feats = feats + [twin] + [shift(twin, "y", s) for s in (1, 2, 3)]
-    live = batch_sizes[lax.axis_index("x") * 2 + lax.axis_index("core")]
-    dhidden, cot, self_t, neigh_t = spread(
-        place, target_cols, live, logit_cotangent, pairs, target_tiles, blocks
-    )
+    hidden, feats = lax.optimization_barrier((hidden, feats))
 
     scores, keep_head, send_head = score(
         place, target_cols, hidden, dhidden, target_tiles, cot, self_t, neigh_t
     )
     scores = lax.all_to_all(scores, ("zr", "y"), 0, 0, tiled=True)
+    hidden, keep_head, send_head = lax.optimization_barrier((hidden, keep_head, send_head))
     keep_head = keep_head + swap(send_head, "core")
     keep, send = grad(place, hidden, dhidden, feats)
     keep = keep + swap(send, "core")
+    keep, scores, keep_head = lax.optimization_barrier((keep, scores, keep_head))
     keep = lax.all_to_all(keep, ("zr", "y"), 0, 0, tiled=True)
-    scores = lax.all_to_all(fan(scores), FEAT, 0, 0, tiled=True)
+    scores = total(scores)
+    scores = [scores] + [shift(scores, "zq", s) for s in (1, 2, 3)]
+    keep, scores = lax.optimization_barrier((keep, scores))
     keep = sum_x(jnp.concatenate([keep.reshape(-1, TILE), keep_head], axis=0))
     results = finish(place, keep, swap(keep, "core"), deep, classes)
-    return (join(scores, classes, target_rows), *results[:4], results[4].reshape(-1))
+    return (join(place, scores, classes), *results[:4], results[4].reshape(-1))
 
 
 def solution(mesh):

time: 190 us -> 201 us (1.058)
  waiting for transfers between devices: 42.6 us -> 60.3 us
  starting transfers between devices: 80.3 us -> 75.6 us
    ppermute x11 -> x14, waiting for transfers between devices: 24.9 us -> 50.3 us  [shift(): return lax.ppermute(value, axis, [(i, (i + by) % 4) for i in range(4)])]
    all_to_all x1 -> x0, starting transfers between devices: 6.1 us -> none  [shards(): scores = lax.all_to_all(fan(scores), FEAT, 0, 0, tiled=True)]
    all_to_all x1, waiting for transfers between devices: 5.87 us -> 0.01 us  [shards(): got = lax.all_to_all(send, FEAT, 0, 0, tiled=True)]
    ppermute x11 -> x14, starting transfers between devices: 19.3 us -> 24.2 us  [shift(): return lax.ppermute(value, axis, [(i, (i + by) % 4) for i in range(4)])]
    all_to_all x1, starting transfers between devices: 9.22 us -> 5.79 us  [shards(): got = lax.all_to_all(send, FEAT, 0, 0, tiled=True)]
    all_to_all x1, starting transfers between devices: 6.8 us -> 3.54 us  [shards(): scores = lax.all_to_all(scores, ('zr', 'y'), 0, 0, tiled=True)]
    ppermute x7, starting transfers between devices: 13 us -> 16.2 us  [swap(): return lax.ppermute(value, axis, [(0, 1), (1, 0)])]
    all_to_all x1, waiting for transfers between devices: 2.92 us -> 0.01 us  [shards(): keep = lax.all_to_all(keep, ('zr', 'y'), 0, 0, tiled=True)]
  transfers between devices with their start and end apart: 26 -> 28, of which waited for: 11 -> 13; matrix products, arithmetic and copies ran while one was open for 3% -> 2% of each run, Pallas kernels for 27% -> 23%
where the time goes in v5:
time: 201 us; the launch traced here: 200 us
  starting transfers between devices  75.6 us (38%)
  waiting for transfers between devices  60.3 us (30%)
  Pallas kernels  54.6 us (27%)
  local copies, waits for them, and re-layouts  6.7 us (3%)
    ppermute x14, waiting for transfers between devices, shift(): return lax.ppermute(value, axis, [(i, (i + by) % 4) for i in range(4)])  50.3 us
    pallas_call x1, Pallas kernels, hop(): pl.pallas_call(hop_kernel, in_specs=[SMEM, SMEM, SMEM, VMEM, VMEM, HBM, H...  27.1 us
    ppermute x14, starting transfers between devices, shift(): return lax.ppermute(value, axis, [(i, (i + by) % 4) for i in range(4)])  24.2 us
    ppermute x7, starting transfers between devices, swap(): return lax.ppermute(value, axis, [(0, 1), (1, 0)])  16.2 us
    all_to_all x1, starting transfers between devices, shards(): weights = lax.all_to_all(packed, FEAT, 0, 0, tiled=True)  12 us
    all_to_all x1, starting transfers between devices, shards(): hidden = lax.all_to_all(hidden, FEAT, 0, 0, tiled=True)  8.3 us
    pallas_call x1, Pallas kernels, spread(): pl.pallas_call(spread_kernel, in_specs=[SMEM, SMEM, SMEM] + [VMEM] * 6, o...  5.94 us
    all_to_all x1, starting transfers between devices, shards(): got = lax.all_to_all(send, FEAT, 0, 0, tiled=True)  5.79 us
  transfers between devices with their start and end apart: 28, of which 13 were waited for; matrix products, arithmetic and copies ran while one was open for 2% of the time, Pallas kernels for 23%

profile of v5, /device:TPU:1, one launch (start us, length us, event | category | flops | bytes accessed | tf_op | source)
XLA Modules:
  0.0 199.8 jit_solution(12014965555384796917)
XLA Ops:
  1.2 1.8 shard_map.172
  3.1 12.0 %all-to-all-start = ((bf16[32,24,512]{2,1,0:T(8,128)(2,1)}), bf16[32,24,512]{2,1,0:T(8,128)(2,1)S(1)}, u32[]{:S(2)}, u32[]{:S(2)}) async-start(bf16[32,24,512]{2,1,0:T(8,128)(2,1)} %get-tuple-element.58._), calls=%async_computation | async-start | bytes 1572864 | tf_op jit(solution)/shard_map/all_to_all | solution.py:394
  15.1 3.5 %collective-permute-start.2 = (bf16[64,256]{1,0:T(8,128)(2,1)}, bf16[64,256]{1,0:T(8,128)(2,1)S(1)}, u32[]{:S(2)}, u32[]{:S(2)}) collective-permute-start(bf16[64,256]{1,0:T(8,128)(2,1)} %get-tuple-element.64.p0), channel_id=1, source_target_pairs={{0,24},{8,0},{16,8},{24,16},{1,25},{9,1},{17,9},{25,17},{2,26},{10... | collective-permute-start | bytes 98312 | tf_op jit(solution)/shard_map/ppermute | solution.py:361
  18.6 2.0 %collective-permute-start.1 = (bf16[64,256]{1,0:T(8,128)(2,1)}, bf16[64,256]{1,0:T(8,128)(2,1)S(1)}, u32[]{:S(2)}, u32[]{:S(2)}) collective-permute-start(bf16[64,256]{1,0:T(8,128)(2,1)} %get-tuple-element.64.p0), channel_id=1, source_target_pairs={{0,16},{8,24},{16,0},{24,8},{1,17},{9,25},{17,1},{25,9},{2,18},{10... | collective-permute-start | bytes 98312 | tf_op jit(solution)/shard_map/ppermute | solution.py:361
  20.6 2.1 %collective-permute-start = (bf16[64,256]{1,0:T(8,128)(2,1)}, bf16[64,256]{1,0:T(8,128)(2,1)S(1)}, u32[]{:S(2)}, u32[]{:S(2)}) collective-permute-start(bf16[64,256]{1,0:T(8,128)(2,1)} %get-tuple-element.64.p0), channel_id=1, source_target_pairs={{0,8},{8,16},{16,24},{24,0},{1,9},{9,17},{17,25},{25,1},{2,10},{10... | collective-permute-start | bytes 98312 | tf_op jit(solution)/shard_map/ppermute | solution.py:361
  22.7 1.4 copy.19.cols
  24.1 27.1 %shard_map.173 = (bf16[32,56,128]{2,1,0:T(8,128)(2,1)}, bf16[32,48,128]{2,1,0:T(8,128)(2,1)}) custom-call(s32[5]{0:T(128)} %stack.23.place, s32[16384]{0:T(1024)} %ids.1, s32[32,8]{1,0:T(8,128)} %copy.19.cols, bf16[24,32768]{1,0:T(8,128)(2,1)} %table.1, f32[1,32]{1,0:T(1,128)} %bitcast.14, bf16[32,8,128,128]{3,2,1,0:T(8,128)(2,1)} %tiles_hbm.1, ...), custom_call_target="tpu_custom_call" | custom-call | flops 1000000000 | bytes 60000000 | tf_op jit(solution)/shard_map/pallas_call | solution.py:84
  51.3 5.8 %all-to-all-start.1 = ((bf16[32,56,128]{2,1,0:T(8,128)(2,1)}), bf16[32,56,128]{2,1,0:T(8,128)(2,1)S(1)}, u32[]{:S(2)}, u32[]{:S(2)}) async-start(bf16[32,56,128]{2,1,0:T(8,128)(2,1)} %get-tuple-element.62), calls=%async_computation.1 | async-start | bytes 917504 | tf_op jit(solution)/shard_map/all_to_all | solution.py:400
  57.2 2.6 %collective-permute-start.4 = (bf16[768,256]{1,0:T(8,128)(2,1)S(1)}, bf16[768,256]{1,0:T(8,128)(2,1)S(1)}, u32[]{:S(2)}, u32[]{:S(2)}) collective-permute-start(bf16[768,256]{1,0:T(8,128)(2,1)S(1)} %get-tuple-element.110), channel_id=1, source_target_pairs={{0,192},{64,0},{128,64},{192,128},{1,193},{65,1},{129,65},{193,129... | collective-permute-start | bytes 1179656 | tf_op jit(solution)/shard_map/ppermute | solution.py:361
  59.7 2.6 %collective-permute-start.5 = (bf16[768,512]{1,0:T(8,128)(2,1)S(1)}, bf16[768,512]{1,0:T(8,128)(2,1)S(1)}, u32[]{:S(2)}, u32[]{:S(2)}) collective-permute-start(bf16[768,512]{1,0:T(8,128)(2,1)S(1)} %bitcast.10), channel_id=1, source_target_pairs={{0,32},{32,0},{1,33},{33,1},{2,34},{34,2},{3,35},{35,3},{4,36},{36... | collective-permute-start | bytes 2359304 | tf_op jit(solution)/shard_map/ppermute | solution.py:365
  62.4 3.4 %collective-permute-done.4.w2 = bf16[768,256]{1,0:T(8,128)(2,1)S(1)} collective-permute-done((bf16[768,256]{1,0:T(8,128)(2,1)S(1)}, bf16[768,256]{1,0:T(8,128)(2,1)S(1)}, u32[]{:S(2)}, u32[]{:S(2)}) %collective-permute-start.4) | collective-permute-done | bytes 393248 | tf_op jit(solution)/shard_map/ppermute | solution.py:361
  65.8 3.3 %collective-permute-start.7 = (bf16[768,256]{1,0:T(8,128)(2,1)S(1)}, bf16[768,256]{1,0:T(8,128)(2,1)}, u32[]{:S(2)}, u32[]{:S(2)}) collective-permute-start(bf16[768,256]{1,0:T(8,128)(2,1)S(1)} %collective-permute-done.4.w2), channel_id=1, source_target_pairs={{0,32},{32,0},{1,33},{33,1},{2,34},{34,2},{3,35},{35,3},{4,36},{36... | collective-permute-start | bytes 1179656 | tf_op jit(solution)/shard_map/ppermute | solution.py:365
  69.1 3.5 %collective-permute-start.6 = (bf16[768,256]{1,0:T(8,128)(2,1)}, bf16[768,256]{1,0:T(8,128)(2,1)}, u32[]{:S(2)}, u32[]{:S(2)}) collective-permute-start(bf16[768,256]{1,0:T(8,128)(2,1)} %collective-permute-done.3.w1), channel_id=1, source_target_pairs={{0,32},{32,0},{1,33},{33,1},{2,34},{34,2},{3,35},{35,3},{4,36},{36... | collective-permute-start | bytes 1179656 | tf_op jit(solution)/shard_map/ppermute | solution.py:365
  72.6 1.2 collective-permute-start.8
  74.4 5.9 %shard_map.175 = (f32[32,128,128]{2,1,0:T(8,128)}, bf16[256,1024]{1,0:T(8,128)(2,1)}, bf16[256,128]{1,0:T(8,128)(2,1)}, bf16[256,128]{1,0:T(8,128)(2,1)}) custom-call(s32[5]{0:T(128)} %stack.23.place, s32[8,8]{1,0:T(8,128)} %cols.4, s32[1]{0:T(128)} %dynamic_slice.3.live, bf16[153,1024]{1,0:T(8,128)(2,1)} %logit_cot.1, ...), custom_call_target="tpu_custom_call" | custom-call | flops 1000000000 | bytes 8000000 | tf_op jit(solution)/shard_map/pallas_call | solution.py:153
  80.4 0.9 copy-done.4
  81.3 0.8 copy-done.3
  82.0 4.0 %shard_map.174 = bf16[32,128,128]{2,1,0:T(8,128)(2,1)} custom-call(s32[5]{0:T(128)} %stack.23.place, bf16[32,56,128]{2,1,0:T(8,128)(2,1)} %copy-done.3, bf16[768,512]{1,0:T(8,128)(2,1)} %bitcast.11, bf16[768,256]{1,0:T(8,128)(2,1)} %collective-permute-done.3.w1, bf16[768,256]{1,0:T(8,128)(2,1)} %copy-done.8, bf16[768,512]{1,0:T(8,128)(2,1)} %copy-done.4, ...), custom_call_target="tpu_custom_call" | custom-call | tf_op jit(solution)/shard_map/pallas_call | solution.py:203
  86.0 8.3 %all-to-all-start.2 = ((bf16[32,128,128]{2,1,0:T(8,128)(2,1)}), bf16[32,128,128]{2,1,0:T(8,128)(2,1)S(1)}, u32[]{:S(2)}, u32[]{:S(2)}) async-start(bf16[32,128,128]{2,1,0:T(8,128)(2,1)} %shard_map.174), calls=%async_computation.2 | async-start | bytes 2097152 | tf_op jit(solution)/shard_map/all_to_all | solution.py:412
  94.3 2.5 %collective-permute-start.11 = (bf16[32,48,128]{2,1,0:T(8,128)(2,1)S(1)}, bf16[32,48,128]{2,1,0:T(8,128)(2,1)S(1)}, u32[]{:S(2)}, u32[]{:S(2)}) collective-permute-start(bf16[32,48,128]{2,1,0:T(8,128)(2,1)S(1)} %copy-done.6), channel_id=1, source_target_pairs={{0,3},{1,0},{2,1},{3,2},{4,7},{5,4},{6,5},{7,6},{8,11},{9,8},{10,9... | collective-permute-start | bytes 1179656 | tf_op jit(solution)/shard_map/ppermute | solution.py:361
  98.0 2.1 %collective-permute-start.14 = (bf16[32,48,128]{2,1,0:T(8,128)(2,1)S(1)}, bf16[32,48,128]{2,1,0:T(8,128)(2,1)S(1)}, u32[]{:S(2)}, u32[]{:S(2)}) collective-permute-start(bf16[32,48,128]{2,1,0:T(8,128)(2,1)S(1)} %collective-permute-done.8.g0), channel_id=1, source_target_pairs={{0,3},{1,0},{2,1},{3,2},{4,7},{5,4},{6,5},{7,6},{8,11},{9,8},{10,9... | collective-permute-start | bytes 1179656 | tf_op jit(solution)/shard_map/ppermute | solution.py:361
  100.1 1.2 collective-permute-start.13
  101.3 13.8 %collective-permute-done.11.f3 = bf16[32,48,128]{2,1,0:T(8,128)(2,1)S(1)} collective-permute-done((bf16[32,48,128]{2,1,0:T(8,128)(2,1)S(1)}, bf16[32,48,128]{2,1,0:T(8,128)(2,1)S(1)}, u32[]{:S(2)}, u32[]{:S(2)}) %collective-permute-start.11) | collective-permute-done | bytes 393248 | tf_op jit(solution)/shard_map/ppermute | solution.py:361
  115.3 13.0 %collective-permute-done.9.f1 = bf16[32,48,128]{2,1,0:T(8,128)(2,1)S(1)} collective-permute-done((bf16[32,48,128]{2,1,0:T(8,128)(2,1)S(1)}, bf16[32,48,128]{2,1,0:T(8,128)(2,1)S(1)}, u32[]{:S(2)}, u32[]{:S(2)}) %collective-permute-start.9) | collective-permute-done | bytes 393248 | tf_op jit(solution)/shard_map/ppermute | solution.py:361
  128.3 4.3 %collective-permute-done.14.g3 = bf16[32,48,128]{2,1,0:T(8,128)(2,1)S(1)} collective-permute-done((bf16[32,48,128]{2,1,0:T(8,128)(2,1)S(1)}, bf16[32,48,128]{2,1,0:T(8,128)(2,1)S(1)}, u32[]{:S(2)}, u32[]{:S(2)}) %collective-permute-start.14) | collective-permute-done | bytes 393248 | tf_op jit(solution)/shard_map/ppermute | solution.py:361
  132.6 2.7 %collective-permute-done.13.g2 = bf16[32,48,128]{2,1,0:T(8,128)(2,1)S(1)} collective-permute-done((bf16[32,48,128]{2,1,0:T(8,128)(2,1)S(1)}, bf16[32,48,128]{2,1,0:T(8,128)(2,1)S(1)}, u32[]{:S(2)}, u32[]{:S(2)}) %collective-permute-start.13) | collective-permute-done | bytes 393248 | tf_op jit(solution)/shard_map/ppermute | solution.py:361
  135.3 0.8 copy-done.13
  136.1 8.1 %collective-permute-done.12.g1 = bf16[32,48,128]{2,1,0:T(8,128)(2,1)} collective-permute-done((bf16[32,48,128]{2,1,0:T(8,128)(2,1)S(1)}, bf16[32,48,128]{2,1,0:T(8,128)(2,1)}, u32[]{:S(2)}, u32[]{:S(2)}) %collective-permute-start.12) | collective-permute-done | bytes 393248 | tf_op jit(solution)/shard_map/ppermute | solution.py:361
  144.2 1.0 copy-done
  145.2 4.5 %shard_map.176 = (bf16[8,160,256]{2,1,0:T(8,128)(2,1)}, f32[64,128]{1,0:T(8,128)}, f32[64,128]{1,0:T(8,128)}) custom-call(s32[5]{0:T(128)} %stack.23.place, s32[8,8]{1,0:T(8,128)} %cols.4, bf16[32,128,128]{2,1,0:T(8,128)(2,1)} %copy-done, f32[32,128,128]{2,1,0:T(8,128)} %get-tuple-element.77.dhidden, bf16[8,8,128,128]{3,2,1,0:T(8,128)(2,1)} %tiles.3, ...), custom_call_target="tpu_custom_call" | custom-call | tf_op jit(solution)/shard_map/pallas_call | solution.py:249
  149.7 3.5 %all-to-all-start.3 = ((bf16[8,160,256]{2,1,0:T(8,128)(2,1)}), bf16[8,160,256]{2,1,0:T(8,128)(2,1)S(1)}, u32[]{:S(2)}, u32[]{:S(2)}) async-start(bf16[8,160,256]{2,1,0:T(8,128)(2,1)} %get-tuple-element.94), calls=%async_computation.3 | async-start | bytes 1310720 | tf_op jit(solution)/shard_map/all_to_all | solution.py:420
  153.3 5.6 %shard_map.177 = (f32[8,24,128]{2,1,0:T(8,128)}, f32[8,24,128]{2,1,0:T(8,128)}) custom-call(s32[5]{0:T(128)} %stack.23.place, bf16[32,128,128]{2,1,0:T(8,128)(2,1)} %copy-done, f32[32,128,128]{2,1,0:T(8,128)} %get-tuple-element.77.dhidden, bf16[32,48,128]{2,1,0:T(8,128)(2,1)} %get-tuple-element.84.f0, bf16[32,48,128]{2,1,0:T(8,128)(2,1)} %copy-done.11, ...), custom_call_target="tpu_custom_call" | custom-call | flops 1000000000 | bytes 7000000 | tf_op jit(solution)/shard_map/pallas_call | solution.py:316
  159.0 0.8 collective-permute-start.15
  159.9 1.1 collective-permute-done.16
  161.0 1.5 add.20
  162.6 5.3 %all-to-all-start.4 = ((f32[8,24,128]{2,1,0:T(8,128)}), f32[8,24,128]{2,1,0:T(8,128)S(1)}, u32[]{:S(2)}, u32[]{:S(2)}) async-start(f32[8,24,128]{2,1,0:T(8,128)} %add.20), calls=%async_computation.4 | async-start | bytes 196608 | tf_op jit(solution)/shard_map/all_to_all | solution.py:426
  167.9 1.8 shard_map.178.s0
  169.7 3.1 %collective-permute-start.19 = (bf16[160,256]{1,0:T(8,128)(2,1)}, bf16[160,256]{1,0:T(8,128)(2,1)S(1)}, u32[]{:S(2)}, u32[]{:S(2)}) collective-permute-start(bf16[160,256]{1,0:T(8,128)(2,1)} %shard_map.178.s0), channel_id=1, source_target_pairs={{0,24},{8,0},{16,8},{24,16},{1,25},{9,1},{17,9},{25,17},{2,26},{10... | collective-permute-start | bytes 245768 | tf_op jit(solution)/shard_map/ppermute | solution.py:361
  172.8 2.2 %collective-permute-start.18 = (bf16[160,256]{1,0:T(8,128)(2,1)}, bf16[160,256]{1,0:T(8,128)(2,1)S(1)}, u32[]{:S(2)}, u32[]{:S(2)}) collective-permute-start(bf16[160,256]{1,0:T(8,128)(2,1)} %shard_map.178.s0), channel_id=1, source_target_pairs={{0,16},{8,24},{16,0},{24,8},{1,17},{9,25},{17,1},{25,9},{2,18},{10... | collective-permute-start | bytes 245768 | tf_op jit(solution)/shard_map/ppermute | solution.py:361
  175.0 1.8 collective-permute-start.17
  176.8 3.5 %collective-permute-done.18.s2 = bf16[160,256]{1,0:T(8,128)(2,1)S(1)} collective-permute-done((bf16[160,256]{1,0:T(8,128)(2,1)}, bf16[160,256]{1,0:T(8,128)(2,1)S(1)}, u32[]{:S(2)}, u32[]{:S(2)}) %collective-permute-start.18) | collective-permute-done | bytes 81952 | tf_op jit(solution)/shard_map/ppermute | solution.py:361
  180.3 1.2 collective-permute-done.17.s1
  181.7 3.8 %collective-permute-done.20 = f32[256,128]{1,0:T(8,128)S(1)} collective-permute-done((f32[256,128]{1,0:T(8,128)S(1)}, f32[256,128]{1,0:T(8,128)S(1)}, u32[]{:S(2)}, u32[]{:S(2)}) %collective-permute-start.20) | collective-permute-done | bytes 131104 | tf_op jit(solution)/shard_map/ppermute | solution.py:369
  185.7 5.0 %collective-permute-done.21 = f32[256,128]{1,0:T(8,128)S(1)} collective-permute-done((f32[256,128]{1,0:T(8,128)S(1)}, f32[256,128]{1,0:T(8,128)S(1)}, u32[]{:S(2)}, u32[]{:S(2)}) %collective-permute-start.21) | collective-permute-done | bytes 131104 | tf_op jit(solution)/shard_map/ppermute | solution.py:370
  190.7 4.7 %collective-permute-start.22 = (f32[256,128]{1,0:T(8,128)S(1)}, f32[256,128]{1,0:T(8,128)S(1)}, u32[]{:S(2)}, u32[]{:S(2)}) collective-permute-start(f32[256,128]{1,0:T(8,128)S(1)} %add.23.keep), channel_id=1, source_target_pairs={{0,32},{32,0},{1,33},{33,1},{2,34},{34,2},{3,35},{35,3},{4,36},{36... | collective-permute-start | bytes 393224 | tf_op jit(solution)/shard_map/ppermute | solution.py:365
  195.3 1.9 shard_map.179
  197.3 0.6 copy-done.14
  197.9 1.9 shard_map.180
  (74 shorter events, 3.2 us)
Async XLA Ops:
  3.1 48.2 %all-to-all-start = ((bf16[32,24,512]{2,1,0:T(8,128)(2,1)}), bf16[32,24,512]{2,1,0:T(8,128)(2,1)S(1)}, u32[]{:S(2)}, u32[]{:S(2)}) async-start(bf16[32,24,512]{2,1,0:T(8,128)(2,1)} %get-tuple-element.58._), calls=%async_computation | async-start | bytes 1572864 | tf_op jit(solution)/shard_map/all_to_all | solution.py:394
  15.1 36.1 %collective-permute-start.2 = (bf16[64,256]{1,0:T(8,128)(2,1)}, bf16[64,256]{1,0:T(8,128)(2,1)S(1)}, u32[]{:S(2)}, u32[]{:S(2)}) collective-permute-start(bf16[64,256]{1,0:T(8,128)(2,1)} %get-tuple-element.64.p0), channel_id=1, source_target_pairs={{0,24},{8,0},{16,8},{24,16},{1,25},{9,1},{17,9},{25,17},{2,26},{10... | collective-permute-start | bytes 98312 | tf_op jit(solution)/shard_map/ppermute | solution.py:361
  18.6 32.7 %collective-permute-start.1 = (bf16[64,256]{1,0:T(8,128)(2,1)}, bf16[64,256]{1,0:T(8,128)(2,1)S(1)}, u32[]{:S(2)}, u32[]{:S(2)}) collective-permute-start(bf16[64,256]{1,0:T(8,128)(2,1)} %get-tuple-element.64.p0), channel_id=1, source_target_pairs={{0,16},{8,24},{16,0},{24,8},{1,17},{9,25},{17,1},{25,9},{2,18},{10... | collective-permute-start | bytes 98312 | tf_op jit(solution)/shard_map/ppermute | solution.py:361
  20.6 30.7 %collective-permute-start = (bf16[64,256]{1,0:T(8,128)(2,1)}, bf16[64,256]{1,0:T(8,128)(2,1)S(1)}, u32[]{:S(2)}, u32[]{:S(2)}) collective-permute-start(bf16[64,256]{1,0:T(8,128)(2,1)} %get-tuple-element.64.p0), channel_id=1, source_target_pairs={{0,8},{8,16},{16,24},{24,0},{1,9},{9,17},{17,25},{25,1},{2,10},{10... | collective-permute-start | bytes 98312 | tf_op jit(solution)/shard_map/ppermute | solution.py:361
  51.2 21.4 %copy-start.6 = (bf16[32,48,128]{2,1,0:T(8,128)(2,1)S(1)}, bf16[32,48,128]{2,1,0:T(8,128)(2,1)}, u32[]{:S(2)}) copy-start(bf16[32,48,128]{2,1,0:T(8,128)(2,1)} %get-tuple-element.84.f0) | copy-start | bytes 1179652
  51.2 22.6 %copy-start.23 = (s32[8]{0:T(128)S(1)}, s32[8]{0:T(128)}, u32[]{:S(2)}) copy-start(s32[8]{0:T(128)} %param.24) | copy-start | bytes 100
  51.2 23.2 %copy-start.19 = (bf16[64,256]{1,0:T(8,128)(2,1)}, bf16[64,256]{1,0:T(8,128)(2,1)S(1)}, u32[]{:S(2)}) copy-start(bf16[64,256]{1,0:T(8,128)(2,1)S(1)} %collective-permute-done.2.p3) | copy-start | bytes 98308
  51.3 23.1 %copy-start.20 = (bf16[64,256]{1,0:T(8,128)(2,1)}, bf16[64,256]{1,0:T(8,128)(2,1)S(1)}, u32[]{:S(2)}) copy-start(bf16[64,256]{1,0:T(8,128)(2,1)S(1)} %collective-permute-done.1.p2) | copy-start | bytes 98308
  51.3 23.1 %copy-start.21 = (bf16[64,256]{1,0:T(8,128)(2,1)}, bf16[64,256]{1,0:T(8,128)(2,1)S(1)}, u32[]{:S(2)}) copy-start(bf16[64,256]{1,0:T(8,128)(2,1)S(1)} %collective-permute-done.p1) | copy-start | bytes 98308
  51.3 29.0 %copy-start.1 = (bf16[32,24,512]{2,1,0:T(8,128)(2,1)}, bf16[32,24,512]{2,1,0:T(8,128)(2,1)S(1)}, u32[]{:S(2)}) copy-start(bf16[32,24,512]{2,1,0:T(8,128)(2,1)S(1)} %all-to-all-done) | copy-start | bytes 2359300
  51.3 29.1 %all-to-all-start.1 = ((bf16[32,56,128]{2,1,0:T(8,128)(2,1)}), bf16[32,56,128]{2,1,0:T(8,128)(2,1)S(1)}, u32[]{:S(2)}, u32[]{:S(2)}) async-start(bf16[32,56,128]{2,1,0:T(8,128)(2,1)} %get-tuple-element.62), calls=%async_computation.1 | async-start | bytes 917504 | tf_op jit(solution)/shard_map/all_to_all | solution.py:400
  57.2 8.6 %collective-permute-start.4 = (bf16[768,256]{1,0:T(8,128)(2,1)S(1)}, bf16[768,256]{1,0:T(8,128)(2,1)S(1)}, u32[]{:S(2)}, u32[]{:S(2)}) collective-permute-start(bf16[768,256]{1,0:T(8,128)(2,1)S(1)} %get-tuple-element.110), channel_id=1, source_target_pairs={{0,192},{64,0},{128,64},{192,128},{1,193},{65,1},{129,65},{193,129... | collective-permute-start | bytes 1179656 | tf_op jit(solution)/shard_map/ppermute | solution.py:361
  59.7 9.3 %collective-permute-start.3 = (bf16[768,256]{1,0:T(8,128)(2,1)S(1)}, bf16[768,256]{1,0:T(8,128)(2,1)}, u32[]{:S(2)}, u32[]{:S(2)}) collective-permute-start(bf16[768,256]{1,0:T(8,128)(2,1)S(1)} %get-tuple-element.111), channel_id=1, source_target_pairs={{0,64},{64,128},{128,192},{192,0},{1,65},{65,129},{129,193},{193,1... | collective-permute-start | bytes 1179656 | tf_op jit(solution)/shard_map/ppermute | solution.py:361
  59.7 20.6 %collective-permute-start.5 = (bf16[768,512]{1,0:T(8,128)(2,1)S(1)}, bf16[768,512]{1,0:T(8,128)(2,1)S(1)}, u32[]{:S(2)}, u32[]{:S(2)}) collective-permute-start(bf16[768,512]{1,0:T(8,128)(2,1)S(1)} %bitcast.10), channel_id=1, source_target_pairs={{0,32},{32,0},{1,33},{33,1},{2,34},{34,2},{3,35},{35,3},{4,36},{36... | collective-permute-start | bytes 2359304 | tf_op jit(solution)/shard_map/ppermute | solution.py:365
  65.8 14.6 %copy-start.8 = (bf16[768,256]{1,0:T(8,128)(2,1)}, bf16[768,256]{1,0:T(8,128)(2,1)S(1)}, u32[]{:S(2)}) copy-start(bf16[768,256]{1,0:T(8,128)(2,1)S(1)} %collective-permute-done.4.w2) | copy-start | bytes 1179652
  65.8 14.6 %collective-permute-start.7 = (bf16[768,256]{1,0:T(8,128)(2,1)S(1)}, bf16[768,256]{1,0:T(8,128)(2,1)}, u32[]{:S(2)}, u32[]{:S(2)}) collective-permute-start(bf16[768,256]{1,0:T(8,128)(2,1)S(1)} %collective-permute-done.4.w2), channel_id=1, source_target_pairs={{0,32},{32,0},{1,33},{33,1},{2,34},{34,2},{3,35},{35,3},{4,36},{36... | collective-permute-start | bytes 1179656 | tf_op jit(solution)/shard_map/ppermute | solution.py:365
  69.1 11.3 %collective-permute-start.6 = (bf16[768,256]{1,0:T(8,128)(2,1)}, bf16[768,256]{1,0:T(8,128)(2,1)}, u32[]{:S(2)}, u32[]{:S(2)}) collective-permute-start(bf16[768,256]{1,0:T(8,128)(2,1)} %collective-permute-done.3.w1), channel_id=1, source_target_pairs={{0,32},{32,0},{1,33},{33,1},{2,34},{34,2},{3,35},{35,3},{4,36},{36... | collective-permute-start | bytes 1179656 | tf_op jit(solution)/shard_map/ppermute | solution.py:365
  72.6 13.4 %collective-permute-start.8 = (bf16[32,48,128]{2,1,0:T(8,128)(2,1)S(1)}, bf16[32,48,128]{2,1,0:T(8,128)(2,1)S(1)}, u32[]{:S(2)}, u32[]{:S(2)}) collective-permute-start(bf16[32,48,128]{2,1,0:T(8,128)(2,1)S(1)} %copy-done.6), channel_id=1, source_target_pairs={{0,4},{4,0},{1,5},{5,1},{2,6},{6,2},{3,7},{7,3},{8,12},{12,8},{9,1... | collective-permute-start | bytes 1179656 | tf_op jit(solution)/shard_map/ppermute | solution.py:365
  86.0 63.7 %copy-start.7 = (bf16[32,48,128]{2,1,0:T(8,128)(2,1)}, bf16[32,48,128]{2,1,0:T(8,128)(2,1)S(1)}, u32[]{:S(2)}) copy-start(bf16[32,48,128]{2,1,0:T(8,128)(2,1)S(1)} %collective-permute-done.8.g0) | copy-start | bytes 1179652
  86.0 58.2 %all-to-all-start.2 = ((bf16[32,128,128]{2,1,0:T(8,128)(2,1)}), bf16[32,128,128]{2,1,0:T(8,128)(2,1)S(1)}, u32[]{:S(2)}, u32[]{:S(2)}) async-start(bf16[32,128,128]{2,1,0:T(8,128)(2,1)} %shard_map.174), calls=%async_computation.2 | async-start | bytes 2097152 | tf_op jit(solution)/shard_map/all_to_all | solution.py:412
  94.3 20.7 %collective-permute-start.11 = (bf16[32,48,128]{2,1,0:T(8,128)(2,1)S(1)}, bf16[32,48,128]{2,1,0:T(8,128)(2,1)S(1)}, u32[]{:S(2)}, u32[]{:S(2)}) collective-permute-start(bf16[32,48,128]{2,1,0:T(8,128)(2,1)S(1)} %copy-done.6), channel_id=1, source_target_pairs={{0,3},{1,0},{2,1},{3,2},{4,7},{5,4},{6,5},{7,6},{8,11},{9,8},{10,9... | collective-permute-start | bytes 1179656 | tf_op jit(solution)/shard_map/ppermute | solution.py:361
  96.8 18.4 %collective-permute-start.10 = (bf16[32,48,128]{2,1,0:T(8,128)(2,1)S(1)}, bf16[32,48,128]{2,1,0:T(8,128)(2,1)S(1)}, u32[]{:S(2)}, u32[]{:S(2)}) collective-permute-start(bf16[32,48,128]{2,1,0:T(8,128)(2,1)S(1)} %copy-done.6), channel_id=1, source_target_pairs={{0,2},{1,3},{2,0},{3,1},{4,6},{5,7},{6,4},{7,5},{8,10},{9,11},{10,... | collective-permute-start | bytes 1179656 | tf_op jit(solution)/shard_map/ppermute | solution.py:361
  97.4 30.9 %collective-permute-start.9 = (bf16[32,48,128]{2,1,0:T(8,128)(2,1)S(1)}, bf16[32,48,128]{2,1,0:T(8,128)(2,1)S(1)}, u32[]{:S(2)}, u32[]{:S(2)}) collective-permute-start(bf16[32,48,128]{2,1,0:T(8,128)(2,1)S(1)} %copy-done.6), channel_id=1, source_target_pairs={{0,1},{1,2},{2,3},{3,0},{4,5},{5,6},{6,7},{7,4},{8,9},{9,10},{10,1... | collective-permute-start | bytes 1179656 | tf_op jit(solution)/shard_map/ppermute | solution.py:361
  98.0 34.6 %collective-permute-start.14 = (bf16[32,48,128]{2,1,0:T(8,128)(2,1)S(1)}, bf16[32,48,128]{2,1,0:T(8,128)(2,1)S(1)}, u32[]{:S(2)}, u32[]{:S(2)}) collective-permute-start(bf16[32,48,128]{2,1,0:T(8,128)(2,1)S(1)} %collective-permute-done.8.g0), channel_id=1, source_target_pairs={{0,3},{1,0},{2,1},{3,2},{4,7},{5,4},{6,5},{7,6},{8,11},{9,8},{10,9... | collective-permute-start | bytes 1179656 | tf_op jit(solution)/shard_map/ppermute | solution.py:361
  100.1 35.2 %collective-permute-start.13 = (bf16[32,48,128]{2,1,0:T(8,128)(2,1)S(1)}, bf16[32,48,128]{2,1,0:T(8,128)(2,1)S(1)}, u32[]{:S(2)}, u32[]{:S(2)}) collective-permute-start(bf16[32,48,128]{2,1,0:T(8,128)(2,1)S(1)} %collective-permute-done.8.g0), channel_id=1, source_target_pairs={{0,2},{1,3},{2,0},{3,1},{4,6},{5,7},{6,4},{7,5},{8,10},{9,11},{10,... | collective-permute-start | bytes 1179656 | tf_op jit(solution)/shard_map/ppermute | solution.py:361
  115.1 38.2 %copy-start.9 = (bf16[32,48,128]{2,1,0:T(8,128)(2,1)}, bf16[32,48,128]{2,1,0:T(8,128)(2,1)S(1)}, u32[]{:S(2)}) copy-start(bf16[32,48,128]{2,1,0:T(8,128)(2,1)S(1)} %collective-permute-done.11.f3) | copy-start | bytes 1179652
  115.1 29.1 %collective-permute-start.12 = (bf16[32,48,128]{2,1,0:T(8,128)(2,1)S(1)}, bf16[32,48,128]{2,1,0:T(8,128)(2,1)}, u32[]{:S(2)}, u32[]{:S(2)}) collective-permute-start(bf16[32,48,128]{2,1,0:T(8,128)(2,1)S(1)} %collective-permute-done.8.g0), channel_id=1, source_target_pairs={{0,1},{1,2},{2,3},{3,0},{4,5},{5,6},{6,7},{7,4},{8,9},{9,10},{10,1... | collective-permute-start | bytes 1179656 | tf_op jit(solution)/shard_map/ppermute | solution.py:361
  115.3 38.0 %copy-start.10 = (bf16[32,48,128]{2,1,0:T(8,128)(2,1)}, bf16[32,48,128]{2,1,0:T(8,128)(2,1)S(1)}, u32[]{:S(2)}) copy-start(bf16[32,48,128]{2,1,0:T(8,128)(2,1)S(1)} %collective-permute-done.10.f2) | copy-start | bytes 1179652
  128.3 25.0 %copy-start.11 = (bf16[32,48,128]{2,1,0:T(8,128)(2,1)}, bf16[32,48,128]{2,1,0:T(8,128)(2,1)S(1)}, u32[]{:S(2)}) copy-start(bf16[32,48,128]{2,1,0:T(8,128)(2,1)S(1)} %collective-permute-done.9.f1) | copy-start | bytes 1179652
  132.6 2.7 %copy-start.12 = (bf16[32,48,128]{2,1,0:T(8,128)(2,1)}, bf16[32,48,128]{2,1,0:T(8,128)(2,1)S(1)}, u32[]{:S(2)}) copy-start(bf16[32,48,128]{2,1,0:T(8,128)(2,1)S(1)} %collective-permute-done.14.g3) | copy-start | bytes 1179652
  144.2 1.0 copy-start
  149.7 12.9 %all-to-all-start.3 = ((bf16[8,160,256]{2,1,0:T(8,128)(2,1)}), bf16[8,160,256]{2,1,0:T(8,128)(2,1)S(1)}, u32[]{:S(2)}, u32[]{:S(2)}) async-start(bf16[8,160,256]{2,1,0:T(8,128)(2,1)} %get-tuple-element.94), calls=%async_computation.3 | async-start | bytes 1310720 | tf_op jit(solution)/shard_map/all_to_all | solution.py:420
  153.3 6.5 %copy-start.22 = (f32[64,128]{1,0:T(8,128)S(1)}, f32[64,128]{1,0:T(8,128)}, u32[]{:S(2)}) copy-start(f32[64,128]{1,0:T(8,128)} %get-tuple-element.96) | copy-start | bytes 98308
  153.3 7.7 %copy-start.18 = (f32[64,128]{1,0:T(8,128)S(1)}, f32[64,128]{1,0:T(8,128)}, u32[]{:S(2)}) copy-start(f32[64,128]{1,0:T(8,128)} %get-tuple-element.95) | copy-start | bytes 98308
  159.0 2.1 %collective-permute-start.15 = (f32[8,24,128]{2,1,0:T(8,128)}, f32[8,24,128]{2,1,0:T(8,128)S(1)}, u32[]{:S(2)}, u32[]{:S(2)}) collective-permute-start(f32[8,24,128]{2,1,0:T(8,128)} %get-tuple-element.93), channel_id=1, source_target_pairs={{0,32},{32,0},{1,33},{33,1},{2,34},{34,2},{3,35},{35,3},{4,36},{36... | collective-permute-start | bytes 294920 | tf_op jit(solution)/shard_map/ppermute | solution.py:365
  159.8 1.2 collective-permute-start.16
  162.6 5.3 %copy-start.2 = (bf16[8,160,256]{2,1,0:T(8,128)(2,1)}, bf16[8,160,256]{2,1,0:T(8,128)(2,1)S(1)}, u32[]{:S(2)}) copy-start(bf16[8,160,256]{2,1,0:T(8,128)(2,1)S(1)} %all-to-all-done.3.parts) | copy-start | bytes 1966084
  162.6 18.9 %all-to-all-start.4 = ((f32[8,24,128]{2,1,0:T(8,128)}), f32[8,24,128]{2,1,0:T(8,128)S(1)}, u32[]{:S(2)}, u32[]{:S(2)}) async-start(f32[8,24,128]{2,1,0:T(8,128)} %add.20), calls=%async_computation.4 | async-start | bytes 196608 | tf_op jit(solution)/shard_map/all_to_all | solution.py:426
  169.7 7.1 %collective-permute-start.19 = (bf16[160,256]{1,0:T(8,128)(2,1)}, bf16[160,256]{1,0:T(8,128)(2,1)S(1)}, u32[]{:S(2)}, u32[]{:S(2)}) collective-permute-start(bf16[160,256]{1,0:T(8,128)(2,1)} %shard_map.178.s0), channel_id=1, source_target_pairs={{0,24},{8,0},{16,8},{24,16},{1,25},{9,1},{17,9},{25,17},{2,26},{10... | collective-permute-start | bytes 245768 | tf_op jit(solution)/shard_map/ppermute | solution.py:361
  172.8 7.5 %collective-permute-start.18 = (bf16[160,256]{1,0:T(8,128)(2,1)}, bf16[160,256]{1,0:T(8,128)(2,1)S(1)}, u32[]{:S(2)}, u32[]{:S(2)}) collective-permute-start(bf16[160,256]{1,0:T(8,128)(2,1)} %shard_map.178.s0), channel_id=1, source_target_pairs={{0,16},{8,24},{16,0},{24,8},{1,17},{9,25},{17,1},{25,9},{2,18},{10... | collective-permute-start | bytes 245768 | tf_op jit(solution)/shard_map/ppermute | solution.py:361
  175.0 6.6 %collective-permute-start.17 = (bf16[160,256]{1,0:T(8,128)(2,1)}, bf16[160,256]{1,0:T(8,128)(2,1)S(1)}, u32[]{:S(2)}, u32[]{:S(2)}) collective-permute-start(bf16[160,256]{1,0:T(8,128)(2,1)} %shard_map.178.s0), channel_id=1, source_target_pairs={{0,8},{8,16},{16,24},{24,0},{1,9},{9,17},{17,25},{25,1},{2,10},{10... | collective-permute-start | bytes 245768 | tf_op jit(solution)/shard_map/ppermute | solution.py:361
  176.8 18.5 %copy-start.15 = (bf16[160,256]{1,0:T(8,128)(2,1)}, bf16[160,256]{1,0:T(8,128)(2,1)S(1)}, u32[]{:S(2)}) copy-start(bf16[160,256]{1,0:T(8,128)(2,1)S(1)} %collective-permute-done.19.s3) | copy-start | bytes 245764
  180.3 15.0 %copy-start.16 = (bf16[160,256]{1,0:T(8,128)(2,1)}, bf16[160,256]{1,0:T(8,128)(2,1)S(1)}, u32[]{:S(2)}) copy-start(bf16[160,256]{1,0:T(8,128)(2,1)S(1)} %collective-permute-done.18.s2) | copy-start | bytes 245764
  181.6 13.8 %copy-start.17 = (bf16[160,256]{1,0:T(8,128)(2,1)}, bf16[160,256]{1,0:T(8,128)(2,1)S(1)}, u32[]{:S(2)}) copy-start(bf16[160,256]{1,0:T(8,128)(2,1)S(1)} %collective-permute-done.17.s1) | copy-start | bytes 245764
  181.6 3.9 %collective-permute-start.20 = (f32[256,128]{1,0:T(8,128)S(1)}, f32[256,128]{1,0:T(8,128)S(1)}, u32[]{:S(2)}, u32[]{:S(2)}) collective-permute-start(f32[256,128]{1,0:T(8,128)S(1)} %pad_maximum_fusion), channel_id=1, source_target_pairs={{0,64},{64,0},{128,192},{192,128},{1,65},{65,1},{129,193},{193,129... | collective-permute-start | bytes 393224 | tf_op jit(solution)/shard_map/ppermute | solution.py:369
  185.5 5.1 %collective-permute-start.21 = (f32[256,128]{1,0:T(8,128)S(1)}, f32[256,128]{1,0:T(8,128)S(1)}, u32[]{:S(2)}, u32[]{:S(2)}) collective-permute-start(f32[256,128]{1,0:T(8,128)S(1)} %fusion), channel_id=1, source_target_pairs={{0,192},{192,0},{64,128},{128,64},{1,193},{193,1},{65,129},{129,65... | collective-permute-start | bytes 393224 | tf_op jit(solution)/shard_map/ppermute | solution.py:370
  190.7 6.6 %copy-start.5 = (f32[256,128]{1,0:T(8,128)}, f32[256,128]{1,0:T(8,128)S(1)}, u32[]{:S(2)}) copy-start(f32[256,128]{1,0:T(8,128)S(1)} %add.23.keep) | copy-start | bytes 393220
  190.7 6.6 %collective-permute-start.22 = (f32[256,128]{1,0:T(8,128)S(1)}, f32[256,128]{1,0:T(8,128)S(1)}, u32[]{:S(2)}, u32[]{:S(2)}) collective-permute-start(f32[256,128]{1,0:T(8,128)S(1)} %add.23.keep), channel_id=1, source_target_pairs={{0,32},{32,0},{1,33},{33,1},{2,34},{34,2},{3,35},{35,3},{4,36},{36... | collective-permute-start | bytes 393224 | tf_op jit(solution)/shard_map/ppermute | solution.py:365
  (4 other events, 3.1 us)

commit v6 on v5

--- a/solution.py
+++ b/solution.py
@@ -395,23 +395,25 @@
     send, feats = hop(
         place, feature_table, node_ids, hop_cols, hidden_bias, hop_tiles, packed
     )
-    pairs = [pair] + [shift(pair, "zq", s) for s in (1, 2, 3)]
-    weights, pairs, send, feats = lax.optimization_barrier((weights, pairs, send, feats))
+    weights, pair, send, feats = lax.optimization_barrier((weights, pair, send, feats))
     got = lax.all_to_all(send, FEAT, 0, 0, tiled=True)
     weights = weights.reshape(-1, 512)
     mine = [weights, shift(weights[:, :256], "x", 1), shift(weights[:, 256:], "x", 3)]
     other = [swap(w, "core") for w in mine]
 
     twin = swap(feats, "zr")
-
+    feats = [feats] + [shift(feats, "y", s) for s in (1, 2, 3)]
+    got, feats, twin = lax.optimization_barrier((got, feats, twin))
+    pairs = [pair] + [shift(pair, "zq", s) for s in (1, 2, 3)]
+
+    hidden = layer(place, got, mine, other)
+    hidden, pairs, twin = lax.optimization_barrier((hidden, pairs, twin))
+    hidden = lax.all_to_all(hidden, FEAT, 0, 0, tiled=True)
+    feats = feats + [twin] + [shift(twin, "y", s) for s in (1, 2, 3)]
     live = batch_sizes[lax.axis_index("x") * 2 + lax.axis_index("core")]
-    ready = spread(place, target_cols, live, logit_cotangent, pairs, target_tiles, blocks)
-    hidden = layer(place, got, mine, other)
-    hidden, ready, feats, twin = lax.optimization_barrier((hidden, ready, feats, twin))
-    dhidden, cot, self_t, neigh_t = ready
-    hidden = lax.all_to_all(hidden, FEAT, 0, 0, tiled=True)
-    feats = [feats] + [shift(feats, "y", s) for s in (1, 2, 3)]
-    feats = feats + [twin] + [shift(twin, "y", s) for s in (1, 2, 3)]
+    dhidden, cot, self_t, neigh_t = spread(
+        place, target_cols, live, logit_cotangent, pairs, target_tiles, blocks
+    )
     hidden, feats = lax.optimization_barrier((hidden, feats))
 
     scores, keep_head, send_head = score(

time: 201 us -> 190 us (0.945)
  waiting for transfers between devices: 60.3 us -> 46.8 us
    ppermute x14, waiting for transfers between devices: 50.3 us -> 39.8 us  [shift(): return lax.ppermute(value, axis, [(i, (i + by) % 4) for i in range(4)])]
    all_to_all x1, starting transfers between devices: 8.3 us -> 4.66 us  [shards(): hidden = lax.all_to_all(hidden, FEAT, 0, 0, tiled=True)]
    ppermute x1, starting transfers between devices: 0.15 us -> 3.2 us  [sum_x(): return value + lax.ppermute(value, 'x', [(0, 3), (3, 0), (1, 2), (2, 1)])]
    ppermute x1, waiting for transfers between devices: 4.97 us -> 2.36 us  [sum_x(): return value + lax.ppermute(value, 'x', [(0, 3), (3, 0), (1, 2), (2, 1)])]
    ppermute x14, starting transfers between devices: 24.2 us -> 26.4 us  [shift(): return lax.ppermute(value, axis, [(i, (i + by) % 4) for i in range(4)])]
    unnamed x49 -> x55, local copies, waits for them, and re-layouts: 5.48 us -> 5.49 us
  transfers between devices with their start and end apart: 28 -> 28, of which waited for: 13 -> 13; matrix products, arithmetic and copies ran while one was open for 2% -> 2% of each run, Pallas kernels for 23% -> 25%
where the time goes in v6:
time: 190 us; the launch traced here: 188 us
  starting transfers between devices  77.6 us (41%)
  Pallas kernels  54.5 us (29%)
  waiting for transfers between devices  46.8 us (25%)
  local copies, waits for them, and re-layouts  6.8 us (4%)
    ppermute x14, waiting for transfers between devices, shift(): return lax.ppermute(value, axis, [(i, (i + by) % 4) for i in range(4)])  39.8 us
    pallas_call x1, Pallas kernels, hop(): pl.pallas_call(hop_kernel, in_specs=[SMEM, SMEM, SMEM, VMEM, VMEM, HBM, H...  27.1 us
    ppermute x14, starting transfers between devices, shift(): return lax.ppermute(value, axis, [(i, (i + by) % 4) for i in range(4)])  26.4 us
    ppermute x7, starting transfers between devices, swap(): return lax.ppermute(value, axis, [(0, 1), (1, 0)])  15.7 us
    all_to_all x1, starting transfers between devices, shards(): weights = lax.all_to_all(packed, FEAT, 0, 0, tiled=True)  12 us
    all_to_all x1, starting transfers between devices, shards(): got = lax.all_to_all(send, FEAT, 0, 0, tiled=True)  6.18 us
    pallas_call x1, Pallas kernels, spread(): pl.pallas_call(spread_kernel, in_specs=[SMEM, SMEM, SMEM] + [VMEM] * 6, o...  5.93 us
    pallas_call x1, Pallas kernels, grad(): pl.pallas_call(grad_kernel, in_specs=[SMEM] + [VMEM] * 10, out_specs=[VME...  5.63 us
  transfers between devices with their start and end apart: 28, of which 13 were waited for; matrix products, arithmetic and copies ran while one was open for 2% of the time, Pallas kernels for 25%

profile of v6, /device:TPU:1, one launch (start us, length us, event | category | flops | bytes accessed | tf_op | source)
XLA Modules:
  0.0 188.3 jit_solution(18357169365699059345)
XLA Ops:
  1.3 1.8 shard_map.172
  3.1 12.0 %all-to-all-start = ((bf16[32,24,512]{2,1,0:T(8,128)(2,1)}), bf16[32,24,512]{2,1,0:T(8,128)(2,1)S(1)}, u32[]{:S(2)}, u32[]{:S(2)}) async-start(bf16[32,24,512]{2,1,0:T(8,128)(2,1)} %get-tuple-element.60._), calls=%async_computation | async-start | bytes 1572864 | tf_op jit(solution)/shard_map/all_to_all | solution.py:394
  15.2 1.4 copy.19.cols
  16.5 27.1 %shard_map.173 = (bf16[32,56,128]{2,1,0:T(8,128)(2,1)}, bf16[32,48,128]{2,1,0:T(8,128)(2,1)}) custom-call(s32[5]{0:T(128)} %stack.23.place, s32[16384]{0:T(1024)} %ids.1, s32[32,8]{1,0:T(8,128)} %copy.19.cols, bf16[24,32768]{1,0:T(8,128)(2,1)} %table.1, f32[1,32]{1,0:T(1,128)} %bitcast.14, bf16[32,8,128,128]{3,2,1,0:T(8,128)(2,1)} %tiles_hbm.1, ...), custom_call_target="tpu_custom_call" | custom-call | flops 1000000000 | bytes 60000000 | tf_op jit(solution)/shard_map/pallas_call | solution.py:84
  43.7 1.3 collective-permute-start.3
  45.0 2.4 %collective-permute-start.2 = (bf16[32,48,128]{2,1,0:T(8,128)(2,1)}, bf16[32,48,128]{2,1,0:T(8,128)(2,1)S(1)}, u32[]{:S(2)}, u32[]{:S(2)}) collective-permute-start(bf16[32,48,128]{2,1,0:T(8,128)(2,1)} %get-tuple-element.88.f0), channel_id=1, source_target_pairs={{0,3},{1,0},{2,1},{3,2},{4,7},{5,4},{6,5},{7,6},{8,11},{9,8},{10,9... | collective-permute-start | bytes 1179656 | tf_op jit(solution)/shard_map/ppermute | solution.py:361
  47.4 6.2 %all-to-all-start.1 = ((bf16[32,56,128]{2,1,0:T(8,128)(2,1)}), bf16[32,56,128]{2,1,0:T(8,128)(2,1)S(1)}, u32[]{:S(2)}, u32[]{:S(2)}) async-start(bf16[32,56,128]{2,1,0:T(8,128)(2,1)} %get-tuple-element.64), calls=%async_computation.1 | async-start | bytes 917504 | tf_op jit(solution)/shard_map/all_to_all | solution.py:399
  53.7 2.6 %collective-permute-start.5 = (bf16[768,256]{1,0:T(8,128)(2,1)S(1)}, bf16[768,256]{1,0:T(8,128)(2,1)S(1)}, u32[]{:S(2)}, u32[]{:S(2)}) collective-permute-start(bf16[768,256]{1,0:T(8,128)(2,1)S(1)} %get-tuple-element.114), channel_id=1, source_target_pairs={{0,192},{64,0},{128,64},{192,128},{1,193},{65,1},{129,65},{193,129... | collective-permute-start | bytes 1179656 | tf_op jit(solution)/shard_map/ppermute | solution.py:361
  56.2 2.4 %collective-permute-start.6 = (bf16[768,512]{1,0:T(8,128)(2,1)S(1)}, bf16[768,512]{1,0:T(8,128)(2,1)S(1)}, u32[]{:S(2)}, u32[]{:S(2)}) collective-permute-start(bf16[768,512]{1,0:T(8,128)(2,1)S(1)} %bitcast.10), channel_id=1, source_target_pairs={{0,32},{32,0},{1,33},{33,1},{2,34},{34,2},{3,35},{35,3},{4,36},{36... | collective-permute-start | bytes 2359304 | tf_op jit(solution)/shard_map/ppermute | solution.py:365
  58.6 3.1 %collective-permute-start.1 = (bf16[32,48,128]{2,1,0:T(8,128)(2,1)S(1)}, bf16[32,48,128]{2,1,0:T(8,128)(2,1)S(1)}, u32[]{:S(2)}, u32[]{:S(2)}) collective-permute-start(bf16[32,48,128]{2,1,0:T(8,128)(2,1)S(1)} %copy-done.6), channel_id=1, source_target_pairs={{0,2},{1,3},{2,0},{3,1},{4,6},{5,7},{6,4},{7,5},{8,10},{9,11},{10,... | collective-permute-start | bytes 1179656 | tf_op jit(solution)/shard_map/ppermute | solution.py:361
  62.6 3.0 %collective-permute-start.8 = (bf16[768,256]{1,0:T(8,128)(2,1)S(1)}, bf16[768,256]{1,0:T(8,128)(2,1)S(1)}, u32[]{:S(2)}, u32[]{:S(2)}) collective-permute-start(bf16[768,256]{1,0:T(8,128)(2,1)S(1)} %collective-permute-done.5.w2), channel_id=1, source_target_pairs={{0,32},{32,0},{1,33},{33,1},{2,34},{34,2},{3,35},{35,3},{4,36},{36... | collective-permute-start | bytes 1179656 | tf_op jit(solution)/shard_map/ppermute | solution.py:365
  65.8 3.3 %collective-permute-start.7 = (bf16[768,256]{1,0:T(8,128)(2,1)}, bf16[768,256]{1,0:T(8,128)(2,1)}, u32[]{:S(2)}, u32[]{:S(2)}) collective-permute-start(bf16[768,256]{1,0:T(8,128)(2,1)} %collective-permute-done.4.w1), channel_id=1, source_target_pairs={{0,32},{32,0},{1,33},{33,1},{2,34},{34,2},{3,35},{35,3},{4,36},{36... | collective-permute-start | bytes 1179656 | tf_op jit(solution)/shard_map/ppermute | solution.py:365
  69.1 5.0 %collective-permute-done.1.f2 = bf16[32,48,128]{2,1,0:T(8,128)(2,1)S(1)} collective-permute-done((bf16[32,48,128]{2,1,0:T(8,128)(2,1)S(1)}, bf16[32,48,128]{2,1,0:T(8,128)(2,1)S(1)}, u32[]{:S(2)}, u32[]{:S(2)}) %collective-permute-start.1) | collective-permute-done | bytes 393248 | tf_op jit(solution)/shard_map/ppermute | solution.py:361
  74.1 2.8 %collective-permute-start.11 = (bf16[64,256]{1,0:T(8,128)(2,1)S(1)}, bf16[64,256]{1,0:T(8,128)(2,1)S(1)}, u32[]{:S(2)}, u32[]{:S(2)}) collective-permute-start(bf16[64,256]{1,0:T(8,128)(2,1)S(1)} %copy-done.21), channel_id=1, source_target_pairs={{0,24},{8,0},{16,8},{24,16},{1,25},{9,1},{17,9},{25,17},{2,26},{10... | collective-permute-start | bytes 98312 | tf_op jit(solution)/shard_map/ppermute | solution.py:361
  76.9 6.0 %collective-permute-done.f1 = bf16[32,48,128]{2,1,0:T(8,128)(2,1)S(1)} collective-permute-done((bf16[32,48,128]{2,1,0:T(8,128)(2,1)S(1)}, bf16[32,48,128]{2,1,0:T(8,128)(2,1)S(1)}, u32[]{:S(2)}, u32[]{:S(2)}) %collective-permute-start) | collective-permute-done | bytes 393248 | tf_op jit(solution)/shard_map/ppermute | solution.py:361
  82.9 4.0 %collective-permute-start.10 = (bf16[64,256]{1,0:T(8,128)(2,1)S(1)}, bf16[64,256]{1,0:T(8,128)(2,1)S(1)}, u32[]{:S(2)}, u32[]{:S(2)}) collective-permute-start(bf16[64,256]{1,0:T(8,128)(2,1)S(1)} %copy-done.21), channel_id=1, source_target_pairs={{0,16},{8,24},{16,0},{24,8},{1,17},{9,25},{17,1},{25,9},{2,18},{10... | collective-permute-start | bytes 98312 | tf_op jit(solution)/shard_map/ppermute | solution.py:361
  86.9 0.7 copy-done.15
  87.7 0.9 collective-permute-start.9
  88.6 0.7 copy-done.3
  89.3 0.9 copy-done.4
  90.2 3.9 %shard_map.174 = bf16[32,128,128]{2,1,0:T(8,128)(2,1)} custom-call(s32[5]{0:T(128)} %stack.23.place, bf16[32,56,128]{2,1,0:T(8,128)(2,1)} %copy-done.3, bf16[768,512]{1,0:T(8,128)(2,1)} %bitcast.11, bf16[768,256]{1,0:T(8,128)(2,1)} %collective-permute-done.4.w1, bf16[768,256]{1,0:T(8,128)(2,1)} %copy-done.11, bf16[768,512]{1,0:T(8,128)(2,1)} %copy-done.4, ...), custom_call_target="tpu_custom_call" | custom-call | tf_op jit(solution)/shard_map/pallas_call | solution.py:203
  94.2 4.7 %all-to-all-start.2 = ((bf16[32,128,128]{2,1,0:T(8,128)(2,1)}), bf16[32,128,128]{2,1,0:T(8,128)(2,1)S(1)}, u32[]{:S(2)}, u32[]{:S(2)}) async-start(bf16[32,128,128]{2,1,0:T(8,128)(2,1)} %shard_map.174), calls=%async_computation.2 | async-start | bytes 2097152 | tf_op jit(solution)/shard_map/all_to_all | solution.py:411
  98.9 2.5 %collective-permute-start.14 = (bf16[32,48,128]{2,1,0:T(8,128)(2,1)S(1)}, bf16[32,48,128]{2,1,0:T(8,128)(2,1)S(1)}, u32[]{:S(2)}, u32[]{:S(2)}) collective-permute-start(bf16[32,48,128]{2,1,0:T(8,128)(2,1)S(1)} %collective-permute-done.3.g0), channel_id=1, source_target_pairs={{0,3},{1,0},{2,1},{3,2},{4,7},{5,4},{6,5},{7,6},{8,11},{9,8},{10,9... | collective-permute-start | bytes 1179656 | tf_op jit(solution)/shard_map/ppermute | solution.py:361
  103.2 5.9 %shard_map.175 = (f32[32,128,128]{2,1,0:T(8,128)}, bf16[256,1024]{1,0:T(8,128)(2,1)}, bf16[256,128]{1,0:T(8,128)(2,1)}, bf16[256,128]{1,0:T(8,128)(2,1)}) custom-call(s32[5]{0:T(128)} %stack.23.place, s32[8,8]{1,0:T(8,128)} %cols.4, s32[1]{0:T(128)} %dynamic_slice.3.live, bf16[153,1024]{1,0:T(8,128)(2,1)} %logit_cot.1, ...), custom_call_target="tpu_custom_call" | custom-call | flops 1000000000 | bytes 8000000 | tf_op jit(solution)/shard_map/pallas_call | solution.py:153
  109.1 10.0 %collective-permute-done.14.g3 = bf16[32,48,128]{2,1,0:T(8,128)(2,1)S(1)} collective-permute-done((bf16[32,48,128]{2,1,0:T(8,128)(2,1)S(1)}, bf16[32,48,128]{2,1,0:T(8,128)(2,1)S(1)}, u32[]{:S(2)}, u32[]{:S(2)}) %collective-permute-start.14) | collective-permute-done | bytes 393248 | tf_op jit(solution)/shard_map/ppermute | solution.py:361
  119.1 1.8 collective-permute-done.13.g2
  120.9 11.4 %collective-permute-done.12.g1 = bf16[32,48,128]{2,1,0:T(8,128)(2,1)S(1)} collective-permute-done((bf16[32,48,128]{2,1,0:T(8,128)(2,1)S(1)}, bf16[32,48,128]{2,1,0:T(8,128)(2,1)S(1)}, u32[]{:S(2)}, u32[]{:S(2)}) %collective-permute-start.12) | collective-permute-done | bytes 393248 | tf_op jit(solution)/shard_map/ppermute | solution.py:361
  132.3 1.0 copy-done
  133.3 4.5 %shard_map.176 = (bf16[8,160,256]{2,1,0:T(8,128)(2,1)}, f32[64,128]{1,0:T(8,128)}, f32[64,128]{1,0:T(8,128)}) custom-call(s32[5]{0:T(128)} %stack.23.place, s32[8,8]{1,0:T(8,128)} %cols.4, bf16[32,128,128]{2,1,0:T(8,128)(2,1)} %copy-done, f32[32,128,128]{2,1,0:T(8,128)} %get-tuple-element.81.dhidden, bf16[8,8,128,128]{3,2,1,0:T(8,128)(2,1)} %tiles.3, ...), custom_call_target="tpu_custom_call" | custom-call | tf_op jit(solution)/shard_map/pallas_call | solution.py:249
  137.8 3.6 %all-to-all-start.3 = ((bf16[8,160,256]{2,1,0:T(8,128)(2,1)}), bf16[8,160,256]{2,1,0:T(8,128)(2,1)S(1)}, u32[]{:S(2)}, u32[]{:S(2)}) async-start(bf16[8,160,256]{2,1,0:T(8,128)(2,1)} %get-tuple-element.98), calls=%async_computation.3 | async-start | bytes 1310720 | tf_op jit(solution)/shard_map/all_to_all | solution.py:422
  141.4 5.6 %shard_map.177 = (f32[8,24,128]{2,1,0:T(8,128)}, f32[8,24,128]{2,1,0:T(8,128)}) custom-call(s32[5]{0:T(128)} %stack.23.place, bf16[32,128,128]{2,1,0:T(8,128)(2,1)} %copy-done, f32[32,128,128]{2,1,0:T(8,128)} %get-tuple-element.81.dhidden, bf16[32,48,128]{2,1,0:T(8,128)(2,1)} %get-tuple-element.88.f0, bf16[32,48,128]{2,1,0:T(8,128)(2,1)} %copy-done.10, ...), custom_call_target="tpu_custom_call" | custom-call | flops 1000000000 | bytes 7000000 | tf_op jit(solution)/shard_map/pallas_call | solution.py:316
  147.6 1.1 collective-permute-done.16
  148.8 1.5 add.20
  150.3 1.2 all-to-all-done.3.parts
  151.5 4.2 %all-to-all-start.4 = ((f32[8,24,128]{2,1,0:T(8,128)}), f32[8,24,128]{2,1,0:T(8,128)S(1)}, u32[]{:S(2)}, u32[]{:S(2)}) async-start(f32[8,24,128]{2,1,0:T(8,128)} %add.20), calls=%async_computation.4 | async-start | bytes 196608 | tf_op jit(solution)/shard_map/all_to_all | solution.py:428
  155.7 1.8 shard_map.178.s0
  157.5 3.2 %collective-permute-start.19 = (bf16[160,256]{1,0:T(8,128)(2,1)}, bf16[160,256]{1,0:T(8,128)(2,1)S(1)}, u32[]{:S(2)}, u32[]{:S(2)}) collective-permute-start(bf16[160,256]{1,0:T(8,128)(2,1)} %shard_map.178.s0), channel_id=1, source_target_pairs={{0,24},{8,0},{16,8},{24,16},{1,25},{9,1},{17,9},{25,17},{2,26},{10... | collective-permute-start | bytes 245768 | tf_op jit(solution)/shard_map/ppermute | solution.py:361
  160.7 2.0 %collective-permute-start.18 = (bf16[160,256]{1,0:T(8,128)(2,1)}, bf16[160,256]{1,0:T(8,128)(2,1)S(1)}, u32[]{:S(2)}, u32[]{:S(2)}) collective-permute-start(bf16[160,256]{1,0:T(8,128)(2,1)} %shard_map.178.s0), channel_id=1, source_target_pairs={{0,16},{8,24},{16,0},{24,8},{1,17},{9,25},{17,1},{25,9},{2,18},{10... | collective-permute-start | bytes 245768 | tf_op jit(solution)/shard_map/ppermute | solution.py:361
  162.6 1.6 collective-permute-start.17
  164.2 4.0 %collective-permute-done.18.s2 = bf16[160,256]{1,0:T(8,128)(2,1)S(1)} collective-permute-done((bf16[160,256]{1,0:T(8,128)(2,1)}, bf16[160,256]{1,0:T(8,128)(2,1)S(1)}, u32[]{:S(2)}, u32[]{:S(2)}) %collective-permute-start.18) | collective-permute-done | bytes 81952 | tf_op jit(solution)/shard_map/ppermute | solution.py:361
  168.2 0.8 collective-permute-done.17.s1
  169.1 1.6 collective-permute-start.20
  170.7 2.4 %collective-permute-done.20 = f32[256,128]{1,0:T(8,128)S(1)} collective-permute-done((f32[256,128]{1,0:T(8,128)S(1)}, f32[256,128]{1,0:T(8,128)S(1)}, u32[]{:S(2)}, u32[]{:S(2)}) %collective-permute-start.20) | collective-permute-done | bytes 131104 | tf_op jit(solution)/shard_map/ppermute | solution.py:369
  173.1 3.2 %collective-permute-start.21 = (f32[256,128]{1,0:T(8,128)S(1)}, f32[256,128]{1,0:T(8,128)S(1)}, u32[]{:S(2)}, u32[]{:S(2)}) collective-permute-start(f32[256,128]{1,0:T(8,128)S(1)} %fusion), channel_id=1, source_target_pairs={{0,192},{192,0},{64,128},{128,64},{1,193},{193,1},{65,129},{129,65... | collective-permute-start | bytes 393224 | tf_op jit(solution)/shard_map/ppermute | solution.py:370
  176.3 2.4 %collective-permute-done.21 = f32[256,128]{1,0:T(8,128)S(1)} collective-permute-done((f32[256,128]{1,0:T(8,128)S(1)}, f32[256,128]{1,0:T(8,128)S(1)}, u32[]{:S(2)}, u32[]{:S(2)}) %collective-permute-start.21) | collective-permute-done | bytes 131104 | tf_op jit(solution)/shard_map/ppermute | solution.py:370
  178.7 5.2 %collective-permute-start.22 = (f32[256,128]{1,0:T(8,128)S(1)}, f32[256,128]{1,0:T(8,128)S(1)}, u32[]{:S(2)}, u32[]{:S(2)}) collective-permute-start(f32[256,128]{1,0:T(8,128)S(1)} %add.23.keep), channel_id=1, source_target_pairs={{0,32},{32,0},{1,33},{33,1},{2,34},{34,2},{3,35},{35,3},{4,36},{36... | collective-permute-start | bytes 393224 | tf_op jit(solution)/shard_map/ppermute | solution.py:365
  183.8 1.9 %shard_map.179 = f32[153,1024]{1,0:T(8,128)} custom-call(s32[5]{0:T(128)} %stack.23.place, bf16[160,256]{1,0:T(8,128)(2,1)} %shard_map.178.s0, bf16[160,256]{1,0:T(8,128)(2,1)} %copy-done.19, bf16[160,256]{1,0:T(8,128)(2,1)} %copy-done.18, bf16[160,256]{1,0:T(8,128)(2,1)} %copy-done.17), custom_call_target="tpu_custom_call" | custom-call | tf_op jit(solution)/shard_map/pallas_call | solution.py:284
  186.4 1.9 shard_map.180
  (80 shorter events, 5.0 us)
Async XLA Ops:
  3.1 40.6 %all-to-all-start = ((bf16[32,24,512]{2,1,0:T(8,128)(2,1)}), bf16[32,24,512]{2,1,0:T(8,128)(2,1)S(1)}, u32[]{:S(2)}, u32[]{:S(2)}) async-start(bf16[32,24,512]{2,1,0:T(8,128)(2,1)} %get-tuple-element.60._), calls=%async_computation | async-start | bytes 1572864 | tf_op jit(solution)/shard_map/all_to_all | solution.py:394
  43.7 14.9 %copy-start.6 = (bf16[32,48,128]{2,1,0:T(8,128)(2,1)S(1)}, bf16[32,48,128]{2,1,0:T(8,128)(2,1)}, u32[]{:S(2)}) copy-start(bf16[32,48,128]{2,1,0:T(8,128)(2,1)} %get-tuple-element.88.f0) | copy-start | bytes 1179652
  43.7 30.4 %copy-start.21 = (bf16[64,256]{1,0:T(8,128)(2,1)S(1)}, bf16[64,256]{1,0:T(8,128)(2,1)}, u32[]{:S(2)}) copy-start(bf16[64,256]{1,0:T(8,128)(2,1)} %get-tuple-element.77.p0) | copy-start | bytes 98308
  43.7 44.9 %copy-start.1 = (bf16[32,24,512]{2,1,0:T(8,128)(2,1)}, bf16[32,24,512]{2,1,0:T(8,128)(2,1)S(1)}, u32[]{:S(2)}) copy-start(bf16[32,24,512]{2,1,0:T(8,128)(2,1)S(1)} %all-to-all-done) | copy-start | bytes 2359300
  43.7 14.9 %collective-permute-start.3 = (bf16[32,48,128]{2,1,0:T(8,128)(2,1)}, bf16[32,48,128]{2,1,0:T(8,128)(2,1)S(1)}, u32[]{:S(2)}, u32[]{:S(2)}) collective-permute-start(bf16[32,48,128]{2,1,0:T(8,128)(2,1)} %get-tuple-element.88.f0), channel_id=1, source_target_pairs={{0,4},{4,0},{1,5},{5,1},{2,6},{6,2},{3,7},{7,3},{8,12},{12,8},{9,1... | collective-permute-start | bytes 1179656 | tf_op jit(solution)/shard_map/ppermute | solution.py:365
  45.0 16.7 %collective-permute-start.2 = (bf16[32,48,128]{2,1,0:T(8,128)(2,1)}, bf16[32,48,128]{2,1,0:T(8,128)(2,1)S(1)}, u32[]{:S(2)}, u32[]{:S(2)}) collective-permute-start(bf16[32,48,128]{2,1,0:T(8,128)(2,1)} %get-tuple-element.88.f0), channel_id=1, source_target_pairs={{0,3},{1,0},{2,1},{3,2},{4,7},{5,4},{6,5},{7,6},{8,11},{9,8},{10,9... | collective-permute-start | bytes 1179656 | tf_op jit(solution)/shard_map/ppermute | solution.py:361
  47.4 41.1 %all-to-all-start.1 = ((bf16[32,56,128]{2,1,0:T(8,128)(2,1)}), bf16[32,56,128]{2,1,0:T(8,128)(2,1)S(1)}, u32[]{:S(2)}, u32[]{:S(2)}) async-start(bf16[32,56,128]{2,1,0:T(8,128)(2,1)} %get-tuple-element.64), calls=%async_computation.1 | async-start | bytes 917504 | tf_op jit(solution)/shard_map/all_to_all | solution.py:399
  53.7 8.9 %collective-permute-start.5 = (bf16[768,256]{1,0:T(8,128)(2,1)S(1)}, bf16[768,256]{1,0:T(8,128)(2,1)S(1)}, u32[]{:S(2)}, u32[]{:S(2)}) collective-permute-start(bf16[768,256]{1,0:T(8,128)(2,1)S(1)} %get-tuple-element.114), channel_id=1, source_target_pairs={{0,192},{64,0},{128,64},{192,128},{1,193},{65,1},{129,65},{193,129... | collective-permute-start | bytes 1179656 | tf_op jit(solution)/shard_map/ppermute | solution.py:361
  56.2 9.6 %collective-permute-start.4 = (bf16[768,256]{1,0:T(8,128)(2,1)S(1)}, bf16[768,256]{1,0:T(8,128)(2,1)}, u32[]{:S(2)}, u32[]{:S(2)}) collective-permute-start(bf16[768,256]{1,0:T(8,128)(2,1)S(1)} %get-tuple-element.115), channel_id=1, source_target_pairs={{0,64},{64,128},{128,192},{192,0},{1,65},{65,129},{129,193},{193,1... | collective-permute-start | bytes 1179656 | tf_op jit(solution)/shard_map/ppermute | solution.py:361
  56.2 32.3 %collective-permute-start.6 = (bf16[768,512]{1,0:T(8,128)(2,1)S(1)}, bf16[768,512]{1,0:T(8,128)(2,1)S(1)}, u32[]{:S(2)}, u32[]{:S(2)}) collective-permute-start(bf16[768,512]{1,0:T(8,128)(2,1)S(1)} %bitcast.10), channel_id=1, source_target_pairs={{0,32},{32,0},{1,33},{33,1},{2,34},{34,2},{3,35},{35,3},{4,36},{36... | collective-permute-start | bytes 2359304 | tf_op jit(solution)/shard_map/ppermute | solution.py:365
  58.6 79.2 %copy-start.7 = (bf16[32,48,128]{2,1,0:T(8,128)(2,1)}, bf16[32,48,128]{2,1,0:T(8,128)(2,1)S(1)}, u32[]{:S(2)}) copy-start(bf16[32,48,128]{2,1,0:T(8,128)(2,1)S(1)} %collective-permute-done.3.g0) | copy-start | bytes 1179652
  58.6 15.5 %collective-permute-start.1 = (bf16[32,48,128]{2,1,0:T(8,128)(2,1)S(1)}, bf16[32,48,128]{2,1,0:T(8,128)(2,1)S(1)}, u32[]{:S(2)}, u32[]{:S(2)}) collective-permute-start(bf16[32,48,128]{2,1,0:T(8,128)(2,1)S(1)} %copy-done.6), channel_id=1, source_target_pairs={{0,2},{1,3},{2,0},{3,1},{4,6},{5,7},{6,4},{7,5},{8,10},{9,11},{10,... | collective-permute-start | bytes 1179656 | tf_op jit(solution)/shard_map/ppermute | solution.py:361
  61.7 76.1 %copy-start.8 = (bf16[32,48,128]{2,1,0:T(8,128)(2,1)}, bf16[32,48,128]{2,1,0:T(8,128)(2,1)S(1)}, u32[]{:S(2)}) copy-start(bf16[32,48,128]{2,1,0:T(8,128)(2,1)S(1)} %collective-permute-done.2.f3) | copy-start | bytes 1179652
  61.7 21.2 %collective-permute-start = (bf16[32,48,128]{2,1,0:T(8,128)(2,1)S(1)}, bf16[32,48,128]{2,1,0:T(8,128)(2,1)S(1)}, u32[]{:S(2)}, u32[]{:S(2)}) collective-permute-start(bf16[32,48,128]{2,1,0:T(8,128)(2,1)S(1)} %copy-done.6), channel_id=1, source_target_pairs={{0,1},{1,2},{2,3},{3,0},{4,5},{5,6},{6,7},{7,4},{8,9},{9,10},{10,1... | collective-permute-start | bytes 1179656 | tf_op jit(solution)/shard_map/ppermute | solution.py:361
  62.6 24.3 %copy-start.11 = (bf16[768,256]{1,0:T(8,128)(2,1)}, bf16[768,256]{1,0:T(8,128)(2,1)S(1)}, u32[]{:S(2)}) copy-start(bf16[768,256]{1,0:T(8,128)(2,1)S(1)} %collective-permute-done.5.w2) | copy-start | bytes 1179652
  62.6 24.3 %collective-permute-start.8 = (bf16[768,256]{1,0:T(8,128)(2,1)S(1)}, bf16[768,256]{1,0:T(8,128)(2,1)S(1)}, u32[]{:S(2)}, u32[]{:S(2)}) collective-permute-start(bf16[768,256]{1,0:T(8,128)(2,1)S(1)} %collective-permute-done.5.w2), channel_id=1, source_target_pairs={{0,32},{32,0},{1,33},{33,1},{2,34},{34,2},{3,35},{35,3},{4,36},{36... | collective-permute-start | bytes 1179656 | tf_op jit(solution)/shard_map/ppermute | solution.py:365
  65.8 22.8 %collective-permute-start.7 = (bf16[768,256]{1,0:T(8,128)(2,1)}, bf16[768,256]{1,0:T(8,128)(2,1)}, u32[]{:S(2)}, u32[]{:S(2)}) collective-permute-start(bf16[768,256]{1,0:T(8,128)(2,1)} %collective-permute-done.4.w1), channel_id=1, source_target_pairs={{0,32},{32,0},{1,33},{33,1},{2,34},{34,2},{3,35},{35,3},{4,36},{36... | collective-permute-start | bytes 1179656 | tf_op jit(solution)/shard_map/ppermute | solution.py:365
  74.1 12.8 %copy-start.9 = (bf16[32,48,128]{2,1,0:T(8,128)(2,1)}, bf16[32,48,128]{2,1,0:T(8,128)(2,1)S(1)}, u32[]{:S(2)}) copy-start(bf16[32,48,128]{2,1,0:T(8,128)(2,1)S(1)} %collective-permute-done.1.f2) | copy-start | bytes 1179652
  74.1 20.0 %collective-permute-start.11 = (bf16[64,256]{1,0:T(8,128)(2,1)S(1)}, bf16[64,256]{1,0:T(8,128)(2,1)S(1)}, u32[]{:S(2)}, u32[]{:S(2)}) collective-permute-start(bf16[64,256]{1,0:T(8,128)(2,1)S(1)} %copy-done.21), channel_id=1, source_target_pairs={{0,24},{8,0},{16,8},{24,16},{1,25},{9,1},{17,9},{25,17},{2,26},{10... | collective-permute-start | bytes 98312 | tf_op jit(solution)/shard_map/ppermute | solution.py:361
  82.9 11.3 %collective-permute-start.10 = (bf16[64,256]{1,0:T(8,128)(2,1)S(1)}, bf16[64,256]{1,0:T(8,128)(2,1)S(1)}, u32[]{:S(2)}, u32[]{:S(2)}) collective-permute-start(bf16[64,256]{1,0:T(8,128)(2,1)S(1)} %copy-done.21), channel_id=1, source_target_pairs={{0,16},{8,24},{16,0},{24,8},{1,17},{9,25},{17,1},{25,9},{2,18},{10... | collective-permute-start | bytes 98312 | tf_op jit(solution)/shard_map/ppermute | solution.py:361
  87.7 6.5 %collective-permute-start.9 = (bf16[64,256]{1,0:T(8,128)(2,1)S(1)}, bf16[64,256]{1,0:T(8,128)(2,1)S(1)}, u32[]{:S(2)}, u32[]{:S(2)}) collective-permute-start(bf16[64,256]{1,0:T(8,128)(2,1)S(1)} %copy-done.21), channel_id=1, source_target_pairs={{0,8},{8,16},{16,24},{24,0},{1,9},{9,17},{17,25},{25,1},{2,10},{10... | collective-permute-start | bytes 98312 | tf_op jit(solution)/shard_map/ppermute | solution.py:361
  94.2 8.4 %copy-start.26 = (s32[8]{0:T(128)S(1)}, s32[8]{0:T(128)}, u32[]{:S(2)}) copy-start(s32[8]{0:T(128)} %param.24) | copy-start | bytes 100
  94.2 9.0 %copy-start.22 = (bf16[64,256]{1,0:T(8,128)(2,1)}, bf16[64,256]{1,0:T(8,128)(2,1)S(1)}, u32[]{:S(2)}) copy-start(bf16[64,256]{1,0:T(8,128)(2,1)S(1)} %collective-permute-done.11.p3) | copy-start | bytes 98308
  94.2 9.0 %copy-start.23 = (bf16[64,256]{1,0:T(8,128)(2,1)}, bf16[64,256]{1,0:T(8,128)(2,1)S(1)}, u32[]{:S(2)}) copy-start(bf16[64,256]{1,0:T(8,128)(2,1)S(1)} %collective-permute-done.10.p2) | copy-start | bytes 98308
  94.2 8.9 %copy-start.24 = (bf16[64,256]{1,0:T(8,128)(2,1)}, bf16[64,256]{1,0:T(8,128)(2,1)S(1)}, u32[]{:S(2)}) copy-start(bf16[64,256]{1,0:T(8,128)(2,1)S(1)} %collective-permute-done.9.p1) | copy-start | bytes 98308
  94.2 38.0 %all-to-all-start.2 = ((bf16[32,128,128]{2,1,0:T(8,128)(2,1)}), bf16[32,128,128]{2,1,0:T(8,128)(2,1)S(1)}, u32[]{:S(2)}, u32[]{:S(2)}) async-start(bf16[32,128,128]{2,1,0:T(8,128)(2,1)} %shard_map.174), calls=%async_computation.2 | async-start | bytes 2097152 | tf_op jit(solution)/shard_map/all_to_all | solution.py:411
  98.9 20.2 %collective-permute-start.14 = (bf16[32,48,128]{2,1,0:T(8,128)(2,1)S(1)}, bf16[32,48,128]{2,1,0:T(8,128)(2,1)S(1)}, u32[]{:S(2)}, u32[]{:S(2)}) collective-permute-start(bf16[32,48,128]{2,1,0:T(8,128)(2,1)S(1)} %collective-permute-done.3.g0), channel_id=1, source_target_pairs={{0,3},{1,0},{2,1},{3,2},{4,7},{5,4},{6,5},{7,6},{8,11},{9,8},{10,9... | collective-permute-start | bytes 1179656 | tf_op jit(solution)/shard_map/ppermute | solution.py:361
  101.4 19.5 %collective-permute-start.13 = (bf16[32,48,128]{2,1,0:T(8,128)(2,1)S(1)}, bf16[32,48,128]{2,1,0:T(8,128)(2,1)S(1)}, u32[]{:S(2)}, u32[]{:S(2)}) collective-permute-start(bf16[32,48,128]{2,1,0:T(8,128)(2,1)S(1)} %collective-permute-done.3.g0), channel_id=1, source_target_pairs={{0,2},{1,3},{2,0},{3,1},{4,6},{5,7},{6,4},{7,5},{8,10},{9,11},{10,... | collective-permute-start | bytes 1179656 | tf_op jit(solution)/shard_map/ppermute | solution.py:361
  102.0 30.3 %collective-permute-start.12 = (bf16[32,48,128]{2,1,0:T(8,128)(2,1)S(1)}, bf16[32,48,128]{2,1,0:T(8,128)(2,1)S(1)}, u32[]{:S(2)}, u32[]{:S(2)}) collective-permute-start(bf16[32,48,128]{2,1,0:T(8,128)(2,1)S(1)} %collective-permute-done.3.g0), channel_id=1, source_target_pairs={{0,1},{1,2},{2,3},{3,0},{4,5},{5,6},{6,7},{7,4},{8,9},{9,10},{10,1... | collective-permute-start | bytes 1179656 | tf_op jit(solution)/shard_map/ppermute | solution.py:361
  119.1 22.3 %copy-start.12 = (bf16[32,48,128]{2,1,0:T(8,128)(2,1)}, bf16[32,48,128]{2,1,0:T(8,128)(2,1)S(1)}, u32[]{:S(2)}) copy-start(bf16[32,48,128]{2,1,0:T(8,128)(2,1)S(1)} %collective-permute-done.14.g3) | copy-start | bytes 1179652
  120.9 20.5 %copy-start.13 = (bf16[32,48,128]{2,1,0:T(8,128)(2,1)}, bf16[32,48,128]{2,1,0:T(8,128)(2,1)S(1)}, u32[]{:S(2)}) copy-start(bf16[32,48,128]{2,1,0:T(8,128)(2,1)S(1)} %collective-permute-done.13.g2) | copy-start | bytes 1179652
  132.3 9.1 %copy-start.14 = (bf16[32,48,128]{2,1,0:T(8,128)(2,1)}, bf16[32,48,128]{2,1,0:T(8,128)(2,1)S(1)}, u32[]{:S(2)}) copy-start(bf16[32,48,128]{2,1,0:T(8,128)(2,1)S(1)} %collective-permute-done.12.g1) | copy-start | bytes 1179652
  137.8 13.7 %all-to-all-start.3 = ((bf16[8,160,256]{2,1,0:T(8,128)(2,1)}), bf16[8,160,256]{2,1,0:T(8,128)(2,1)S(1)}, u32[]{:S(2)}, u32[]{:S(2)}) async-start(bf16[8,160,256]{2,1,0:T(8,128)(2,1)} %get-tuple-element.98), calls=%async_computation.3 | async-start | bytes 1310720 | tf_op jit(solution)/shard_map/all_to_all | solution.py:422
  141.4 6.2 %copy-start.25 = (f32[64,128]{1,0:T(8,128)S(1)}, f32[64,128]{1,0:T(8,128)}, u32[]{:S(2)}) copy-start(f32[64,128]{1,0:T(8,128)} %get-tuple-element.100) | copy-start | bytes 98308
  141.4 7.3 %copy-start.20 = (f32[64,128]{1,0:T(8,128)S(1)}, f32[64,128]{1,0:T(8,128)}, u32[]{:S(2)}) copy-start(f32[64,128]{1,0:T(8,128)} %get-tuple-element.99) | copy-start | bytes 98308
  147.0 1.7 collective-permute-start.15
  147.5 1.2 collective-permute-start.16
  151.5 17.6 %all-to-all-start.4 = ((f32[8,24,128]{2,1,0:T(8,128)}), f32[8,24,128]{2,1,0:T(8,128)S(1)}, u32[]{:S(2)}, u32[]{:S(2)}) async-start(f32[8,24,128]{2,1,0:T(8,128)} %add.20), calls=%async_computation.4 | async-start | bytes 196608 | tf_op jit(solution)/shard_map/all_to_all | solution.py:428
  157.5 6.7 %collective-permute-start.19 = (bf16[160,256]{1,0:T(8,128)(2,1)}, bf16[160,256]{1,0:T(8,128)(2,1)S(1)}, u32[]{:S(2)}, u32[]{:S(2)}) collective-permute-start(bf16[160,256]{1,0:T(8,128)(2,1)} %shard_map.178.s0), channel_id=1, source_target_pairs={{0,24},{8,0},{16,8},{24,16},{1,25},{9,1},{17,9},{25,17},{2,26},{10... | collective-permute-start | bytes 245768 | tf_op jit(solution)/shard_map/ppermute | solution.py:361
  160.7 7.6 %collective-permute-start.18 = (bf16[160,256]{1,0:T(8,128)(2,1)}, bf16[160,256]{1,0:T(8,128)(2,1)S(1)}, u32[]{:S(2)}, u32[]{:S(2)}) collective-permute-start(bf16[160,256]{1,0:T(8,128)(2,1)} %shard_map.178.s0), channel_id=1, source_target_pairs={{0,16},{8,24},{16,0},{24,8},{1,17},{9,25},{17,1},{25,9},{2,18},{10... | collective-permute-start | bytes 245768 | tf_op jit(solution)/shard_map/ppermute | solution.py:361
  162.6 6.4 %collective-permute-start.17 = (bf16[160,256]{1,0:T(8,128)(2,1)}, bf16[160,256]{1,0:T(8,128)(2,1)S(1)}, u32[]{:S(2)}, u32[]{:S(2)}) collective-permute-start(bf16[160,256]{1,0:T(8,128)(2,1)} %shard_map.178.s0), channel_id=1, source_target_pairs={{0,8},{8,16},{16,24},{24,0},{1,9},{9,17},{17,25},{25,1},{2,10},{10... | collective-permute-start | bytes 245768 | tf_op jit(solution)/shard_map/ppermute | solution.py:361
  164.2 19.6 %copy-start.17 = (bf16[160,256]{1,0:T(8,128)(2,1)}, bf16[160,256]{1,0:T(8,128)(2,1)S(1)}, u32[]{:S(2)}) copy-start(bf16[160,256]{1,0:T(8,128)(2,1)S(1)} %collective-permute-done.19.s3) | copy-start | bytes 245764
  168.2 15.6 %copy-start.18 = (bf16[160,256]{1,0:T(8,128)(2,1)}, bf16[160,256]{1,0:T(8,128)(2,1)S(1)}, u32[]{:S(2)}) copy-start(bf16[160,256]{1,0:T(8,128)(2,1)S(1)} %collective-permute-done.18.s2) | copy-start | bytes 245764
  169.1 14.8 %copy-start.19 = (bf16[160,256]{1,0:T(8,128)(2,1)}, bf16[160,256]{1,0:T(8,128)(2,1)S(1)}, u32[]{:S(2)}) copy-start(bf16[160,256]{1,0:T(8,128)(2,1)S(1)} %collective-permute-done.17.s1) | copy-start | bytes 245764
  169.1 4.0 %collective-permute-start.20 = (f32[256,128]{1,0:T(8,128)S(1)}, f32[256,128]{1,0:T(8,128)S(1)}, u32[]{:S(2)}, u32[]{:S(2)}) collective-permute-start(f32[256,128]{1,0:T(8,128)S(1)} %pad_maximum_fusion), channel_id=1, source_target_pairs={{0,64},{64,0},{128,192},{192,128},{1,65},{65,1},{129,193},{193,129... | collective-permute-start | bytes 393224 | tf_op jit(solution)/shard_map/ppermute | solution.py:369
  173.1 5.6 %collective-permute-start.21 = (f32[256,128]{1,0:T(8,128)S(1)}, f32[256,128]{1,0:T(8,128)S(1)}, u32[]{:S(2)}, u32[]{:S(2)}) collective-permute-start(f32[256,128]{1,0:T(8,128)S(1)} %fusion), channel_id=1, source_target_pairs={{0,192},{192,0},{64,128},{128,64},{1,193},{193,1},{65,129},{129,65... | collective-permute-start | bytes 393224 | tf_op jit(solution)/shard_map/ppermute | solution.py:370
  178.7 7.1 %copy-start.5 = (f32[256,128]{1,0:T(8,128)}, f32[256,128]{1,0:T(8,128)S(1)}, u32[]{:S(2)}) copy-start(f32[256,128]{1,0:T(8,128)S(1)} %add.23.keep) | copy-start | bytes 393220
  178.7 7.1 %collective-permute-start.22 = (f32[256,128]{1,0:T(8,128)S(1)}, f32[256,128]{1,0:T(8,128)S(1)}, u32[]{:S(2)}, u32[]{:S(2)}) collective-permute-start(f32[256,128]{1,0:T(8,128)S(1)} %add.23.keep), channel_id=1, source_target_pairs={{0,32},{32,0},{1,33},{33,1},{2,34},{34,2},{3,35},{35,3},{4,36},{36... | collective-permute-start | bytes 393224 | tf_op jit(solution)/shard_map/ppermute | solution.py:365
  (7 other events, 12.3 us)

commit v7 on v6

--- a/solution.py
+++ b/solution.py
@@ -260,7 +260,8 @@
     total = parts[0].astype(F32)
     for j in range(1, parts.shape[0]):
         total = total + parts[j].astype(F32)
-    out[...] = total.astype(BF)
+    for d in range(out.shape[0]):
+        out[d] = total.astype(BF)
 
 
 def total(parts):
@@ -268,43 +269,49 @@
         total_kernel,
         in_specs=[VMEM],
         out_specs=VMEM,
-        out_shape=jax.ShapeDtypeStruct(parts.shape[1:], BF),
+        out_shape=jax.ShapeDtypeStruct((4,) + parts.shape[1:], BF),
         compiler_params=LIMIT,
     )(parts)
 
 
-def logit_kernel(place, s0, s1, s2, s3, out):
+def logit_kernel(parts, out):
     classes = out.shape[0]
-    for s, part in enumerate((s0, s1, s2, s3)):
-        at = aligned(lax.rem(place[2] + 4 - s, 4), 256)
-        out[:, at] = part[...].astype(F32)[0:classes]
-
-
-def join(place, parts, classes):
+    for j in range(parts.shape[0]):
+        out[:, 256 * j : 256 * (j + 1)] = parts[j].astype(F32)[0:classes]
+
+
+def join(parts, classes):
     return pl.pallas_call(
         logit_kernel,
-        in_specs=[SMEM] + [VMEM] * 4,
+        in_specs=[VMEM],
         out_specs=VMEM,
-        out_shape=jax.ShapeDtypeStruct((classes, 4 * parts[0].shape[1]), F32),
-        compiler_params=LIMIT,
-    )(place, *parts)
-
-
-def grad_kernel(place, hidden, dhidden, f0, f1, f2, f3, g0, g1, g2, g3, keep, send, total):
+        out_shape=jax.ShapeDtypeStruct((classes, 4 * parts.shape[2]), F32),
+        compiler_params=LIMIT,
+    )(parts)
+
+
+def grad_kernel(
+    place, hidden, dhidden, f0, f1, f2, e2, f3, g0, g1, g2, d2, g3, keep, send, total
+):
     core, zr, y = place[0], place[3], place[4]
     blocks, deep, _ = f0.shape
     half = deep // 2
-    parts = (f0, f1, f2, f3, g0, g1, g2, g3)
     total[...] = jnp.zeros_like(total)
 
-    def grow(b, carry):
-        low = jnp.where(hidden[b].astype(F32) > 0.0, dhidden[b], 0.0).astype(BF)
-        stack = jnp.concatenate([part[b] for part in parts], axis=0)
-        total[...] += lax.dot_general(stack, low, NT, preferred_element_type=F32)
-        return carry
-
-    lax.fori_loop(0, blocks, grow, 0, unroll=4)
-    for j in range(len(parts)):
+    for side in range(2):
+        first = side * (blocks // 2)
+        far, twin = ((f2, g2), (e2, d2))[side]
+
+        def grow(i, carry):
+            b = first + i
+            low = jnp.where(hidden[b].astype(F32) > 0.0, dhidden[b], 0.0).astype(BF)
+            parts = [f0[b], f1[b], far[i], f3[b], g0[b], g1[b], twin[i], g3[b]]
+            stack = jnp.concatenate(parts, axis=0)
+            total[...] += lax.dot_general(stack, low, NT, preferred_element_type=F32)
+            return carry
+
+        lax.fori_loop(0, blocks // 2, grow, 0, unroll=4)
+    for j in range(8):
         owner = 4 * (zr if j < 4 else 1 - zr) + lax.rem(y + 8 - j, 4)
         keep[owner] = total[pl.ds(pl.multiple_of(j * deep + core * half, 8), half), :]
         send[owner] = total[pl.ds(pl.multiple_of(j * deep + (1 - core) * half, 8), half), :]
@@ -315,7 +322,7 @@
     shape = jax.ShapeDtypeStruct((8, deep // 2, TILE), F32)
     return pl.pallas_call(
         grad_kernel,
-        in_specs=[SMEM] + [VMEM] * 10,
+        in_specs=[SMEM] + [VMEM] * 12,
         out_specs=[VMEM, VMEM],
         scratch_shapes=[pltpu.VMEM((8 * deep, TILE), F32)],
         out_shape=[shape, shape],
@@ -361,6 +368,12 @@
     return lax.ppermute(value, axis, [(i, (i + by) % 4) for i in range(4)])
 
 
+def relay(value, near):
+    half = value.shape[0] // 2
+    far = [shift(near[0][:half], "y", 1), shift(near[1][half:], "y", 3)]
+    return [value, near[0], *far, near[1]]
+
+
 def swap(value, axis):
     return lax.ppermute(value, axis, [(0, 1), (1, 0)])
 
@@ -402,14 +415,15 @@
     other = [swap(w, "core") for w in mine]
 
     twin = swap(feats, "zr")
-    feats = [feats] + [shift(feats, "y", s) for s in (1, 2, 3)]
-    got, feats, twin = lax.optimization_barrier((got, feats, twin))
+    near = [shift(feats, "y", s) for s in (1, 3)]
     pairs = [pair] + [shift(pair, "zq", s) for s in (1, 2, 3)]
 
     hidden = layer(place, got, mine, other)
-    hidden, pairs, twin = lax.optimization_barrier((hidden, pairs, twin))
+    hidden, pairs, near, feats, twin = lax.optimization_barrier(
+        (hidden, pairs, near, feats, twin)
+    )
     hidden = lax.all_to_all(hidden, FEAT, 0, 0, tiled=True)
-    feats = feats + [twin] + [shift(twin, "y", s) for s in (1, 2, 3)]
+    feats = relay(feats, near) + relay(twin, [shift(twin, "y", s) for s in (1, 3)])
     live = batch_sizes[lax.axis_index("x") * 2 + lax.axis_index("core")]
     dhidden, cot, self_t, neigh_t = spread(
         place, target_cols, live, logit_cotangent, pairs, target_tiles, blocks
@@ -426,12 +440,11 @@
     keep = keep + swap(send, "core")
     keep, scores, keep_head = lax.optimization_barrier((keep, scores, keep_head))
     keep = lax.all_to_all(keep, ("zr", "y"), 0, 0, tiled=True)
-    scores = total(scores)
-    scores = [scores] + [shift(scores, "zq", s) for s in (1, 2, 3)]
-    keep, scores = lax.optimization_barrier((keep, scores))
+    keep, scores = lax.optimization_barrier((keep, total(scores)))
+    scores = lax.all_to_all(scores, "zq", 0, 0, tiled=True)
     keep = sum_x(jnp.concatenate([keep.reshape(-1, TILE), keep_head], axis=0))
     results = finish(place, keep, swap(keep, "core"), deep, classes)
-    return (join(place, scores, classes), *results[:4], results[4].reshape(-1))
+    return (join(scores, classes), *results[:4], results[4].reshape(-1))
 
 
 def solution(mesh):

time: 190 us -> 179 us (0.942)
  waiting for transfers between devices: 46.8 us -> 32.8 us
  local copies, waits for them, and re-layouts: 6.8 us -> 9.47 us
    ppermute x14 -> x13, waiting for transfers between devices: 39.8 us -> 22.1 us  [shift(): return lax.ppermute(value, axis, [(i, (i + by) % 4) for i in range(4)])]
    all_to_all x0 -> x1, starting transfers between devices: none -> 5.25 us  [shards(): scores = lax.all_to_all(scores, 'zq', 0, 0, tiled=True)]
    all_to_all x1, waiting for transfers between devices: 0.01 us -> 3.47 us  [shards(): keep = lax.all_to_all(keep, ('zr', 'y'), 0, 0, tiled=True)]
    ppermute x1, starting transfers between devices: 3.2 us -> 0.09 us  [sum_x(): return value + lax.ppermute(value, 'x', [(0, 3), (3, 0), (1, 2), (2, 1)])]
    all_to_all x1, starting transfers between devices: 6.18 us -> 9.21 us  [shards(): got = lax.all_to_all(send, FEAT, 0, 0, tiled=True)]
    slice x0 -> x4, local copies, waits for them, and re-layouts: none -> 2.81 us  [relay(): far = [shift(near[0][:half], 'y', 1), shift(near[1][half:], 'y', 3)]]
    ppermute x1, waiting for transfers between devices: 2.36 us -> 5.02 us  [sum_x(): return value + lax.ppermute(value, 'x', [(0, 3), (3, 0), (1, 2), (2, 1)])]
    ppermute x7, starting transfers between devices: 15.7 us -> 13.1 us  [swap(): return lax.ppermute(value, axis, [(0, 1), (1, 0)])]
  transfers between devices with their start and end apart: 28 -> 28, of which waited for: 13 -> 8; matrix products, arithmetic and copies ran while one was open for 2% -> 4% of each run, Pallas kernels for 25% -> 26%
where the time goes in v7:
time: 179 us; the launch traced here: 178 us
  starting transfers between devices  79 us (44%)
  Pallas kernels  54.6 us (31%)
  waiting for transfers between devices  32.8 us (18%)
  local copies, waits for them, and re-layouts  9.47 us (5%)
    pallas_call x1, Pallas kernels, hop(): pl.pallas_call(hop_kernel, in_specs=[SMEM, SMEM, SMEM, VMEM, VMEM, HBM, H...  27.2 us
    ppermute x13, starting transfers between devices, shift(): return lax.ppermute(value, axis, [(i, (i + by) % 4) for i in range(4)])  24.2 us
    ppermute x13, waiting for transfers between devices, shift(): return lax.ppermute(value, axis, [(i, (i + by) % 4) for i in range(4)])  22.1 us
    ppermute x7, starting transfers between devices, swap(): return lax.ppermute(value, axis, [(0, 1), (1, 0)])  13.1 us
    all_to_all x1, starting transfers between devices, shards(): weights = lax.all_to_all(packed, FEAT, 0, 0, tiled=True)  12 us
    all_to_all x1, starting transfers between devices, shards(): got = lax.all_to_all(send, FEAT, 0, 0, tiled=True)  9.21 us
    all_to_all x1, starting transfers between devices, shards(): hidden = lax.all_to_all(hidden, FEAT, 0, 0, tiled=True)  6 us
    pallas_call x1, Pallas kernels, spread(): pl.pallas_call(spread_kernel, in_specs=[SMEM, SMEM, SMEM] + [VMEM] * 6, o...  5.92 us
  transfers between devices with their start and end apart: 28, of which 8 were waited for; matrix products, arithmetic and copies ran while one was open for 4% of the time, Pallas kernels for 26%

profile of v7, /device:TPU:1, one launch (start us, length us, event | category | flops | bytes accessed | tf_op | source)
XLA Modules:
  0.0 178.5 jit_solution(7195085428703092219)
XLA Ops:
  0.6 0.6 stack.23.place
  1.3 1.8 %shard_map.172 = (bf16[32,24,512]{2,1,0:T(8,128)(2,1)}, bf16[64,256]{1,0:T(8,128)(2,1)}) custom-call(s32[5]{0:T(128)} %stack.23.place, bf16[24,1024]{1,0:T(8,128)(2,1)} %own.1, bf16[24,1024]{1,0:T(8,128)(2,1)} %neigh.1, bf16[32,153]{1,0:T(8,128)(2,1)} %head_self.1, bf16[32,153]{1,0:T(8,128)(2,1)} %head_neigh.1), custom_call_target="tpu_custom_call" | custom-call | tf_op jit(solution)/shard_map/pallas_call | solution.py:116
  3.1 12.0 %all-to-all-start = ((bf16[32,24,512]{2,1,0:T(8,128)(2,1)}), bf16[32,24,512]{2,1,0:T(8,128)(2,1)S(1)}, u32[]{:S(2)}, u32[]{:S(2)}) async-start(bf16[32,24,512]{2,1,0:T(8,128)(2,1)} %get-tuple-element.56._), calls=%async_computation | async-start | bytes 1572864 | tf_op jit(solution)/shard_map/all_to_all | solution.py:407
  15.1 1.4 copy.19.cols
  16.5 27.2 %shard_map.173 = (bf16[32,56,128]{2,1,0:T(8,128)(2,1)}, bf16[32,48,128]{2,1,0:T(8,128)(2,1)}) custom-call(s32[5]{0:T(128)} %stack.23.place, s32[16384]{0:T(1024)} %ids.1, s32[32,8]{1,0:T(8,128)} %copy.19.cols, bf16[24,32768]{1,0:T(8,128)(2,1)} %table.1, f32[1,32]{1,0:T(1,128)} %bitcast.14, bf16[32,8,128,128]{3,2,1,0:T(8,128)(2,1)} %tiles_hbm.1, ...), custom_call_target="tpu_custom_call" | custom-call | flops 1000000000 | bytes 60000000 | tf_op jit(solution)/shard_map/pallas_call | solution.py:84
  43.7 0.8 fusion.1
  44.5 2.5 %collective-permute-start.1 = (bf16[768,256]{1,0:T(8,128)(2,1)}, bf16[768,256]{1,0:T(8,128)(2,1)S(1)}, u32[]{:S(2)}, u32[]{:S(2)}) collective-permute-start(bf16[768,256]{1,0:T(8,128)(2,1)} %get-tuple-element.106), channel_id=1, source_target_pairs={{0,192},{64,0},{128,64},{192,128},{1,193},{65,1},{129,65},{193,129... | collective-permute-start | bytes 1179656 | tf_op jit(solution)/shard_map/ppermute | solution.py:368
  47.0 9.2 %all-to-all-start.1 = ((bf16[32,56,128]{2,1,0:T(8,128)(2,1)}), bf16[32,56,128]{2,1,0:T(8,128)(2,1)S(1)}, u32[]{:S(2)}, u32[]{:S(2)}) async-start(bf16[32,56,128]{2,1,0:T(8,128)(2,1)} %get-tuple-element.60), calls=%async_computation.1 | async-start | bytes 917504 | tf_op jit(solution)/shard_map/all_to_all | solution.py:412
  56.3 1.9 %collective-permute-start.2 = (bf16[768,512]{1,0:T(8,128)(2,1)S(1)}, bf16[768,512]{1,0:T(8,128)(2,1)S(1)}, u32[]{:S(2)}, u32[]{:S(2)}) collective-permute-start(bf16[768,512]{1,0:T(8,128)(2,1)S(1)} %bitcast.10), channel_id=1, source_target_pairs={{0,32},{32,0},{1,33},{33,1},{2,34},{34,2},{3,35},{35,3},{4,36},{36... | collective-permute-start | bytes 2359304 | tf_op jit(solution)/shard_map/ppermute | solution.py:378
  58.3 8.0 %collective-permute-done.w1 = bf16[768,256]{1,0:T(8,128)(2,1)S(1)} collective-permute-done((bf16[768,256]{1,0:T(8,128)(2,1)S(1)}, bf16[768,256]{1,0:T(8,128)(2,1)S(1)}, u32[]{:S(2)}, u32[]{:S(2)}) %collective-permute-start) | collective-permute-done | bytes 393248 | tf_op jit(solution)/shard_map/ppermute | solution.py:368
  66.3 2.7 %collective-permute-start.3 = (bf16[768,256]{1,0:T(8,128)(2,1)S(1)}, bf16[768,256]{1,0:T(8,128)(2,1)S(1)}, u32[]{:S(2)}, u32[]{:S(2)}) collective-permute-start(bf16[768,256]{1,0:T(8,128)(2,1)S(1)} %collective-permute-done.w1), channel_id=1, source_target_pairs={{0,32},{32,0},{1,33},{33,1},{2,34},{34,2},{3,35},{35,3},{4,36},{36... | collective-permute-start | bytes 1179656 | tf_op jit(solution)/shard_map/ppermute | solution.py:378
  69.0 3.4 %collective-permute-start.7 = (bf16[64,256]{1,0:T(8,128)(2,1)S(1)}, bf16[64,256]{1,0:T(8,128)(2,1)S(1)}, u32[]{:S(2)}, u32[]{:S(2)}) collective-permute-start(bf16[64,256]{1,0:T(8,128)(2,1)S(1)} %copy-done.22), channel_id=1, source_target_pairs={{0,24},{8,0},{16,8},{24,16},{1,25},{9,1},{17,9},{25,17},{2,26},{10... | collective-permute-start | bytes 98312 | tf_op jit(solution)/shard_map/ppermute | solution.py:368
  72.7 0.9 collective-permute-done.7.p3
  73.6 2.4 %collective-permute-start.9 = (bf16[32,48,128]{2,1,0:T(8,128)(2,1)S(1)}, bf16[32,48,128]{2,1,0:T(8,128)(2,1)S(1)}, u32[]{:S(2)}, u32[]{:S(2)}) collective-permute-start(bf16[32,48,128]{2,1,0:T(8,128)(2,1)S(1)} %copy-done.11), channel_id=1, source_target_pairs={{0,3},{1,0},{2,1},{3,2},{4,7},{5,4},{6,5},{7,6},{8,11},{9,8},{10,9... | collective-permute-start | bytes 1179656 | tf_op jit(solution)/shard_map/ppermute | solution.py:368
  76.2 5.5 %collective-permute-start.6 = (bf16[64,256]{1,0:T(8,128)(2,1)S(1)}, bf16[64,256]{1,0:T(8,128)(2,1)S(1)}, u32[]{:S(2)}, u32[]{:S(2)}) collective-permute-start(bf16[64,256]{1,0:T(8,128)(2,1)S(1)} %copy-done.22), channel_id=1, source_target_pairs={{0,16},{8,24},{16,0},{24,8},{1,17},{9,25},{17,1},{25,9},{2,18},{10... | collective-permute-start | bytes 98312 | tf_op jit(solution)/shard_map/ppermute | solution.py:368
  81.7 1.6 collective-permute-start.5
  83.3 0.8 copy-done.3
  84.1 4.0 %shard_map.174 = bf16[32,128,128]{2,1,0:T(8,128)(2,1)} custom-call(s32[5]{0:T(128)} %stack.23.place, bf16[32,56,128]{2,1,0:T(8,128)(2,1)} %copy-done.3, bf16[768,512]{1,0:T(8,128)(2,1)} %bitcast.11, bf16[768,256]{1,0:T(8,128)(2,1)} %copy-done.13, bf16[768,256]{1,0:T(8,128)(2,1)} %copy-done.12, bf16[768,512]{1,0:T(8,128)(2,1)} %copy-done.9, ...), custom_call_target="tpu_custom_call" | custom-call | tf_op jit(solution)/shard_map/pallas_call | solution.py:203
  88.1 6.0 %all-to-all-start.2 = ((bf16[32,128,128]{2,1,0:T(8,128)(2,1)}), bf16[32,128,128]{2,1,0:T(8,128)(2,1)S(1)}, u32[]{:S(2)}, u32[]{:S(2)}) async-start(bf16[32,128,128]{2,1,0:T(8,128)(2,1)} %shard_map.174), calls=%async_computation.2 | async-start | bytes 2097152 | tf_op jit(solution)/shard_map/all_to_all | solution.py:425
  94.1 2.5 %collective-permute-start.15 = (bf16[32,48,128]{2,1,0:T(8,128)(2,1)}, bf16[32,48,128]{2,1,0:T(8,128)(2,1)S(1)}, u32[]{:S(2)}, u32[]{:S(2)}) collective-permute-start(bf16[32,48,128]{2,1,0:T(8,128)(2,1)} %collective-permute-done.10.g0), channel_id=1, source_target_pairs={{0,3},{1,0},{2,1},{3,2},{4,7},{5,4},{6,5},{7,6},{8,11},{9,8},{10,9... | collective-permute-start | bytes 1179656 | tf_op jit(solution)/shard_map/ppermute | solution.py:368
  96.6 0.7 slice.20
  97.3 0.7 slice.21
  98.0 2.7 %collective-permute-start.12 = (bf16[16,48,128]{2,1,0:T(8,128)(2,1)}, bf16[16,48,128]{2,1,0:T(8,128)(2,1)S(1)}, u32[]{:S(2)}, u32[]{:S(2)}) collective-permute-start(bf16[16,48,128]{2,1,0:T(8,128)(2,1)} %slice.21), channel_id=1, source_target_pairs={{0,3},{1,0},{2,1},{3,2},{4,7},{5,4},{6,5},{7,6},{8,11},{9,8},{10,9... | collective-permute-start | bytes 589832 | tf_op jit(solution)/shard_map/ppermute | solution.py:368
  100.7 11.5 %collective-permute-done.15.g3 = bf16[32,48,128]{2,1,0:T(8,128)(2,1)S(1)} collective-permute-done((bf16[32,48,128]{2,1,0:T(8,128)(2,1)}, bf16[32,48,128]{2,1,0:T(8,128)(2,1)S(1)}, u32[]{:S(2)}, u32[]{:S(2)}) %collective-permute-start.15) | collective-permute-done | bytes 393248 | tf_op jit(solution)/shard_map/ppermute | solution.py:368
  112.2 0.7 slice.27
  112.9 3.5 %collective-permute-start.16 = (bf16[16,48,128]{2,1,0:T(8,128)(2,1)}, bf16[16,48,128]{2,1,0:T(8,128)(2,1)S(1)}, u32[]{:S(2)}, u32[]{:S(2)}) collective-permute-start(bf16[16,48,128]{2,1,0:T(8,128)(2,1)} %slice.27), channel_id=1, source_target_pairs={{0,3},{1,0},{2,1},{3,2},{4,7},{5,4},{6,5},{7,6},{8,11},{9,8},{10,9... | collective-permute-start | bytes 589832 | tf_op jit(solution)/shard_map/ppermute | solution.py:368
  116.4 0.7 slice.26
  117.1 0.6 dynamic_slice.3.live
  117.7 5.9 %shard_map.175 = (f32[32,128,128]{2,1,0:T(8,128)}, bf16[256,1024]{1,0:T(8,128)(2,1)}, bf16[256,128]{1,0:T(8,128)(2,1)}, bf16[256,128]{1,0:T(8,128)(2,1)}) custom-call(s32[5]{0:T(128)} %stack.23.place, s32[8,8]{1,0:T(8,128)} %cols.4, s32[1]{0:T(128)} %dynamic_slice.3.live, bf16[153,1024]{1,0:T(8,128)(2,1)} %logit_cot.1, ...), custom_call_target="tpu_custom_call" | custom-call | flops 1000000000 | bytes 8000000 | tf_op jit(solution)/shard_map/pallas_call | solution.py:153
  123.7 1.7 collective-permute-done.14.g2
  125.4 1.0 copy-done
  126.4 4.5 %shard_map.176 = (bf16[8,160,256]{2,1,0:T(8,128)(2,1)}, f32[64,128]{1,0:T(8,128)}, f32[64,128]{1,0:T(8,128)}) custom-call(s32[5]{0:T(128)} %stack.23.place, s32[8,8]{1,0:T(8,128)} %cols.4, bf16[32,128,128]{2,1,0:T(8,128)(2,1)} %copy-done, f32[32,128,128]{2,1,0:T(8,128)} %get-tuple-element.74.dhidden, bf16[8,8,128,128]{3,2,1,0:T(8,128)(2,1)} %tiles.3, ...), custom_call_target="tpu_custom_call" | custom-call | tf_op jit(solution)/shard_map/pallas_call | solution.py:249
  131.0 3.5 %all-to-all-start.3 = ((bf16[8,160,256]{2,1,0:T(8,128)(2,1)}), bf16[8,160,256]{2,1,0:T(8,128)(2,1)S(1)}, u32[]{:S(2)}, u32[]{:S(2)}) async-start(bf16[8,160,256]{2,1,0:T(8,128)(2,1)} %get-tuple-element.93), calls=%async_computation.3 | async-start | bytes 1310720 | tf_op jit(solution)/shard_map/all_to_all | solution.py:436
  134.6 5.6 %shard_map.177 = (f32[8,24,128]{2,1,0:T(8,128)}, f32[8,24,128]{2,1,0:T(8,128)}) custom-call(s32[5]{0:T(128)} %stack.23.place, bf16[32,128,128]{2,1,0:T(8,128)(2,1)} %copy-done, f32[32,128,128]{2,1,0:T(8,128)} %get-tuple-element.74.dhidden, bf16[32,48,128]{2,1,0:T(8,128)(2,1)} %get-tuple-element.81.f0, bf16[32,48,128]{2,1,0:T(8,128)(2,1)} %copy-done.6, ...), custom_call_target="tpu_custom_call" | custom-call | flops 1000000000 | bytes 7000000 | tf_op jit(solution)/shard_map/pallas_call | solution.py:323
  140.2 4.9 %collective-permute-start.17 = (f32[8,24,128]{2,1,0:T(8,128)}, f32[8,24,128]{2,1,0:T(8,128)S(1)}, u32[]{:S(2)}, u32[]{:S(2)}) collective-permute-start(f32[8,24,128]{2,1,0:T(8,128)} %get-tuple-element.92), channel_id=1, source_target_pairs={{0,32},{32,0},{1,33},{33,1},{2,34},{34,2},{3,35},{35,3},{4,36},{36... | collective-permute-start | bytes 294920 | tf_op jit(solution)/shard_map/ppermute | solution.py:378
  145.2 1.1 collective-permute-done.18
  146.4 1.5 add.20
  147.9 5.4 %all-to-all-start.4 = ((f32[8,24,128]{2,1,0:T(8,128)}), f32[8,24,128]{2,1,0:T(8,128)S(1)}, u32[]{:S(2)}, u32[]{:S(2)}) async-start(f32[8,24,128]{2,1,0:T(8,128)} %add.20), calls=%async_computation.4 | async-start | bytes 196608 | tf_op jit(solution)/shard_map/all_to_all | solution.py:442
  153.3 1.9 %shard_map.178 = bf16[4,160,256]{2,1,0:T(8,128)(2,1)} custom-call(bf16[8,160,256]{2,1,0:T(8,128)(2,1)} %copy-done.2), custom_call_target="tpu_custom_call" | custom-call | tf_op jit(solution)/shard_map/pallas_call | solution.py:268
  155.2 3.5 %all-to-all-done.4 = f32[8,24,128]{2,1,0:T(8,128)S(1)} async-done(((f32[8,24,128]{2,1,0:T(8,128)}), f32[8,24,128]{2,1,0:T(8,128)S(1)}, u32[]{:S(2)}, u32[]{:S(2)}) %all-to-all-start.4) | async-done | bytes 98336 | tf_op jit(solution)/shard_map/all_to_all | solution.py:442
  158.8 5.2 %all-to-all-start.5 = ((bf16[4,160,256]{2,1,0:T(8,128)(2,1)}), bf16[4,160,256]{2,1,0:T(8,128)(2,1)S(1)}, u32[]{:S(2)}, u32[]{:S(2)}) async-start(bf16[4,160,256]{2,1,0:T(8,128)(2,1)} %shard_map.178), calls=%async_computation.5 | async-start | bytes 655360 | tf_op jit(solution)/shard_map/all_to_all | solution.py:444
  164.2 5.0 %collective-permute-done.20 = f32[256,128]{1,0:T(8,128)S(1)} collective-permute-done((f32[256,128]{1,0:T(8,128)S(1)}, f32[256,128]{1,0:T(8,128)S(1)}, u32[]{:S(2)}, u32[]{:S(2)}) %collective-permute-start.20) | collective-permute-done | bytes 131104 | tf_op jit(solution)/shard_map/ppermute | solution.py:383
  169.3 3.1 %collective-permute-start.21 = (f32[256,128]{1,0:T(8,128)S(1)}, f32[256,128]{1,0:T(8,128)S(1)}, u32[]{:S(2)}, u32[]{:S(2)}) collective-permute-start(f32[256,128]{1,0:T(8,128)S(1)} %add.23.keep), channel_id=1, source_target_pairs={{0,32},{32,0},{1,33},{33,1},{2,34},{34,2},{3,35},{35,3},{4,36},{36... | collective-permute-start | bytes 393224 | tf_op jit(solution)/shard_map/ppermute | solution.py:378
  172.4 1.0 collective-permute-done.21.rest
  173.4 0.7 copy-done.20
  174.0 1.9 %shard_map.180 = (f32[24,1024]{1,0:T(8,128)}, f32[24,1024]{1,0:T(8,128)}, f32[32,153]{1,0:T(8,128)}, f32[32,153]{1,0:T(8,128)}, f32[1,32]{1,0:T(1,128)}) custom-call(s32[5]{0:T(128)} %stack.23.place, f32[256,128]{1,0:T(8,128)} %copy-done.10, f32[256,128]{1,0:T(8,128)} %copy-done.20), custom_call_target="tpu_custom_call" | custom-call | tf_op jit(solution)/shard_map/pallas_call | solution.py:358
  175.9 0.7 copy-done.4
  176.6 1.9 %shard_map.179 = f32[153,1024]{1,0:T(8,128)} custom-call(bf16[4,160,256]{2,1,0:T(8,128)(2,1)} %copy-done.4), custom_call_target="tpu_custom_call" | custom-call | tf_op jit(solution)/shard_map/pallas_call | solution.py:284
  (86 shorter events, 1.1 us)
Async XLA Ops:
  3.1 40.6 %all-to-all-start = ((bf16[32,24,512]{2,1,0:T(8,128)(2,1)}), bf16[32,24,512]{2,1,0:T(8,128)(2,1)S(1)}, u32[]{:S(2)}, u32[]{:S(2)}) async-start(bf16[32,24,512]{2,1,0:T(8,128)(2,1)} %get-tuple-element.56._), calls=%async_computation | async-start | bytes 1572864 | tf_op jit(solution)/shard_map/all_to_all | solution.py:407
  43.6 25.4 %copy-start.22 = (bf16[64,256]{1,0:T(8,128)(2,1)S(1)}, bf16[64,256]{1,0:T(8,128)(2,1)}, u32[]{:S(2)}) copy-start(bf16[64,256]{1,0:T(8,128)(2,1)} %get-tuple-element.70.p0) | copy-start | bytes 98308
  43.7 28.8 %copy-start.11 = (bf16[32,48,128]{2,1,0:T(8,128)(2,1)S(1)}, bf16[32,48,128]{2,1,0:T(8,128)(2,1)}, u32[]{:S(2)}) copy-start(bf16[32,48,128]{2,1,0:T(8,128)(2,1)} %get-tuple-element.81.f0) | copy-start | bytes 1179652
  43.7 39.6 %copy-start.1 = (bf16[32,24,512]{2,1,0:T(8,128)(2,1)}, bf16[32,24,512]{2,1,0:T(8,128)(2,1)S(1)}, u32[]{:S(2)}) copy-start(bf16[32,24,512]{2,1,0:T(8,128)(2,1)S(1)} %all-to-all-done) | copy-start | bytes 2359300
  44.5 13.7 %collective-permute-start.1 = (bf16[768,256]{1,0:T(8,128)(2,1)}, bf16[768,256]{1,0:T(8,128)(2,1)S(1)}, u32[]{:S(2)}, u32[]{:S(2)}) collective-permute-start(bf16[768,256]{1,0:T(8,128)(2,1)} %get-tuple-element.106), channel_id=1, source_target_pairs={{0,192},{64,0},{128,64},{192,128},{1,193},{65,1},{129,65},{193,129... | collective-permute-start | bytes 1179656 | tf_op jit(solution)/shard_map/ppermute | solution.py:368
  47.0 36.3 %all-to-all-start.1 = ((bf16[32,56,128]{2,1,0:T(8,128)(2,1)}), bf16[32,56,128]{2,1,0:T(8,128)(2,1)S(1)}, u32[]{:S(2)}, u32[]{:S(2)}) async-start(bf16[32,56,128]{2,1,0:T(8,128)(2,1)} %get-tuple-element.60), calls=%async_computation.1 | async-start | bytes 917504 | tf_op jit(solution)/shard_map/all_to_all | solution.py:412
  56.2 10.1 %collective-permute-start = (bf16[768,256]{1,0:T(8,128)(2,1)S(1)}, bf16[768,256]{1,0:T(8,128)(2,1)S(1)}, u32[]{:S(2)}, u32[]{:S(2)}) collective-permute-start(bf16[768,256]{1,0:T(8,128)(2,1)S(1)} %get-tuple-element.107), channel_id=1, source_target_pairs={{0,64},{64,128},{128,192},{192,0},{1,65},{65,129},{129,193},{193,1... | collective-permute-start | bytes 1179656 | tf_op jit(solution)/shard_map/ppermute | solution.py:368
  56.3 25.3 %collective-permute-start.2 = (bf16[768,512]{1,0:T(8,128)(2,1)S(1)}, bf16[768,512]{1,0:T(8,128)(2,1)S(1)}, u32[]{:S(2)}, u32[]{:S(2)}) collective-permute-start(bf16[768,512]{1,0:T(8,128)(2,1)S(1)} %bitcast.10), channel_id=1, source_target_pairs={{0,32},{32,0},{1,33},{33,1},{2,34},{34,2},{3,35},{35,3},{4,36},{36... | collective-permute-start | bytes 2359304 | tf_op jit(solution)/shard_map/ppermute | solution.py:378
  58.2 17.9 %copy-start.12 = (bf16[768,256]{1,0:T(8,128)(2,1)}, bf16[768,256]{1,0:T(8,128)(2,1)S(1)}, u32[]{:S(2)}) copy-start(bf16[768,256]{1,0:T(8,128)(2,1)S(1)} %collective-permute-done.1.w2) | copy-start | bytes 1179652
  58.2 17.9 %collective-permute-start.4 = (bf16[768,256]{1,0:T(8,128)(2,1)S(1)}, bf16[768,256]{1,0:T(8,128)(2,1)S(1)}, u32[]{:S(2)}, u32[]{:S(2)}) collective-permute-start(bf16[768,256]{1,0:T(8,128)(2,1)S(1)} %collective-permute-done.1.w2), channel_id=1, source_target_pairs={{0,32},{32,0},{1,33},{33,1},{2,34},{34,2},{3,35},{35,3},{4,36},{36... | collective-permute-start | bytes 1179656 | tf_op jit(solution)/shard_map/ppermute | solution.py:378
  66.3 15.3 %copy-start.13 = (bf16[768,256]{1,0:T(8,128)(2,1)}, bf16[768,256]{1,0:T(8,128)(2,1)S(1)}, u32[]{:S(2)}) copy-start(bf16[768,256]{1,0:T(8,128)(2,1)S(1)} %collective-permute-done.w1) | copy-start | bytes 1179652
  66.3 9.8 %collective-permute-start.3 = (bf16[768,256]{1,0:T(8,128)(2,1)S(1)}, bf16[768,256]{1,0:T(8,128)(2,1)S(1)}, u32[]{:S(2)}, u32[]{:S(2)}) collective-permute-start(bf16[768,256]{1,0:T(8,128)(2,1)S(1)} %collective-permute-done.w1), channel_id=1, source_target_pairs={{0,32},{32,0},{1,33},{33,1},{2,34},{34,2},{3,35},{35,3},{4,36},{36... | collective-permute-start | bytes 1179656 | tf_op jit(solution)/shard_map/ppermute | solution.py:378
  69.0 4.6 %collective-permute-start.7 = (bf16[64,256]{1,0:T(8,128)(2,1)S(1)}, bf16[64,256]{1,0:T(8,128)(2,1)S(1)}, u32[]{:S(2)}, u32[]{:S(2)}) collective-permute-start(bf16[64,256]{1,0:T(8,128)(2,1)S(1)} %copy-done.22), channel_id=1, source_target_pairs={{0,24},{8,0},{16,8},{24,16},{1,25},{9,1},{17,9},{25,17},{2,26},{10... | collective-permute-start | bytes 98312 | tf_op jit(solution)/shard_map/ppermute | solution.py:368
  72.4 15.6 %collective-permute-start.10 = (bf16[32,48,128]{2,1,0:T(8,128)(2,1)S(1)}, bf16[32,48,128]{2,1,0:T(8,128)(2,1)}, u32[]{:S(2)}, u32[]{:S(2)}) collective-permute-start(bf16[32,48,128]{2,1,0:T(8,128)(2,1)S(1)} %copy-done.11), channel_id=1, source_target_pairs={{0,4},{4,0},{1,5},{5,1},{2,6},{6,2},{3,7},{7,3},{8,12},{12,8},{9,1... | collective-permute-start | bytes 1179656 | tf_op jit(solution)/shard_map/ppermute | solution.py:378
  73.6 44.0 %copy-start.23 = (bf16[64,256]{1,0:T(8,128)(2,1)}, bf16[64,256]{1,0:T(8,128)(2,1)S(1)}, u32[]{:S(2)}) copy-start(bf16[64,256]{1,0:T(8,128)(2,1)S(1)} %collective-permute-done.7.p3) | copy-start | bytes 98308
  73.6 14.4 %collective-permute-start.9 = (bf16[32,48,128]{2,1,0:T(8,128)(2,1)S(1)}, bf16[32,48,128]{2,1,0:T(8,128)(2,1)S(1)}, u32[]{:S(2)}, u32[]{:S(2)}) collective-permute-start(bf16[32,48,128]{2,1,0:T(8,128)(2,1)S(1)} %copy-done.11), channel_id=1, source_target_pairs={{0,3},{1,0},{2,1},{3,2},{4,7},{5,4},{6,5},{7,6},{8,11},{9,8},{10,9... | collective-permute-start | bytes 1179656 | tf_op jit(solution)/shard_map/ppermute | solution.py:368
  76.1 5.6 %copy-start.14 = (bf16[768,256]{1,0:T(8,128)(2,1)}, bf16[768,256]{1,0:T(8,128)(2,1)S(1)}, u32[]{:S(2)}) copy-start(bf16[768,256]{1,0:T(8,128)(2,1)S(1)} %collective-permute-done.4.o2) | copy-start | bytes 1179652
  76.1 12.0 %collective-permute-start.8 = (bf16[32,48,128]{2,1,0:T(8,128)(2,1)S(1)}, bf16[32,48,128]{2,1,0:T(8,128)(2,1)S(1)}, u32[]{:S(2)}, u32[]{:S(2)}) collective-permute-start(bf16[32,48,128]{2,1,0:T(8,128)(2,1)S(1)} %copy-done.11), channel_id=1, source_target_pairs={{0,1},{1,2},{2,3},{3,0},{4,5},{5,6},{6,7},{7,4},{8,9},{9,10},{10,1... | collective-permute-start | bytes 1179656 | tf_op jit(solution)/shard_map/ppermute | solution.py:368
  76.2 11.9 %collective-permute-start.6 = (bf16[64,256]{1,0:T(8,128)(2,1)S(1)}, bf16[64,256]{1,0:T(8,128)(2,1)S(1)}, u32[]{:S(2)}, u32[]{:S(2)}) collective-permute-start(bf16[64,256]{1,0:T(8,128)(2,1)S(1)} %copy-done.22), channel_id=1, source_target_pairs={{0,16},{8,24},{16,0},{24,8},{1,17},{9,25},{17,1},{25,9},{2,18},{10... | collective-permute-start | bytes 98312 | tf_op jit(solution)/shard_map/ppermute | solution.py:368
  81.7 6.4 %collective-permute-start.5 = (bf16[64,256]{1,0:T(8,128)(2,1)S(1)}, bf16[64,256]{1,0:T(8,128)(2,1)S(1)}, u32[]{:S(2)}, u32[]{:S(2)}) collective-permute-start(bf16[64,256]{1,0:T(8,128)(2,1)S(1)} %copy-done.22), channel_id=1, source_target_pairs={{0,8},{8,16},{16,24},{24,0},{1,9},{9,17},{17,25},{25,1},{2,10},{10... | collective-permute-start | bytes 98312 | tf_op jit(solution)/shard_map/ppermute | solution.py:368
  88.0 29.1 %copy-start.27 = (s32[8]{0:T(128)S(1)}, s32[8]{0:T(128)}, u32[]{:S(2)}) copy-start(s32[8]{0:T(128)} %param.24) | copy-start | bytes 100
  88.0 29.7 %copy-start.24 = (bf16[64,256]{1,0:T(8,128)(2,1)}, bf16[64,256]{1,0:T(8,128)(2,1)S(1)}, u32[]{:S(2)}) copy-start(bf16[64,256]{1,0:T(8,128)(2,1)S(1)} %collective-permute-done.6.p2) | copy-start | bytes 98308
  88.0 29.6 %copy-start.25 = (bf16[64,256]{1,0:T(8,128)(2,1)}, bf16[64,256]{1,0:T(8,128)(2,1)S(1)}, u32[]{:S(2)}) copy-start(bf16[64,256]{1,0:T(8,128)(2,1)S(1)} %collective-permute-done.5.p1) | copy-start | bytes 98308
  88.1 35.5 %copy-start.5 = (bf16[32,48,128]{2,1,0:T(8,128)(2,1)}, bf16[32,48,128]{2,1,0:T(8,128)(2,1)S(1)}, u32[]{:S(2)}) copy-start(bf16[32,48,128]{2,1,0:T(8,128)(2,1)S(1)} %collective-permute-done.9.f3) | copy-start | bytes 1179652
  88.1 35.5 %copy-start.6 = (bf16[32,48,128]{2,1,0:T(8,128)(2,1)}, bf16[32,48,128]{2,1,0:T(8,128)(2,1)S(1)}, u32[]{:S(2)}) copy-start(bf16[32,48,128]{2,1,0:T(8,128)(2,1)S(1)} %collective-permute-done.8.f1) | copy-start | bytes 1179652
  88.1 37.3 %all-to-all-start.2 = ((bf16[32,128,128]{2,1,0:T(8,128)(2,1)}), bf16[32,128,128]{2,1,0:T(8,128)(2,1)S(1)}, u32[]{:S(2)}, u32[]{:S(2)}) async-start(bf16[32,128,128]{2,1,0:T(8,128)(2,1)} %shard_map.174), calls=%async_computation.2 | async-start | bytes 2097152 | tf_op jit(solution)/shard_map/all_to_all | solution.py:425
  94.1 18.1 %collective-permute-start.15 = (bf16[32,48,128]{2,1,0:T(8,128)(2,1)}, bf16[32,48,128]{2,1,0:T(8,128)(2,1)S(1)}, u32[]{:S(2)}, u32[]{:S(2)}) collective-permute-start(bf16[32,48,128]{2,1,0:T(8,128)(2,1)} %collective-permute-done.10.g0), channel_id=1, source_target_pairs={{0,3},{1,0},{2,1},{3,2},{4,7},{5,4},{6,5},{7,6},{8,11},{9,8},{10,9... | collective-permute-start | bytes 1179656 | tf_op jit(solution)/shard_map/ppermute | solution.py:368
  96.6 19.8 %collective-permute-start.13 = (bf16[32,48,128]{2,1,0:T(8,128)(2,1)}, bf16[32,48,128]{2,1,0:T(8,128)(2,1)S(1)}, u32[]{:S(2)}, u32[]{:S(2)}) collective-permute-start(bf16[32,48,128]{2,1,0:T(8,128)(2,1)} %collective-permute-done.10.g0), channel_id=1, source_target_pairs={{0,1},{1,2},{2,3},{3,0},{4,5},{5,6},{6,7},{7,4},{8,9},{9,10},{10,1... | collective-permute-start | bytes 1179656 | tf_op jit(solution)/shard_map/ppermute | solution.py:368
  98.0 25.6 %collective-permute-start.12 = (bf16[16,48,128]{2,1,0:T(8,128)(2,1)}, bf16[16,48,128]{2,1,0:T(8,128)(2,1)S(1)}, u32[]{:S(2)}, u32[]{:S(2)}) collective-permute-start(bf16[16,48,128]{2,1,0:T(8,128)(2,1)} %slice.21), channel_id=1, source_target_pairs={{0,3},{1,0},{2,1},{3,2},{4,7},{5,4},{6,5},{7,6},{8,11},{9,8},{10,9... | collective-permute-start | bytes 589832 | tf_op jit(solution)/shard_map/ppermute | solution.py:368
  100.7 23.0 %collective-permute-start.11 = (bf16[16,48,128]{2,1,0:T(8,128)(2,1)}, bf16[16,48,128]{2,1,0:T(8,128)(2,1)S(1)}, u32[]{:S(2)}, u32[]{:S(2)}) collective-permute-start(bf16[16,48,128]{2,1,0:T(8,128)(2,1)} %slice.20), channel_id=1, source_target_pairs={{0,1},{1,2},{2,3},{3,0},{4,5},{5,6},{6,7},{7,4},{8,9},{9,10},{10,1... | collective-permute-start | bytes 589832 | tf_op jit(solution)/shard_map/ppermute | solution.py:368
  112.2 11.5 %copy-start.7 = (bf16[32,48,128]{2,1,0:T(8,128)(2,1)}, bf16[32,48,128]{2,1,0:T(8,128)(2,1)S(1)}, u32[]{:S(2)}) copy-start(bf16[32,48,128]{2,1,0:T(8,128)(2,1)S(1)} %collective-permute-done.15.g3) | copy-start | bytes 1179652
  112.9 10.8 %collective-permute-start.16 = (bf16[16,48,128]{2,1,0:T(8,128)(2,1)}, bf16[16,48,128]{2,1,0:T(8,128)(2,1)S(1)}, u32[]{:S(2)}, u32[]{:S(2)}) collective-permute-start(bf16[16,48,128]{2,1,0:T(8,128)(2,1)} %slice.27), channel_id=1, source_target_pairs={{0,3},{1,0},{2,1},{3,2},{4,7},{5,4},{6,5},{7,6},{8,11},{9,8},{10,9... | collective-permute-start | bytes 589832 | tf_op jit(solution)/shard_map/ppermute | solution.py:368
  116.4 14.6 %copy-start.8 = (bf16[32,48,128]{2,1,0:T(8,128)(2,1)}, bf16[32,48,128]{2,1,0:T(8,128)(2,1)S(1)}, u32[]{:S(2)}) copy-start(bf16[32,48,128]{2,1,0:T(8,128)(2,1)S(1)} %collective-permute-done.13.g1) | copy-start | bytes 1179652
  117.1 8.3 %collective-permute-start.14 = (bf16[16,48,128]{2,1,0:T(8,128)(2,1)}, bf16[16,48,128]{2,1,0:T(8,128)(2,1)S(1)}, u32[]{:S(2)}, u32[]{:S(2)}) collective-permute-start(bf16[16,48,128]{2,1,0:T(8,128)(2,1)} %slice.26), channel_id=1, source_target_pairs={{0,1},{1,2},{2,3},{3,0},{4,5},{5,6},{6,7},{7,4},{8,9},{9,10},{10,1... | collective-permute-start | bytes 589832 | tf_op jit(solution)/shard_map/ppermute | solution.py:368
  123.6 10.9 %copy-start.16 = (bf16[16,48,128]{2,1,0:T(8,128)(2,1)}, bf16[16,48,128]{2,1,0:T(8,128)(2,1)S(1)}, u32[]{:S(2)}) copy-start(bf16[16,48,128]{2,1,0:T(8,128)(2,1)S(1)} %collective-permute-done.12.e2) | copy-start | bytes 589828
  123.7 10.9 %copy-start.17 = (bf16[16,48,128]{2,1,0:T(8,128)(2,1)}, bf16[16,48,128]{2,1,0:T(8,128)(2,1)S(1)}, u32[]{:S(2)}) copy-start(bf16[16,48,128]{2,1,0:T(8,128)(2,1)S(1)} %collective-permute-done.11.f2) | copy-start | bytes 589828
  123.7 10.9 %copy-start.18 = (bf16[16,48,128]{2,1,0:T(8,128)(2,1)}, bf16[16,48,128]{2,1,0:T(8,128)(2,1)S(1)}, u32[]{:S(2)}) copy-start(bf16[16,48,128]{2,1,0:T(8,128)(2,1)S(1)} %collective-permute-done.16.d2) | copy-start | bytes 589828
  125.4 9.1 %copy-start.19 = (bf16[16,48,128]{2,1,0:T(8,128)(2,1)}, bf16[16,48,128]{2,1,0:T(8,128)(2,1)S(1)}, u32[]{:S(2)}) copy-start(bf16[16,48,128]{2,1,0:T(8,128)(2,1)S(1)} %collective-permute-done.14.g2) | copy-start | bytes 589828
  131.0 16.9 %all-to-all-start.3 = ((bf16[8,160,256]{2,1,0:T(8,128)(2,1)}), bf16[8,160,256]{2,1,0:T(8,128)(2,1)S(1)}, u32[]{:S(2)}, u32[]{:S(2)}) async-start(bf16[8,160,256]{2,1,0:T(8,128)(2,1)} %get-tuple-element.93), calls=%async_computation.3 | async-start | bytes 1310720 | tf_op jit(solution)/shard_map/all_to_all | solution.py:436
  134.6 10.6 %copy-start.26 = (f32[64,128]{1,0:T(8,128)S(1)}, f32[64,128]{1,0:T(8,128)}, u32[]{:S(2)}) copy-start(f32[64,128]{1,0:T(8,128)} %get-tuple-element.95) | copy-start | bytes 98308
  134.6 11.8 %copy-start.21 = (f32[64,128]{1,0:T(8,128)S(1)}, f32[64,128]{1,0:T(8,128)}, u32[]{:S(2)}) copy-start(f32[64,128]{1,0:T(8,128)} %get-tuple-element.94) | copy-start | bytes 98308
  140.2 6.1 %collective-permute-start.17 = (f32[8,24,128]{2,1,0:T(8,128)}, f32[8,24,128]{2,1,0:T(8,128)S(1)}, u32[]{:S(2)}, u32[]{:S(2)}) collective-permute-start(f32[8,24,128]{2,1,0:T(8,128)} %get-tuple-element.92), channel_id=1, source_target_pairs={{0,32},{32,0},{1,33},{33,1},{2,34},{34,2},{3,35},{35,3},{4,36},{36... | collective-permute-start | bytes 294920 | tf_op jit(solution)/shard_map/ppermute | solution.py:378
  145.1 1.2 collective-permute-start.18
  147.9 10.8 %all-to-all-start.4 = ((f32[8,24,128]{2,1,0:T(8,128)}), f32[8,24,128]{2,1,0:T(8,128)S(1)}, u32[]{:S(2)}, u32[]{:S(2)}) async-start(f32[8,24,128]{2,1,0:T(8,128)} %add.20), calls=%async_computation.4 | async-start | bytes 196608 | tf_op jit(solution)/shard_map/all_to_all | solution.py:442
  158.7 5.4 %collective-permute-start.19 = (f32[256,128]{1,0:T(8,128)S(1)}, f32[256,128]{1,0:T(8,128)S(1)}, u32[]{:S(2)}, u32[]{:S(2)}) collective-permute-start(f32[256,128]{1,0:T(8,128)S(1)} %pad_maximum_fusion), channel_id=1, source_target_pairs={{0,64},{64,0},{128,192},{192,128},{1,65},{65,1},{129,193},{193,129... | collective-permute-start | bytes 393224 | tf_op jit(solution)/shard_map/ppermute | solution.py:382
  158.8 17.0 %all-to-all-start.5 = ((bf16[4,160,256]{2,1,0:T(8,128)(2,1)}), bf16[4,160,256]{2,1,0:T(8,128)(2,1)S(1)}, u32[]{:S(2)}, u32[]{:S(2)}) async-start(bf16[4,160,256]{2,1,0:T(8,128)(2,1)} %shard_map.178), calls=%async_computation.5 | async-start | bytes 655360 | tf_op jit(solution)/shard_map/all_to_all | solution.py:444
  164.1 5.1 %collective-permute-start.20 = (f32[256,128]{1,0:T(8,128)S(1)}, f32[256,128]{1,0:T(8,128)S(1)}, u32[]{:S(2)}, u32[]{:S(2)}) collective-permute-start(f32[256,128]{1,0:T(8,128)S(1)} %fusion), channel_id=1, source_target_pairs={{0,192},{192,0},{64,128},{128,64},{1,193},{193,1},{65,129},{129,65... | collective-permute-start | bytes 393224 | tf_op jit(solution)/shard_map/ppermute | solution.py:383
  169.3 4.1 %collective-permute-start.21 = (f32[256,128]{1,0:T(8,128)S(1)}, f32[256,128]{1,0:T(8,128)S(1)}, u32[]{:S(2)}, u32[]{:S(2)}) collective-permute-start(f32[256,128]{1,0:T(8,128)S(1)} %add.23.keep), channel_id=1, source_target_pairs={{0,32},{32,0},{1,33},{33,1},{2,34},{34,2},{3,35},{35,3},{4,36},{36... | collective-permute-start | bytes 393224 | tf_op jit(solution)/shard_map/ppermute | solution.py:378
  (8 other events, 19.8 us)

commit v8 on v7

--- a/solution.py
+++ b/solution.py
@@ -126,17 +126,20 @@
 
 
 def spread_kernel(
-    place, cols, live, logit_cot, p0, p1, p2, p3, tiles, out, cot, self_t, neigh_t, own, neigh
+    place, cols, live, logit_cot, pair, quad, tiles, out, cot, self_t, neigh_t, own, neigh
 ):
     classes, slots = logit_cot.shape
     lane = lax.broadcasted_iota(jnp.int32, (classes, slots), 1)
     kept = jnp.where(lane < live[0], logit_cot[...].astype(F32), 0.0)
     cot[...] = jnp.concatenate([kept, jnp.zeros((256 - classes, slots), F32)], axis=0).astype(BF)
     out[...] = jnp.zeros_like(out)
-    for s, part in enumerate((p0, p1, p2, p3)):
-        at = aligned(lax.rem(place[2] + 4 - s, 4), 32)
-        own[at, :] = part[0:32]
-        neigh[at, :] = part[32:64]
+    zq = place[2]
+    low, high = 2 * (zq // 2), 2 - 2 * (zq // 2)
+    odd = lax.rem(zq, 2)
+    for part, first in ((pair, low), (quad, high)):
+        for j, at in enumerate((first + odd, first + 1 - odd)):
+            own[aligned(at, 32), :] = part[64 * j : 64 * j + 32]
+            neigh[aligned(at, 32), :] = part[64 * j + 32 : 64 * j + 64]
     self_t[...] = own[...].astype(F32).T.astype(BF)
     neigh_t[...] = neigh[...].astype(F32).T.astype(BF)
     for r in range(tiles.shape[0]):
@@ -149,10 +152,10 @@
             out[cols[r, k]] += jnp.dot(back, tiles[r, k], preferred_element_type=F32)
 
 
-def spread(place, cols, live, logit_cot, pairs, tiles, blocks):
+def spread(place, cols, live, logit_cot, pair, quad, tiles, blocks):
     return pl.pallas_call(
         spread_kernel,
-        in_specs=[SMEM, SMEM, SMEM] + [VMEM] * 6,
+        in_specs=[SMEM, SMEM, SMEM] + [VMEM] * 4,
         out_specs=[VMEM] * 4,
         scratch_shapes=[pltpu.VMEM((TILE, 256), BF)] * 2,
         out_shape=[
@@ -163,7 +166,7 @@
         ],
         compiler_params=LIMIT,
         cost_estimate=pl.CostEstimate(flops=10**9, bytes_accessed=8 * 10**6, transcendentals=0),
-    )(place, cols, live.reshape(1), logit_cot, *pairs, tiles)
+    )(place, cols, live.reshape(1), logit_cot, pair, quad, tiles)
 
 
 def layer_kernel(place, got, w0, w1, w2, o0, o1, o2, out, mine, other):
@@ -378,11 +381,6 @@
     return lax.ppermute(value, axis, [(0, 1), (1, 0)])
 
 
-def sum_x(value):
-    value = value + lax.ppermute(value, "x", [(0, 1), (1, 0), (2, 3), (3, 2)])
-    return value + lax.ppermute(value, "x", [(0, 3), (3, 0), (1, 2), (2, 1)])
-
-
 def shards(
     feature_table,
     node_ids,
@@ -408,26 +406,33 @@
     send, feats = hop(
         place, feature_table, node_ids, hop_cols, hidden_bias, hop_tiles, packed
     )
-    weights, pair, send, feats = lax.optimization_barrier((weights, pair, send, feats))
+    peer = lax.ppermute(pair, "zq", [(0, 1), (1, 0), (2, 3), (3, 2)])
+    weights, pair, peer, send, feats = lax.optimization_barrier(
+        (weights, pair, peer, send, feats)
+    )
     got = lax.all_to_all(send, FEAT, 0, 0, tiled=True)
     weights = weights.reshape(-1, 512)
     mine = [weights, shift(weights[:, :256], "x", 1), shift(weights[:, 256:], "x", 3)]
+
+    mine, feats = lax.optimization_barrier((mine, feats))
     other = [swap(w, "core") for w in mine]
-
     twin = swap(feats, "zr")
     near = [shift(feats, "y", s) for s in (1, 3)]
-    pairs = [pair] + [shift(pair, "zq", s) for s in (1, 2, 3)]
+    pair = jnp.concatenate([pair, peer], axis=0)
+    quad = lax.ppermute(pair, "zq", [(0, 2), (2, 0), (1, 3), (3, 1)])
 
     hidden = layer(place, got, mine, other)
-    hidden, pairs, near, feats, twin = lax.optimization_barrier(
-        (hidden, pairs, near, feats, twin)
+    hidden, pair, quad, near, feats, twin = lax.optimization_barrier(
+        (hidden, pair, quad, near, feats, twin)
     )
     hidden = lax.all_to_all(hidden, FEAT, 0, 0, tiled=True)
-    feats = relay(feats, near) + relay(twin, [shift(twin, "y", s) for s in (1, 3)])
+    feats = relay(feats, near)
+    near = [shift(twin, "y", s) for s in (1, 3)]
     live = batch_sizes[lax.axis_index("x") * 2 + lax.axis_index("core")]
-    dhidden, cot, self_t, neigh_t = spread(
-        place, target_cols, live, logit_cotangent, pairs, target_tiles, blocks
-    )
+    ready = spread(place, target_cols, live, logit_cotangent, pair, quad, target_tiles, blocks)
+    ready, near = lax.optimization_barrier((ready, near))
+    dhidden, cot, self_t, neigh_t = ready
+    feats = feats + relay(twin, near)
     hidden, feats = lax.optimization_barrier((hidden, feats))
 
     scores, keep_head, send_head = score(
@@ -441,8 +446,10 @@
     keep, scores, keep_head = lax.optimization_barrier((keep, scores, keep_head))
     keep = lax.all_to_all(keep, ("zr", "y"), 0, 0, tiled=True)
     keep, scores = lax.optimization_barrier((keep, total(scores)))
+    keep = jnp.concatenate([keep.reshape(-1, TILE), keep_head], axis=0)
     scores = lax.all_to_all(scores, "zq", 0, 0, tiled=True)
-    keep = sum_x(jnp.concatenate([keep.reshape(-1, TILE), keep_head], axis=0))
+    keep = keep + lax.ppermute(keep, "x", [(0, 1), (1, 0), (2, 3), (3, 2)])
+    keep = keep + lax.ppermute(keep, "x", [(0, 3), (3, 0), (1, 2), (2, 1)])
     results = finish(place, keep, swap(keep, "core"), deep, classes)
     return (join(scores, classes), *results[:4], results[4].reshape(-1))
 

time: 179 us -> 171 us (0.955)
  starting transfers between devices: 79 us -> 70.4 us
    ppermute x13 -> x10, starting transfers between devices: 24.2 us -> 11.9 us  [shift(): return lax.ppermute(value, axis, [(i, (i + by) % 4) for i in range(4)])]
    ppermute x2 -> x4, starting transfers between devices: 0.19 us -> 8.44 us  [the longest x1 3.34 us: shards(): quad = lax.ppermute(pair, 'zq', [(0, 2), (2, 0), (1, 3), (3, 1)])]
    ppermute x7, starting transfers between devices: 13.1 us -> 10.1 us  [swap(): return lax.ppermute(value, axis, [(0, 1), (1, 0)])]
    slice x4, local copies, waits for them, and re-layouts: 2.81 us -> 0.06 us  [relay(): far = [shift(near[0][:half], 'y', 1), shift(near[1][half:], 'y', 3)]]
    unnamed x57 -> x54, local copies, waits for them, and re-layouts: 4.64 us -> 6.99 us
    ppermute x2 -> x4, waiting for transfers between devices: 5.02 us -> 7.2 us  [the longest x1 4.67 us: shards(): quad = lax.ppermute(pair, 'zq', [(0, 2), (2, 0), (1, 3), (3, 1)])]
    all_to_all x1, starting transfers between devices: 9.21 us -> 7.42 us  [shards(): got = lax.all_to_all(send, FEAT, 0, 0, tiled=True)]
    ppermute x13 -> x10, waiting for transfers between devices: 22.1 us -> 21 us  [shift(): return lax.ppermute(value, axis, [(i, (i + by) % 4) for i in range(4)])]
  transfers between devices with their start and end apart: 28 -> 27, of which waited for: 8 -> 12; matrix products, arithmetic and copies ran while one was open for 4% -> 2% of each run, Pallas kernels for 26% -> 27%
where the time goes in v8:
time: 171 us; the launch traced here: 170 us
  starting transfers between devices  70.4 us (41%)
  Pallas kernels  54.6 us (32%)
  waiting for transfers between devices  33.8 us (20%)
  local copies, waits for them, and re-layouts  8.31 us (5%)
    pallas_call x1, Pallas kernels, hop(): pl.pallas_call(hop_kernel, in_specs=[SMEM, SMEM, SMEM, VMEM, VMEM, HBM, H...  27.1 us
    ppermute x10, waiting for transfers between devices, shift(): return lax.ppermute(value, axis, [(i, (i + by) % 4) for i in range(4)])  21 us
    all_to_all x1, starting transfers between devices, shards(): weights = lax.all_to_all(packed, FEAT, 0, 0, tiled=True)  12 us
    ppermute x10, starting transfers between devices, shift(): return lax.ppermute(value, axis, [(i, (i + by) % 4) for i in range(4)])  11.9 us
    ppermute x7, starting transfers between devices, swap(): return lax.ppermute(value, axis, [(0, 1), (1, 0)])  10.1 us
    all_to_all x1, starting transfers between devices, shards(): got = lax.all_to_all(send, FEAT, 0, 0, tiled=True)  7.42 us
    unnamed x54, local copies, waits for them, and re-layouts  6.99 us
    pallas_call x1, Pallas kernels, spread(): pl.pallas_call(spread_kernel, in_specs=[SMEM, SMEM, SMEM] + [VMEM] * 4, o...  5.94 us
  transfers between devices with their start and end apart: 27, of which 12 were waited for; matrix products, arithmetic and copies ran while one was open for 2% of the time, Pallas kernels for 27%

profile of v8, /device:TPU:1, one launch (start us, length us, event | category | flops | bytes accessed | tf_op | source)
XLA Modules:
  0.0 169.6 jit_solution(502786369071422398)
XLA Ops:
  1.3 1.8 %shard_map.172 = (bf16[32,24,512]{2,1,0:T(8,128)(2,1)}, bf16[64,256]{1,0:T(8,128)(2,1)}) custom-call(s32[5]{0:T(128)} %stack.23.place, bf16[24,1024]{1,0:T(8,128)(2,1)} %own.1, bf16[24,1024]{1,0:T(8,128)(2,1)} %neigh.1, bf16[32,153]{1,0:T(8,128)(2,1)} %head_self.1, bf16[32,153]{1,0:T(8,128)(2,1)} %head_neigh.1), custom_call_target="tpu_custom_call" | custom-call | tf_op jit(solution)/shard_map/pallas_call | solution.py:116
  3.1 12.0 %all-to-all-start = ((bf16[32,24,512]{2,1,0:T(8,128)(2,1)}), bf16[32,24,512]{2,1,0:T(8,128)(2,1)S(1)}, u32[]{:S(2)}, u32[]{:S(2)}) async-start(bf16[32,24,512]{2,1,0:T(8,128)(2,1)} %get-tuple-element.65._), calls=%async_computation | async-start | bytes 1572864 | tf_op jit(solution)/shard_map/all_to_all | solution.py:405
  15.1 2.2 %collective-permute-start = (bf16[64,256]{1,0:T(8,128)(2,1)}, bf16[64,256]{1,0:T(8,128)(2,1)S(1)}, u32[]{:S(2)}, u32[]{:S(2)}) collective-permute-start(bf16[64,256]{1,0:T(8,128)(2,1)} %get-tuple-element.75), channel_id=1, source_target_pairs={{0,8},{8,0},{16,24},{24,16},{1,9},{9,1},{17,25},{25,17},{2,10},{10... | collective-permute-start | bytes 98312 | tf_op jit(solution)/shard_map/ppermute | solution.py:409
  17.3 1.4 copy.19.cols
  18.7 27.1 %shard_map.173 = (bf16[32,56,128]{2,1,0:T(8,128)(2,1)}, bf16[32,48,128]{2,1,0:T(8,128)(2,1)}) custom-call(s32[5]{0:T(128)} %stack.23.place, s32[16384]{0:T(1024)} %ids.1, s32[32,8]{1,0:T(8,128)} %copy.19.cols, bf16[24,32768]{1,0:T(8,128)(2,1)} %table.1, f32[1,32]{1,0:T(1,128)} %bitcast.14, bf16[32,8,128,128]{3,2,1,0:T(8,128)(2,1)} %tiles_hbm.1, ...), custom_call_target="tpu_custom_call" | custom-call | flops 1000000000 | bytes 60000000 | tf_op jit(solution)/shard_map/pallas_call | solution.py:84
  46.0 2.6 %collective-permute-start.2 = (bf16[768,256]{1,0:T(8,128)(2,1)S(1)}, bf16[768,256]{1,0:T(8,128)(2,1)}, u32[]{:S(2)}, u32[]{:S(2)}) collective-permute-start(bf16[768,256]{1,0:T(8,128)(2,1)S(1)} %get-tuple-element.124), channel_id=1, source_target_pairs={{0,192},{64,0},{128,64},{192,128},{1,193},{65,1},{129,65},{193,129... | collective-permute-start | bytes 1179656 | tf_op jit(solution)/shard_map/ppermute | solution.py:371
  48.5 7.4 %all-to-all-start.1 = ((bf16[32,56,128]{2,1,0:T(8,128)(2,1)}), bf16[32,56,128]{2,1,0:T(8,128)(2,1)S(1)}, u32[]{:S(2)}, u32[]{:S(2)}) async-start(bf16[32,56,128]{2,1,0:T(8,128)(2,1)} %get-tuple-element.69), calls=%async_computation.1 | async-start | bytes 917504 | tf_op jit(solution)/shard_map/all_to_all | solution.py:413
  56.0 2.6 %collective-permute-done.1.w1 = bf16[768,256]{1,0:T(8,128)(2,1)S(1)} collective-permute-done((bf16[768,256]{1,0:T(8,128)(2,1)S(1)}, bf16[768,256]{1,0:T(8,128)(2,1)S(1)}, u32[]{:S(2)}, u32[]{:S(2)}) %collective-permute-start.1) | collective-permute-done | bytes 393248 | tf_op jit(solution)/shard_map/ppermute | solution.py:371
  58.5 2.7 %collective-permute-start.3 = (bf16[768,512]{1,0:T(8,128)(2,1)S(1)}, bf16[768,512]{1,0:T(8,128)(2,1)S(1)}, u32[]{:S(2)}, u32[]{:S(2)}) collective-permute-start(bf16[768,512]{1,0:T(8,128)(2,1)S(1)} %bitcast.10), channel_id=1, source_target_pairs={{0,32},{32,0},{1,33},{33,1},{2,34},{34,2},{3,35},{35,3},{4,36},{36... | collective-permute-start | bytes 2359304 | tf_op jit(solution)/shard_map/ppermute | solution.py:381
  61.8 1.2 collective-permute-start.9
  63.0 2.4 %collective-permute-start.8 = (bf16[32,48,128]{2,1,0:T(8,128)(2,1)S(1)}, bf16[32,48,128]{2,1,0:T(8,128)(2,1)S(1)}, u32[]{:S(2)}, u32[]{:S(2)}) collective-permute-start(bf16[32,48,128]{2,1,0:T(8,128)(2,1)S(1)} %copy-done.11), channel_id=1, source_target_pairs={{0,3},{1,0},{2,1},{3,2},{4,7},{5,4},{6,5},{7,6},{8,11},{9,8},{10,9... | collective-permute-start | bytes 1179656 | tf_op jit(solution)/shard_map/ppermute | solution.py:371
  65.4 0.8 copy-done.13
  66.3 0.7 copy-done.14
  67.1 3.3 %collective-permute-start.6 = (bf16[128,256]{1,0:T(8,128)(2,1)S(1)}, bf16[128,256]{1,0:T(8,128)(2,1)S(1)}, u32[]{:S(2)}, u32[]{:S(2)}) collective-permute-start(bf16[128,256]{1,0:T(8,128)(2,1)S(1)} %constant_dynamic-update-slice_fusion.pair), channel_id=1, source_target_pairs={{0,16},{16,0},{8,24},{24,8},{1,17},{17,1},{9,25},{25,9},{2,18},{18... | collective-permute-start | bytes 196616 | tf_op jit(solution)/shard_map/ppermute | solution.py:422
  70.4 0.8 copy-done.3
  71.2 0.9 copy-done.9
  72.1 4.0 %shard_map.174 = bf16[32,128,128]{2,1,0:T(8,128)(2,1)} custom-call(s32[5]{0:T(128)} %stack.23.place, bf16[32,56,128]{2,1,0:T(8,128)(2,1)} %copy-done.3, bf16[768,512]{1,0:T(8,128)(2,1)} %bitcast.11, bf16[768,256]{1,0:T(8,128)(2,1)} %copy-done.12, bf16[768,256]{1,0:T(8,128)(2,1)} %collective-permute-done.2.w2, bf16[768,512]{1,0:T(8,128)(2,1)} %copy-done.9, ...), custom_call_target="tpu_custom_call" | custom-call | tf_op jit(solution)/shard_map/pallas_call | solution.py:206
  76.0 4.7 %collective-permute-done.6.quad = bf16[128,256]{1,0:T(8,128)(2,1)S(1)} collective-permute-done((bf16[128,256]{1,0:T(8,128)(2,1)S(1)}, bf16[128,256]{1,0:T(8,128)(2,1)S(1)}, u32[]{:S(2)}, u32[]{:S(2)}) %collective-permute-start.6) | collective-permute-done | bytes 65568 | tf_op jit(solution)/shard_map/ppermute | solution.py:422
  80.7 5.8 %all-to-all-start.2 = ((bf16[32,128,128]{2,1,0:T(8,128)(2,1)}), bf16[32,128,128]{2,1,0:T(8,128)(2,1)S(1)}, u32[]{:S(2)}, u32[]{:S(2)}) async-start(bf16[32,128,128]{2,1,0:T(8,128)(2,1)} %shard_map.174), calls=%async_computation.2 | async-start | bytes 2097152 | tf_op jit(solution)/shard_map/all_to_all | solution.py:428
  86.5 2.5 %collective-permute-start.13 = (bf16[32,48,128]{2,1,0:T(8,128)(2,1)}, bf16[32,48,128]{2,1,0:T(8,128)(2,1)S(1)}, u32[]{:S(2)}, u32[]{:S(2)}) collective-permute-start(bf16[32,48,128]{2,1,0:T(8,128)(2,1)} %collective-permute-done.9.g0), channel_id=1, source_target_pairs={{0,3},{1,0},{2,1},{3,2},{4,7},{5,4},{6,5},{7,6},{8,11},{9,8},{10,9... | collective-permute-start | bytes 1179656 | tf_op jit(solution)/shard_map/ppermute | solution.py:371
  89.7 2.8 %collective-permute-start.11 = (bf16[16,48,128]{2,1,0:T(8,128)(2,1)S(1)}, bf16[16,48,128]{2,1,0:T(8,128)(2,1)S(1)}, u32[]{:S(2)}, u32[]{:S(2)}) collective-permute-start(bf16[16,48,128]{2,1,0:T(8,128)(2,1)S(1)} %slice.21), channel_id=1, source_target_pairs={{0,3},{1,0},{2,1},{3,2},{4,7},{5,4},{6,5},{7,6},{8,11},{9,8},{10,9... | collective-permute-start | bytes 589832 | tf_op jit(solution)/shard_map/ppermute | solution.py:371
  92.5 5.9 %shard_map.175 = (f32[32,128,128]{2,1,0:T(8,128)}, bf16[256,1024]{1,0:T(8,128)(2,1)}, bf16[256,128]{1,0:T(8,128)(2,1)}, bf16[256,128]{1,0:T(8,128)(2,1)}) custom-call(s32[5]{0:T(128)} %stack.23.place, s32[8,8]{1,0:T(8,128)} %cols.4, s32[1]{0:T(128)} %dynamic_slice.3.live, bf16[153,1024]{1,0:T(8,128)(2,1)} %logit_cot.1, bf16[128,256]{1,0:T(8,128)(2,1)} %copy-done.22, ...), custom_call_target="tpu_custom_call" | custom-call | flops 1000000000 | bytes 8000000 | tf_op jit(solution)/shard_map/pallas_call | solution.py:156
  98.4 6.1 %collective-permute-done.13.g3 = bf16[32,48,128]{2,1,0:T(8,128)(2,1)S(1)} collective-permute-done((bf16[32,48,128]{2,1,0:T(8,128)(2,1)}, bf16[32,48,128]{2,1,0:T(8,128)(2,1)S(1)}, u32[]{:S(2)}, u32[]{:S(2)}) %collective-permute-start.13) | collective-permute-done | bytes 393248 | tf_op jit(solution)/shard_map/ppermute | solution.py:371
  104.5 2.7 %collective-permute-done.12.g1 = bf16[32,48,128]{2,1,0:T(8,128)(2,1)S(1)} collective-permute-done((bf16[32,48,128]{2,1,0:T(8,128)(2,1)}, bf16[32,48,128]{2,1,0:T(8,128)(2,1)S(1)}, u32[]{:S(2)}, u32[]{:S(2)}) %collective-permute-start.12) | collective-permute-done | bytes 393248 | tf_op jit(solution)/shard_map/ppermute | solution.py:371
  107.3 0.9 collective-permute-start.15
  108.2 0.7 collective-permute-start.14
  108.8 2.1 %collective-permute-done.11.e2 = bf16[16,48,128]{2,1,0:T(8,128)(2,1)S(1)} collective-permute-done((bf16[16,48,128]{2,1,0:T(8,128)(2,1)S(1)}, bf16[16,48,128]{2,1,0:T(8,128)(2,1)S(1)}, u32[]{:S(2)}, u32[]{:S(2)}) %collective-permute-start.11) | collective-permute-done | bytes 196640 | tf_op jit(solution)/shard_map/ppermute | solution.py:371
  110.9 3.9 %collective-permute-done.10.f2 = bf16[16,48,128]{2,1,0:T(8,128)(2,1)S(1)} collective-permute-done((bf16[16,48,128]{2,1,0:T(8,128)(2,1)S(1)}, bf16[16,48,128]{2,1,0:T(8,128)(2,1)S(1)}, u32[]{:S(2)}, u32[]{:S(2)}) %collective-permute-start.10) | collective-permute-done | bytes 196640 | tf_op jit(solution)/shard_map/ppermute | solution.py:371
  115.4 3.0 %collective-permute-done.14.g2 = bf16[16,48,128]{2,1,0:T(8,128)(2,1)S(1)} collective-permute-done((bf16[16,48,128]{2,1,0:T(8,128)(2,1)S(1)}, bf16[16,48,128]{2,1,0:T(8,128)(2,1)S(1)}, u32[]{:S(2)}, u32[]{:S(2)}) %collective-permute-start.14) | collective-permute-done | bytes 196640 | tf_op jit(solution)/shard_map/ppermute | solution.py:371
  118.4 1.0 copy-done
  119.4 4.5 %shard_map.176 = (bf16[8,160,256]{2,1,0:T(8,128)(2,1)}, f32[64,128]{1,0:T(8,128)}, f32[64,128]{1,0:T(8,128)}) custom-call(s32[5]{0:T(128)} %stack.23.place, s32[8,8]{1,0:T(8,128)} %cols.4, bf16[32,128,128]{2,1,0:T(8,128)(2,1)} %copy-done, f32[32,128,128]{2,1,0:T(8,128)} %get-tuple-element.92.dhidden, bf16[8,8,128,128]{3,2,1,0:T(8,128)(2,1)} %tiles.3, ...), custom_call_target="tpu_custom_call" | custom-call | tf_op jit(solution)/shard_map/pallas_call | solution.py:252
  123.9 3.6 %all-to-all-start.3 = ((bf16[8,160,256]{2,1,0:T(8,128)(2,1)}), bf16[8,160,256]{2,1,0:T(8,128)(2,1)S(1)}, u32[]{:S(2)}, u32[]{:S(2)}) async-start(bf16[8,160,256]{2,1,0:T(8,128)(2,1)} %get-tuple-element.111), calls=%async_computation.3 | async-start | bytes 1310720 | tf_op jit(solution)/shard_map/all_to_all | solution.py:441
  127.6 5.6 %shard_map.177 = (f32[8,24,128]{2,1,0:T(8,128)}, f32[8,24,128]{2,1,0:T(8,128)}) custom-call(s32[5]{0:T(128)} %stack.23.place, bf16[32,128,128]{2,1,0:T(8,128)(2,1)} %copy-done, f32[32,128,128]{2,1,0:T(8,128)} %get-tuple-element.92.dhidden, bf16[32,48,128]{2,1,0:T(8,128)(2,1)} %get-tuple-element.99.f0, bf16[32,48,128]{2,1,0:T(8,128)(2,1)} %copy-done.6, ...), custom_call_target="tpu_custom_call" | custom-call | flops 1000000000 | bytes 7000000 | tf_op jit(solution)/shard_map/pallas_call | solution.py:326
  133.2 2.2 %collective-permute-start.16 = (f32[8,24,128]{2,1,0:T(8,128)}, f32[8,24,128]{2,1,0:T(8,128)S(1)}, u32[]{:S(2)}, u32[]{:S(2)}) collective-permute-start(f32[8,24,128]{2,1,0:T(8,128)} %get-tuple-element.110), channel_id=1, source_target_pairs={{0,32},{32,0},{1,33},{33,1},{2,34},{34,2},{3,35},{35,3},{4,36},{36... | collective-permute-start | bytes 294920 | tf_op jit(solution)/shard_map/ppermute | solution.py:381
  135.5 1.1 collective-permute-done.17
  136.7 1.5 add.20
  138.2 5.3 %all-to-all-start.4 = ((f32[8,24,128]{2,1,0:T(8,128)}), f32[8,24,128]{2,1,0:T(8,128)S(1)}, u32[]{:S(2)}, u32[]{:S(2)}) async-start(f32[8,24,128]{2,1,0:T(8,128)} %add.20), calls=%async_computation.4 | async-start | bytes 196608 | tf_op jit(solution)/shard_map/all_to_all | solution.py:447
  143.6 1.9 %shard_map.178 = bf16[4,160,256]{2,1,0:T(8,128)(2,1)} custom-call(bf16[8,160,256]{2,1,0:T(8,128)(2,1)} %copy-done.2), custom_call_target="tpu_custom_call" | custom-call | tf_op jit(solution)/shard_map/pallas_call | solution.py:271
  145.5 3.5 %all-to-all-done.4 = f32[8,24,128]{2,1,0:T(8,128)S(1)} async-done(((f32[8,24,128]{2,1,0:T(8,128)}), f32[8,24,128]{2,1,0:T(8,128)S(1)}, u32[]{:S(2)}, u32[]{:S(2)}) %all-to-all-start.4) | async-done | bytes 98336 | tf_op jit(solution)/shard_map/all_to_all | solution.py:447
  149.2 5.7 %all-to-all-start.5 = ((bf16[4,160,256]{2,1,0:T(8,128)(2,1)}), bf16[4,160,256]{2,1,0:T(8,128)(2,1)S(1)}, u32[]{:S(2)}, u32[]{:S(2)}) async-start(bf16[4,160,256]{2,1,0:T(8,128)(2,1)} %shard_map.178), calls=%async_computation.5 | async-start | bytes 655360 | tf_op jit(solution)/shard_map/all_to_all | solution.py:450
  155.0 2.6 %collective-permute-start.19 = (f32[256,128]{1,0:T(8,128)S(1)}, f32[256,128]{1,0:T(8,128)S(1)}, u32[]{:S(2)}, u32[]{:S(2)}) collective-permute-start(f32[256,128]{1,0:T(8,128)S(1)} %fusion), channel_id=1, source_target_pairs={{0,192},{192,0},{64,128},{128,64},{1,193},{193,1},{65,129},{129,65... | collective-permute-start | bytes 393224 | tf_op jit(solution)/shard_map/ppermute | solution.py:452
  157.6 2.5 %collective-permute-done.19 = f32[256,128]{1,0:T(8,128)S(1)} collective-permute-done((f32[256,128]{1,0:T(8,128)S(1)}, f32[256,128]{1,0:T(8,128)S(1)}, u32[]{:S(2)}, u32[]{:S(2)}) %collective-permute-start.19) | collective-permute-done | bytes 131104 | tf_op jit(solution)/shard_map/ppermute | solution.py:452
  160.1 3.4 %collective-permute-start.20 = (f32[256,128]{1,0:T(8,128)S(1)}, f32[256,128]{1,0:T(8,128)S(1)}, u32[]{:S(2)}, u32[]{:S(2)}) collective-permute-start(f32[256,128]{1,0:T(8,128)S(1)} %add.23.keep), channel_id=1, source_target_pairs={{0,32},{32,0},{1,33},{33,1},{2,34},{34,2},{3,35},{35,3},{4,36},{36... | collective-permute-start | bytes 393224 | tf_op jit(solution)/shard_map/ppermute | solution.py:381
  163.5 1.0 collective-permute-done.20.rest
  164.5 0.6 copy-done.19
  165.2 1.9 %shard_map.180 = (f32[24,1024]{1,0:T(8,128)}, f32[24,1024]{1,0:T(8,128)}, f32[32,153]{1,0:T(8,128)}, f32[32,153]{1,0:T(8,128)}, f32[1,32]{1,0:T(1,128)}) custom-call(s32[5]{0:T(128)} %stack.23.place, f32[256,128]{1,0:T(8,128)} %copy-done.10, f32[256,128]{1,0:T(8,128)} %copy-done.19), custom_call_target="tpu_custom_call" | custom-call | tf_op jit(solution)/shard_map/pallas_call | solution.py:361
  167.0 0.7 copy-done.4
  167.7 1.9 %shard_map.179 = f32[153,1024]{1,0:T(8,128)} custom-call(bf16[4,160,256]{2,1,0:T(8,128)(2,1)} %copy-done.4), custom_call_target="tpu_custom_call" | custom-call | tf_op jit(solution)/shard_map/pallas_call | solution.py:287
  (82 shorter events, 3.1 us)
Async XLA Ops:
  3.1 42.8 %all-to-all-start = ((bf16[32,24,512]{2,1,0:T(8,128)(2,1)}), bf16[32,24,512]{2,1,0:T(8,128)(2,1)S(1)}, u32[]{:S(2)}, u32[]{:S(2)}) async-start(bf16[32,24,512]{2,1,0:T(8,128)(2,1)} %get-tuple-element.65._), calls=%async_computation | async-start | bytes 1572864 | tf_op jit(solution)/shard_map/all_to_all | solution.py:405
  15.1 30.7 %collective-permute-start = (bf16[64,256]{1,0:T(8,128)(2,1)}, bf16[64,256]{1,0:T(8,128)(2,1)S(1)}, u32[]{:S(2)}, u32[]{:S(2)}) collective-permute-start(bf16[64,256]{1,0:T(8,128)(2,1)} %get-tuple-element.75), channel_id=1, source_target_pairs={{0,8},{8,0},{16,24},{24,16},{1,9},{9,1},{17,25},{25,17},{2,10},{10... | collective-permute-start | bytes 98312 | tf_op jit(solution)/shard_map/ppermute | solution.py:409
  45.8 15.9 %copy-start.11 = (bf16[32,48,128]{2,1,0:T(8,128)(2,1)S(1)}, bf16[32,48,128]{2,1,0:T(8,128)(2,1)}, u32[]{:S(2)}) copy-start(bf16[32,48,128]{2,1,0:T(8,128)(2,1)} %get-tuple-element.99.f0) | copy-start | bytes 1179652
  45.9 20.4 %copy-start.21 = (bf16[64,256]{1,0:T(8,128)(2,1)S(1)}, bf16[64,256]{1,0:T(8,128)(2,1)}, u32[]{:S(2)}) copy-start(bf16[64,256]{1,0:T(8,128)(2,1)} %get-tuple-element.75) | copy-start | bytes 98308
  45.9 24.5 %copy-start.1 = (bf16[32,24,512]{2,1,0:T(8,128)(2,1)}, bf16[32,24,512]{2,1,0:T(8,128)(2,1)S(1)}, u32[]{:S(2)}) copy-start(bf16[32,24,512]{2,1,0:T(8,128)(2,1)S(1)} %all-to-all-done) | copy-start | bytes 2359300
  46.0 10.0 %collective-permute-start.2 = (bf16[768,256]{1,0:T(8,128)(2,1)S(1)}, bf16[768,256]{1,0:T(8,128)(2,1)}, u32[]{:S(2)}, u32[]{:S(2)}) collective-permute-start(bf16[768,256]{1,0:T(8,128)(2,1)S(1)} %get-tuple-element.124), channel_id=1, source_target_pairs={{0,192},{64,0},{128,64},{192,128},{1,193},{65,1},{129,65},{193,129... | collective-permute-start | bytes 1179656 | tf_op jit(solution)/shard_map/ppermute | solution.py:371
  48.5 10.0 %collective-permute-start.1 = (bf16[768,256]{1,0:T(8,128)(2,1)S(1)}, bf16[768,256]{1,0:T(8,128)(2,1)S(1)}, u32[]{:S(2)}, u32[]{:S(2)}) collective-permute-start(bf16[768,256]{1,0:T(8,128)(2,1)S(1)} %get-tuple-element.125), channel_id=1, source_target_pairs={{0,64},{64,128},{128,192},{192,0},{1,65},{65,129},{129,193},{193,1... | collective-permute-start | bytes 1179656 | tf_op jit(solution)/shard_map/ppermute | solution.py:371
  48.5 21.9 %all-to-all-start.1 = ((bf16[32,56,128]{2,1,0:T(8,128)(2,1)}), bf16[32,56,128]{2,1,0:T(8,128)(2,1)S(1)}, u32[]{:S(2)}, u32[]{:S(2)}) async-start(bf16[32,56,128]{2,1,0:T(8,128)(2,1)} %get-tuple-element.69), calls=%async_computation.1 | async-start | bytes 917504 | tf_op jit(solution)/shard_map/all_to_all | solution.py:413
  58.5 6.8 %copy-start.12 = (bf16[768,256]{1,0:T(8,128)(2,1)}, bf16[768,256]{1,0:T(8,128)(2,1)S(1)}, u32[]{:S(2)}) copy-start(bf16[768,256]{1,0:T(8,128)(2,1)S(1)} %collective-permute-done.1.w1) | copy-start | bytes 1179652
  58.5 11.9 %collective-permute-start.3 = (bf16[768,512]{1,0:T(8,128)(2,1)S(1)}, bf16[768,512]{1,0:T(8,128)(2,1)S(1)}, u32[]{:S(2)}, u32[]{:S(2)}) collective-permute-start(bf16[768,512]{1,0:T(8,128)(2,1)S(1)} %bitcast.10), channel_id=1, source_target_pairs={{0,32},{32,0},{1,33},{33,1},{2,34},{34,2},{3,35},{35,3},{4,36},{36... | collective-permute-start | bytes 2359304 | tf_op jit(solution)/shard_map/ppermute | solution.py:381
  61.3 4.1 %collective-permute-start.4 = (bf16[768,256]{1,0:T(8,128)(2,1)S(1)}, bf16[768,256]{1,0:T(8,128)(2,1)S(1)}, u32[]{:S(2)}, u32[]{:S(2)}) collective-permute-start(bf16[768,256]{1,0:T(8,128)(2,1)S(1)} %collective-permute-done.1.w1), channel_id=1, source_target_pairs={{0,32},{32,0},{1,33},{33,1},{2,34},{34,2},{3,35},{35,3},{4,36},{36... | collective-permute-start | bytes 1179656 | tf_op jit(solution)/shard_map/ppermute | solution.py:381
  61.3 5.0 %collective-permute-start.5 = (bf16[768,256]{1,0:T(8,128)(2,1)}, bf16[768,256]{1,0:T(8,128)(2,1)S(1)}, u32[]{:S(2)}, u32[]{:S(2)}) collective-permute-start(bf16[768,256]{1,0:T(8,128)(2,1)} %collective-permute-done.2.w2), channel_id=1, source_target_pairs={{0,32},{32,0},{1,33},{33,1},{2,34},{34,2},{3,35},{35,3},{4,36},{36... | collective-permute-start | bytes 1179656 | tf_op jit(solution)/shard_map/ppermute | solution.py:381
  61.8 18.9 %collective-permute-start.9 = (bf16[32,48,128]{2,1,0:T(8,128)(2,1)S(1)}, bf16[32,48,128]{2,1,0:T(8,128)(2,1)}, u32[]{:S(2)}, u32[]{:S(2)}) collective-permute-start(bf16[32,48,128]{2,1,0:T(8,128)(2,1)S(1)} %copy-done.11), channel_id=1, source_target_pairs={{0,4},{4,0},{1,5},{5,1},{2,6},{6,2},{3,7},{7,3},{8,12},{12,8},{9,1... | collective-permute-start | bytes 1179656 | tf_op jit(solution)/shard_map/ppermute | solution.py:381
  63.0 17.7 %collective-permute-start.8 = (bf16[32,48,128]{2,1,0:T(8,128)(2,1)S(1)}, bf16[32,48,128]{2,1,0:T(8,128)(2,1)S(1)}, u32[]{:S(2)}, u32[]{:S(2)}) collective-permute-start(bf16[32,48,128]{2,1,0:T(8,128)(2,1)S(1)} %copy-done.11), channel_id=1, source_target_pairs={{0,3},{1,0},{2,1},{3,2},{4,7},{5,4},{6,5},{7,6},{8,11},{9,8},{10,9... | collective-permute-start | bytes 1179656 | tf_op jit(solution)/shard_map/ppermute | solution.py:371
  66.1 14.6 %collective-permute-start.7 = (bf16[32,48,128]{2,1,0:T(8,128)(2,1)S(1)}, bf16[32,48,128]{2,1,0:T(8,128)(2,1)S(1)}, u32[]{:S(2)}, u32[]{:S(2)}) collective-permute-start(bf16[32,48,128]{2,1,0:T(8,128)(2,1)S(1)} %copy-done.11), channel_id=1, source_target_pairs={{0,1},{1,2},{2,3},{3,0},{4,5},{5,6},{6,7},{7,4},{8,9},{9,10},{10,1... | collective-permute-start | bytes 1179656 | tf_op jit(solution)/shard_map/ppermute | solution.py:371
  66.3 26.2 %copy-start.22 = (bf16[128,256]{1,0:T(8,128)(2,1)}, bf16[128,256]{1,0:T(8,128)(2,1)S(1)}, u32[]{:S(2)}) copy-start(bf16[128,256]{1,0:T(8,128)(2,1)S(1)} %constant_dynamic-update-slice_fusion.pair) | copy-start | bytes 196612
  67.1 13.6 %collective-permute-start.6 = (bf16[128,256]{1,0:T(8,128)(2,1)S(1)}, bf16[128,256]{1,0:T(8,128)(2,1)S(1)}, u32[]{:S(2)}, u32[]{:S(2)}) collective-permute-start(bf16[128,256]{1,0:T(8,128)(2,1)S(1)} %constant_dynamic-update-slice_fusion.pair), channel_id=1, source_target_pairs={{0,16},{16,0},{8,24},{24,8},{1,17},{17,1},{9,25},{25,9},{2,18},{18... | collective-permute-start | bytes 196616 | tf_op jit(solution)/shard_map/ppermute | solution.py:422
  71.2 0.9 copy-start.9
  76.0 13.1 %copy-start.25 = (s32[8]{0:T(128)S(1)}, s32[8]{0:T(128)}, u32[]{:S(2)}) copy-start(s32[8]{0:T(128)} %param.24) | copy-start | bytes 100
  80.7 11.8 %copy-start.23 = (bf16[128,256]{1,0:T(8,128)(2,1)}, bf16[128,256]{1,0:T(8,128)(2,1)S(1)}, u32[]{:S(2)}) copy-start(bf16[128,256]{1,0:T(8,128)(2,1)S(1)} %collective-permute-done.6.quad) | copy-start | bytes 196612
  80.7 17.7 %copy-start.5 = (bf16[32,48,128]{2,1,0:T(8,128)(2,1)}, bf16[32,48,128]{2,1,0:T(8,128)(2,1)S(1)}, u32[]{:S(2)}) copy-start(bf16[32,48,128]{2,1,0:T(8,128)(2,1)S(1)} %collective-permute-done.8.f3) | copy-start | bytes 1179652
  80.7 17.7 %copy-start.6 = (bf16[32,48,128]{2,1,0:T(8,128)(2,1)}, bf16[32,48,128]{2,1,0:T(8,128)(2,1)S(1)}, u32[]{:S(2)}) copy-start(bf16[32,48,128]{2,1,0:T(8,128)(2,1)S(1)} %collective-permute-done.7.f1) | copy-start | bytes 1179652
  80.7 37.7 %all-to-all-start.2 = ((bf16[32,128,128]{2,1,0:T(8,128)(2,1)}), bf16[32,128,128]{2,1,0:T(8,128)(2,1)S(1)}, u32[]{:S(2)}, u32[]{:S(2)}) async-start(bf16[32,128,128]{2,1,0:T(8,128)(2,1)} %shard_map.174), calls=%async_computation.2 | async-start | bytes 2097152 | tf_op jit(solution)/shard_map/all_to_all | solution.py:428
  86.5 18.0 %collective-permute-start.13 = (bf16[32,48,128]{2,1,0:T(8,128)(2,1)}, bf16[32,48,128]{2,1,0:T(8,128)(2,1)S(1)}, u32[]{:S(2)}, u32[]{:S(2)}) collective-permute-start(bf16[32,48,128]{2,1,0:T(8,128)(2,1)} %collective-permute-done.9.g0), channel_id=1, source_target_pairs={{0,3},{1,0},{2,1},{3,2},{4,7},{5,4},{6,5},{7,6},{8,11},{9,8},{10,9... | collective-permute-start | bytes 1179656 | tf_op jit(solution)/shard_map/ppermute | solution.py:371
  89.1 18.2 %collective-permute-start.12 = (bf16[32,48,128]{2,1,0:T(8,128)(2,1)}, bf16[32,48,128]{2,1,0:T(8,128)(2,1)S(1)}, u32[]{:S(2)}, u32[]{:S(2)}) collective-permute-start(bf16[32,48,128]{2,1,0:T(8,128)(2,1)} %collective-permute-done.9.g0), channel_id=1, source_target_pairs={{0,1},{1,2},{2,3},{3,0},{4,5},{5,6},{6,7},{7,4},{8,9},{9,10},{10,1... | collective-permute-start | bytes 1179656 | tf_op jit(solution)/shard_map/ppermute | solution.py:371
  89.7 21.2 %collective-permute-start.11 = (bf16[16,48,128]{2,1,0:T(8,128)(2,1)S(1)}, bf16[16,48,128]{2,1,0:T(8,128)(2,1)S(1)}, u32[]{:S(2)}, u32[]{:S(2)}) collective-permute-start(bf16[16,48,128]{2,1,0:T(8,128)(2,1)S(1)} %slice.21), channel_id=1, source_target_pairs={{0,3},{1,0},{2,1},{3,2},{4,7},{5,4},{6,5},{7,6},{8,11},{9,8},{10,9... | collective-permute-start | bytes 589832 | tf_op jit(solution)/shard_map/ppermute | solution.py:371
  92.4 22.3 %collective-permute-start.10 = (bf16[16,48,128]{2,1,0:T(8,128)(2,1)S(1)}, bf16[16,48,128]{2,1,0:T(8,128)(2,1)S(1)}, u32[]{:S(2)}, u32[]{:S(2)}) collective-permute-start(bf16[16,48,128]{2,1,0:T(8,128)(2,1)S(1)} %slice.20), channel_id=1, source_target_pairs={{0,1},{1,2},{2,3},{3,0},{4,5},{5,6},{6,7},{7,4},{8,9},{9,10},{10,1... | collective-permute-start | bytes 589832 | tf_op jit(solution)/shard_map/ppermute | solution.py:371
  104.5 19.4 %copy-start.7 = (bf16[32,48,128]{2,1,0:T(8,128)(2,1)}, bf16[32,48,128]{2,1,0:T(8,128)(2,1)S(1)}, u32[]{:S(2)}) copy-start(bf16[32,48,128]{2,1,0:T(8,128)(2,1)S(1)} %collective-permute-done.13.g3) | copy-start | bytes 1179652
  107.2 16.7 %copy-start.8 = (bf16[32,48,128]{2,1,0:T(8,128)(2,1)}, bf16[32,48,128]{2,1,0:T(8,128)(2,1)S(1)}, u32[]{:S(2)}) copy-start(bf16[32,48,128]{2,1,0:T(8,128)(2,1)S(1)} %collective-permute-done.12.g1) | copy-start | bytes 1179652
  107.3 8.1 %collective-permute-start.15 = (bf16[16,48,128]{2,1,0:T(8,128)(2,1)S(1)}, bf16[16,48,128]{2,1,0:T(8,128)(2,1)S(1)}, u32[]{:S(2)}, u32[]{:S(2)}) collective-permute-start(bf16[16,48,128]{2,1,0:T(8,128)(2,1)S(1)} %slice.23), channel_id=1, source_target_pairs={{0,3},{1,0},{2,1},{3,2},{4,7},{5,4},{6,5},{7,6},{8,11},{9,8},{10,9... | collective-permute-start | bytes 589832 | tf_op jit(solution)/shard_map/ppermute | solution.py:371
  108.2 10.2 %collective-permute-start.14 = (bf16[16,48,128]{2,1,0:T(8,128)(2,1)S(1)}, bf16[16,48,128]{2,1,0:T(8,128)(2,1)S(1)}, u32[]{:S(2)}, u32[]{:S(2)}) collective-permute-start(bf16[16,48,128]{2,1,0:T(8,128)(2,1)S(1)} %slice.22), channel_id=1, source_target_pairs={{0,1},{1,2},{2,3},{3,0},{4,5},{5,6},{6,7},{7,4},{8,9},{9,10},{10,1... | collective-permute-start | bytes 589832 | tf_op jit(solution)/shard_map/ppermute | solution.py:371
  110.9 16.6 %copy-start.15 = (bf16[16,48,128]{2,1,0:T(8,128)(2,1)}, bf16[16,48,128]{2,1,0:T(8,128)(2,1)S(1)}, u32[]{:S(2)}) copy-start(bf16[16,48,128]{2,1,0:T(8,128)(2,1)S(1)} %collective-permute-done.11.e2) | copy-start | bytes 589828
  114.8 12.8 %copy-start.16 = (bf16[16,48,128]{2,1,0:T(8,128)(2,1)}, bf16[16,48,128]{2,1,0:T(8,128)(2,1)S(1)}, u32[]{:S(2)}) copy-start(bf16[16,48,128]{2,1,0:T(8,128)(2,1)S(1)} %collective-permute-done.10.f2) | copy-start | bytes 589828
  115.4 12.2 %copy-start.17 = (bf16[16,48,128]{2,1,0:T(8,128)(2,1)}, bf16[16,48,128]{2,1,0:T(8,128)(2,1)S(1)}, u32[]{:S(2)}) copy-start(bf16[16,48,128]{2,1,0:T(8,128)(2,1)S(1)} %collective-permute-done.15.d2) | copy-start | bytes 589828
  118.4 9.2 %copy-start.18 = (bf16[16,48,128]{2,1,0:T(8,128)(2,1)}, bf16[16,48,128]{2,1,0:T(8,128)(2,1)S(1)}, u32[]{:S(2)}) copy-start(bf16[16,48,128]{2,1,0:T(8,128)(2,1)S(1)} %collective-permute-done.14.g2) | copy-start | bytes 589828
  118.4 1.0 copy-start
  123.9 14.3 %all-to-all-start.3 = ((bf16[8,160,256]{2,1,0:T(8,128)(2,1)}), bf16[8,160,256]{2,1,0:T(8,128)(2,1)S(1)}, u32[]{:S(2)}, u32[]{:S(2)}) async-start(bf16[8,160,256]{2,1,0:T(8,128)(2,1)} %get-tuple-element.111), calls=%async_computation.3 | async-start | bytes 1310720 | tf_op jit(solution)/shard_map/all_to_all | solution.py:441
  127.5 7.9 %copy-start.24 = (f32[64,128]{1,0:T(8,128)S(1)}, f32[64,128]{1,0:T(8,128)}, u32[]{:S(2)}) copy-start(f32[64,128]{1,0:T(8,128)} %get-tuple-element.113) | copy-start | bytes 98308
  127.6 9.1 %copy-start.20 = (f32[64,128]{1,0:T(8,128)S(1)}, f32[64,128]{1,0:T(8,128)}, u32[]{:S(2)}) copy-start(f32[64,128]{1,0:T(8,128)} %get-tuple-element.112) | copy-start | bytes 98308
  133.2 3.5 %collective-permute-start.16 = (f32[8,24,128]{2,1,0:T(8,128)}, f32[8,24,128]{2,1,0:T(8,128)S(1)}, u32[]{:S(2)}, u32[]{:S(2)}) collective-permute-start(f32[8,24,128]{2,1,0:T(8,128)} %get-tuple-element.110), channel_id=1, source_target_pairs={{0,32},{32,0},{1,33},{33,1},{2,34},{34,2},{3,35},{35,3},{4,36},{36... | collective-permute-start | bytes 294920 | tf_op jit(solution)/shard_map/ppermute | solution.py:381
  135.4 1.2 collective-permute-start.17
  138.2 5.3 %copy-start.2 = (bf16[8,160,256]{2,1,0:T(8,128)(2,1)}, bf16[8,160,256]{2,1,0:T(8,128)(2,1)S(1)}, u32[]{:S(2)}) copy-start(bf16[8,160,256]{2,1,0:T(8,128)(2,1)S(1)} %all-to-all-done.3.parts) | copy-start | bytes 1966084
  138.2 10.7 %all-to-all-start.4 = ((f32[8,24,128]{2,1,0:T(8,128)}), f32[8,24,128]{2,1,0:T(8,128)S(1)}, u32[]{:S(2)}, u32[]{:S(2)}) async-start(f32[8,24,128]{2,1,0:T(8,128)} %add.20), calls=%async_computation.4 | async-start | bytes 196608 | tf_op jit(solution)/shard_map/all_to_all | solution.py:447
  149.0 6.0 %collective-permute-start.18 = (f32[256,128]{1,0:T(8,128)S(1)}, f32[256,128]{1,0:T(8,128)S(1)}, u32[]{:S(2)}, u32[]{:S(2)}) collective-permute-start(f32[256,128]{1,0:T(8,128)S(1)} %pad_maximum_fusion), channel_id=1, source_target_pairs={{0,64},{64,0},{128,192},{192,128},{1,65},{65,1},{129,193},{193,129... | collective-permute-start | bytes 393224 | tf_op jit(solution)/shard_map/ppermute | solution.py:451
  149.2 17.8 %all-to-all-start.5 = ((bf16[4,160,256]{2,1,0:T(8,128)(2,1)}), bf16[4,160,256]{2,1,0:T(8,128)(2,1)S(1)}, u32[]{:S(2)}, u32[]{:S(2)}) async-start(bf16[4,160,256]{2,1,0:T(8,128)(2,1)} %shard_map.178), calls=%async_computation.5 | async-start | bytes 655360 | tf_op jit(solution)/shard_map/all_to_all | solution.py:450
  155.0 5.1 %collective-permute-start.19 = (f32[256,128]{1,0:T(8,128)S(1)}, f32[256,128]{1,0:T(8,128)S(1)}, u32[]{:S(2)}, u32[]{:S(2)}) collective-permute-start(f32[256,128]{1,0:T(8,128)S(1)} %fusion), channel_id=1, source_target_pairs={{0,192},{192,0},{64,128},{128,64},{1,193},{193,1},{65,129},{129,65... | collective-permute-start | bytes 393224 | tf_op jit(solution)/shard_map/ppermute | solution.py:452
  160.1 4.4 %copy-start.10 = (f32[256,128]{1,0:T(8,128)}, f32[256,128]{1,0:T(8,128)S(1)}, u32[]{:S(2)}) copy-start(f32[256,128]{1,0:T(8,128)S(1)} %add.23.keep) | copy-start | bytes 393220
  160.1 4.4 %collective-permute-start.20 = (f32[256,128]{1,0:T(8,128)S(1)}, f32[256,128]{1,0:T(8,128)S(1)}, u32[]{:S(2)}, u32[]{:S(2)}) collective-permute-start(f32[256,128]{1,0:T(8,128)S(1)} %add.23.keep), channel_id=1, source_target_pairs={{0,32},{32,0},{1,33},{33,1},{2,34},{34,2},{3,35},{35,3},{4,36},{36... | collective-permute-start | bytes 393224 | tf_op jit(solution)/shard_map/ppermute | solution.py:381
  (5 other events, 3.7 us)

commit v9 on v8

--- a/solution.py
+++ b/solution.py
@@ -48,7 +48,7 @@
         rows[aligned(b, TILE), 0:width] = table[:, aligned(b, TILE)].astype(F32).T
         return carry
 
-    lax.fori_loop(0, table.shape[1] // TILE, turn, 0, unroll=8)
+    lax.fori_loop(0, table.shape[1] // TILE, turn, 0, unroll=16)
     step = 64
 
     def pick(g, carry):
@@ -76,7 +76,7 @@
         out[r] = jnp.concatenate([both, term], axis=0).astype(BF)
         return carry
 
-    lax.fori_loop(0, blocks, merge, 0, unroll=2)
+    lax.fori_loop(0, blocks, merge, 0, unroll=4)
 
 
 def hop(place, table, ids, cols, bias, tiles, after):
@@ -134,10 +134,9 @@
     cot[...] = jnp.concatenate([kept, jnp.zeros((256 - classes, slots), F32)], axis=0).astype(BF)
     out[...] = jnp.zeros_like(out)
     zq = place[2]
-    low, high = 2 * (zq // 2), 2 - 2 * (zq // 2)
-    odd = lax.rem(zq, 2)
-    for part, first in ((pair, low), (quad, high)):
-        for j, at in enumerate((first + odd, first + 1 - odd)):
+    side, odd = lax.rem(zq, 2), zq // 2
+    for part, first in ((pair, side), (quad, 1 - side)):
+        for j, at in enumerate((first + 2 * odd, first + 2 - 2 * odd)):
             own[aligned(at, 32), :] = part[64 * j : 64 * j + 32]
             neigh[aligned(at, 32), :] = part[64 * j + 32 : 64 * j + 64]
     self_t[...] = own[...].astype(F32).T.astype(BF)
@@ -406,7 +405,7 @@
     send, feats = hop(
         place, feature_table, node_ids, hop_cols, hidden_bias, hop_tiles, packed
     )
-    peer = lax.ppermute(pair, "zq", [(0, 1), (1, 0), (2, 3), (3, 2)])
+    peer = lax.ppermute(pair, "zq", [(0, 2), (2, 0), (1, 3), (3, 1)])
     weights, pair, peer, send, feats = lax.optimization_barrier(
         (weights, pair, peer, send, feats)
     )
@@ -419,20 +418,18 @@
     twin = swap(feats, "zr")
     near = [shift(feats, "y", s) for s in (1, 3)]
     pair = jnp.concatenate([pair, peer], axis=0)
-    quad = lax.ppermute(pair, "zq", [(0, 2), (2, 0), (1, 3), (3, 1)])
+    quad = lax.ppermute(pair, "zq", [(0, 1), (1, 0), (2, 3), (3, 2)])
 
     hidden = layer(place, got, mine, other)
-    hidden, pair, quad, near, feats, twin = lax.optimization_barrier(
-        (hidden, pair, quad, near, feats, twin)
+    twins = [shift(twin, "y", s) for s in (1, 3)]
+    hidden, pair, quad, near, feats, twin, twins = lax.optimization_barrier(
+        (hidden, pair, quad, near, feats, twin, twins)
     )
     hidden = lax.all_to_all(hidden, FEAT, 0, 0, tiled=True)
-    feats = relay(feats, near)
-    near = [shift(twin, "y", s) for s in (1, 3)]
+    feats = relay(feats, near) + relay(twin, twins)
     live = batch_sizes[lax.axis_index("x") * 2 + lax.axis_index("core")]
     ready = spread(place, target_cols, live, logit_cotangent, pair, quad, target_tiles, blocks)
-    ready, near = lax.optimization_barrier((ready, near))
     dhidden, cot, self_t, neigh_t = ready
-    feats = feats + relay(twin, near)
     hidden, feats = lax.optimization_barrier((hidden, feats))
 
     scores, keep_head, send_head = score(

time: 171 us -> 171 us (level)
  Pallas kernels: 54.6 us -> 51.9 us
  local copies, waits for them, and re-layouts: 8.31 us -> 11 us
    ppermute x7, waiting for transfers between devices: 2.11 us -> 9.73 us  [swap(): return lax.ppermute(value, axis, [(0, 1), (1, 0)])]
    ppermute x10, waiting for transfers between devices: 21 us -> 14.1 us  [shift(): return lax.ppermute(value, axis, [(i, (i + by) % 4) for i in range(4)])]
    ppermute x2, waiting for transfers between devices: 4.67 us -> 0.01 us  [the longest x1 0.01 us: shards(): peer = lax.ppermute(pair, 'zq', [(0, 2), (2, 0), (1, 3), (3, 1)])]
    all_to_all x1, waiting for transfers between devices: 0.01 us -> 3.68 us  [shards(): hidden = lax.all_to_all(hidden, FEAT, 0, 0, tiled=True)]
    all_to_all x1, starting transfers between devices: 7.42 us -> 4.43 us  [shards(): got = lax.all_to_all(send, FEAT, 0, 0, tiled=True)]
    slice x4, local copies, waits for them, and re-layouts: 0.06 us -> 2.79 us  [relay(): far = [shift(near[0][:half], 'y', 1), shift(near[1][half:], 'y', 3)]]
    pallas_call x1, Pallas kernels: 27.1 us -> 24.4 us  [hop(): pl.pallas_call(hop_kernel, in_specs=[SMEM, SMEM, SMEM, VMEM, VMEM, HBM, H...]
    all_to_all x1, starting transfers between devices: 5.72 us -> 3.46 us  [shards(): scores = lax.all_to_all(scores, 'zq', 0, 0, tiled=True)]
  transfers between devices with their start and end apart: 27 -> 27, of which waited for: 12 -> 12; matrix products, arithmetic and copies ran while one was open for 2% -> 4% of each run, Pallas kernels for 27% -> 26%
where the time goes in v9:
time: 171 us; the launch traced here: 170 us
  starting transfers between devices  70 us (41%)
  Pallas kernels  51.9 us (30%)
  waiting for transfers between devices  34.2 us (20%)
  local copies, waits for them, and re-layouts  11 us (6%)
    pallas_call x1, Pallas kernels, hop(): pl.pallas_call(hop_kernel, in_specs=[SMEM, SMEM, SMEM, VMEM, VMEM, HBM, H...  24.4 us
    ppermute x10, waiting for transfers between devices, shift(): return lax.ppermute(value, axis, [(i, (i + by) % 4) for i in range(4)])  14.1 us
    ppermute x10, starting transfers between devices, shift(): return lax.ppermute(value, axis, [(i, (i + by) % 4) for i in range(4)])  12.5 us
    ppermute x7, starting transfers between devices, swap(): return lax.ppermute(value, axis, [(0, 1), (1, 0)])  12.2 us
    all_to_all x1, starting transfers between devices, shards(): weights = lax.all_to_all(packed, FEAT, 0, 0, tiled=True)  12 us
    ppermute x7, waiting for transfers between devices, swap(): return lax.ppermute(value, axis, [(0, 1), (1, 0)])  9.73 us
    unnamed x56, local copies, waits for them, and re-layouts  6.86 us
    pallas_call x1, Pallas kernels, spread(): pl.pallas_call(spread_kernel, in_specs=[SMEM, SMEM, SMEM] + [VMEM] * 4, o...  5.93 us
  transfers between devices with their start and end apart: 27, of which 12 were waited for; matrix products, arithmetic and copies ran while one was open for 4% of the time, Pallas kernels for 26%

profile of v9, /device:TPU:1, one launch (start us, length us, event | category | flops | bytes accessed | tf_op | source)
XLA Modules:
  0.0 169.6 jit_solution(8869557847056784964)
XLA Ops:
  1.3 1.8 %shard_map.172 = (bf16[32,24,512]{2,1,0:T(8,128)(2,1)}, bf16[64,256]{1,0:T(8,128)(2,1)}) custom-call(s32[5]{0:T(128)} %stack.23.place, bf16[24,1024]{1,0:T(8,128)(2,1)} %own.1, bf16[24,1024]{1,0:T(8,128)(2,1)} %neigh.1, bf16[32,153]{1,0:T(8,128)(2,1)} %head_self.1, bf16[32,153]{1,0:T(8,128)(2,1)} %head_neigh.1), custom_call_target="tpu_custom_call" | custom-call | tf_op jit(solution)/shard_map/pallas_call | solution.py:116
  3.1 12.0 %all-to-all-start = ((bf16[32,24,512]{2,1,0:T(8,128)(2,1)}), bf16[32,24,512]{2,1,0:T(8,128)(2,1)S(1)}, u32[]{:S(2)}, u32[]{:S(2)}) async-start(bf16[32,24,512]{2,1,0:T(8,128)(2,1)} %get-tuple-element.61._), calls=%async_computation | async-start | bytes 1572864 | tf_op jit(solution)/shard_map/all_to_all | solution.py:404
  15.2 5.2 %collective-permute-start = (bf16[64,256]{1,0:T(8,128)(2,1)}, bf16[64,256]{1,0:T(8,128)(2,1)S(1)}, u32[]{:S(2)}, u32[]{:S(2)}) collective-permute-start(bf16[64,256]{1,0:T(8,128)(2,1)} %get-tuple-element.71), channel_id=1, source_target_pairs={{0,16},{16,0},{8,24},{24,8},{1,17},{17,1},{9,25},{25,9},{2,18},{18... | collective-permute-start | bytes 98312 | tf_op jit(solution)/shard_map/ppermute | solution.py:408
  20.4 1.4 copy.19.cols
  21.8 24.4 %shard_map.173 = (bf16[32,56,128]{2,1,0:T(8,128)(2,1)}, bf16[32,48,128]{2,1,0:T(8,128)(2,1)}) custom-call(s32[5]{0:T(128)} %stack.23.place, s32[16384]{0:T(1024)} %ids.1, s32[32,8]{1,0:T(8,128)} %copy.19.cols, bf16[24,32768]{1,0:T(8,128)(2,1)} %table.1, f32[1,32]{1,0:T(1,128)} %bitcast.14, bf16[32,8,128,128]{3,2,1,0:T(8,128)(2,1)} %tiles_hbm.1, ...), custom_call_target="tpu_custom_call" | custom-call | flops 1000000000 | bytes 60000000 | tf_op jit(solution)/shard_map/pallas_call | solution.py:84
  46.3 2.6 %collective-permute-start.2 = (bf16[768,256]{1,0:T(8,128)(2,1)S(1)}, bf16[768,256]{1,0:T(8,128)(2,1)S(1)}, u32[]{:S(2)}, u32[]{:S(2)}) collective-permute-start(bf16[768,256]{1,0:T(8,128)(2,1)S(1)} %get-tuple-element.116), channel_id=1, source_target_pairs={{0,192},{64,0},{128,64},{192,128},{1,193},{65,1},{129,65},{193,129... | collective-permute-start | bytes 1179656 | tf_op jit(solution)/shard_map/ppermute | solution.py:370
  48.9 4.4 %all-to-all-start.1 = ((bf16[32,56,128]{2,1,0:T(8,128)(2,1)}), bf16[32,56,128]{2,1,0:T(8,128)(2,1)S(1)}, u32[]{:S(2)}, u32[]{:S(2)}) async-start(bf16[32,56,128]{2,1,0:T(8,128)(2,1)} %get-tuple-element.65), calls=%async_computation.1 | async-start | bytes 917504 | tf_op jit(solution)/shard_map/all_to_all | solution.py:412
  53.3 2.4 %collective-permute-done.2.w2 = bf16[768,256]{1,0:T(8,128)(2,1)S(1)} collective-permute-done((bf16[768,256]{1,0:T(8,128)(2,1)S(1)}, bf16[768,256]{1,0:T(8,128)(2,1)S(1)}, u32[]{:S(2)}, u32[]{:S(2)}) %collective-permute-start.2) | collective-permute-done | bytes 393248 | tf_op jit(solution)/shard_map/ppermute | solution.py:370
  55.8 3.1 %collective-permute-done.1.w1 = bf16[768,256]{1,0:T(8,128)(2,1)S(1)} collective-permute-done((bf16[768,256]{1,0:T(8,128)(2,1)S(1)}, bf16[768,256]{1,0:T(8,128)(2,1)S(1)}, u32[]{:S(2)}, u32[]{:S(2)}) %collective-permute-start.1) | collective-permute-done | bytes 393248 | tf_op jit(solution)/shard_map/ppermute | solution.py:370
  58.9 2.7 %collective-permute-start.3 = (bf16[768,512]{1,0:T(8,128)(2,1)S(1)}, bf16[768,512]{1,0:T(8,128)(2,1)S(1)}, u32[]{:S(2)}, u32[]{:S(2)}) collective-permute-start(bf16[768,512]{1,0:T(8,128)(2,1)S(1)} %bitcast.10), channel_id=1, source_target_pairs={{0,32},{32,0},{1,33},{33,1},{2,34},{34,2},{3,35},{35,3},{4,36},{36... | collective-permute-start | bytes 2359304 | tf_op jit(solution)/shard_map/ppermute | solution.py:380
  61.9 0.8 collective-permute-start.5
  62.7 2.4 %collective-permute-start.8 = (bf16[32,48,128]{2,1,0:T(8,128)(2,1)S(1)}, bf16[32,48,128]{2,1,0:T(8,128)(2,1)S(1)}, u32[]{:S(2)}, u32[]{:S(2)}) collective-permute-start(bf16[32,48,128]{2,1,0:T(8,128)(2,1)S(1)} %copy-done.11), channel_id=1, source_target_pairs={{0,3},{1,0},{2,1},{3,2},{4,7},{5,4},{6,5},{7,6},{8,11},{9,8},{10,9... | collective-permute-start | bytes 1179656 | tf_op jit(solution)/shard_map/ppermute | solution.py:370
  65.9 7.6 %collective-permute-done.9.g0 = bf16[32,48,128]{2,1,0:T(8,128)(2,1)} collective-permute-done((bf16[32,48,128]{2,1,0:T(8,128)(2,1)S(1)}, bf16[32,48,128]{2,1,0:T(8,128)(2,1)}, u32[]{:S(2)}, u32[]{:S(2)}) %collective-permute-start.9) | collective-permute-done | bytes 393248 | tf_op jit(solution)/shard_map/ppermute | solution.py:380
  73.5 2.3 %collective-permute-start.11 = (bf16[32,48,128]{2,1,0:T(8,128)(2,1)}, bf16[32,48,128]{2,1,0:T(8,128)(2,1)S(1)}, u32[]{:S(2)}, u32[]{:S(2)}) collective-permute-start(bf16[32,48,128]{2,1,0:T(8,128)(2,1)} %collective-permute-done.9.g0), channel_id=1, source_target_pairs={{0,3},{1,0},{2,1},{3,2},{4,7},{5,4},{6,5},{7,6},{8,11},{9,8},{10,9... | collective-permute-start | bytes 1179656 | tf_op jit(solution)/shard_map/ppermute | solution.py:370
  75.8 0.8 copy-done.15
  76.6 0.9 copy-done.9
  77.5 2.4 %collective-permute-start.6 = (bf16[128,256]{1,0:T(8,128)(2,1)S(1)}, bf16[128,256]{1,0:T(8,128)(2,1)S(1)}, u32[]{:S(2)}, u32[]{:S(2)}) collective-permute-start(bf16[128,256]{1,0:T(8,128)(2,1)S(1)} %constant_dynamic-update-slice_fusion.pair), channel_id=1, source_target_pairs={{0,8},{8,0},{16,24},{24,16},{1,9},{9,1},{17,25},{25,17},{2,10},{10... | collective-permute-start | bytes 196616 | tf_op jit(solution)/shard_map/ppermute | solution.py:421
  79.9 0.8 copy-done.3
  80.7 3.9 %shard_map.174 = bf16[32,128,128]{2,1,0:T(8,128)(2,1)} custom-call(s32[5]{0:T(128)} %stack.23.place, bf16[32,56,128]{2,1,0:T(8,128)(2,1)} %copy-done.3, bf16[768,512]{1,0:T(8,128)(2,1)} %bitcast.11, bf16[768,256]{1,0:T(8,128)(2,1)} %copy-done.13, bf16[768,256]{1,0:T(8,128)(2,1)} %copy-done.12, bf16[768,512]{1,0:T(8,128)(2,1)} %copy-done.9, ...), custom_call_target="tpu_custom_call" | custom-call | tf_op jit(solution)/shard_map/pallas_call | solution.py:205
  84.7 2.4 %collective-permute-done.10.g1 = bf16[32,48,128]{2,1,0:T(8,128)(2,1)S(1)} collective-permute-done((bf16[32,48,128]{2,1,0:T(8,128)(2,1)}, bf16[32,48,128]{2,1,0:T(8,128)(2,1)S(1)}, u32[]{:S(2)}, u32[]{:S(2)}) %collective-permute-start.10) | collective-permute-done | bytes 393248 | tf_op jit(solution)/shard_map/ppermute | solution.py:370
  87.1 4.9 %all-to-all-start.2 = ((bf16[32,128,128]{2,1,0:T(8,128)(2,1)}), bf16[32,128,128]{2,1,0:T(8,128)(2,1)S(1)}, u32[]{:S(2)}, u32[]{:S(2)}) async-start(bf16[32,128,128]{2,1,0:T(8,128)(2,1)} %shard_map.174), calls=%async_computation.2 | async-start | bytes 2097152 | tf_op jit(solution)/shard_map/all_to_all | solution.py:428
  92.0 0.7 slice.20
  92.7 0.7 slice.21
  93.4 0.7 slice.22
  94.1 0.7 slice.23
  94.8 2.4 %collective-permute-start.15 = (bf16[16,48,128]{2,1,0:T(8,128)(2,1)}, bf16[16,48,128]{2,1,0:T(8,128)(2,1)S(1)}, u32[]{:S(2)}, u32[]{:S(2)}) collective-permute-start(bf16[16,48,128]{2,1,0:T(8,128)(2,1)} %slice.23), channel_id=1, source_target_pairs={{0,3},{1,0},{2,1},{3,2},{4,7},{5,4},{6,5},{7,6},{8,11},{9,8},{10,9... | collective-permute-start | bytes 589832 | tf_op jit(solution)/shard_map/ppermute | solution.py:370
  97.3 2.7 %collective-permute-start.13 = (bf16[16,48,128]{2,1,0:T(8,128)(2,1)}, bf16[16,48,128]{2,1,0:T(8,128)(2,1)S(1)}, u32[]{:S(2)}, u32[]{:S(2)}) collective-permute-start(bf16[16,48,128]{2,1,0:T(8,128)(2,1)} %slice.21), channel_id=1, source_target_pairs={{0,3},{1,0},{2,1},{3,2},{4,7},{5,4},{6,5},{7,6},{8,11},{9,8},{10,9... | collective-permute-start | bytes 589832 | tf_op jit(solution)/shard_map/ppermute | solution.py:370
  100.5 5.9 %shard_map.175 = (f32[32,128,128]{2,1,0:T(8,128)}, bf16[256,1024]{1,0:T(8,128)(2,1)}, bf16[256,128]{1,0:T(8,128)(2,1)}, bf16[256,128]{1,0:T(8,128)(2,1)}) custom-call(s32[5]{0:T(128)} %stack.23.place, s32[8,8]{1,0:T(8,128)} %cols.4, s32[1]{0:T(128)} %dynamic_slice.3.live, bf16[153,1024]{1,0:T(8,128)(2,1)} %logit_cot.1, bf16[128,256]{1,0:T(8,128)(2,1)} %copy-done.23, ...), custom_call_target="tpu_custom_call" | custom-call | flops 1000000000 | bytes 8000000 | tf_op jit(solution)/shard_map/pallas_call | solution.py:155
  106.5 5.8 %collective-permute-done.13.e2 = bf16[16,48,128]{2,1,0:T(8,128)(2,1)S(1)} collective-permute-done((bf16[16,48,128]{2,1,0:T(8,128)(2,1)}, bf16[16,48,128]{2,1,0:T(8,128)(2,1)S(1)}, u32[]{:S(2)}, u32[]{:S(2)}) %collective-permute-start.13) | collective-permute-done | bytes 196640 | tf_op jit(solution)/shard_map/ppermute | solution.py:370
  112.7 3.7 %all-to-all-done.2.hidden = bf16[32,128,128]{2,1,0:T(8,128)(2,1)S(1)} async-done(((bf16[32,128,128]{2,1,0:T(8,128)(2,1)}), bf16[32,128,128]{2,1,0:T(8,128)(2,1)S(1)}, u32[]{:S(2)}, u32[]{:S(2)}) %all-to-all-start.2) | async-done | bytes 1048608 | tf_op jit(solution)/shard_map/all_to_all | solution.py:428
  116.4 1.0 copy-done
  117.4 4.5 %shard_map.176 = (bf16[8,160,256]{2,1,0:T(8,128)(2,1)}, f32[64,128]{1,0:T(8,128)}, f32[64,128]{1,0:T(8,128)}) custom-call(s32[5]{0:T(128)} %stack.23.place, s32[8,8]{1,0:T(8,128)} %cols.4, bf16[32,128,128]{2,1,0:T(8,128)(2,1)} %copy-done, f32[32,128,128]{2,1,0:T(8,128)} %get-tuple-element.84.dhidden, bf16[8,8,128,128]{3,2,1,0:T(8,128)(2,1)} %tiles.3, ...), custom_call_target="tpu_custom_call" | custom-call | tf_op jit(solution)/shard_map/pallas_call | solution.py:251
  122.0 4.9 %all-to-all-start.3 = ((bf16[8,160,256]{2,1,0:T(8,128)(2,1)}), bf16[8,160,256]{2,1,0:T(8,128)(2,1)S(1)}, u32[]{:S(2)}, u32[]{:S(2)}) async-start(bf16[8,160,256]{2,1,0:T(8,128)(2,1)} %get-tuple-element.103), calls=%async_computation.3 | async-start | bytes 1310720 | tf_op jit(solution)/shard_map/all_to_all | solution.py:438
  126.9 5.6 %shard_map.177 = (f32[8,24,128]{2,1,0:T(8,128)}, f32[8,24,128]{2,1,0:T(8,128)}) custom-call(s32[5]{0:T(128)} %stack.23.place, bf16[32,128,128]{2,1,0:T(8,128)(2,1)} %copy-done, f32[32,128,128]{2,1,0:T(8,128)} %get-tuple-element.84.dhidden, bf16[32,48,128]{2,1,0:T(8,128)(2,1)} %get-tuple-element.91.f0, bf16[32,48,128]{2,1,0:T(8,128)(2,1)} %copy-done.6, ...), custom_call_target="tpu_custom_call" | custom-call | flops 1000000000 | bytes 7000000 | tf_op jit(solution)/shard_map/pallas_call | solution.py:325
  132.5 4.4 %collective-permute-start.16 = (f32[8,24,128]{2,1,0:T(8,128)}, f32[8,24,128]{2,1,0:T(8,128)S(1)}, u32[]{:S(2)}, u32[]{:S(2)}) collective-permute-start(f32[8,24,128]{2,1,0:T(8,128)} %get-tuple-element.102), channel_id=1, source_target_pairs={{0,32},{32,0},{1,33},{33,1},{2,34},{34,2},{3,35},{35,3},{4,36},{36... | collective-permute-start | bytes 294920 | tf_op jit(solution)/shard_map/ppermute | solution.py:380
  136.9 1.1 collective-permute-done.17
  138.1 1.5 add.20
  139.6 5.4 %all-to-all-start.4 = ((f32[8,24,128]{2,1,0:T(8,128)}), f32[8,24,128]{2,1,0:T(8,128)S(1)}, u32[]{:S(2)}, u32[]{:S(2)}) async-start(f32[8,24,128]{2,1,0:T(8,128)} %add.20), calls=%async_computation.4 | async-start | bytes 196608 | tf_op jit(solution)/shard_map/all_to_all | solution.py:444
  145.1 1.9 %shard_map.178 = bf16[4,160,256]{2,1,0:T(8,128)(2,1)} custom-call(bf16[8,160,256]{2,1,0:T(8,128)(2,1)} %copy-done.2), custom_call_target="tpu_custom_call" | custom-call | tf_op jit(solution)/shard_map/pallas_call | solution.py:270
  147.0 3.5 %all-to-all-done.4 = f32[8,24,128]{2,1,0:T(8,128)S(1)} async-done(((f32[8,24,128]{2,1,0:T(8,128)}), f32[8,24,128]{2,1,0:T(8,128)S(1)}, u32[]{:S(2)}, u32[]{:S(2)}) %all-to-all-start.4) | async-done | bytes 98336 | tf_op jit(solution)/shard_map/all_to_all | solution.py:444
  150.6 3.5 %all-to-all-start.5 = ((bf16[4,160,256]{2,1,0:T(8,128)(2,1)}), bf16[4,160,256]{2,1,0:T(8,128)(2,1)S(1)}, u32[]{:S(2)}, u32[]{:S(2)}) async-start(bf16[4,160,256]{2,1,0:T(8,128)(2,1)} %shard_map.178), calls=%async_computation.5 | async-start | bytes 655360 | tf_op jit(solution)/shard_map/all_to_all | solution.py:447
  154.4 2.3 %collective-permute-start.19 = (f32[256,128]{1,0:T(8,128)S(1)}, f32[256,128]{1,0:T(8,128)S(1)}, u32[]{:S(2)}, u32[]{:S(2)}) collective-permute-start(f32[256,128]{1,0:T(8,128)S(1)} %fusion), channel_id=1, source_target_pairs={{0,192},{192,0},{64,128},{128,64},{1,193},{193,1},{65,129},{129,65... | collective-permute-start | bytes 393224 | tf_op jit(solution)/shard_map/ppermute | solution.py:449
  156.7 2.8 %collective-permute-done.19 = f32[256,128]{1,0:T(8,128)S(1)} collective-permute-done((f32[256,128]{1,0:T(8,128)S(1)}, f32[256,128]{1,0:T(8,128)S(1)}, u32[]{:S(2)}, u32[]{:S(2)}) %collective-permute-start.19) | collective-permute-done | bytes 131104 | tf_op jit(solution)/shard_map/ppermute | solution.py:449
  159.5 4.0 %collective-permute-start.20 = (f32[256,128]{1,0:T(8,128)S(1)}, f32[256,128]{1,0:T(8,128)S(1)}, u32[]{:S(2)}, u32[]{:S(2)}) collective-permute-start(f32[256,128]{1,0:T(8,128)S(1)} %add.23.keep), channel_id=1, source_target_pairs={{0,32},{32,0},{1,33},{33,1},{2,34},{34,2},{3,35},{35,3},{4,36},{36... | collective-permute-start | bytes 393224 | tf_op jit(solution)/shard_map/ppermute | solution.py:380
  163.5 1.0 collective-permute-done.20.rest
  165.2 1.9 %shard_map.180 = (f32[24,1024]{1,0:T(8,128)}, f32[24,1024]{1,0:T(8,128)}, f32[32,153]{1,0:T(8,128)}, f32[32,153]{1,0:T(8,128)}, f32[1,32]{1,0:T(1,128)}) custom-call(s32[5]{0:T(128)} %stack.23.place, f32[256,128]{1,0:T(8,128)} %copy-done.10, f32[256,128]{1,0:T(8,128)} %copy-done.20), custom_call_target="tpu_custom_call" | custom-call | tf_op jit(solution)/shard_map/pallas_call | solution.py:360
  167.0 0.7 copy-done.4
  167.8 1.9 %shard_map.179 = f32[153,1024]{1,0:T(8,128)} custom-call(bf16[4,160,256]{2,1,0:T(8,128)(2,1)} %copy-done.4), custom_call_target="tpu_custom_call" | custom-call | tf_op jit(solution)/shard_map/pallas_call | solution.py:286
  (84 shorter events, 4.2 us)
Async XLA Ops:
  3.1 43.1 %all-to-all-start = ((bf16[32,24,512]{2,1,0:T(8,128)(2,1)}), bf16[32,24,512]{2,1,0:T(8,128)(2,1)S(1)}, u32[]{:S(2)}, u32[]{:S(2)}) async-start(bf16[32,24,512]{2,1,0:T(8,128)(2,1)} %get-tuple-element.61._), calls=%async_computation | async-start | bytes 1572864 | tf_op jit(solution)/shard_map/all_to_all | solution.py:404
  15.2 31.1 %collective-permute-start = (bf16[64,256]{1,0:T(8,128)(2,1)}, bf16[64,256]{1,0:T(8,128)(2,1)S(1)}, u32[]{:S(2)}, u32[]{:S(2)}) collective-permute-start(bf16[64,256]{1,0:T(8,128)(2,1)} %get-tuple-element.71), channel_id=1, source_target_pairs={{0,16},{16,0},{8,24},{24,8},{1,17},{17,1},{9,25},{25,9},{2,18},{18... | collective-permute-start | bytes 98312 | tf_op jit(solution)/shard_map/ppermute | solution.py:408
  46.2 15.4 %copy-start.11 = (bf16[32,48,128]{2,1,0:T(8,128)(2,1)S(1)}, bf16[32,48,128]{2,1,0:T(8,128)(2,1)}, u32[]{:S(2)}) copy-start(bf16[32,48,128]{2,1,0:T(8,128)(2,1)} %get-tuple-element.91.f0) | copy-start | bytes 1179652
  46.2 30.4 %copy-start.22 = (bf16[64,256]{1,0:T(8,128)(2,1)S(1)}, bf16[64,256]{1,0:T(8,128)(2,1)}, u32[]{:S(2)}) copy-start(bf16[64,256]{1,0:T(8,128)(2,1)} %get-tuple-element.71) | copy-start | bytes 98308
  46.2 33.7 %copy-start.1 = (bf16[32,24,512]{2,1,0:T(8,128)(2,1)}, bf16[32,24,512]{2,1,0:T(8,128)(2,1)S(1)}, u32[]{:S(2)}) copy-start(bf16[32,24,512]{2,1,0:T(8,128)(2,1)S(1)} %all-to-all-done) | copy-start | bytes 2359300
  46.3 9.4 %collective-permute-start.2 = (bf16[768,256]{1,0:T(8,128)(2,1)S(1)}, bf16[768,256]{1,0:T(8,128)(2,1)S(1)}, u32[]{:S(2)}, u32[]{:S(2)}) collective-permute-start(bf16[768,256]{1,0:T(8,128)(2,1)S(1)} %get-tuple-element.116), channel_id=1, source_target_pairs={{0,192},{64,0},{128,64},{192,128},{1,193},{65,1},{129,65},{193,129... | collective-permute-start | bytes 1179656 | tf_op jit(solution)/shard_map/ppermute | solution.py:370
  48.9 10.0 %collective-permute-start.1 = (bf16[768,256]{1,0:T(8,128)(2,1)S(1)}, bf16[768,256]{1,0:T(8,128)(2,1)S(1)}, u32[]{:S(2)}, u32[]{:S(2)}) collective-permute-start(bf16[768,256]{1,0:T(8,128)(2,1)S(1)} %get-tuple-element.117), channel_id=1, source_target_pairs={{0,64},{64,128},{128,192},{192,0},{1,65},{65,129},{129,193},{193,1... | collective-permute-start | bytes 1179656 | tf_op jit(solution)/shard_map/ppermute | solution.py:370
  48.9 31.1 %all-to-all-start.1 = ((bf16[32,56,128]{2,1,0:T(8,128)(2,1)}), bf16[32,56,128]{2,1,0:T(8,128)(2,1)S(1)}, u32[]{:S(2)}, u32[]{:S(2)}) async-start(bf16[32,56,128]{2,1,0:T(8,128)(2,1)} %get-tuple-element.65), calls=%async_computation.1 | async-start | bytes 917504 | tf_op jit(solution)/shard_map/all_to_all | solution.py:412
  55.7 20.1 %copy-start.12 = (bf16[768,256]{1,0:T(8,128)(2,1)}, bf16[768,256]{1,0:T(8,128)(2,1)S(1)}, u32[]{:S(2)}) copy-start(bf16[768,256]{1,0:T(8,128)(2,1)S(1)} %collective-permute-done.2.w2) | copy-start | bytes 1179652
  58.9 6.2 %copy-start.13 = (bf16[768,256]{1,0:T(8,128)(2,1)}, bf16[768,256]{1,0:T(8,128)(2,1)S(1)}, u32[]{:S(2)}) copy-start(bf16[768,256]{1,0:T(8,128)(2,1)S(1)} %collective-permute-done.1.w1) | copy-start | bytes 1179652
  58.9 17.7 %collective-permute-start.3 = (bf16[768,512]{1,0:T(8,128)(2,1)S(1)}, bf16[768,512]{1,0:T(8,128)(2,1)S(1)}, u32[]{:S(2)}, u32[]{:S(2)}) collective-permute-start(bf16[768,512]{1,0:T(8,128)(2,1)S(1)} %bitcast.10), channel_id=1, source_target_pairs={{0,32},{32,0},{1,33},{33,1},{2,34},{34,2},{3,35},{35,3},{4,36},{36... | collective-permute-start | bytes 2359304 | tf_op jit(solution)/shard_map/ppermute | solution.py:380
  61.6 3.5 %collective-permute-start.4 = (bf16[768,256]{1,0:T(8,128)(2,1)S(1)}, bf16[768,256]{1,0:T(8,128)(2,1)S(1)}, u32[]{:S(2)}, u32[]{:S(2)}) collective-permute-start(bf16[768,256]{1,0:T(8,128)(2,1)S(1)} %collective-permute-done.1.w1), channel_id=1, source_target_pairs={{0,32},{32,0},{1,33},{33,1},{2,34},{34,2},{3,35},{35,3},{4,36},{36... | collective-permute-start | bytes 1179656 | tf_op jit(solution)/shard_map/ppermute | solution.py:380
  61.6 11.9 %collective-permute-start.9 = (bf16[32,48,128]{2,1,0:T(8,128)(2,1)S(1)}, bf16[32,48,128]{2,1,0:T(8,128)(2,1)}, u32[]{:S(2)}, u32[]{:S(2)}) collective-permute-start(bf16[32,48,128]{2,1,0:T(8,128)(2,1)S(1)} %copy-done.11), channel_id=1, source_target_pairs={{0,4},{4,0},{1,5},{5,1},{2,6},{6,2},{3,7},{7,3},{8,12},{12,8},{9,1... | collective-permute-start | bytes 1179656 | tf_op jit(solution)/shard_map/ppermute | solution.py:380
  61.9 13.9 %collective-permute-start.5 = (bf16[768,256]{1,0:T(8,128)(2,1)S(1)}, bf16[768,256]{1,0:T(8,128)(2,1)S(1)}, u32[]{:S(2)}, u32[]{:S(2)}) collective-permute-start(bf16[768,256]{1,0:T(8,128)(2,1)S(1)} %collective-permute-done.2.w2), channel_id=1, source_target_pairs={{0,32},{32,0},{1,33},{33,1},{2,34},{34,2},{3,35},{35,3},{4,36},{36... | collective-permute-start | bytes 1179656 | tf_op jit(solution)/shard_map/ppermute | solution.py:380
  62.7 22.0 %collective-permute-start.8 = (bf16[32,48,128]{2,1,0:T(8,128)(2,1)S(1)}, bf16[32,48,128]{2,1,0:T(8,128)(2,1)S(1)}, u32[]{:S(2)}, u32[]{:S(2)}) collective-permute-start(bf16[32,48,128]{2,1,0:T(8,128)(2,1)S(1)} %copy-done.11), channel_id=1, source_target_pairs={{0,3},{1,0},{2,1},{3,2},{4,7},{5,4},{6,5},{7,6},{8,11},{9,8},{10,9... | collective-permute-start | bytes 1179656 | tf_op jit(solution)/shard_map/ppermute | solution.py:370
  65.1 19.6 %collective-permute-start.7 = (bf16[32,48,128]{2,1,0:T(8,128)(2,1)S(1)}, bf16[32,48,128]{2,1,0:T(8,128)(2,1)S(1)}, u32[]{:S(2)}, u32[]{:S(2)}) collective-permute-start(bf16[32,48,128]{2,1,0:T(8,128)(2,1)S(1)} %copy-done.11), channel_id=1, source_target_pairs={{0,1},{1,2},{2,3},{3,0},{4,5},{5,6},{6,7},{7,4},{8,9},{9,10},{10,1... | collective-permute-start | bytes 1179656 | tf_op jit(solution)/shard_map/ppermute | solution.py:370
  73.5 11.2 %collective-permute-start.11 = (bf16[32,48,128]{2,1,0:T(8,128)(2,1)}, bf16[32,48,128]{2,1,0:T(8,128)(2,1)S(1)}, u32[]{:S(2)}, u32[]{:S(2)}) collective-permute-start(bf16[32,48,128]{2,1,0:T(8,128)(2,1)} %collective-permute-done.9.g0), channel_id=1, source_target_pairs={{0,3},{1,0},{2,1},{3,2},{4,7},{5,4},{6,5},{7,6},{8,11},{9,8},{10,9... | collective-permute-start | bytes 1179656 | tf_op jit(solution)/shard_map/ppermute | solution.py:370
  76.6 10.5 %collective-permute-start.10 = (bf16[32,48,128]{2,1,0:T(8,128)(2,1)}, bf16[32,48,128]{2,1,0:T(8,128)(2,1)S(1)}, u32[]{:S(2)}, u32[]{:S(2)}) collective-permute-start(bf16[32,48,128]{2,1,0:T(8,128)(2,1)} %collective-permute-done.9.g0), channel_id=1, source_target_pairs={{0,1},{1,2},{2,3},{3,0},{4,5},{5,6},{6,7},{7,4},{8,9},{9,10},{10,1... | collective-permute-start | bytes 1179656 | tf_op jit(solution)/shard_map/ppermute | solution.py:370
  76.6 23.9 %copy-start.23 = (bf16[128,256]{1,0:T(8,128)(2,1)}, bf16[128,256]{1,0:T(8,128)(2,1)S(1)}, u32[]{:S(2)}) copy-start(bf16[128,256]{1,0:T(8,128)(2,1)S(1)} %constant_dynamic-update-slice_fusion.pair) | copy-start | bytes 196612
  77.5 7.2 %collective-permute-start.6 = (bf16[128,256]{1,0:T(8,128)(2,1)S(1)}, bf16[128,256]{1,0:T(8,128)(2,1)S(1)}, u32[]{:S(2)}, u32[]{:S(2)}) collective-permute-start(bf16[128,256]{1,0:T(8,128)(2,1)S(1)} %constant_dynamic-update-slice_fusion.pair), channel_id=1, source_target_pairs={{0,8},{8,0},{16,24},{24,16},{1,9},{9,1},{17,25},{25,17},{2,10},{10... | collective-permute-start | bytes 196616 | tf_op jit(solution)/shard_map/ppermute | solution.py:421
  84.7 15.3 %copy-start.26 = (s32[8]{0:T(128)S(1)}, s32[8]{0:T(128)}, u32[]{:S(2)}) copy-start(s32[8]{0:T(128)} %param.24) | copy-start | bytes 100
  84.7 15.9 %copy-start.24 = (bf16[128,256]{1,0:T(8,128)(2,1)}, bf16[128,256]{1,0:T(8,128)(2,1)S(1)}, u32[]{:S(2)}) copy-start(bf16[128,256]{1,0:T(8,128)(2,1)S(1)} %collective-permute-done.6.quad) | copy-start | bytes 196612
  84.7 21.8 %copy-start.5 = (bf16[32,48,128]{2,1,0:T(8,128)(2,1)}, bf16[32,48,128]{2,1,0:T(8,128)(2,1)S(1)}, u32[]{:S(2)}) copy-start(bf16[32,48,128]{2,1,0:T(8,128)(2,1)S(1)} %collective-permute-done.8.f3) | copy-start | bytes 1179652
  84.7 21.8 %copy-start.6 = (bf16[32,48,128]{2,1,0:T(8,128)(2,1)}, bf16[32,48,128]{2,1,0:T(8,128)(2,1)S(1)}, u32[]{:S(2)}) copy-start(bf16[32,48,128]{2,1,0:T(8,128)(2,1)S(1)} %collective-permute-done.7.f1) | copy-start | bytes 1179652
  84.7 21.8 %copy-start.7 = (bf16[32,48,128]{2,1,0:T(8,128)(2,1)}, bf16[32,48,128]{2,1,0:T(8,128)(2,1)S(1)}, u32[]{:S(2)}) copy-start(bf16[32,48,128]{2,1,0:T(8,128)(2,1)S(1)} %collective-permute-done.11.g3) | copy-start | bytes 1179652
  87.1 19.4 %copy-start.8 = (bf16[32,48,128]{2,1,0:T(8,128)(2,1)}, bf16[32,48,128]{2,1,0:T(8,128)(2,1)S(1)}, u32[]{:S(2)}) copy-start(bf16[32,48,128]{2,1,0:T(8,128)(2,1)S(1)} %collective-permute-done.10.g1) | copy-start | bytes 1179652
  87.1 29.3 %all-to-all-start.2 = ((bf16[32,128,128]{2,1,0:T(8,128)(2,1)}), bf16[32,128,128]{2,1,0:T(8,128)(2,1)S(1)}, u32[]{:S(2)}, u32[]{:S(2)}) async-start(bf16[32,128,128]{2,1,0:T(8,128)(2,1)} %shard_map.174), calls=%async_computation.2 | async-start | bytes 2097152 | tf_op jit(solution)/shard_map/all_to_all | solution.py:428
  94.8 11.7 %collective-permute-start.15 = (bf16[16,48,128]{2,1,0:T(8,128)(2,1)}, bf16[16,48,128]{2,1,0:T(8,128)(2,1)S(1)}, u32[]{:S(2)}, u32[]{:S(2)}) collective-permute-start(bf16[16,48,128]{2,1,0:T(8,128)(2,1)} %slice.23), channel_id=1, source_target_pairs={{0,3},{1,0},{2,1},{3,2},{4,7},{5,4},{6,5},{7,6},{8,11},{9,8},{10,9... | collective-permute-start | bytes 589832 | tf_op jit(solution)/shard_map/ppermute | solution.py:370
  97.3 9.3 %collective-permute-start.14 = (bf16[16,48,128]{2,1,0:T(8,128)(2,1)}, bf16[16,48,128]{2,1,0:T(8,128)(2,1)S(1)}, u32[]{:S(2)}, u32[]{:S(2)}) collective-permute-start(bf16[16,48,128]{2,1,0:T(8,128)(2,1)} %slice.22), channel_id=1, source_target_pairs={{0,1},{1,2},{2,3},{3,0},{4,5},{5,6},{6,7},{7,4},{8,9},{9,10},{10,1... | collective-permute-start | bytes 589832 | tf_op jit(solution)/shard_map/ppermute | solution.py:370
  97.3 15.0 %collective-permute-start.13 = (bf16[16,48,128]{2,1,0:T(8,128)(2,1)}, bf16[16,48,128]{2,1,0:T(8,128)(2,1)S(1)}, u32[]{:S(2)}, u32[]{:S(2)}) collective-permute-start(bf16[16,48,128]{2,1,0:T(8,128)(2,1)} %slice.21), channel_id=1, source_target_pairs={{0,3},{1,0},{2,1},{3,2},{4,7},{5,4},{6,5},{7,6},{8,11},{9,8},{10,9... | collective-permute-start | bytes 589832 | tf_op jit(solution)/shard_map/ppermute | solution.py:370
  99.9 12.8 %collective-permute-start.12 = (bf16[16,48,128]{2,1,0:T(8,128)(2,1)}, bf16[16,48,128]{2,1,0:T(8,128)(2,1)S(1)}, u32[]{:S(2)}, u32[]{:S(2)}) collective-permute-start(bf16[16,48,128]{2,1,0:T(8,128)(2,1)} %slice.20), channel_id=1, source_target_pairs={{0,1},{1,2},{2,3},{3,0},{4,5},{5,6},{6,7},{7,4},{8,9},{9,10},{10,1... | collective-permute-start | bytes 589832 | tf_op jit(solution)/shard_map/ppermute | solution.py:370
  106.5 15.4 %copy-start.16 = (bf16[16,48,128]{2,1,0:T(8,128)(2,1)}, bf16[16,48,128]{2,1,0:T(8,128)(2,1)S(1)}, u32[]{:S(2)}) copy-start(bf16[16,48,128]{2,1,0:T(8,128)(2,1)S(1)} %collective-permute-done.15.d2) | copy-start | bytes 589828
  106.5 15.4 %copy-start.17 = (bf16[16,48,128]{2,1,0:T(8,128)(2,1)}, bf16[16,48,128]{2,1,0:T(8,128)(2,1)S(1)}, u32[]{:S(2)}) copy-start(bf16[16,48,128]{2,1,0:T(8,128)(2,1)S(1)} %collective-permute-done.14.g2) | copy-start | bytes 589828
  112.3 9.6 %copy-start.18 = (bf16[16,48,128]{2,1,0:T(8,128)(2,1)}, bf16[16,48,128]{2,1,0:T(8,128)(2,1)S(1)}, u32[]{:S(2)}) copy-start(bf16[16,48,128]{2,1,0:T(8,128)(2,1)S(1)} %collective-permute-done.13.e2) | copy-start | bytes 589828
  112.7 9.2 %copy-start.19 = (bf16[16,48,128]{2,1,0:T(8,128)(2,1)}, bf16[16,48,128]{2,1,0:T(8,128)(2,1)S(1)}, u32[]{:S(2)}) copy-start(bf16[16,48,128]{2,1,0:T(8,128)(2,1)S(1)} %collective-permute-done.12.f2) | copy-start | bytes 589828
  116.4 1.0 copy-start
  122.0 17.7 %all-to-all-start.3 = ((bf16[8,160,256]{2,1,0:T(8,128)(2,1)}), bf16[8,160,256]{2,1,0:T(8,128)(2,1)S(1)}, u32[]{:S(2)}, u32[]{:S(2)}) async-start(bf16[8,160,256]{2,1,0:T(8,128)(2,1)} %get-tuple-element.103), calls=%async_computation.3 | async-start | bytes 1310720 | tf_op jit(solution)/shard_map/all_to_all | solution.py:438
  126.9 10.0 %copy-start.25 = (f32[64,128]{1,0:T(8,128)S(1)}, f32[64,128]{1,0:T(8,128)}, u32[]{:S(2)}) copy-start(f32[64,128]{1,0:T(8,128)} %get-tuple-element.105) | copy-start | bytes 98308
  126.9 11.2 %copy-start.21 = (f32[64,128]{1,0:T(8,128)S(1)}, f32[64,128]{1,0:T(8,128)}, u32[]{:S(2)}) copy-start(f32[64,128]{1,0:T(8,128)} %get-tuple-element.104) | copy-start | bytes 98308
  132.5 5.6 %collective-permute-start.16 = (f32[8,24,128]{2,1,0:T(8,128)}, f32[8,24,128]{2,1,0:T(8,128)S(1)}, u32[]{:S(2)}, u32[]{:S(2)}) collective-permute-start(f32[8,24,128]{2,1,0:T(8,128)} %get-tuple-element.102), channel_id=1, source_target_pairs={{0,32},{32,0},{1,33},{33,1},{2,34},{34,2},{3,35},{35,3},{4,36},{36... | collective-permute-start | bytes 294920 | tf_op jit(solution)/shard_map/ppermute | solution.py:380
  136.9 1.2 collective-permute-start.17
  139.6 5.4 %copy-start.2 = (bf16[8,160,256]{2,1,0:T(8,128)(2,1)}, bf16[8,160,256]{2,1,0:T(8,128)(2,1)S(1)}, u32[]{:S(2)}) copy-start(bf16[8,160,256]{2,1,0:T(8,128)(2,1)S(1)} %all-to-all-done.3.parts) | copy-start | bytes 1966084
  139.6 10.8 %all-to-all-start.4 = ((f32[8,24,128]{2,1,0:T(8,128)}), f32[8,24,128]{2,1,0:T(8,128)S(1)}, u32[]{:S(2)}, u32[]{:S(2)}) async-start(f32[8,24,128]{2,1,0:T(8,128)} %add.20), calls=%async_computation.4 | async-start | bytes 196608 | tf_op jit(solution)/shard_map/all_to_all | solution.py:444
  150.5 3.9 %collective-permute-start.18 = (f32[256,128]{1,0:T(8,128)S(1)}, f32[256,128]{1,0:T(8,128)S(1)}, u32[]{:S(2)}, u32[]{:S(2)}) collective-permute-start(f32[256,128]{1,0:T(8,128)S(1)} %pad_maximum_fusion), channel_id=1, source_target_pairs={{0,64},{64,0},{128,192},{192,128},{1,65},{65,1},{129,193},{193,129... | collective-permute-start | bytes 393224 | tf_op jit(solution)/shard_map/ppermute | solution.py:448
  150.6 16.5 %all-to-all-start.5 = ((bf16[4,160,256]{2,1,0:T(8,128)(2,1)}), bf16[4,160,256]{2,1,0:T(8,128)(2,1)S(1)}, u32[]{:S(2)}, u32[]{:S(2)}) async-start(bf16[4,160,256]{2,1,0:T(8,128)(2,1)} %shard_map.178), calls=%async_computation.5 | async-start | bytes 655360 | tf_op jit(solution)/shard_map/all_to_all | solution.py:447
  154.4 5.1 %collective-permute-start.19 = (f32[256,128]{1,0:T(8,128)S(1)}, f32[256,128]{1,0:T(8,128)S(1)}, u32[]{:S(2)}, u32[]{:S(2)}) collective-permute-start(f32[256,128]{1,0:T(8,128)S(1)} %fusion), channel_id=1, source_target_pairs={{0,192},{192,0},{64,128},{128,64},{1,193},{193,1},{65,129},{129,65... | collective-permute-start | bytes 393224 | tf_op jit(solution)/shard_map/ppermute | solution.py:449
  159.5 5.0 %copy-start.10 = (f32[256,128]{1,0:T(8,128)}, f32[256,128]{1,0:T(8,128)S(1)}, u32[]{:S(2)}) copy-start(f32[256,128]{1,0:T(8,128)S(1)} %add.23.keep) | copy-start | bytes 393220
  159.5 5.0 %collective-permute-start.20 = (f32[256,128]{1,0:T(8,128)S(1)}, f32[256,128]{1,0:T(8,128)S(1)}, u32[]{:S(2)}, u32[]{:S(2)}) collective-permute-start(f32[256,128]{1,0:T(8,128)S(1)} %add.23.keep), channel_id=1, source_target_pairs={{0,32},{32,0},{1,33},{33,1},{2,34},{34,2},{3,35},{35,3},{4,36},{36... | collective-permute-start | bytes 393224 | tf_op jit(solution)/shard_map/ppermute | solution.py:380
  (6 other events, 4.6 us)

commit v10 on v8

--- a/solution.py
+++ b/solution.py
@@ -48,7 +48,7 @@
         rows[aligned(b, TILE), 0:width] = table[:, aligned(b, TILE)].astype(F32).T
         return carry
 
-    lax.fori_loop(0, table.shape[1] // TILE, turn, 0, unroll=8)
+    lax.fori_loop(0, table.shape[1] // TILE, turn, 0, unroll=16)
     step = 64
 
     def pick(g, carry):
@@ -76,7 +76,7 @@
         out[r] = jnp.concatenate([both, term], axis=0).astype(BF)
         return carry
 
-    lax.fori_loop(0, blocks, merge, 0, unroll=2)
+    lax.fori_loop(0, blocks, merge, 0, unroll=4)
 
 
 def hop(place, table, ids, cols, bias, tiles, after):

time: 171 us -> 168 us (0.982)
  Pallas kernels: 54.6 us -> 51.9 us
    pallas_call x1, Pallas kernels: 27.1 us -> 24.4 us  [hop(): pl.pallas_call(hop_kernel, in_specs=[SMEM, SMEM, SMEM, VMEM, VMEM, HBM, H...]
  transfers between devices with their start and end apart: 27 -> 27, of which waited for: 12 -> 12; matrix products, arithmetic and copies ran while one was open for 2% -> 2% of each run, Pallas kernels for 27% -> 26%
where the time goes in v10:
time: 168 us; the launch traced here: 167 us
  starting transfers between devices  70.4 us (42%)
  Pallas kernels  51.9 us (31%)
  waiting for transfers between devices  33.8 us (20%)
  local copies, waits for them, and re-layouts  8.31 us (5%)
    pallas_call x1, Pallas kernels, hop(): pl.pallas_call(hop_kernel, in_specs=[SMEM, SMEM, SMEM, VMEM, VMEM, HBM, H...  24.4 us
    ppermute x10, waiting for transfers between devices, shift(): return lax.ppermute(value, axis, [(i, (i + by) % 4) for i in range(4)])  20.9 us
    all_to_all x1, starting transfers between devices, shards(): weights = lax.all_to_all(packed, FEAT, 0, 0, tiled=True)  12 us
    ppermute x10, starting transfers between devices, shift(): return lax.ppermute(value, axis, [(i, (i + by) % 4) for i in range(4)])  11.9 us
    ppermute x7, starting transfers between devices, swap(): return lax.ppermute(value, axis, [(0, 1), (1, 0)])  10.2 us
    all_to_all x1, starting transfers between devices, shards(): got = lax.all_to_all(send, FEAT, 0, 0, tiled=True)  7.42 us
    unnamed x54, local copies, waits for them, and re-layouts  6.99 us
    pallas_call x1, Pallas kernels, spread(): pl.pallas_call(spread_kernel, in_specs=[SMEM, SMEM, SMEM] + [VMEM] * 4, o...  5.94 us
  transfers between devices with their start and end apart: 27, of which 12 were waited for; matrix products, arithmetic and copies ran while one was open for 2% of the time, Pallas kernels for 26%

profile of v10, /device:TPU:1, one launch (start us, length us, event | category | flops | bytes accessed | tf_op | source)
XLA Modules:
  0.0 166.9 jit_solution(5954716023909700389)
XLA Ops:
  1.3 1.8 %shard_map.172 = (bf16[32,24,512]{2,1,0:T(8,128)(2,1)}, bf16[64,256]{1,0:T(8,128)(2,1)}) custom-call(s32[5]{0:T(128)} %stack.23.place, bf16[24,1024]{1,0:T(8,128)(2,1)} %own.1, bf16[24,1024]{1,0:T(8,128)(2,1)} %neigh.1, bf16[32,153]{1,0:T(8,128)(2,1)} %head_self.1, bf16[32,153]{1,0:T(8,128)(2,1)} %head_neigh.1), custom_call_target="tpu_custom_call" | custom-call | tf_op jit(solution)/shard_map/pallas_call | solution.py:116
  3.1 12.0 %all-to-all-start = ((bf16[32,24,512]{2,1,0:T(8,128)(2,1)}), bf16[32,24,512]{2,1,0:T(8,128)(2,1)S(1)}, u32[]{:S(2)}, u32[]{:S(2)}) async-start(bf16[32,24,512]{2,1,0:T(8,128)(2,1)} %get-tuple-element.65._), calls=%async_computation | async-start | bytes 1572864 | tf_op jit(solution)/shard_map/all_to_all | solution.py:405
  15.1 2.2 %collective-permute-start = (bf16[64,256]{1,0:T(8,128)(2,1)}, bf16[64,256]{1,0:T(8,128)(2,1)S(1)}, u32[]{:S(2)}, u32[]{:S(2)}) collective-permute-start(bf16[64,256]{1,0:T(8,128)(2,1)} %get-tuple-element.75), channel_id=1, source_target_pairs={{0,8},{8,0},{16,24},{24,16},{1,9},{9,1},{17,25},{25,17},{2,10},{10... | collective-permute-start | bytes 98312 | tf_op jit(solution)/shard_map/ppermute | solution.py:409
  17.3 1.4 copy.19.cols
  18.7 24.4 %shard_map.173 = (bf16[32,56,128]{2,1,0:T(8,128)(2,1)}, bf16[32,48,128]{2,1,0:T(8,128)(2,1)}) custom-call(s32[5]{0:T(128)} %stack.23.place, s32[16384]{0:T(1024)} %ids.1, s32[32,8]{1,0:T(8,128)} %copy.19.cols, bf16[24,32768]{1,0:T(8,128)(2,1)} %table.1, f32[1,32]{1,0:T(1,128)} %bitcast.14, bf16[32,8,128,128]{3,2,1,0:T(8,128)(2,1)} %tiles_hbm.1, ...), custom_call_target="tpu_custom_call" | custom-call | flops 1000000000 | bytes 60000000 | tf_op jit(solution)/shard_map/pallas_call | solution.py:84
  43.3 2.6 %collective-permute-start.2 = (bf16[768,256]{1,0:T(8,128)(2,1)S(1)}, bf16[768,256]{1,0:T(8,128)(2,1)}, u32[]{:S(2)}, u32[]{:S(2)}) collective-permute-start(bf16[768,256]{1,0:T(8,128)(2,1)S(1)} %get-tuple-element.124), channel_id=1, source_target_pairs={{0,192},{64,0},{128,64},{192,128},{1,193},{65,1},{129,65},{193,129... | collective-permute-start | bytes 1179656 | tf_op jit(solution)/shard_map/ppermute | solution.py:371
  45.8 7.4 %all-to-all-start.1 = ((bf16[32,56,128]{2,1,0:T(8,128)(2,1)}), bf16[32,56,128]{2,1,0:T(8,128)(2,1)S(1)}, u32[]{:S(2)}, u32[]{:S(2)}) async-start(bf16[32,56,128]{2,1,0:T(8,128)(2,1)} %get-tuple-element.69), calls=%async_computation.1 | async-start | bytes 917504 | tf_op jit(solution)/shard_map/all_to_all | solution.py:413
  53.3 2.6 %collective-permute-done.1.w1 = bf16[768,256]{1,0:T(8,128)(2,1)S(1)} collective-permute-done((bf16[768,256]{1,0:T(8,128)(2,1)S(1)}, bf16[768,256]{1,0:T(8,128)(2,1)S(1)}, u32[]{:S(2)}, u32[]{:S(2)}) %collective-permute-start.1) | collective-permute-done | bytes 393248 | tf_op jit(solution)/shard_map/ppermute | solution.py:371
  55.8 2.7 %collective-permute-start.3 = (bf16[768,512]{1,0:T(8,128)(2,1)S(1)}, bf16[768,512]{1,0:T(8,128)(2,1)S(1)}, u32[]{:S(2)}, u32[]{:S(2)}) collective-permute-start(bf16[768,512]{1,0:T(8,128)(2,1)S(1)} %bitcast.10), channel_id=1, source_target_pairs={{0,32},{32,0},{1,33},{33,1},{2,34},{34,2},{3,35},{35,3},{4,36},{36... | collective-permute-start | bytes 2359304 | tf_op jit(solution)/shard_map/ppermute | solution.py:381
  59.1 1.2 collective-permute-start.9
  60.3 2.4 %collective-permute-start.8 = (bf16[32,48,128]{2,1,0:T(8,128)(2,1)S(1)}, bf16[32,48,128]{2,1,0:T(8,128)(2,1)S(1)}, u32[]{:S(2)}, u32[]{:S(2)}) collective-permute-start(bf16[32,48,128]{2,1,0:T(8,128)(2,1)S(1)} %copy-done.11), channel_id=1, source_target_pairs={{0,3},{1,0},{2,1},{3,2},{4,7},{5,4},{6,5},{7,6},{8,11},{9,8},{10,9... | collective-permute-start | bytes 1179656 | tf_op jit(solution)/shard_map/ppermute | solution.py:371
  62.7 0.8 copy-done.13
  63.6 0.7 copy-done.14
  64.3 3.3 %collective-permute-start.6 = (bf16[128,256]{1,0:T(8,128)(2,1)S(1)}, bf16[128,256]{1,0:T(8,128)(2,1)S(1)}, u32[]{:S(2)}, u32[]{:S(2)}) collective-permute-start(bf16[128,256]{1,0:T(8,128)(2,1)S(1)} %constant_dynamic-update-slice_fusion.pair), channel_id=1, source_target_pairs={{0,16},{16,0},{8,24},{24,8},{1,17},{17,1},{9,25},{25,9},{2,18},{18... | collective-permute-start | bytes 196616 | tf_op jit(solution)/shard_map/ppermute | solution.py:422
  67.7 0.8 copy-done.3
  68.5 0.9 copy-done.9
  69.3 4.0 %shard_map.174 = bf16[32,128,128]{2,1,0:T(8,128)(2,1)} custom-call(s32[5]{0:T(128)} %stack.23.place, bf16[32,56,128]{2,1,0:T(8,128)(2,1)} %copy-done.3, bf16[768,512]{1,0:T(8,128)(2,1)} %bitcast.11, bf16[768,256]{1,0:T(8,128)(2,1)} %copy-done.12, bf16[768,256]{1,0:T(8,128)(2,1)} %collective-permute-done.2.w2, bf16[768,512]{1,0:T(8,128)(2,1)} %copy-done.9, ...), custom_call_target="tpu_custom_call" | custom-call | tf_op jit(solution)/shard_map/pallas_call | solution.py:206
  73.3 4.7 %collective-permute-done.6.quad = bf16[128,256]{1,0:T(8,128)(2,1)S(1)} collective-permute-done((bf16[128,256]{1,0:T(8,128)(2,1)S(1)}, bf16[128,256]{1,0:T(8,128)(2,1)S(1)}, u32[]{:S(2)}, u32[]{:S(2)}) %collective-permute-start.6) | collective-permute-done | bytes 65568 | tf_op jit(solution)/shard_map/ppermute | solution.py:422
  78.0 5.8 %all-to-all-start.2 = ((bf16[32,128,128]{2,1,0:T(8,128)(2,1)}), bf16[32,128,128]{2,1,0:T(8,128)(2,1)S(1)}, u32[]{:S(2)}, u32[]{:S(2)}) async-start(bf16[32,128,128]{2,1,0:T(8,128)(2,1)} %shard_map.174), calls=%async_computation.2 | async-start | bytes 2097152 | tf_op jit(solution)/shard_map/all_to_all | solution.py:428
  83.8 2.5 %collective-permute-start.13 = (bf16[32,48,128]{2,1,0:T(8,128)(2,1)}, bf16[32,48,128]{2,1,0:T(8,128)(2,1)S(1)}, u32[]{:S(2)}, u32[]{:S(2)}) collective-permute-start(bf16[32,48,128]{2,1,0:T(8,128)(2,1)} %collective-permute-done.9.g0), channel_id=1, source_target_pairs={{0,3},{1,0},{2,1},{3,2},{4,7},{5,4},{6,5},{7,6},{8,11},{9,8},{10,9... | collective-permute-start | bytes 1179656 | tf_op jit(solution)/shard_map/ppermute | solution.py:371
  87.0 2.8 %collective-permute-start.11 = (bf16[16,48,128]{2,1,0:T(8,128)(2,1)S(1)}, bf16[16,48,128]{2,1,0:T(8,128)(2,1)S(1)}, u32[]{:S(2)}, u32[]{:S(2)}) collective-permute-start(bf16[16,48,128]{2,1,0:T(8,128)(2,1)S(1)} %slice.21), channel_id=1, source_target_pairs={{0,3},{1,0},{2,1},{3,2},{4,7},{5,4},{6,5},{7,6},{8,11},{9,8},{10,9... | collective-permute-start | bytes 589832 | tf_op jit(solution)/shard_map/ppermute | solution.py:371
  89.8 5.9 %shard_map.175 = (f32[32,128,128]{2,1,0:T(8,128)}, bf16[256,1024]{1,0:T(8,128)(2,1)}, bf16[256,128]{1,0:T(8,128)(2,1)}, bf16[256,128]{1,0:T(8,128)(2,1)}) custom-call(s32[5]{0:T(128)} %stack.23.place, s32[8,8]{1,0:T(8,128)} %cols.4, s32[1]{0:T(128)} %dynamic_slice.3.live, bf16[153,1024]{1,0:T(8,128)(2,1)} %logit_cot.1, bf16[128,256]{1,0:T(8,128)(2,1)} %copy-done.22, ...), custom_call_target="tpu_custom_call" | custom-call | flops 1000000000 | bytes 8000000 | tf_op jit(solution)/shard_map/pallas_call | solution.py:156
  95.7 6.1 %collective-permute-done.13.g3 = bf16[32,48,128]{2,1,0:T(8,128)(2,1)S(1)} collective-permute-done((bf16[32,48,128]{2,1,0:T(8,128)(2,1)}, bf16[32,48,128]{2,1,0:T(8,128)(2,1)S(1)}, u32[]{:S(2)}, u32[]{:S(2)}) %collective-permute-start.13) | collective-permute-done | bytes 393248 | tf_op jit(solution)/shard_map/ppermute | solution.py:371
  101.8 2.7 %collective-permute-done.12.g1 = bf16[32,48,128]{2,1,0:T(8,128)(2,1)S(1)} collective-permute-done((bf16[32,48,128]{2,1,0:T(8,128)(2,1)}, bf16[32,48,128]{2,1,0:T(8,128)(2,1)S(1)}, u32[]{:S(2)}, u32[]{:S(2)}) %collective-permute-start.12) | collective-permute-done | bytes 393248 | tf_op jit(solution)/shard_map/ppermute | solution.py:371
  104.6 0.9 collective-permute-start.15
  105.5 0.7 collective-permute-start.14
  106.1 2.1 %collective-permute-done.11.e2 = bf16[16,48,128]{2,1,0:T(8,128)(2,1)S(1)} collective-permute-done((bf16[16,48,128]{2,1,0:T(8,128)(2,1)S(1)}, bf16[16,48,128]{2,1,0:T(8,128)(2,1)S(1)}, u32[]{:S(2)}, u32[]{:S(2)}) %collective-permute-start.11) | collective-permute-done | bytes 196640 | tf_op jit(solution)/shard_map/ppermute | solution.py:371
  108.2 3.9 %collective-permute-done.10.f2 = bf16[16,48,128]{2,1,0:T(8,128)(2,1)S(1)} collective-permute-done((bf16[16,48,128]{2,1,0:T(8,128)(2,1)S(1)}, bf16[16,48,128]{2,1,0:T(8,128)(2,1)S(1)}, u32[]{:S(2)}, u32[]{:S(2)}) %collective-permute-start.10) | collective-permute-done | bytes 196640 | tf_op jit(solution)/shard_map/ppermute | solution.py:371
  112.7 3.0 %collective-permute-done.14.g2 = bf16[16,48,128]{2,1,0:T(8,128)(2,1)S(1)} collective-permute-done((bf16[16,48,128]{2,1,0:T(8,128)(2,1)S(1)}, bf16[16,48,128]{2,1,0:T(8,128)(2,1)S(1)}, u32[]{:S(2)}, u32[]{:S(2)}) %collective-permute-start.14) | collective-permute-done | bytes 196640 | tf_op jit(solution)/shard_map/ppermute | solution.py:371
  115.7 1.0 copy-done
  116.7 4.5 %shard_map.176 = (bf16[8,160,256]{2,1,0:T(8,128)(2,1)}, f32[64,128]{1,0:T(8,128)}, f32[64,128]{1,0:T(8,128)}) custom-call(s32[5]{0:T(128)} %stack.23.place, s32[8,8]{1,0:T(8,128)} %cols.4, bf16[32,128,128]{2,1,0:T(8,128)(2,1)} %copy-done, f32[32,128,128]{2,1,0:T(8,128)} %get-tuple-element.92.dhidden, bf16[8,8,128,128]{3,2,1,0:T(8,128)(2,1)} %tiles.3, ...), custom_call_target="tpu_custom_call" | custom-call | tf_op jit(solution)/shard_map/pallas_call | solution.py:252
  121.2 3.6 %all-to-all-start.3 = ((bf16[8,160,256]{2,1,0:T(8,128)(2,1)}), bf16[8,160,256]{2,1,0:T(8,128)(2,1)S(1)}, u32[]{:S(2)}, u32[]{:S(2)}) async-start(bf16[8,160,256]{2,1,0:T(8,128)(2,1)} %get-tuple-element.111), calls=%async_computation.3 | async-start | bytes 1310720 | tf_op jit(solution)/shard_map/all_to_all | solution.py:441
  124.9 5.6 %shard_map.177 = (f32[8,24,128]{2,1,0:T(8,128)}, f32[8,24,128]{2,1,0:T(8,128)}) custom-call(s32[5]{0:T(128)} %stack.23.place, bf16[32,128,128]{2,1,0:T(8,128)(2,1)} %copy-done, f32[32,128,128]{2,1,0:T(8,128)} %get-tuple-element.92.dhidden, bf16[32,48,128]{2,1,0:T(8,128)(2,1)} %get-tuple-element.99.f0, bf16[32,48,128]{2,1,0:T(8,128)(2,1)} %copy-done.6, ...), custom_call_target="tpu_custom_call" | custom-call | flops 1000000000 | bytes 7000000 | tf_op jit(solution)/shard_map/pallas_call | solution.py:326
  130.5 2.2 %collective-permute-start.16 = (f32[8,24,128]{2,1,0:T(8,128)}, f32[8,24,128]{2,1,0:T(8,128)S(1)}, u32[]{:S(2)}, u32[]{:S(2)}) collective-permute-start(f32[8,24,128]{2,1,0:T(8,128)} %get-tuple-element.110), channel_id=1, source_target_pairs={{0,32},{32,0},{1,33},{33,1},{2,34},{34,2},{3,35},{35,3},{4,36},{36... | collective-permute-start | bytes 294920 | tf_op jit(solution)/shard_map/ppermute | solution.py:381
  132.8 1.1 collective-permute-done.17
  134.0 1.5 add.20
  135.5 5.3 %all-to-all-start.4 = ((f32[8,24,128]{2,1,0:T(8,128)}), f32[8,24,128]{2,1,0:T(8,128)S(1)}, u32[]{:S(2)}, u32[]{:S(2)}) async-start(f32[8,24,128]{2,1,0:T(8,128)} %add.20), calls=%async_computation.4 | async-start | bytes 196608 | tf_op jit(solution)/shard_map/all_to_all | solution.py:447
  140.9 1.9 %shard_map.178 = bf16[4,160,256]{2,1,0:T(8,128)(2,1)} custom-call(bf16[8,160,256]{2,1,0:T(8,128)(2,1)} %copy-done.2), custom_call_target="tpu_custom_call" | custom-call | tf_op jit(solution)/shard_map/pallas_call | solution.py:271
  142.8 3.5 %all-to-all-done.4 = f32[8,24,128]{2,1,0:T(8,128)S(1)} async-done(((f32[8,24,128]{2,1,0:T(8,128)}), f32[8,24,128]{2,1,0:T(8,128)S(1)}, u32[]{:S(2)}, u32[]{:S(2)}) %all-to-all-start.4) | async-done | bytes 98336 | tf_op jit(solution)/shard_map/all_to_all | solution.py:447
  146.5 5.7 %all-to-all-start.5 = ((bf16[4,160,256]{2,1,0:T(8,128)(2,1)}), bf16[4,160,256]{2,1,0:T(8,128)(2,1)S(1)}, u32[]{:S(2)}, u32[]{:S(2)}) async-start(bf16[4,160,256]{2,1,0:T(8,128)(2,1)} %shard_map.178), calls=%async_computation.5 | async-start | bytes 655360 | tf_op jit(solution)/shard_map/all_to_all | solution.py:450
  152.3 2.6 %collective-permute-start.19 = (f32[256,128]{1,0:T(8,128)S(1)}, f32[256,128]{1,0:T(8,128)S(1)}, u32[]{:S(2)}, u32[]{:S(2)}) collective-permute-start(f32[256,128]{1,0:T(8,128)S(1)} %fusion), channel_id=1, source_target_pairs={{0,192},{192,0},{64,128},{128,64},{1,193},{193,1},{65,129},{129,65... | collective-permute-start | bytes 393224 | tf_op jit(solution)/shard_map/ppermute | solution.py:452
  154.9 2.5 %collective-permute-done.19 = f32[256,128]{1,0:T(8,128)S(1)} collective-permute-done((f32[256,128]{1,0:T(8,128)S(1)}, f32[256,128]{1,0:T(8,128)S(1)}, u32[]{:S(2)}, u32[]{:S(2)}) %collective-permute-start.19) | collective-permute-done | bytes 131104 | tf_op jit(solution)/shard_map/ppermute | solution.py:452
  157.4 3.4 %collective-permute-start.20 = (f32[256,128]{1,0:T(8,128)S(1)}, f32[256,128]{1,0:T(8,128)S(1)}, u32[]{:S(2)}, u32[]{:S(2)}) collective-permute-start(f32[256,128]{1,0:T(8,128)S(1)} %add.23.keep), channel_id=1, source_target_pairs={{0,32},{32,0},{1,33},{33,1},{2,34},{34,2},{3,35},{35,3},{4,36},{36... | collective-permute-start | bytes 393224 | tf_op jit(solution)/shard_map/ppermute | solution.py:381
  160.8 1.0 collective-permute-done.20.rest
  161.8 0.6 copy-done.19
  162.5 1.9 %shard_map.180 = (f32[24,1024]{1,0:T(8,128)}, f32[24,1024]{1,0:T(8,128)}, f32[32,153]{1,0:T(8,128)}, f32[32,153]{1,0:T(8,128)}, f32[1,32]{1,0:T(1,128)}) custom-call(s32[5]{0:T(128)} %stack.23.place, f32[256,128]{1,0:T(8,128)} %copy-done.10, f32[256,128]{1,0:T(8,128)} %copy-done.19), custom_call_target="tpu_custom_call" | custom-call | tf_op jit(solution)/shard_map/pallas_call | solution.py:361
  164.3 0.7 copy-done.4
  165.0 1.9 %shard_map.179 = f32[153,1024]{1,0:T(8,128)} custom-call(bf16[4,160,256]{2,1,0:T(8,128)(2,1)} %copy-done.4), custom_call_target="tpu_custom_call" | custom-call | tf_op jit(solution)/shard_map/pallas_call | solution.py:287
  (82 shorter events, 3.1 us)
Async XLA Ops:
  3.1 40.1 %all-to-all-start = ((bf16[32,24,512]{2,1,0:T(8,128)(2,1)}), bf16[32,24,512]{2,1,0:T(8,128)(2,1)S(1)}, u32[]{:S(2)}, u32[]{:S(2)}) async-start(bf16[32,24,512]{2,1,0:T(8,128)(2,1)} %get-tuple-element.65._), calls=%async_computation | async-start | bytes 1572864 | tf_op jit(solution)/shard_map/all_to_all | solution.py:405
  15.1 28.0 %collective-permute-start = (bf16[64,256]{1,0:T(8,128)(2,1)}, bf16[64,256]{1,0:T(8,128)(2,1)S(1)}, u32[]{:S(2)}, u32[]{:S(2)}) collective-permute-start(bf16[64,256]{1,0:T(8,128)(2,1)} %get-tuple-element.75), channel_id=1, source_target_pairs={{0,8},{8,0},{16,24},{24,16},{1,9},{9,1},{17,25},{25,17},{2,10},{10... | collective-permute-start | bytes 98312 | tf_op jit(solution)/shard_map/ppermute | solution.py:409
  43.1 15.9 %copy-start.11 = (bf16[32,48,128]{2,1,0:T(8,128)(2,1)S(1)}, bf16[32,48,128]{2,1,0:T(8,128)(2,1)}, u32[]{:S(2)}) copy-start(bf16[32,48,128]{2,1,0:T(8,128)(2,1)} %get-tuple-element.99.f0) | copy-start | bytes 1179652
  43.2 20.4 %copy-start.21 = (bf16[64,256]{1,0:T(8,128)(2,1)S(1)}, bf16[64,256]{1,0:T(8,128)(2,1)}, u32[]{:S(2)}) copy-start(bf16[64,256]{1,0:T(8,128)(2,1)} %get-tuple-element.75) | copy-start | bytes 98308
  43.2 24.5 %copy-start.1 = (bf16[32,24,512]{2,1,0:T(8,128)(2,1)}, bf16[32,24,512]{2,1,0:T(8,128)(2,1)S(1)}, u32[]{:S(2)}) copy-start(bf16[32,24,512]{2,1,0:T(8,128)(2,1)S(1)} %all-to-all-done) | copy-start | bytes 2359300
  43.3 10.0 %collective-permute-start.2 = (bf16[768,256]{1,0:T(8,128)(2,1)S(1)}, bf16[768,256]{1,0:T(8,128)(2,1)}, u32[]{:S(2)}, u32[]{:S(2)}) collective-permute-start(bf16[768,256]{1,0:T(8,128)(2,1)S(1)} %get-tuple-element.124), channel_id=1, source_target_pairs={{0,192},{64,0},{128,64},{192,128},{1,193},{65,1},{129,65},{193,129... | collective-permute-start | bytes 1179656 | tf_op jit(solution)/shard_map/ppermute | solution.py:371
  45.8 10.0 %collective-permute-start.1 = (bf16[768,256]{1,0:T(8,128)(2,1)S(1)}, bf16[768,256]{1,0:T(8,128)(2,1)S(1)}, u32[]{:S(2)}, u32[]{:S(2)}) collective-permute-start(bf16[768,256]{1,0:T(8,128)(2,1)S(1)} %get-tuple-element.125), channel_id=1, source_target_pairs={{0,64},{64,128},{128,192},{192,0},{1,65},{65,129},{129,193},{193,1... | collective-permute-start | bytes 1179656 | tf_op jit(solution)/shard_map/ppermute | solution.py:371
  45.8 21.9 %all-to-all-start.1 = ((bf16[32,56,128]{2,1,0:T(8,128)(2,1)}), bf16[32,56,128]{2,1,0:T(8,128)(2,1)S(1)}, u32[]{:S(2)}, u32[]{:S(2)}) async-start(bf16[32,56,128]{2,1,0:T(8,128)(2,1)} %get-tuple-element.69), calls=%async_computation.1 | async-start | bytes 917504 | tf_op jit(solution)/shard_map/all_to_all | solution.py:413
  55.8 6.8 %copy-start.12 = (bf16[768,256]{1,0:T(8,128)(2,1)}, bf16[768,256]{1,0:T(8,128)(2,1)S(1)}, u32[]{:S(2)}) copy-start(bf16[768,256]{1,0:T(8,128)(2,1)S(1)} %collective-permute-done.1.w1) | copy-start | bytes 1179652
  55.8 11.9 %collective-permute-start.3 = (bf16[768,512]{1,0:T(8,128)(2,1)S(1)}, bf16[768,512]{1,0:T(8,128)(2,1)S(1)}, u32[]{:S(2)}, u32[]{:S(2)}) collective-permute-start(bf16[768,512]{1,0:T(8,128)(2,1)S(1)} %bitcast.10), channel_id=1, source_target_pairs={{0,32},{32,0},{1,33},{33,1},{2,34},{34,2},{3,35},{35,3},{4,36},{36... | collective-permute-start | bytes 2359304 | tf_op jit(solution)/shard_map/ppermute | solution.py:381
  58.6 4.1 %collective-permute-start.4 = (bf16[768,256]{1,0:T(8,128)(2,1)S(1)}, bf16[768,256]{1,0:T(8,128)(2,1)S(1)}, u32[]{:S(2)}, u32[]{:S(2)}) collective-permute-start(bf16[768,256]{1,0:T(8,128)(2,1)S(1)} %collective-permute-done.1.w1), channel_id=1, source_target_pairs={{0,32},{32,0},{1,33},{33,1},{2,34},{34,2},{3,35},{35,3},{4,36},{36... | collective-permute-start | bytes 1179656 | tf_op jit(solution)/shard_map/ppermute | solution.py:381
  58.6 5.0 %collective-permute-start.5 = (bf16[768,256]{1,0:T(8,128)(2,1)}, bf16[768,256]{1,0:T(8,128)(2,1)S(1)}, u32[]{:S(2)}, u32[]{:S(2)}) collective-permute-start(bf16[768,256]{1,0:T(8,128)(2,1)} %collective-permute-done.2.w2), channel_id=1, source_target_pairs={{0,32},{32,0},{1,33},{33,1},{2,34},{34,2},{3,35},{35,3},{4,36},{36... | collective-permute-start | bytes 1179656 | tf_op jit(solution)/shard_map/ppermute | solution.py:381
  59.1 18.9 %collective-permute-start.9 = (bf16[32,48,128]{2,1,0:T(8,128)(2,1)S(1)}, bf16[32,48,128]{2,1,0:T(8,128)(2,1)}, u32[]{:S(2)}, u32[]{:S(2)}) collective-permute-start(bf16[32,48,128]{2,1,0:T(8,128)(2,1)S(1)} %copy-done.11), channel_id=1, source_target_pairs={{0,4},{4,0},{1,5},{5,1},{2,6},{6,2},{3,7},{7,3},{8,12},{12,8},{9,1... | collective-permute-start | bytes 1179656 | tf_op jit(solution)/shard_map/ppermute | solution.py:381
  60.3 17.7 %collective-permute-start.8 = (bf16[32,48,128]{2,1,0:T(8,128)(2,1)S(1)}, bf16[32,48,128]{2,1,0:T(8,128)(2,1)S(1)}, u32[]{:S(2)}, u32[]{:S(2)}) collective-permute-start(bf16[32,48,128]{2,1,0:T(8,128)(2,1)S(1)} %copy-done.11), channel_id=1, source_target_pairs={{0,3},{1,0},{2,1},{3,2},{4,7},{5,4},{6,5},{7,6},{8,11},{9,8},{10,9... | collective-permute-start | bytes 1179656 | tf_op jit(solution)/shard_map/ppermute | solution.py:371
  63.4 14.6 %collective-permute-start.7 = (bf16[32,48,128]{2,1,0:T(8,128)(2,1)S(1)}, bf16[32,48,128]{2,1,0:T(8,128)(2,1)S(1)}, u32[]{:S(2)}, u32[]{:S(2)}) collective-permute-start(bf16[32,48,128]{2,1,0:T(8,128)(2,1)S(1)} %copy-done.11), channel_id=1, source_target_pairs={{0,1},{1,2},{2,3},{3,0},{4,5},{5,6},{6,7},{7,4},{8,9},{9,10},{10,1... | collective-permute-start | bytes 1179656 | tf_op jit(solution)/shard_map/ppermute | solution.py:371
  63.6 26.2 %copy-start.22 = (bf16[128,256]{1,0:T(8,128)(2,1)}, bf16[128,256]{1,0:T(8,128)(2,1)S(1)}, u32[]{:S(2)}) copy-start(bf16[128,256]{1,0:T(8,128)(2,1)S(1)} %constant_dynamic-update-slice_fusion.pair) | copy-start | bytes 196612
  64.3 13.6 %collective-permute-start.6 = (bf16[128,256]{1,0:T(8,128)(2,1)S(1)}, bf16[128,256]{1,0:T(8,128)(2,1)S(1)}, u32[]{:S(2)}, u32[]{:S(2)}) collective-permute-start(bf16[128,256]{1,0:T(8,128)(2,1)S(1)} %constant_dynamic-update-slice_fusion.pair), channel_id=1, source_target_pairs={{0,16},{16,0},{8,24},{24,8},{1,17},{17,1},{9,25},{25,9},{2,18},{18... | collective-permute-start | bytes 196616 | tf_op jit(solution)/shard_map/ppermute | solution.py:422
  68.5 0.9 copy-start.9
  73.3 13.1 %copy-start.25 = (s32[8]{0:T(128)S(1)}, s32[8]{0:T(128)}, u32[]{:S(2)}) copy-start(s32[8]{0:T(128)} %param.24) | copy-start | bytes 100
  78.0 11.8 %copy-start.23 = (bf16[128,256]{1,0:T(8,128)(2,1)}, bf16[128,256]{1,0:T(8,128)(2,1)S(1)}, u32[]{:S(2)}) copy-start(bf16[128,256]{1,0:T(8,128)(2,1)S(1)} %collective-permute-done.6.quad) | copy-start | bytes 196612
  78.0 17.7 %copy-start.5 = (bf16[32,48,128]{2,1,0:T(8,128)(2,1)}, bf16[32,48,128]{2,1,0:T(8,128)(2,1)S(1)}, u32[]{:S(2)}) copy-start(bf16[32,48,128]{2,1,0:T(8,128)(2,1)S(1)} %collective-permute-done.8.f3) | copy-start | bytes 1179652
  78.0 17.7 %copy-start.6 = (bf16[32,48,128]{2,1,0:T(8,128)(2,1)}, bf16[32,48,128]{2,1,0:T(8,128)(2,1)S(1)}, u32[]{:S(2)}) copy-start(bf16[32,48,128]{2,1,0:T(8,128)(2,1)S(1)} %collective-permute-done.7.f1) | copy-start | bytes 1179652
  78.0 37.7 %all-to-all-start.2 = ((bf16[32,128,128]{2,1,0:T(8,128)(2,1)}), bf16[32,128,128]{2,1,0:T(8,128)(2,1)S(1)}, u32[]{:S(2)}, u32[]{:S(2)}) async-start(bf16[32,128,128]{2,1,0:T(8,128)(2,1)} %shard_map.174), calls=%async_computation.2 | async-start | bytes 2097152 | tf_op jit(solution)/shard_map/all_to_all | solution.py:428
  83.8 18.0 %collective-permute-start.13 = (bf16[32,48,128]{2,1,0:T(8,128)(2,1)}, bf16[32,48,128]{2,1,0:T(8,128)(2,1)S(1)}, u32[]{:S(2)}, u32[]{:S(2)}) collective-permute-start(bf16[32,48,128]{2,1,0:T(8,128)(2,1)} %collective-permute-done.9.g0), channel_id=1, source_target_pairs={{0,3},{1,0},{2,1},{3,2},{4,7},{5,4},{6,5},{7,6},{8,11},{9,8},{10,9... | collective-permute-start | bytes 1179656 | tf_op jit(solution)/shard_map/ppermute | solution.py:371
  86.4 18.2 %collective-permute-start.12 = (bf16[32,48,128]{2,1,0:T(8,128)(2,1)}, bf16[32,48,128]{2,1,0:T(8,128)(2,1)S(1)}, u32[]{:S(2)}, u32[]{:S(2)}) collective-permute-start(bf16[32,48,128]{2,1,0:T(8,128)(2,1)} %collective-permute-done.9.g0), channel_id=1, source_target_pairs={{0,1},{1,2},{2,3},{3,0},{4,5},{5,6},{6,7},{7,4},{8,9},{9,10},{10,1... | collective-permute-start | bytes 1179656 | tf_op jit(solution)/shard_map/ppermute | solution.py:371
  87.0 21.2 %collective-permute-start.11 = (bf16[16,48,128]{2,1,0:T(8,128)(2,1)S(1)}, bf16[16,48,128]{2,1,0:T(8,128)(2,1)S(1)}, u32[]{:S(2)}, u32[]{:S(2)}) collective-permute-start(bf16[16,48,128]{2,1,0:T(8,128)(2,1)S(1)} %slice.21), channel_id=1, source_target_pairs={{0,3},{1,0},{2,1},{3,2},{4,7},{5,4},{6,5},{7,6},{8,11},{9,8},{10,9... | collective-permute-start | bytes 589832 | tf_op jit(solution)/shard_map/ppermute | solution.py:371
  89.7 22.3 %collective-permute-start.10 = (bf16[16,48,128]{2,1,0:T(8,128)(2,1)S(1)}, bf16[16,48,128]{2,1,0:T(8,128)(2,1)S(1)}, u32[]{:S(2)}, u32[]{:S(2)}) collective-permute-start(bf16[16,48,128]{2,1,0:T(8,128)(2,1)S(1)} %slice.20), channel_id=1, source_target_pairs={{0,1},{1,2},{2,3},{3,0},{4,5},{5,6},{6,7},{7,4},{8,9},{9,10},{10,1... | collective-permute-start | bytes 589832 | tf_op jit(solution)/shard_map/ppermute | solution.py:371
  101.8 19.4 %copy-start.7 = (bf16[32,48,128]{2,1,0:T(8,128)(2,1)}, bf16[32,48,128]{2,1,0:T(8,128)(2,1)S(1)}, u32[]{:S(2)}) copy-start(bf16[32,48,128]{2,1,0:T(8,128)(2,1)S(1)} %collective-permute-done.13.g3) | copy-start | bytes 1179652
  104.5 16.7 %copy-start.8 = (bf16[32,48,128]{2,1,0:T(8,128)(2,1)}, bf16[32,48,128]{2,1,0:T(8,128)(2,1)S(1)}, u32[]{:S(2)}) copy-start(bf16[32,48,128]{2,1,0:T(8,128)(2,1)S(1)} %collective-permute-done.12.g1) | copy-start | bytes 1179652
  104.6 8.1 %collective-permute-start.15 = (bf16[16,48,128]{2,1,0:T(8,128)(2,1)S(1)}, bf16[16,48,128]{2,1,0:T(8,128)(2,1)S(1)}, u32[]{:S(2)}, u32[]{:S(2)}) collective-permute-start(bf16[16,48,128]{2,1,0:T(8,128)(2,1)S(1)} %slice.23), channel_id=1, source_target_pairs={{0,3},{1,0},{2,1},{3,2},{4,7},{5,4},{6,5},{7,6},{8,11},{9,8},{10,9... | collective-permute-start | bytes 589832 | tf_op jit(solution)/shard_map/ppermute | solution.py:371
  105.5 10.2 %collective-permute-start.14 = (bf16[16,48,128]{2,1,0:T(8,128)(2,1)S(1)}, bf16[16,48,128]{2,1,0:T(8,128)(2,1)S(1)}, u32[]{:S(2)}, u32[]{:S(2)}) collective-permute-start(bf16[16,48,128]{2,1,0:T(8,128)(2,1)S(1)} %slice.22), channel_id=1, source_target_pairs={{0,1},{1,2},{2,3},{3,0},{4,5},{5,6},{6,7},{7,4},{8,9},{9,10},{10,1... | collective-permute-start | bytes 589832 | tf_op jit(solution)/shard_map/ppermute | solution.py:371
  108.2 16.6 %copy-start.15 = (bf16[16,48,128]{2,1,0:T(8,128)(2,1)}, bf16[16,48,128]{2,1,0:T(8,128)(2,1)S(1)}, u32[]{:S(2)}) copy-start(bf16[16,48,128]{2,1,0:T(8,128)(2,1)S(1)} %collective-permute-done.11.e2) | copy-start | bytes 589828
  112.1 12.8 %copy-start.16 = (bf16[16,48,128]{2,1,0:T(8,128)(2,1)}, bf16[16,48,128]{2,1,0:T(8,128)(2,1)S(1)}, u32[]{:S(2)}) copy-start(bf16[16,48,128]{2,1,0:T(8,128)(2,1)S(1)} %collective-permute-done.10.f2) | copy-start | bytes 589828
  112.7 12.2 %copy-start.17 = (bf16[16,48,128]{2,1,0:T(8,128)(2,1)}, bf16[16,48,128]{2,1,0:T(8,128)(2,1)S(1)}, u32[]{:S(2)}) copy-start(bf16[16,48,128]{2,1,0:T(8,128)(2,1)S(1)} %collective-permute-done.15.d2) | copy-start | bytes 589828
  115.7 9.2 %copy-start.18 = (bf16[16,48,128]{2,1,0:T(8,128)(2,1)}, bf16[16,48,128]{2,1,0:T(8,128)(2,1)S(1)}, u32[]{:S(2)}) copy-start(bf16[16,48,128]{2,1,0:T(8,128)(2,1)S(1)} %collective-permute-done.14.g2) | copy-start | bytes 589828
  115.7 1.0 copy-start
  121.2 14.3 %all-to-all-start.3 = ((bf16[8,160,256]{2,1,0:T(8,128)(2,1)}), bf16[8,160,256]{2,1,0:T(8,128)(2,1)S(1)}, u32[]{:S(2)}, u32[]{:S(2)}) async-start(bf16[8,160,256]{2,1,0:T(8,128)(2,1)} %get-tuple-element.111), calls=%async_computation.3 | async-start | bytes 1310720 | tf_op jit(solution)/shard_map/all_to_all | solution.py:441
  124.8 7.9 %copy-start.24 = (f32[64,128]{1,0:T(8,128)S(1)}, f32[64,128]{1,0:T(8,128)}, u32[]{:S(2)}) copy-start(f32[64,128]{1,0:T(8,128)} %get-tuple-element.113) | copy-start | bytes 98308
  124.8 9.1 %copy-start.20 = (f32[64,128]{1,0:T(8,128)S(1)}, f32[64,128]{1,0:T(8,128)}, u32[]{:S(2)}) copy-start(f32[64,128]{1,0:T(8,128)} %get-tuple-element.112) | copy-start | bytes 98308
  130.5 3.5 %collective-permute-start.16 = (f32[8,24,128]{2,1,0:T(8,128)}, f32[8,24,128]{2,1,0:T(8,128)S(1)}, u32[]{:S(2)}, u32[]{:S(2)}) collective-permute-start(f32[8,24,128]{2,1,0:T(8,128)} %get-tuple-element.110), channel_id=1, source_target_pairs={{0,32},{32,0},{1,33},{33,1},{2,34},{34,2},{3,35},{35,3},{4,36},{36... | collective-permute-start | bytes 294920 | tf_op jit(solution)/shard_map/ppermute | solution.py:381
  132.7 1.2 collective-permute-start.17
  135.5 5.3 %copy-start.2 = (bf16[8,160,256]{2,1,0:T(8,128)(2,1)}, bf16[8,160,256]{2,1,0:T(8,128)(2,1)S(1)}, u32[]{:S(2)}) copy-start(bf16[8,160,256]{2,1,0:T(8,128)(2,1)S(1)} %all-to-all-done.3.parts) | copy-start | bytes 1966084
  135.5 10.7 %all-to-all-start.4 = ((f32[8,24,128]{2,1,0:T(8,128)}), f32[8,24,128]{2,1,0:T(8,128)S(1)}, u32[]{:S(2)}, u32[]{:S(2)}) async-start(f32[8,24,128]{2,1,0:T(8,128)} %add.20), calls=%async_computation.4 | async-start | bytes 196608 | tf_op jit(solution)/shard_map/all_to_all | solution.py:447
  146.3 6.0 %collective-permute-start.18 = (f32[256,128]{1,0:T(8,128)S(1)}, f32[256,128]{1,0:T(8,128)S(1)}, u32[]{:S(2)}, u32[]{:S(2)}) collective-permute-start(f32[256,128]{1,0:T(8,128)S(1)} %pad_maximum_fusion), channel_id=1, source_target_pairs={{0,64},{64,0},{128,192},{192,128},{1,65},{65,1},{129,193},{193,129... | collective-permute-start | bytes 393224 | tf_op jit(solution)/shard_map/ppermute | solution.py:451
  146.5 17.8 %all-to-all-start.5 = ((bf16[4,160,256]{2,1,0:T(8,128)(2,1)}), bf16[4,160,256]{2,1,0:T(8,128)(2,1)S(1)}, u32[]{:S(2)}, u32[]{:S(2)}) async-start(bf16[4,160,256]{2,1,0:T(8,128)(2,1)} %shard_map.178), calls=%async_computation.5 | async-start | bytes 655360 | tf_op jit(solution)/shard_map/all_to_all | solution.py:450
  152.3 5.1 %collective-permute-start.19 = (f32[256,128]{1,0:T(8,128)S(1)}, f32[256,128]{1,0:T(8,128)S(1)}, u32[]{:S(2)}, u32[]{:S(2)}) collective-permute-start(f32[256,128]{1,0:T(8,128)S(1)} %fusion), channel_id=1, source_target_pairs={{0,192},{192,0},{64,128},{128,64},{1,193},{193,1},{65,129},{129,65... | collective-permute-start | bytes 393224 | tf_op jit(solution)/shard_map/ppermute | solution.py:452
  157.4 4.4 %copy-start.10 = (f32[256,128]{1,0:T(8,128)}, f32[256,128]{1,0:T(8,128)S(1)}, u32[]{:S(2)}) copy-start(f32[256,128]{1,0:T(8,128)S(1)} %add.23.keep) | copy-start | bytes 393220
  157.4 4.4 %collective-permute-start.20 = (f32[256,128]{1,0:T(8,128)S(1)}, f32[256,128]{1,0:T(8,128)S(1)}, u32[]{:S(2)}, u32[]{:S(2)}) collective-permute-start(f32[256,128]{1,0:T(8,128)S(1)} %add.23.keep), channel_id=1, source_target_pairs={{0,32},{32,0},{1,33},{33,1},{2,34},{34,2},{3,35},{35,3},{4,36},{36... | collective-permute-start | bytes 393224 | tf_op jit(solution)/shard_map/ppermute | solution.py:381
  (5 other events, 3.7 us)
